TPU v7x, 32 devices: a whole 2x2x4 slice. The times are simulated.
32 devices in a mesh: energy: 4 (over x, core), atom: 8 (over z, y).
Axes of the slice: x: 2, y: 2, z: 4, core: 2. Of those that a mesh axis runs over, the one named last changes fastest.
Arguments:
- green_blocks: bfloat16 [32, 16, 16, 1024], P('energy', None, None, 'atom'), may hold values from -6 to 6
- derivative: bfloat16 [16, 16, 16], replicated, may hold values from -0.75 to 0.75
- phonon_weight: float32 [8, 1024], P(None, 'atom'), may hold values from 0.02 to 0.3
- occupation: float32 [8], replicated, may hold values from 0.1 to 3
- mode_shift: int32 [8], replicated, may hold values from 1 to 16, as said below
- neighbours: int32 [1024, 16], P('atom'), may hold values from 0 to 1023, as said below
Outputs:
- self_energy: float32 [32, 16, 16, 1024], P('energy', None, None, 'atom')
Inputs may be any that keep to these rules, and one draw needn't show every extreme that they name: `mode_shift`: shifts rise strictly with the mode; the first is 1 and the last 16. Slabs are runs of 128 consecutive atoms. For every atom, neighbours 0 to 13 lie in its own slab and the last 2 in other slabs. Over the atoms of one slab, at most 74 of these remote neighbours lie in any one other slab; in an order of the other slabs that differs from slab to slab, exactly 74 lie in each of the first 3 slabs, the rest in the next one and none in the others. One slab, drawn anew, receives exactly 74 from every other slab.
All inputs are finite; a program needn't handle non-finite values.
Results may differ from a plain program's by a relative error of at most 0.005.
Values may be sent and summed in bfloat16 or wider, within the bound.
No kernel may reach another device: no remote copies, remote signals or barrier semaphores. Data moves between devices by JAX's collectives and lax.ppermute only.
A program may use at most 64 MiB of HBM per device.

v0:
```python
import jax
import jax.numpy as jnp
from jax import lax
from jax.sharding import PartitionSpec as P

REMOTE_BONDS = 2
LOCAL_BONDS = 14


def sandwich(matrix, block):
    left_product = jnp.einsum(
        "pr,ersn->epsn", matrix, block, preferred_element_type=jnp.float32
    ).astype(jnp.bfloat16)
    return jnp.einsum("epsn,qs->epqn", left_product, matrix, preferred_element_type=jnp.float32)


def place_sum(values, targets, width):
    onehot = (targets[:, None] == lax.iota(jnp.int32, width)[None, :]).astype(jnp.float32)
    return jnp.dot(
        values, onehot, precision=lax.Precision.HIGHEST, preferred_element_type=jnp.float32
    )


def per_device(green_blocks, derivative, phonon_weight, occupation, mode_shift, neighbours):
    energy_rows = green_blocks.shape[0]
    orbital = green_blocks.shape[1]
    atom_rows = green_blocks.shape[3]
    square = orbital * orbital
    flat_green = green_blocks.reshape(energy_rows, square, atom_rows)
    occupied = occupation[:, None]
    couplings = jnp.concatenate(
        [phonon_weight * (occupied + 1.0), phonon_weight * occupied], 0
    ).astype(jnp.bfloat16)
    offsets = jnp.concatenate([mode_shift, -mode_shift])
    own_energy = lax.axis_index("energy") * energy_rows + lax.iota(jnp.int32, energy_rows)
    segment = lax.all_gather(flat_green, "energy", axis=0, tiled=True)
    length = segment.shape[0]
    other_energy = lax.iota(jnp.int32, length)
    distance = own_energy[:, None] - other_energy[None, :]
    matches = (distance[None, :, :] == offsets[:, None, None]).astype(jnp.bfloat16)
    mixing = jnp.dot(
        matches.reshape(offsets.shape[0], energy_rows * length).T,
        couplings,
        preferred_element_type=jnp.float32,
    )
    mixing = mixing.astype(jnp.bfloat16).reshape(energy_rows, length, atom_rows)
    mixed = jnp.einsum("xyb,ynb->xnb", mixing, segment, preferred_element_type=jnp.float32).astype(
        jnp.bfloat16
    )
    mixed_blocks = mixed.reshape(energy_rows, orbital, orbital, atom_rows)
    local_target = neighbours % atom_rows

    def add_bond(column, running):
        bond_term = sandwich(derivative[column], mixed_blocks).reshape(
            energy_rows * square, atom_rows
        )
        return running + place_sum(bond_term, local_target[:, column], atom_rows)

    empty_sum = jnp.zeros((energy_rows * square, atom_rows), jnp.float32)
    local_part = lax.fori_loop(0, LOCAL_BONDS, add_bond, empty_sum)
    peer_count = lax.axis_size("atom")
    remote_ids = neighbours[:, LOCAL_BONDS:].reshape(-1)
    remote_count = remote_ids.shape[0]
    capacity = (2 * remote_count + peer_count - 2) // (peer_count - 1)
    slot_count = peer_count * capacity
    target_slab = remote_ids // atom_rows
    members = (target_slab[:, None] == lax.iota(jnp.int32, peer_count)[None, :]).astype(jnp.int32)
    earlier_count = jnp.sum((jnp.cumsum(members, 0) - members) * members, 1)
    placement = target_slab * capacity + earlier_count
    direction = lax.iota(jnp.int32, remote_count) % REMOTE_BONDS
    labels = (
        jnp.zeros((1, slot_count), jnp.int32)
        .at[0, placement]
        .set(remote_ids % atom_rows * REMOTE_BONDS + direction)
    )
    placement = placement.reshape(atom_rows, REMOTE_BONDS)
    payload = jnp.zeros((energy_rows * square, slot_count), jnp.float32)
    for remote_bond in range(REMOTE_BONDS):
        bond_term = sandwich(derivative[LOCAL_BONDS + remote_bond], mixed_blocks)
        payload = payload.at[:, placement[:, remote_bond]].set(
            bond_term.reshape(energy_rows * square, atom_rows)
        )
    incoming = lax.all_to_all(payload, "atom", split_axis=1, concat_axis=1, tiled=True)
    arrived_labels = lax.all_to_all(labels, "atom", split_axis=1, concat_axis=1, tiled=True)
    incoming, targets = (incoming, arrived_labels[0] // REMOTE_BONDS)
    combined = local_part + place_sum(incoming, targets, atom_rows)
    return combined.reshape(energy_rows, orbital, orbital, atom_rows)


def solution(mesh):
    in_specs = (P("energy", None, None, "atom"), P(), P(None, "atom"), P(), P(), P("atom", None))
    out_specs = P("energy", None, None, "atom")
    return jax.shard_map(
        per_device, mesh=mesh, in_specs=in_specs, out_specs=out_specs, check_vma=False
    )
```

profile of v0, /device:TPU:0, one launch (start us, length us, event | category | flops | bytes accessed | tf_op | source)
XLA Modules:
  0.0 198.7 jit_solution(5795806847927161119)
XLA Ops:
  6.5 2.2 %copy.31 = bf16[8,256,128]{1,0,2:T(8,128)(2,1)} copy(bf16[8,256,128]{2,1,0:T(8,128)(2,1)} %bitcast.96) | data formatting | bytes 1048576 | tf_op jit(solution)/shard_map/reshape | solution.py:29
  11.0 1.4 scatter_custom_fusion.2
  13.1 7.3 %all-to-all-start.1 = ((s32[1,8,74]{2,0,1:T(1,128)}), s32[1,8,74]{2,0,1:T(1,128)S(1)}, u32[]{:S(2)}, u32[]{:S(2)}) async-start(s32[1,8,74]{2,0,1:T(1,128)} %all_to_all.17), calls=%async_computation.1 | async-start | bytes 8192 | tf_op jit(solution)/shard_map/all_to_all | solution.py:84
  25.0 1.8 all-to-all-done.1
  28.1 6.4 %all-gather.2.cloned.1.call-done = bf16[32,256,128]{1,0,2:T(8,128)(2,1)} async-done(((bf16[8,256,128]{1,0,2:T(8,128)(2,1)}), bf16[32,256,128]{1,0,2:T(8,128)(2,1)}) %all-gather.2.cloned.1.call-update) | async-done | bytes 2097168 | tf_op jit(solution)/shard_map/all_gather | solution.py:36
  34.5 2.0 fusion.12
  39.9 1.3 copy.38
  42.2 1.4 copy.41
  43.6 4.4 %scatter_custom_fusion = f32[2048,592]{0,1:T(8,128)} fusion(s32[128]{0:T(128)S(1)} %get-tuple-element.134, f32[]{:T(128)} %constant.94.clone.1, f32[2048,128]{0,1:T(8,128)} %copy.38), kind=kCustom, calls=%fused_computation.18 | custom fusion | bytes 5898244 | tf_op jit(solution)/shard_map/scatter | solution.py:80
  48.0 5.8 %scatter_custom_fusion.1 = f32[2048,592]{0,1:T(8,128)} fusion(f32[2048,592]{0,1:T(8,128)} %scatter_custom_fusion, s32[128]{0:T(128)S(1)} %get-tuple-element.133, f32[2048,128]{0,1:T(8,128)S(1)} %copy-done), kind=kCustom, calls=%fused_computation.27 | custom fusion | bytes 5898240 | tf_op jit(solution)/shard_map/scatter | solution.py:80
  53.8 4.3 %all_to_all.14 = f32[2048,8,74]{0,2,1:T(8,128)} reshape(f32[2048,592]{0,1:T(8,128)} %scatter_custom_fusion.1) | data formatting | bytes 9699328 | tf_op jit(solution)/shard_map/all_to_all | solution.py:83
  58.1 5.5 %all-to-all-start = ((f32[2048,8,74]{0,2,1:T(8,128)}), f32[2048,8,74]{0,2,1:T(8,128)}, u32[]{:S(2)}, u32[]{:S(2)}) async-start(f32[2048,8,74]{0,2,1:T(8,128)} %all_to_all.14), calls=%async_computation | async-start | bytes 10485760 | tf_op jit(solution)/shard_map/all_to_all | solution.py:83
  63.6 43.7 %while.14 = (s32[]{:T(128)}, f32[2048,128]{1,0:T(8,128)S(1)}, bf16[16,16,16]{2,1,0:T(8,128)(2,1)}, bf16[8,16,16,128]{3,1,2,0:T(8,128)(2,1)S(1)}, s32[128,16]{0,1:T(8,128)S(1)}, /*index=5*/s32[]{:T(128)}, s32[]{:T(128)}) while((s32[]{:T(128)}, f32[2048,128]{1,0:T(8,128)S(1)}, bf16[16,16,16]{2,1,0:T(8,128)(2,1)}, ...), condition=%wide.region_1.2_spmd.clone, body=%wide.region_0.1_spmd.clone.sunk | while | flops 420233216 | bytes 5778011 | solution.py:60
  65.6 1.1 convolution_add_fusion.3
  68.7 1.1 convolution_add_fusion.3
  71.8 1.1 convolution_add_fusion.3
  74.9 1.1 convolution_add_fusion.3
  78.1 1.1 convolution_add_fusion.3
  81.2 1.1 convolution_add_fusion.3
  96.8 1.1 convolution_add_fusion.3
  103.1 1.1 convolution_add_fusion.3
  107.3 72.5 %all-to-all-done = f32[2048,8,74]{0,2,1:T(8,128)} async-done(((f32[2048,8,74]{0,2,1:T(8,128)}), f32[2048,8,74]{0,2,1:T(8,128)}, u32[]{:S(2)}, u32[]{:S(2)}) %all-to-all-start) | async-done | bytes 4849696 | tf_op jit(solution)/shard_map/all_to_all | solution.py:83
  179.8 4.3 %all_to_all.16 = f32[2048,592]{0,1:T(8,128)} reshape(f32[2048,8,74]{0,2,1:T(8,128)} %all-to-all-done) | data formatting | bytes 9699328 | tf_op jit(solution)/shard_map/all_to_all | solution.py:83
  184.1 7.8 %convolution_add_fusion.1 = f32[2048,128]{1,0:T(8,128)} fusion(f32[2048,128]{1,0:T(8,128)S(1)} %get-tuple-element.99, f32[2048,592]{0,1:T(8,128)} %all_to_all.16, s32[592]{0:T(1024)S(1)} %add_select_fusion.2), kind=kOutput, calls=%fused_computation.17 | convolution fusion | flops 1862608896 | bytes 6949184 | tf_op jit(solution)/shard_map/dot_general | solution.py:19
  (94 shorter events, 47.1 us)
Async XLA Ops:
  6.5 27.9 %all-gather.2.cloned.1.call-start = ((), (), s32[]{:S(2)}) async-start(), calls=%async_computation.2 | async-start | bytes 2621440 | tf_op jit(solution)/shard_map/all_gather | solution.py:36
  13.1 13.7 %all-to-all-start.1 = ((s32[1,8,74]{2,0,1:T(1,128)}), s32[1,8,74]{2,0,1:T(1,128)S(1)}, u32[]{:S(2)}, u32[]{:S(2)}) async-start(s32[1,8,74]{2,0,1:T(1,128)} %all_to_all.17), calls=%async_computation.1 | async-start | bytes 8192 | tf_op jit(solution)/shard_map/all_to_all | solution.py:84
  43.6 4.4 %copy-start = (f32[2048,128]{0,1:T(8,128)S(1)}, f32[2048,128]{0,1:T(8,128)}, u32[]{:S(2)}) copy-start(f32[2048,128]{0,1:T(8,128)} %copy.41) | copy-start | bytes 3145732
  58.1 121.7 %all-to-all-start = ((f32[2048,8,74]{0,2,1:T(8,128)}), f32[2048,8,74]{0,2,1:T(8,128)}, u32[]{:S(2)}, u32[]{:S(2)}) async-start(f32[2048,8,74]{0,2,1:T(8,128)} %all_to_all.14), calls=%async_computation | async-start | bytes 10485760 | tf_op jit(solution)/shard_map/all_to_all | solution.py:83
Sparse Core Ops, SparseCore 0:
  8.9 25.5 all-gather.1
where the time goes:
time: 200 us; the launch traced here: 199 us
  waiting for transfers between devices  80.7 us (40%)
  matrix products  56.8 us (28%)
  local copies, waits for them, and re-layouts  29.1 us (15%)
  between operations  13.5 us (7%)
  starting transfers between devices  12.8 us (6%)
  other arithmetic  5.14 us (3%)
    all_to_all x1, waiting for transfers between devices, per_device(): lax.all_to_all(payload, 'atom', split_axis=1, concat_axis=1, tiled=True)  72.5 us
    dot_general x15, matrix products, place_sum(): jnp.dot(values, onehot, precision=lax.Precision.HIGHEST, preferred_elemen...  23.8 us
    dot_general x16, matrix products, sandwich(): jnp.einsum('epsn,qs->epqn', left_product, matrix, preferred_element_type=...  15.5 us
    dot_general x16, matrix products, sandwich(): jnp.einsum('pr,ersn->epsn', matrix, block, preferred_element_type=jnp.flo...  15.2 us
    scatter x2, local copies, waits for them, and re-layouts, per_device(): payload.at[:, placement[:, remote_bond]]  10.2 us
    all_to_all x2, local copies, waits for them, and re-layouts, per_device(): lax.all_to_all(payload, 'atom', split_axis=1, concat_axis=1, tiled=True)  8.62 us
    all_to_all x1, starting transfers between devices, per_device(): lax.all_to_all(labels, 'atom', split_axis=1, concat_axis=1, tiled=True)  7.28 us
    all_gather x1, waiting for transfers between devices, per_device(): segment = lax.all_gather(flat_green, 'energy', axis=0, tiled=True)  6.38 us
  transfers between devices with their start and end apart: 3, of which 3 were waited for; matrix products, arithmetic and copies ran while one was open for 26% of the time, Pallas kernels for 0%

commit v1 on v0

v1 whole, which is shorter than its diff:
```python
import functools

import jax
import jax.numpy as jnp
from jax import lax
from jax.experimental import pallas as pl
from jax.experimental.pallas import tpu as pltpu
from jax.sharding import PartitionSpec as P

REMOTE_BONDS = 2
CHUNKS = 2
VMEM_LIMIT = 48 * 1024 * 1024

VMEM = pl.BlockSpec(memory_space=pltpu.VMEM)
SMEM = pl.BlockSpec(memory_space=pltpu.SMEM)
ANY = pl.BlockSpec(memory_space=pl.ANY)


def params():
    return pltpu.CompilerParams(vmem_limit_bytes=VMEM_LIMIT)


def cost(flops, nbytes):
    return pl.CostEstimate(flops=int(flops), bytes_accessed=int(nbytes), transcendentals=0)


def swap(value, axis, mask):
    count = lax.axis_size(axis)
    return lax.ppermute(value, axis, [(i, i ^ mask) for i in range(count)])


def load_pair(own_ref, mate_ref, pair_ref, sems):
    rows = own_ref.shape[0]
    core = lax.axis_index("energy") % 2
    copies = [
        pltpu.make_async_copy(own_ref, pair_ref.at[pl.ds(core * rows, rows)], sems.at[0]),
        pltpu.make_async_copy(mate_ref, pair_ref.at[pl.ds((1 - core) * rows, rows)], sems.at[1]),
    ]
    for copy in copies:
        copy.start()
    for copy in copies:
        copy.wait()


def mix_terms(terms, pair_ref, store):
    square = pair_ref.shape[1]
    step = min(64, square)

    def body(block, carry):
        rows = pl.ds(pl.multiple_of(block * step, step), step)
        total = None
        for slot, weight in terms:
            term = weight * pair_ref[slot, rows, :].astype(jnp.float32)
            total = term if total is None else total + term
        store(rows, total)
        return carry

    lax.fori_loop(0, square // step, body, 0)


def couplings(weight_ref, occupation_ref, mode):
    weight = weight_ref[pl.ds(mode, 1), :]
    occupied = occupation_ref[mode]
    emission = (weight * (occupied + 1.0)).astype(jnp.bfloat16).astype(jnp.float32)
    absorption = (weight * occupied).astype(jnp.bfloat16).astype(jnp.float32)
    return emission, absorption


def clipped(source, base, span, weight):
    slot = source - base
    inside = jnp.logical_and(slot >= 0, slot < span)
    return jnp.clip(slot, 0, span - 1), weight * jnp.where(inside, 1.0, 0.0)


def mix_away_kernel(
    offset, first, shift_ref, occupation_ref, weight_ref, own_ref, mate_ref, out_ref, pair_ref, sems
):
    rows = own_ref.shape[0]
    modes = weight_ref.shape[0]
    me = lax.axis_index("energy")
    base = me // 2 * 2 * rows
    target = me ^ (2 * offset)
    above = target > me
    load_pair(own_ref, mate_ref, pair_ref, sems)
    for row in range(out_ref.shape[0]):
        energy = target * rows + first + row
        terms = []
        for mode in range(modes):
            emission, absorption = couplings(weight_ref, occupation_ref, mode)
            weight = jnp.where(above, emission, absorption)
            shift = shift_ref[mode]
            source = energy + jnp.where(above, -shift, shift)
            terms.append(clipped(source, base, 2 * rows, weight))

        def store(rows_at, total, row=row):
            out_ref[row, rows_at, :] = total.astype(out_ref.dtype)

        mix_terms(terms, pair_ref, store)


def mix_own_kernel(
    shift_ref, occupation_ref, weight_ref, own_ref, mate_ref, *rest
):
    out_refs, (pair_ref, sems) = rest[:-2], rest[-2:]
    rows = own_ref.shape[0]
    modes = weight_ref.shape[0]
    me = lax.axis_index("energy")
    base = me // 2 * 2 * rows
    load_pair(own_ref, mate_ref, pair_ref, sems)
    part = out_refs[0].shape[0]
    for index, out_ref in enumerate(out_refs):
        for row in range(part):
            energy = me * rows + index * part + row
            terms = []
            for mode in range(modes):
                emission, absorption = couplings(weight_ref, occupation_ref, mode)
                shift = shift_ref[mode]
                terms.append(clipped(energy - shift, base, 2 * rows, emission))
                terms.append(clipped(energy + shift, base, 2 * rows, absorption))

            def store(rows_at, total, row=row, out_ref=out_ref):
                out_ref[row, rows_at, :] = total

            mix_terms(terms, pair_ref, store)


def hot(columns, width):
    lanes = lax.broadcasted_iota(jnp.int32, (columns.shape[0], width), 1)
    return jnp.where(columns == lanes, 1.0, 0.0).astype(jnp.bfloat16)


def prepare_kernel(derivative_ref, neighbours_ref, local_k_ref, remote_k_ref, local_hot_ref):
    bonds, orbital, _ = derivative_ref.shape
    square = orbital * orbital
    atoms = neighbours_ref.shape[0]
    local_bonds = bonds - REMOTE_BONDS
    row = lax.broadcasted_iota(jnp.int32, (square, orbital), 0)
    row_of = lax.broadcasted_iota(jnp.int32, (square, orbital), 1)
    column = lax.broadcasted_iota(jnp.int32, (orbital, square), 1)
    column_of = lax.broadcasted_iota(jnp.int32, (orbital, square), 0)

    def pick(condition):
        return jnp.where(condition, 1.0, 0.0).astype(jnp.bfloat16)

    row_high, row_low = pick(row // orbital == row_of), pick(row % orbital == row_of)
    column_high, column_low = pick(column // orbital == column_of), pick(column % orbital == column_of)

    def spread(left, matrix, right):
        wide = jnp.dot(matrix, right, preferred_element_type=jnp.float32).astype(jnp.bfloat16)
        return jnp.dot(left, wide, preferred_element_type=jnp.float32)

    for bond in range(bonds):
        matrix = derivative_ref[bond]
        product = (
            spread(row_high, matrix, column_high) * spread(row_low, matrix, column_low)
        ).astype(jnp.bfloat16)
        if bond < local_bonds:
            local_k_ref[:, bond * square : (bond + 1) * square] = product
        else:
            at = bond - local_bonds
            remote_k_ref[:, at * square : (at + 1) * square] = product
    first = lax.axis_index("atom") * atoms
    for bond in range(local_bonds):
        local_hot_ref[:, bond * atoms : (bond + 1) * atoms] = hot(
            neighbours_ref[:, bond : bond + 1] - first, atoms
        )


def remote_hot_kernel(masks, flip, targets_ref, out_ref):
    bonds = targets_ref.shape[1]
    me = lax.axis_index("atom")
    atoms = out_ref.shape[0] // len(masks)
    for place, mask in enumerate(masks):
        source = me ^ mask
        ids = targets_ref[pl.ds(pl.multiple_of(source * atoms, atoms), atoms), :]
        for which, slab in enumerate((me, me ^ flip)):
            for bond in range(bonds):
                at = (which * bonds + bond) * atoms
                out_ref[place * atoms : (place + 1) * atoms, at : at + atoms] = hot(
                    ids[:, bond : bond + 1] - slab * atoms, atoms
                )


def local_kernel(mixed_ref, hot_ref, k_ref, out_ref, sums_ref):
    rows, square, atoms = mixed_ref.shape
    bonds = hot_ref.shape[1] // atoms
    group = sums_ref.shape[1] // atoms
    for start in range(0, rows, group):
        for inner in range(group):
            summed = jnp.dot(
                mixed_ref[start + inner], hot_ref[...], preferred_element_type=jnp.float32
            ).astype(jnp.bfloat16)
            for bond in range(bonds):
                sums_ref[bond * square : (bond + 1) * square, inner * atoms : (inner + 1) * atoms] = (
                    summed[:, bond * atoms : (bond + 1) * atoms]
                )
        result = jnp.dot(k_ref[...], sums_ref[...], preferred_element_type=jnp.float32)
        for inner in range(group):
            out_ref[start + inner] = result[:, inner * atoms : (inner + 1) * atoms]


def remote_kernel(source_count, *refs):
    source_refs = refs[:source_count]
    hot_ref, k_ref, local_ref, out_ref, away_ref = refs[source_count:]
    rows, square, atoms = local_ref.shape
    bonds = k_ref.shape[1] // square
    for row in range(rows):
        sources = jnp.concatenate([ref[row] for ref in source_refs], axis=1)
        summed = jnp.dot(sources, hot_ref[...], preferred_element_type=jnp.float32).astype(
            jnp.bfloat16
        )
        stacked = jnp.concatenate(
            [
                jnp.concatenate(
                    [
                        summed[:, (which * bonds + bond) * atoms : (which * bonds + bond + 1) * atoms]
                        for which in range(2)
                    ],
                    axis=1,
                )
                for bond in range(bonds)
            ],
            axis=0,
        )
        result = jnp.dot(k_ref[...], stacked, preferred_element_type=jnp.float32)
        out_ref[row] = result[:, :atoms] + local_ref[row]
        away_ref[row] = result[:, atoms:].astype(away_ref.dtype)


def per_device(green_blocks, derivative, phonon_weight, occupation, mode_shift, neighbours):
    rows, orbital, _, atoms = green_blocks.shape
    square = orbital * orbital
    bonds = derivative.shape[0]
    local_bonds = bonds - REMOTE_BONDS
    pairs = lax.axis_size("energy") // 2
    slabs = lax.axis_size("atom")
    flip = 2
    high = [4 * i for i in range(slabs // 4)]
    masks = high + [mask ^ 1 for mask in high]
    chunks = min(CHUNKS, rows)
    part = rows // chunks
    green = green_blocks.reshape(rows, square, atoms)
    block = jax.ShapeDtypeStruct((part, square, atoms), jnp.bfloat16)
    wide_block = jax.ShapeDtypeStruct((part, square, atoms), jnp.float32)
    pair_scratch = [
        pltpu.VMEM((2 * rows, square, atoms), jnp.bfloat16),
        pltpu.SemaphoreType.DMA((2,)),
    ]

    targets = lax.all_gather(neighbours[:, local_bonds:], "atom", axis=0, tiled=True)
    mate = swap(green, "energy", 1)

    local_k, remote_k, local_hot = pl.pallas_call(
        prepare_kernel,
        out_shape=(
            jax.ShapeDtypeStruct((square, local_bonds * square), jnp.bfloat16),
            jax.ShapeDtypeStruct((square, REMOTE_BONDS * square), jnp.bfloat16),
            jax.ShapeDtypeStruct((atoms, local_bonds * atoms), jnp.bfloat16),
        ),
        in_specs=[VMEM, VMEM],
        out_specs=(VMEM, VMEM, VMEM),
        compiler_params=params(),
        cost_estimate=cost(2e9, 3e6),
    )(derivative, neighbours)
    remote_hot = pl.pallas_call(
        functools.partial(remote_hot_kernel, masks, flip),
        out_shape=jax.ShapeDtypeStruct(
            (len(masks) * atoms, 2 * REMOTE_BONDS * atoms), jnp.bfloat16
        ),
        in_specs=[VMEM],
        out_specs=VMEM,
        compiler_params=params(),
        cost_estimate=cost(1e8, 1e6),
    )(targets)

    mix_in_specs = [SMEM, SMEM, VMEM, ANY, ANY]
    mix_args = (mode_shift, occupation, phonon_weight, green, mate)

    arrived = []
    for chunk in range(chunks):
        received = []
        for offset in range(1, pairs):
            away = pl.pallas_call(
                functools.partial(mix_away_kernel, offset, chunk * part),
                out_shape=block,
                in_specs=mix_in_specs,
                out_specs=VMEM,
                scratch_shapes=pair_scratch,
                compiler_params=params(),
                cost_estimate=cost(1e9, 2e6),
            )(*mix_args)
            received.append(swap(away, "energy", 2 * offset))
        arrived.append(received)
    own = pl.pallas_call(
        mix_own_kernel,
        out_shape=(wide_block,) * chunks,
        in_specs=mix_in_specs,
        out_specs=(VMEM,) * chunks,
        scratch_shapes=pair_scratch,
        compiler_params=params(),
        cost_estimate=cost(2e9, 2e6),
    )(*mix_args)

    results = []
    for chunk in range(chunks):
        total = own[chunk]
        for received in arrived[chunk]:
            total = total + received.astype(jnp.float32)
        mixed = total.astype(jnp.bfloat16)
        across = [mixed] + [swap(mixed, "atom", mask) for mask in high[1:]]
        sources = across + [swap(value, "atom", 1) for value in across]
        local = pl.pallas_call(
            local_kernel,
            out_shape=wide_block,
            in_specs=[VMEM] * 3,
            out_specs=VMEM,
            scratch_shapes=[
                pltpu.VMEM((local_bonds * square, min(2, part) * atoms), jnp.bfloat16)
            ],
            compiler_params=params(),
            cost_estimate=cost(2e9, 3e6),
        )(mixed, local_hot, local_k)
        partial, away = pl.pallas_call(
            functools.partial(remote_kernel, len(sources)),
            out_shape=(wide_block, block),
            in_specs=[VMEM] * (len(sources) + 3),
            out_specs=(VMEM, VMEM),
            compiler_params=params(),
            cost_estimate=cost(1e9, 3e6),
        )(*sources, remote_hot, remote_k, local)
        results.append((partial, swap(away, "atom", flip)))
    combined = jnp.concatenate(
        [partial + received.astype(jnp.float32) for partial, received in results], 0
    )
    return combined.reshape(rows, orbital, orbital, atoms)


def solution(mesh):
    in_specs = (P("energy", None, None, "atom"), P(), P(None, "atom"), P(), P(), P("atom", None))
    out_specs = P("energy", None, None, "atom")
    return jax.shard_map(
        per_device, mesh=mesh, in_specs=in_specs, out_specs=out_specs, check_vma=False
    )
```

time: 200 us -> 93.4 us (0.47)
  waiting for transfers between devices: 80.7 us -> 21.4 us
  matrix products: 56.8 us -> 0 us
  blocking collectives: 0 us -> 31.6 us
  local copies, waits for them, and re-layouts: 29.1 us -> 3.23 us
  Pallas kernels: 0 us -> 18.6 us
  between operations: 13.5 us -> 0.15 us
  starting transfers between devices: 12.8 us -> 17 us
  other arithmetic: 5.14 us -> 1.24 us
    all_to_all x2 -> x0, waiting for transfers between devices: 74.3 us -> none  [the longest x1 72.5 us: per_device(): lax.all_to_all(payload, 'atom', split_axis=1, concat_axis=1, tiled=True)]
    dot_general x49 -> x0, matrix products: 56.8 us -> none  [the longest x15 23.8 us: place_sum(): jnp.dot(values, onehot, precision=lax.Precision.HIGHEST, preferred_elemen...]
    all_gather x0 -> x1, blocking collectives: none -> 31.6 us  [per_device(): lax.all_gather(neighbours[:, local_bonds:], 'atom', axis=0, tiled=True)]
    ppermute x0 -> x11, waiting for transfers between devices: none -> 21.4 us  [swap(): return lax.ppermute(value, axis, [(i, i ^ mask) for i in range(count)])]
    pallas_call x0 -> x9, Pallas kernels: none -> 18.6 us  [the longest x2 5.55 us: per_device(): pl.pallas_call(local_kernel, out_shape=wide_block, in_specs=[VMEM] * 3, o...]
    ppermute x0 -> x11, starting transfers between devices: none -> 17 us  [swap(): return lax.ppermute(value, axis, [(i, i ^ mask) for i in range(count)])]
    all_to_all x2 -> x0, starting transfers between devices: 12.8 us -> none  [the longest x1 7.28 us: per_device(): lax.all_to_all(labels, 'atom', split_axis=1, concat_axis=1, tiled=True)]
    scatter x3 -> x0, local copies, waits for them, and re-layouts: 11.6 us -> none  [the longest x2 10.2 us: per_device(): payload.at[:, placement[:, remote_bond]]]
  transfers between devices with their start and end apart: 3 -> 11, of which waited for: 3 -> 5; matrix products, arithmetic and copies ran while one was open for 26% -> 0% of each run, Pallas kernels for 0% -> 19%
where the time goes in v1:
time: 93.4 us; the launch traced here: 93.2 us
  blocking collectives  31.6 us (34%)
  waiting for transfers between devices  21.4 us (23%)
  Pallas kernels  18.6 us (20%)
  starting transfers between devices  17 us (18%)
  local copies, waits for them, and re-layouts  3.23 us (3%)
  other arithmetic  1.24 us (1%)
    all_gather x1, blocking collectives, per_device(): lax.all_gather(neighbours[:, local_bonds:], 'atom', axis=0, tiled=True)  31.6 us
    ppermute x11, waiting for transfers between devices, swap(): return lax.ppermute(value, axis, [(i, i ^ mask) for i in range(count)])  21.4 us
    ppermute x11, starting transfers between devices, swap(): return lax.ppermute(value, axis, [(i, i ^ mask) for i in range(count)])  17 us
    pallas_call x2, Pallas kernels, per_device(): pl.pallas_call(local_kernel, out_shape=wide_block, in_specs=[VMEM] * 3, o...  5.55 us
    pallas_call x2, Pallas kernels, per_device(): pl.pallas_call(functools.partial(remote_kernel, len(sources)), out_shape=...  3.57 us
    pallas_call x1, Pallas kernels, per_device(): pl.pallas_call(prepare_kernel, out_shape=(jax.ShapeDtypeStruct((square, l...  3.36 us
    pallas_call x1, Pallas kernels, per_device(): pl.pallas_call(mix_own_kernel, out_shape=(wide_block,) * chunks, in_specs...  3.16 us
    unnamed x13, local copies, waits for them, and re-layouts  3.15 us
  transfers between devices with their start and end apart: 11, of which 5 were waited for; matrix products, arithmetic and copies ran while one was open for 0% of the time, Pallas kernels for 19%

profile of v1, /device:TPU:0, one launch (start us, length us, event | category | flops | bytes accessed | tf_op | source)
XLA Modules:
  0.0 93.2 jit_solution(16271769786538458915)
XLA Ops:
  0.5 1.7 %collective-permute-done.mate_ref = bf16[8,256,128]{2,1,0:T(8,128)(2,1)S(1)} collective-permute-done((bf16[8,256,128]{2,1,0:T(8,128)(2,1)}, bf16[8,256,128]{2,1,0:T(8,128)(2,1)S(1)}, u32[]{:S(2)}, u32[]{:S(2)}) %collective-permute-start) | collective-permute-done | bytes 524320 | tf_op jit(solution)/shard_map/ppermute | solution.py:29
  2.2 1.0 %copy-done = bf16[8,16,16,128]{3,2,1,0:T(8,128)(2,1)S(1)} copy-done((bf16[8,16,16,128]{3,2,1,0:T(8,128)(2,1)S(1)}, bf16[8,16,16,128]{3,2,1,0:T(8,128)(2,1)}, u32[]{:S(2)}) %copy-start) | copy-done | bytes 524312
  3.2 0.7 copy-done.2
  3.9 0.7 copy-done.3
  5.2 1.3 %shard_map.65 = bf16[4,256,128]{2,1,0:T(8,128)(2,1)S(1)} custom-call(s32[8]{0:T(128)S(1)} %copy-done.3, f32[8]{0:T(128)S(1)} %copy-done.4, f32[8,128]{1,0:T(8,128)S(1)} %copy-done.2, bf16[8,256,128]{2,1,0:T(8,128)(2,1)S(1)} %bitcast.3, bf16[8,256,128]{2,1,0:T(8,128)(2,1)S(1)} %collective-permute-done.mate_ref), custom_call_target="tpu_custom_call" | custom-call | flops 1000000000 | bytes 2000000 | tf_op jit(solution)/shard_map/pallas_call | solution.py:283
  6.6 2.9 %collective-permute-start.1 = (bf16[4,256,128]{2,1,0:T(8,128)(2,1)S(1)}, bf16[4,256,128]{2,1,0:T(8,128)(2,1)S(1)}, u32[]{:S(2)}, u32[]{:S(2)}) collective-permute-start(bf16[4,256,128]{2,1,0:T(8,128)(2,1)S(1)} %shard_map.65), channel_id=1, source_target_pairs={{0,16},{8,24},{16,0},{24,8},{1,17},{9,25},{17,1},{25,9},{2,18},{10... | collective-permute-start | bytes 786440 | tf_op jit(solution)/shard_map/ppermute | solution.py:29
  9.5 1.3 %shard_map.70 = bf16[4,256,128]{2,1,0:T(8,128)(2,1)S(1)} custom-call(s32[8]{0:T(128)S(1)} %copy-done.3, f32[8]{0:T(128)S(1)} %copy-done.4, f32[8,128]{1,0:T(8,128)S(1)} %copy-done.2, bf16[8,256,128]{2,1,0:T(8,128)(2,1)S(1)} %bitcast.4, bf16[8,256,128]{2,1,0:T(8,128)(2,1)S(1)} %collective-permute-done.mate_ref), custom_call_target="tpu_custom_call" | custom-call | flops 1000000000 | bytes 2000000 | tf_op jit(solution)/shard_map/pallas_call | solution.py:283
  10.9 3.2 %shard_map.64 = (f32[4,256,128]{2,1,0:T(8,128)S(1)}, f32[4,256,128]{2,1,0:T(8,128)S(1)}) custom-call(s32[8]{0:T(128)S(1)} %copy-done.3, f32[8]{0:T(128)S(1)} %copy-done.4, f32[8,128]{1,0:T(8,128)S(1)} %copy-done.2, bf16[8,256,128]{2,1,0:T(8,128)(2,1)S(1)} %bitcast.5, bf16[8,256,128]{2,1,0:T(8,128)(2,1)S(1)} %collective-permute-done.mate_ref), custom_call_target="tpu_custom_call" | custom-call | flops 2000000000 | bytes 2000000 | tf_op jit(solution)/shard_map/pallas_call | solution.py:294
  14.1 2.5 %collective-permute-done.1 = bf16[4,256,128]{2,1,0:T(8,128)(2,1)S(1)} collective-permute-done((bf16[4,256,128]{2,1,0:T(8,128)(2,1)S(1)}, bf16[4,256,128]{2,1,0:T(8,128)(2,1)S(1)}, u32[]{:S(2)}, u32[]{:S(2)}) %collective-permute-start.1) | collective-permute-done | bytes 262176 | tf_op jit(solution)/shard_map/ppermute | solution.py:29
  16.6 3.2 %collective-permute-start.2 = (bf16[4,256,128]{2,1,0:T(8,128)(2,1)S(1)}, bf16[4,256,128]{2,1,0:T(8,128)(2,1)S(1)}, u32[]{:S(2)}, u32[]{:S(2)}) collective-permute-start(bf16[4,256,128]{2,1,0:T(8,128)(2,1)S(1)} %add_convert_fusion.1.mixed_ref.refs_0_), channel_id=1, source_target_pairs={{0,4},{1,5},{2,6},{3,7},{4,0},{5,1},{6,2},{7,3},{8,12},{9,13},{10,... | collective-permute-start | bytes 786440 | tf_op jit(solution)/shard_map/ppermute | solution.py:29
  20.0 1.6 %collective-permute-start.3 = (bf16[4,256,128]{2,1,0:T(8,128)(2,1)S(1)}, bf16[4,256,128]{2,1,0:T(8,128)(2,1)S(1)}, u32[]{:S(2)}, u32[]{:S(2)}) collective-permute-start(bf16[4,256,128]{2,1,0:T(8,128)(2,1)S(1)} %add_convert_fusion.1.mixed_ref.refs_0_), channel_id=1, source_target_pairs={{0,1},{1,0},{2,3},{3,2},{4,5},{5,4},{6,7},{7,6},{8,9},{9,8},{10,11... | collective-permute-start | bytes 786440 | tf_op jit(solution)/shard_map/ppermute | solution.py:29
  21.8 2.9 %collective-permute-start.7 = (bf16[4,256,128]{2,1,0:T(8,128)(2,1)S(1)}, bf16[4,256,128]{2,1,0:T(8,128)(2,1)S(1)}, u32[]{:S(2)}, u32[]{:S(2)}) collective-permute-start(bf16[4,256,128]{2,1,0:T(8,128)(2,1)S(1)} %add_convert_fusion.mixed_ref.refs_0_), channel_id=1, source_target_pairs={{0,4},{1,5},{2,6},{3,7},{4,0},{5,1},{6,2},{7,3},{8,12},{9,13},{10,... | collective-permute-start | bytes 786440 | tf_op jit(solution)/shard_map/ppermute | solution.py:29
  24.7 12.6 %collective-permute-done.2.refs_1_ = bf16[4,256,128]{2,1,0:T(8,128)(2,1)S(1)} collective-permute-done((bf16[4,256,128]{2,1,0:T(8,128)(2,1)S(1)}, bf16[4,256,128]{2,1,0:T(8,128)(2,1)S(1)}, u32[]{:S(2)}, u32[]{:S(2)}) %collective-permute-start.2) | collective-permute-done | bytes 262176 | tf_op jit(solution)/shard_map/ppermute | solution.py:29
  37.3 1.5 %collective-permute-start.4 = (bf16[4,256,128]{2,1,0:T(8,128)(2,1)S(1)}, bf16[4,256,128]{2,1,0:T(8,128)(2,1)S(1)}, u32[]{:S(2)}, u32[]{:S(2)}) collective-permute-start(bf16[4,256,128]{2,1,0:T(8,128)(2,1)S(1)} %collective-permute-done.2.refs_1_), channel_id=1, source_target_pairs={{0,1},{1,0},{2,3},{3,2},{4,5},{5,4},{6,7},{7,6},{8,9},{9,8},{10,11... | collective-permute-start | bytes 786440 | tf_op jit(solution)/shard_map/ppermute | solution.py:29
  38.8 3.4 %shard_map.67 = (bf16[256,3584]{1,0:T(8,128)(2,1)S(1)}, bf16[256,512]{1,0:T(8,128)(2,1)S(1)}, bf16[128,1792]{1,0:T(8,128)(2,1)S(1)}) custom-call(bf16[16,16,16]{2,1,0:T(8,128)(2,1)S(1)} %copy-done.1, s32[128,16]{1,0:T(8,128)S(1)} %copy.7.neighbours_ref), custom_call_target="tpu_custom_call" | custom-call | flops 2000000000 | bytes 3000000 | tf_op jit(solution)/shard_map/pallas_call | solution.py:253
  42.3 31.6 %all_gather.3.targets_ref = s32[1024,2]{1,0:T(8,128)S(1)} all-gather(s32[128,2]{1,0:T(8,128)S(1)} %slice.4), channel_id=1, replica_groups=mesh['energy'=4,'atom'=8] {'atom'}, dimensions={0}, use_global_device_ids=true | all-gather | bytes 9216 | tf_op jit(solution)/shard_map/all_gather | solution.py:250
  74.3 2.8 %shard_map.68.refs_6_ = f32[4,256,128]{2,1,0:T(8,128)S(1)} custom-call(bf16[4,256,128]{2,1,0:T(8,128)(2,1)S(1)} %add_convert_fusion.1.mixed_ref.refs_0_, bf16[128,1792]{1,0:T(8,128)(2,1)S(1)} %get-tuple-element.16.hot_ref, bf16[256,3584]{1,0:T(8,128)(2,1)S(1)} %get-tuple-element.17.k_ref), custom_call_target="tpu_custom_call" | custom-call | flops 2000000000 | bytes 3000000 | tf_op jit(solution)/shard_map/pallas_call | solution.py:312
  77.1 2.1 %collective-permute-start.9 = (bf16[4,256,128]{2,1,0:T(8,128)(2,1)S(1)}, bf16[4,256,128]{2,1,0:T(8,128)(2,1)S(1)}, u32[]{:S(2)}, u32[]{:S(2)}) collective-permute-start(bf16[4,256,128]{2,1,0:T(8,128)(2,1)S(1)} %collective-permute-done.7.refs_1_), channel_id=1, source_target_pairs={{0,1},{1,0},{2,3},{3,2},{4,5},{5,4},{6,7},{7,6},{8,9},{9,8},{10,11... | collective-permute-start | bytes 786440 | tf_op jit(solution)/shard_map/ppermute | solution.py:29
  79.2 1.8 %shard_map.69 = (f32[4,256,128]{2,1,0:T(8,128)S(1)}, bf16[4,256,128]{2,1,0:T(8,128)(2,1)S(1)}) custom-call(bf16[4,256,128]{2,1,0:T(8,128)(2,1)S(1)} %add_convert_fusion.1.mixed_ref.refs_0_, bf16[4,256,128]{2,1,0:T(8,128)(2,1)S(1)} %collective-permute-done.2.refs_1_, bf16[4,256,128]{2,1,0:T(8,128)(2,1)S(1)} %collective-permute-done.3.refs_2_, ...), custom_call_target="tpu_custom_call" | custom-call | flops 1000000000 | bytes 3000000 | tf_op jit(solution)/shard_map/pallas_call | solution.py:323
  81.1 2.8 %shard_map.71.refs_6_ = f32[4,256,128]{2,1,0:T(8,128)S(1)} custom-call(bf16[4,256,128]{2,1,0:T(8,128)(2,1)S(1)} %add_convert_fusion.mixed_ref.refs_0_, bf16[128,1792]{1,0:T(8,128)(2,1)S(1)} %get-tuple-element.16.hot_ref, bf16[256,3584]{1,0:T(8,128)(2,1)S(1)} %get-tuple-element.17.k_ref), custom_call_target="tpu_custom_call" | custom-call | flops 2000000000 | bytes 3000000 | tf_op jit(solution)/shard_map/pallas_call | solution.py:312
  83.9 1.8 %shard_map.72 = (f32[4,256,128]{2,1,0:T(8,128)S(1)}, bf16[4,256,128]{2,1,0:T(8,128)(2,1)S(1)}) custom-call(bf16[4,256,128]{2,1,0:T(8,128)(2,1)S(1)} %add_convert_fusion.mixed_ref.refs_0_, bf16[4,256,128]{2,1,0:T(8,128)(2,1)S(1)} %collective-permute-done.7.refs_1_, bf16[4,256,128]{2,1,0:T(8,128)(2,1)S(1)} %collective-permute-done.8.refs_2_, ...), custom_call_target="tpu_custom_call" | custom-call | flops 1000000000 | bytes 3000000 | tf_op jit(solution)/shard_map/pallas_call | solution.py:323
  85.7 2.1 %collective-permute-start.10 = (bf16[4,256,128]{2,1,0:T(8,128)(2,1)S(1)}, bf16[4,256,128]{2,1,0:T(8,128)(2,1)S(1)}, u32[]{:S(2)}, u32[]{:S(2)}) collective-permute-start(bf16[4,256,128]{2,1,0:T(8,128)(2,1)S(1)} %get-tuple-element.22), channel_id=1, source_target_pairs={{0,2},{1,3},{2,0},{3,1},{4,6},{5,7},{6,4},{7,5},{8,10},{9,11},{10,... | collective-permute-start | bytes 786440 | tf_op jit(solution)/shard_map/ppermute | solution.py:29
  87.8 4.3 %collective-permute-done.10 = bf16[4,256,128]{2,1,0:T(8,128)(2,1)S(1)} collective-permute-done((bf16[4,256,128]{2,1,0:T(8,128)(2,1)S(1)}, bf16[4,256,128]{2,1,0:T(8,128)(2,1)S(1)}, u32[]{:S(2)}, u32[]{:S(2)}) %collective-permute-start.10) | collective-permute-done | bytes 262176 | tf_op jit(solution)/shard_map/ppermute | solution.py:29
  92.2 1.0 %pad_maximum_fusion = f32[8,256,128]{2,1,0:T(8,128)} fusion(f32[4,256,128]{2,1,0:T(8,128)S(1)} %convert_add_fusion, f32[4,256,128]{2,1,0:T(8,128)S(1)} %convert_add_fusion.1), kind=kLoop, calls=%fused_computation | loop fusion | flops 262144 | bytes 2097152 | tf_op jit(solution)/shard_map/concatenate | solution.py:332
  (27 shorter events, 2.3 us)
Async XLA Ops:
  0.0 2.2 %collective-permute-start = (bf16[8,256,128]{2,1,0:T(8,128)(2,1)}, bf16[8,256,128]{2,1,0:T(8,128)(2,1)S(1)}, u32[]{:S(2)}, u32[]{:S(2)}) collective-permute-start(bf16[8,256,128]{2,1,0:T(8,128)(2,1)} %bitcast.2), channel_id=1, source_target_pairs={{0,8},{8,0},{16,24},{24,16},{1,9},{9,1},{17,25},{25,17},{2,10},{10... | collective-permute-start | bytes 1572872 | tf_op jit(solution)/shard_map/ppermute | solution.py:29
  2.2 1.0 %copy-start = (bf16[8,16,16,128]{3,2,1,0:T(8,128)(2,1)S(1)}, bf16[8,16,16,128]{3,2,1,0:T(8,128)(2,1)}, u32[]{:S(2)}) copy-start(bf16[8,16,16,128]{3,2,1,0:T(8,128)(2,1)} %param.6) | copy-start | bytes 1572868
  3.2 0.7 copy-start.2
  3.9 0.7 copy-start.3
  4.6 0.7 copy-start.4
  6.6 10.0 %collective-permute-start.1 = (bf16[4,256,128]{2,1,0:T(8,128)(2,1)S(1)}, bf16[4,256,128]{2,1,0:T(8,128)(2,1)S(1)}, u32[]{:S(2)}, u32[]{:S(2)}) collective-permute-start(bf16[4,256,128]{2,1,0:T(8,128)(2,1)S(1)} %shard_map.65), channel_id=1, source_target_pairs={{0,16},{8,24},{16,0},{24,8},{1,17},{9,25},{17,1},{25,9},{2,18},{10... | collective-permute-start | bytes 786440 | tf_op jit(solution)/shard_map/ppermute | solution.py:29
  10.8 9.1 %copy-start.5 = (s32[128,16]{0,1:T(8,128)S(1)}, s32[128,16]{0,1:T(8,128)}, u32[]{:S(2)}) copy-start(s32[128,16]{0,1:T(8,128)} %param.11) | copy-start | bytes 24580
  10.8 10.9 %collective-permute-start.6 = (bf16[4,256,128]{2,1,0:T(8,128)(2,1)S(1)}, bf16[4,256,128]{2,1,0:T(8,128)(2,1)S(1)}, u32[]{:S(2)}, u32[]{:S(2)}) collective-permute-start(bf16[4,256,128]{2,1,0:T(8,128)(2,1)S(1)} %shard_map.70), channel_id=1, source_target_pairs={{0,16},{8,24},{16,0},{24,8},{1,17},{9,25},{17,1},{25,9},{2,18},{10... | collective-permute-start | bytes 786440 | tf_op jit(solution)/shard_map/ppermute | solution.py:29
  14.1 24.8 %copy-start.1 = (bf16[16,16,16]{2,1,0:T(8,128)(2,1)S(1)}, bf16[16,16,16]{2,1,0:T(8,128)(2,1)}, u32[]{:S(2)}) copy-start(bf16[16,16,16]{2,1,0:T(8,128)(2,1)} %derivative_ref.1) | copy-start | bytes 24580
  16.6 20.7 %collective-permute-start.2 = (bf16[4,256,128]{2,1,0:T(8,128)(2,1)S(1)}, bf16[4,256,128]{2,1,0:T(8,128)(2,1)S(1)}, u32[]{:S(2)}, u32[]{:S(2)}) collective-permute-start(bf16[4,256,128]{2,1,0:T(8,128)(2,1)S(1)} %add_convert_fusion.1.mixed_ref.refs_0_), channel_id=1, source_target_pairs={{0,4},{1,5},{2,6},{3,7},{4,0},{5,1},{6,2},{7,3},{8,12},{9,13},{10,... | collective-permute-start | bytes 786440 | tf_op jit(solution)/shard_map/ppermute | solution.py:29
  20.0 59.3 %collective-permute-start.3 = (bf16[4,256,128]{2,1,0:T(8,128)(2,1)S(1)}, bf16[4,256,128]{2,1,0:T(8,128)(2,1)S(1)}, u32[]{:S(2)}, u32[]{:S(2)}) collective-permute-start(bf16[4,256,128]{2,1,0:T(8,128)(2,1)S(1)} %add_convert_fusion.1.mixed_ref.refs_0_), channel_id=1, source_target_pairs={{0,1},{1,0},{2,3},{3,2},{4,5},{5,4},{6,7},{7,6},{8,9},{9,8},{10,11... | collective-permute-start | bytes 786440 | tf_op jit(solution)/shard_map/ppermute | solution.py:29
  21.8 55.4 %collective-permute-start.7 = (bf16[4,256,128]{2,1,0:T(8,128)(2,1)S(1)}, bf16[4,256,128]{2,1,0:T(8,128)(2,1)S(1)}, u32[]{:S(2)}, u32[]{:S(2)}) collective-permute-start(bf16[4,256,128]{2,1,0:T(8,128)(2,1)S(1)} %add_convert_fusion.mixed_ref.refs_0_), channel_id=1, source_target_pairs={{0,4},{1,5},{2,6},{3,7},{4,0},{5,1},{6,2},{7,3},{8,12},{9,13},{10,... | collective-permute-start | bytes 786440 | tf_op jit(solution)/shard_map/ppermute | solution.py:29
  37.3 41.9 %collective-permute-start.4 = (bf16[4,256,128]{2,1,0:T(8,128)(2,1)S(1)}, bf16[4,256,128]{2,1,0:T(8,128)(2,1)S(1)}, u32[]{:S(2)}, u32[]{:S(2)}) collective-permute-start(bf16[4,256,128]{2,1,0:T(8,128)(2,1)S(1)} %collective-permute-done.2.refs_1_), channel_id=1, source_target_pairs={{0,1},{1,0},{2,3},{3,2},{4,5},{5,4},{6,7},{7,6},{8,9},{9,8},{10,11... | collective-permute-start | bytes 786440 | tf_op jit(solution)/shard_map/ppermute | solution.py:29
  74.3 9.6 %collective-permute-start.8 = (bf16[4,256,128]{2,1,0:T(8,128)(2,1)S(1)}, bf16[4,256,128]{2,1,0:T(8,128)(2,1)S(1)}, u32[]{:S(2)}, u32[]{:S(2)}) collective-permute-start(bf16[4,256,128]{2,1,0:T(8,128)(2,1)S(1)} %add_convert_fusion.mixed_ref.refs_0_), channel_id=1, source_target_pairs={{0,1},{1,0},{2,3},{3,2},{4,5},{5,4},{6,7},{7,6},{8,9},{9,8},{10,11... | collective-permute-start | bytes 786440 | tf_op jit(solution)/shard_map/ppermute | solution.py:29
  77.1 6.7 %collective-permute-start.9 = (bf16[4,256,128]{2,1,0:T(8,128)(2,1)S(1)}, bf16[4,256,128]{2,1,0:T(8,128)(2,1)S(1)}, u32[]{:S(2)}, u32[]{:S(2)}) collective-permute-start(bf16[4,256,128]{2,1,0:T(8,128)(2,1)S(1)} %collective-permute-done.7.refs_1_), channel_id=1, source_target_pairs={{0,1},{1,0},{2,3},{3,2},{4,5},{5,4},{6,7},{7,6},{8,9},{9,8},{10,11... | collective-permute-start | bytes 786440 | tf_op jit(solution)/shard_map/ppermute | solution.py:29
  81.0 6.8 %collective-permute-start.5 = (bf16[4,256,128]{2,1,0:T(8,128)(2,1)S(1)}, bf16[4,256,128]{2,1,0:T(8,128)(2,1)S(1)}, u32[]{:S(2)}, u32[]{:S(2)}) collective-permute-start(bf16[4,256,128]{2,1,0:T(8,128)(2,1)S(1)} %get-tuple-element.19), channel_id=1, source_target_pairs={{0,2},{1,3},{2,0},{3,1},{4,6},{5,7},{6,4},{7,5},{8,10},{9,11},{10,... | collective-permute-start | bytes 786440 | tf_op jit(solution)/shard_map/ppermute | solution.py:29
  85.7 6.4 %collective-permute-start.10 = (bf16[4,256,128]{2,1,0:T(8,128)(2,1)S(1)}, bf16[4,256,128]{2,1,0:T(8,128)(2,1)S(1)}, u32[]{:S(2)}, u32[]{:S(2)}) collective-permute-start(bf16[4,256,128]{2,1,0:T(8,128)(2,1)S(1)} %get-tuple-element.22), channel_id=1, source_target_pairs={{0,2},{1,3},{2,0},{3,1},{4,6},{5,7},{6,4},{7,5},{8,10},{9,11},{10,... | collective-permute-start | bytes 786440 | tf_op jit(solution)/shard_map/ppermute | solution.py:29

commit v2 on v0

v2 whole, which is shorter than its diff:
```python
import functools

import jax
import jax.numpy as jnp
from jax import lax
from jax.experimental import pallas as pl
from jax.experimental.pallas import tpu as pltpu
from jax.sharding import PartitionSpec as P

REMOTE_BONDS = 2
CHUNKS = 2
ID_ROWS = 16
COST = 1.0
SUBLANES = 8
VMEM_LIMIT = 48 * 1024 * 1024

VMEM = pl.BlockSpec(memory_space=pltpu.VMEM)
HBM = pl.BlockSpec(memory_space=pltpu.HBM)
ANY = pl.BlockSpec(memory_space=pl.ANY)
F32, BF16 = jnp.float32, jnp.bfloat16


def params():
    return pltpu.CompilerParams(vmem_limit_bytes=VMEM_LIMIT)


def cost(flops, nbytes):
    return pl.CostEstimate(flops=int(flops * COST), bytes_accessed=int(nbytes * COST), transcendentals=0)


def swap(value, axis, mask):
    count = lax.axis_size(axis)
    return lax.ppermute(value, axis, [(i, i ^ mask) for i in range(count)])


def dot(left, right):
    return jnp.dot(left, right, preferred_element_type=F32)


def dot_nt(left, right):
    return lax.dot_general(left, right, (((1,), (1,)), ((), ())), preferred_element_type=F32)


def table_kernel(
    shift_hbm, occupation_hbm, weight_hbm, table_ref, shift_ref, occupation_ref, weight_ref, sems
):
    groups, rows, spare = table_ref.shape[:3]
    span = spare - 1
    modes = weight_ref.shape[0]
    copies = [
        pltpu.make_async_copy(shift_hbm, shift_ref, sems.at[0]),
        pltpu.make_async_copy(occupation_hbm, occupation_ref, sems.at[1]),
        pltpu.make_async_copy(weight_hbm, weight_ref, sems.at[2]),
    ]
    for copy in copies:
        copy.start()
    table_ref[...] = jnp.zeros_like(table_ref)
    for copy in copies:
        copy.wait()
    me = lax.axis_index("energy")
    base = me // 2 * span

    def put(group, row, source, value):
        slot = source - base
        inside = jnp.logical_and(slot >= 0, slot < span)
        table_ref[group, row, jnp.where(inside, slot, span)] = value

    for mode in range(modes):
        shift = shift_ref[mode]
        occupied = occupation_ref[mode]
        weight = jnp.broadcast_to(weight_ref[mode : mode + 1, :], table_ref.shape[3:])
        emission = (weight * (occupied + 1.0)).astype(BF16).astype(F32)
        absorption = (weight * occupied).astype(BF16).astype(F32)
        for group in range(groups):
            target = me ^ (2 * group)
            for row in range(rows):
                energy = target * rows + row
                if group == 0:
                    put(group, row, energy - shift, emission)
                    put(group, row, energy + shift, absorption)
                else:
                    above = target > me
                    put(
                        group,
                        row,
                        jnp.where(above, energy - shift, energy + shift),
                        jnp.where(above, emission, absorption),
                    )


def mix_kernel(group, first, table_ref, pair_ref, *rest):
    out_ref = rest[-1]
    span, square, atoms = pair_ref.shape
    rows = out_ref.shape[0]
    tile = table_ref.shape[3]
    step = min(32, square)

    def body(block, carry):
        at = pl.multiple_of(block * step, step)
        totals = [None] * rows
        for slot in range(span):
            values = pair_ref[slot, pl.ds(at, step), :].astype(F32).reshape(
                step // tile, tile, atoms
            )
            for row in range(rows):
                term = table_ref[group, first + row, slot][None] * values
                totals[row] = term if totals[row] is None else totals[row] + term
        for row in range(rows):
            out_ref[row, pl.ds(at, step), :] = totals[row].reshape(step, atoms).astype(out_ref.dtype)
        return carry

    lax.fori_loop(0, square // step, body, 0)


def hot(row, width):
    numbers = lax.broadcasted_iota(jnp.int32, (width, row.shape[1]), 0)
    return jnp.where(row == numbers, 1.0, 0.0).astype(BF16)


def prepare_kernel(derivative_ref, columns_ref, after_ref, local_k_ref, remote_k_ref, local_hot_ref):
    bonds, orbital, _ = derivative_ref.shape
    square = orbital * orbital
    atoms = columns_ref.shape[1]
    local_bonds = bonds - REMOTE_BONDS
    row = lax.broadcasted_iota(jnp.int32, (square, orbital), 0)
    row_of = lax.broadcasted_iota(jnp.int32, (square, orbital), 1)
    column = lax.broadcasted_iota(jnp.int32, (orbital, square), 1)
    column_of = lax.broadcasted_iota(jnp.int32, (orbital, square), 0)

    def pick(condition):
        return jnp.where(condition, 1.0, 0.0).astype(BF16)

    row_high, row_low = pick(row // orbital == row_of), pick(row % orbital == row_of)
    column_high, column_low = pick(column // orbital == column_of), pick(column % orbital == column_of)

    def spread(left, matrix, right):
        return dot(left, dot(matrix, right).astype(BF16))

    for bond in range(bonds):
        matrix = derivative_ref[bond]
        product = (
            spread(row_high, matrix, column_high) * spread(row_low, matrix, column_low)
        ).astype(BF16)
        if bond < local_bonds:
            local_k_ref[:, bond * square : (bond + 1) * square] = product
        else:
            at = bond - local_bonds
            remote_k_ref[:, at * square : (at + 1) * square] = product
    first = lax.axis_index("atom") * atoms
    for bond in range(local_bonds):
        local_hot_ref[bond * atoms : (bond + 1) * atoms, :] = hot(
            columns_ref[bond : bond + 1, :] - first, atoms
        )


def remote_hot_kernel(bonds, flip, *refs):
    id_refs, out_ref = refs[:-1], refs[-1]
    atoms = id_refs[0].shape[1]
    me = lax.axis_index("atom")
    for place, ids_ref in enumerate(id_refs):
        ids = ids_ref[...].astype(F32).astype(jnp.int32)
        for which, slab in enumerate((me, me ^ flip)):
            for bond in range(bonds):
                at = (which * bonds + bond) * atoms
                number = (ids[2 * bond : 2 * bond + 1, :] - slab) * atoms + ids[
                    2 * bond + 1 : 2 * bond + 2, :
                ]
                out_ref[at : at + atoms, place * atoms : (place + 1) * atoms] = hot(number, atoms)


def local_kernel(mixed_ref, hot_ref, k_ref, *rest):
    out_ref, sums_ref = rest[-2:]
    rows, square, atoms = out_ref.shape
    bonds = hot_ref.shape[0] // atoms
    group = sums_ref.shape[1] // atoms
    for start in range(0, rows, group):
        count = min(group, rows - start)
        for inner in range(count):
            at = (start + inner) * square
            summed = dot_nt(mixed_ref[at : at + square, :], hot_ref[...]).astype(BF16)
            for bond in range(bonds):
                sums_ref[bond * square : (bond + 1) * square, inner * atoms : (inner + 1) * atoms] = (
                    summed[:, bond * atoms : (bond + 1) * atoms]
                )
        result = dot(k_ref[...], sums_ref[:, : count * atoms])
        for inner in range(count):
            out_ref[start + inner] = result[:, inner * atoms : (inner + 1) * atoms]


def remote_kernel(offsets, *refs):
    source_refs = refs[: len(offsets)]
    hot_ref, k_ref, local_ref = refs[len(offsets) : len(offsets) + 3]
    out_ref, away_ref = refs[-2:]
    rows, square, atoms = local_ref.shape
    bonds = k_ref.shape[1] // square
    for row in range(rows):
        sources = jnp.concatenate(
            [
                ref[offset + row * square : offset + (row + 1) * square, :]
                for offset, ref in zip(offsets, source_refs)
            ],
            axis=1,
        )
        summed = dot_nt(sources, hot_ref[...]).astype(BF16)
        stacked = jnp.concatenate(
            [
                jnp.concatenate(
                    [
                        summed[:, (which * bonds + bond) * atoms : (which * bonds + bond + 1) * atoms]
                        for which in range(2)
                    ],
                    axis=1,
                )
                for bond in range(bonds)
            ],
            axis=0,
        )
        result = dot(k_ref[...], stacked)
        out_ref[row] = result[:, :atoms] + local_ref[row]
        away_ref[row] = result[:, atoms:].astype(away_ref.dtype)


def per_device(green_blocks, derivative, phonon_weight, occupation, mode_shift, neighbours):
    rows, orbital, _, atoms = green_blocks.shape
    square = orbital * orbital
    bonds = derivative.shape[0]
    modes = phonon_weight.shape[0]
    local_bonds = bonds - REMOTE_BONDS
    pairs = lax.axis_size("energy") // 2
    slabs = lax.axis_size("atom")
    flip = 2
    high = [4 * i for i in range(slabs // 4)]
    chunks = min(CHUNKS, rows)
    last = max(1, 3 * rows // 8)
    sizes = [rows - last, last] if chunks == 2 else [rows]
    firsts = [sum(sizes[:chunk]) for chunk in range(chunks)]
    green = green_blocks.reshape(rows, square, atoms)
    columns = neighbours.T

    mate = swap(green, "energy", 1)
    table = pl.pallas_call(
        table_kernel,
        out_shape=jax.ShapeDtypeStruct((pairs, rows, 2 * rows + 1, SUBLANES, atoms), F32),
        in_specs=[HBM] * 3,
        out_specs=VMEM,
        scratch_shapes=[
            pltpu.SMEM((modes,), jnp.int32),
            pltpu.SMEM((modes,), F32),
            pltpu.VMEM((modes, atoms), F32),
            pltpu.SemaphoreType.DMA((3,)),
        ],
        compiler_params=params(),
        cost_estimate=cost(1e6, 1e6),
    )(mode_shift, occupation, phonon_weight)
    odd = lax.axis_index("energy") % 2 == 1
    pair = jnp.where(
        odd, jnp.concatenate([mate, green], 0), jnp.concatenate([green, mate], 0)
    )

    def mix(group, chunk, kind, after):
        return pl.pallas_call(
            functools.partial(mix_kernel, group, firsts[chunk]),
            out_shape=jax.ShapeDtypeStruct((sizes[chunk], square, atoms), kind),
            in_specs=[VMEM, VMEM] + [ANY] * len(after),
            out_specs=VMEM,
            compiler_params=params(),
            cost_estimate=cost(5e8, 1e6),
        )(table, pair, *after)

    def prepare(after):
        return pl.pallas_call(
            prepare_kernel,
            out_shape=(
                jax.ShapeDtypeStruct((square, local_bonds * square), BF16),
                jax.ShapeDtypeStruct((square, REMOTE_BONDS * square), BF16),
                jax.ShapeDtypeStruct((local_bonds * atoms, atoms), BF16),
            ),
            in_specs=[VMEM, VMEM, ANY],
            out_specs=(VMEM, VMEM, VMEM),
            compiler_params=params(),
            cost_estimate=cost(2e9, 3e6),
        )(derivative, columns, after)

    def local_sum(chunk, after):
        return pl.pallas_call(
            local_kernel,
            out_shape=jax.ShapeDtypeStruct((sizes[chunk], square, atoms), F32),
            in_specs=[VMEM] * 3 + [ANY] * len(after),
            out_specs=VMEM,
            scratch_shapes=[
                pltpu.VMEM((local_bonds * square, min(2, sizes[chunk]) * atoms), BF16)
            ],
            compiler_params=params(),
            cost_estimate=cost(2e9, 3e6),
        )(mixed[chunk], local_hot, local_k, *after)

    remote_ids = columns[local_bonds:, :]
    ids = jnp.stack([remote_ids // atoms, remote_ids % atoms], 1).reshape(-1, atoms)
    ids = jnp.pad(ids, ((0, ID_ROWS - ids.shape[0]), (0, 0))).astype(BF16)

    own, arrived = [], []
    after = []
    for chunk in range(chunks):
        away = [mix(group, chunk, BF16, after) for group in range(1, pairs)]
        arrived.append([swap(value, "energy", 2 * group) for group, value in enumerate(away, 1)])
        if chunk == 0:
            local_k, remote_k, local_hot = prepare(away[0])
            own.append(mix(0, chunk, F32, [local_hot]))
            after = own[-1:]
        else:
            after = away[:1]
    mixed, local = [], []
    for chunk in range(chunks):
        if chunk > 0:
            own.append(mix(0, chunk, F32, after + mixed[-1:] + local[-1:]))
        total = own[chunk]
        for received in arrived[chunk]:
            total = total + received.astype(F32)
        total = total.astype(BF16).reshape(-1, atoms)
        mixed.append(jnp.concatenate([total, ids], 0) if chunk == 0 else total)
        if chunk > 0:
            local.append(local_sum(chunk - 1, mixed[-1:]))
    local.append(local_sum(chunks - 1, local[-1:]))

    beside = swap(jnp.concatenate(mixed, 0), "atom", 1)
    starts = [sum(value.shape[0] for value in mixed[:chunk]) for chunk in range(chunks)]

    remote_hot = None
    results = []
    for chunk in range(chunks):
        across = [swap(mixed[chunk], "atom", mask) for mask in high[1:]]
        beyond = [swap(value, "atom", 1) for value in across]
        sources = [mixed[chunk], beside] + across + beyond
        offsets = [0, starts[chunk]] + [0] * (len(across) + len(beyond))
        if remote_hot is None:
            ends = sizes[0] * square
            id_blocks = [
                value[offset + ends : offset + ends + ID_ROWS]
                for offset, value in zip(offsets, sources)
            ]
            remote_hot = pl.pallas_call(
                functools.partial(remote_hot_kernel, REMOTE_BONDS, flip),
                out_shape=jax.ShapeDtypeStruct(
                    (2 * REMOTE_BONDS * atoms, len(sources) * atoms), BF16
                ),
                in_specs=[VMEM] * len(sources),
                out_specs=VMEM,
                compiler_params=params(),
                cost_estimate=cost(1e8, 1e6),
            )(*id_blocks)
        after = local[-1:] + [partial for partial, _ in results[-1:]]
        partial, away = pl.pallas_call(
            functools.partial(remote_kernel, offsets),
            out_shape=(
                jax.ShapeDtypeStruct((sizes[chunk], square, atoms), F32),
                jax.ShapeDtypeStruct((sizes[chunk], square, atoms), BF16),
            ),
            in_specs=[VMEM] * (len(sources) + 3) + [ANY] * len(after),
            out_specs=(VMEM, VMEM),
            compiler_params=params(),
            cost_estimate=cost(1e9, 3e6),
        )(*sources, remote_hot, remote_k, local[chunk], *after)
        results.append((partial, swap(away, "atom", flip)))
    combined = jnp.concatenate(
        [partial + received.astype(F32) for partial, received in results], 0
    )
    return combined.reshape(rows, orbital, orbital, atoms)


def solution(mesh):
    in_specs = (P("energy", None, None, "atom"), P(), P(None, "atom"), P(), P(), P("atom", None))
    out_specs = P("energy", None, None, "atom")
    return jax.shard_map(
        per_device, mesh=mesh, in_specs=in_specs, out_specs=out_specs, check_vma=False
    )
```

time: 200 us -> 66.3 us (0.33)
  matrix products: 56.8 us -> 0 us
  waiting for transfers between devices: 80.7 us -> 31.7 us
  local copies, waits for them, and re-layouts: 29.1 us -> 2.03 us
  Pallas kernels: 0 us -> 15.9 us
  between operations: 13.5 us -> 0.19 us
  other arithmetic: 5.14 us -> 1.55 us
  starting transfers between devices: 12.8 us -> 14.8 us
    all_to_all x2 -> x0, waiting for transfers between devices: 74.3 us -> none  [the longest x1 72.5 us: per_device(): lax.all_to_all(payload, 'atom', split_axis=1, concat_axis=1, tiled=True)]
    dot_general x49 -> x0, matrix products: 56.8 us -> none  [the longest x15 23.8 us: place_sum(): jnp.dot(values, onehot, precision=lax.Precision.HIGHEST, preferred_elemen...]
    ppermute x0 -> x10, waiting for transfers between devices: none -> 31.7 us  [swap(): return lax.ppermute(value, axis, [(i, i ^ mask) for i in range(count)])]
    pallas_call x0 -> x11, Pallas kernels: none -> 15.9 us  [the longest x2 4.71 us: local_sum(): pl.pallas_call(local_kernel, out_shape=jax.ShapeDtypeStruct((sizes[chunk]...]
    ppermute x0 -> x10, starting transfers between devices: none -> 14.8 us  [swap(): return lax.ppermute(value, axis, [(i, i ^ mask) for i in range(count)])]
    all_to_all x2 -> x0, starting transfers between devices: 12.8 us -> none  [the longest x1 7.28 us: per_device(): lax.all_to_all(labels, 'atom', split_axis=1, concat_axis=1, tiled=True)]
    scatter x3 -> x0, local copies, waits for them, and re-layouts: 11.6 us -> none  [the longest x2 10.2 us: per_device(): payload.at[:, placement[:, remote_bond]]]
    all_to_all x4 -> x0, local copies, waits for them, and re-layouts: 9.82 us -> none  [the longest x2 8.62 us: per_device(): lax.all_to_all(payload, 'atom', split_axis=1, concat_axis=1, tiled=True)]
  transfers between devices with their start and end apart: 3 -> 10, of which waited for: 3 -> 6; matrix products, arithmetic and copies ran while one was open for 26% -> 0% of each run, Pallas kernels for 0% -> 21%
where the time goes in v2:
time: 66.3 us; the launch traced here: 66.1 us
  waiting for transfers between devices  31.7 us (48%)
  Pallas kernels  15.9 us (24%)
  starting transfers between devices  14.8 us (22%)
  local copies, waits for them, and re-layouts  2.03 us (3%)
  other arithmetic  1.55 us (2%)
    ppermute x10, waiting for transfers between devices, swap(): return lax.ppermute(value, axis, [(i, i ^ mask) for i in range(count)])  31.7 us
    ppermute x10, starting transfers between devices, swap(): return lax.ppermute(value, axis, [(i, i ^ mask) for i in range(count)])  14.8 us
    pallas_call x2, Pallas kernels, local_sum(): pl.pallas_call(local_kernel, out_shape=jax.ShapeDtypeStruct((sizes[chunk]...  4.71 us
    pallas_call x2, Pallas kernels, per_device(): pl.pallas_call(functools.partial(remote_kernel, offsets), out_shape=(jax....  3.76 us
    pallas_call x1, Pallas kernels, prepare(): pl.pallas_call(prepare_kernel, out_shape=(jax.ShapeDtypeStruct((square, l...  3.35 us
    pallas_call x4, Pallas kernels, mix(): pl.pallas_call(functools.partial(mix_kernel, group, firsts[chunk]), out_s...  2.76 us
    unnamed x12, local copies, waits for them, and re-layouts  2.01 us
  transfers between devices with their start and end apart: 10, of which 6 were waited for; matrix products, arithmetic and copies ran while one was open for 0% of the time, Pallas kernels for 21%

profile of v2, /device:TPU:0, one launch (start us, length us, event | category | flops | bytes accessed | tf_op | source)
XLA Modules:
  0.0 66.1 jit_solution(18081760866494608431)
XLA Ops:
  0.5 0.7 %copy-done = f32[8,128]{1,0:T(8,128)S(1)} copy-done((f32[8,128]{1,0:T(8,128)S(1)}, f32[8,128]{1,0:T(8,128)}, u32[]{:S(2)}) %copy-start) | copy-done | bytes 4120
  1.1 0.7 copy-done.1
  1.8 0.7 copy-done.2
  2.5 1.2 %shard_map.64.table_ref = f32[2,8,17,8,128]{4,3,2,1,0:T(8,128)S(1)} custom-call(s32[8]{0:T(128)S(1)} %copy-done.1, f32[8]{0:T(128)S(1)} %copy-done.2, f32[8,128]{1,0:T(8,128)S(1)} %copy-done), custom_call_target="tpu_custom_call" | custom-call | flops 1000000 | bytes 1000000 | tf_op jit(solution)/shard_map/pallas_call | solution.py:241
  3.9 0.8 %shard_map.65.after_ref = bf16[5,256,128]{2,1,0:T(8,128)(2,1)S(1)} custom-call(f32[2,8,17,8,128]{4,3,2,1,0:T(8,128)S(1)} %shard_map.64.table_ref, bf16[16,256,128]{2,1,0:T(8,128)(2,1)S(1)} %maximum_select_fusion.pair_ref), custom_call_target="tpu_custom_call" | custom-call | flops 500000000 | bytes 1000000 | tf_op jit(solution)/shard_map/pallas_call | solution.py:261
  4.7 2.6 %collective-permute-start.1 = (bf16[5,256,128]{2,1,0:T(8,128)(2,1)S(1)}, bf16[5,256,128]{2,1,0:T(8,128)(2,1)S(1)}, u32[]{:S(2)}, u32[]{:S(2)}) collective-permute-start(bf16[5,256,128]{2,1,0:T(8,128)(2,1)S(1)} %shard_map.65.after_ref), channel_id=1, source_target_pairs={{0,16},{8,24},{16,0},{24,8},{1,17},{9,25},{17,1},{25,9},{2,18},{10... | collective-permute-start | bytes 983048 | tf_op jit(solution)/shard_map/ppermute | solution.py:33
  7.3 3.4 %shard_map.66 = (bf16[256,3584]{1,0:T(8,128)(2,1)S(1)}, bf16[256,512]{1,0:T(8,128)(2,1)S(1)}, bf16[1792,128]{1,0:T(8,128)(2,1)S(1)}) custom-call(bf16[16,16,16]{2,1,0:T(8,128)(2,1)S(1)} %copy-done.4, s32[16,128]{1,0:T(8,128)S(1)} %bitcast.16, bf16[5,256,128]{2,1,0:T(8,128)(2,1)S(1)} %shard_map.65.after_ref), custom_call_target="tpu_custom_call" | custom-call | flops 2000000000 | bytes 3000000 | tf_op jit(solution)/shard_map/pallas_call | solution.py:271
  10.6 0.8 %shard_map.67.rest_0_ = f32[5,256,128]{2,1,0:T(8,128)S(1)} custom-call(f32[2,8,17,8,128]{4,3,2,1,0:T(8,128)S(1)} %shard_map.64.table_ref, bf16[16,256,128]{2,1,0:T(8,128)(2,1)S(1)} %maximum_select_fusion.pair_ref, bf16[1792,128]{1,0:T(8,128)(2,1)S(1)} %get-tuple-element.12.rest_0_.hot_ref), custom_call_target="tpu_custom_call" | custom-call | flops 500000000 | bytes 1000000 | tf_op jit(solution)/shard_map/pallas_call | solution.py:261
  12.1 3.7 %collective-permute-done.1 = bf16[5,256,128]{2,1,0:T(8,128)(2,1)S(1)} collective-permute-done((bf16[5,256,128]{2,1,0:T(8,128)(2,1)S(1)}, bf16[5,256,128]{2,1,0:T(8,128)(2,1)S(1)}, u32[]{:S(2)}, u32[]{:S(2)}) %collective-permute-start.1) | collective-permute-done | bytes 327712 | tf_op jit(solution)/shard_map/ppermute | solution.py:33
  15.9 3.1 %collective-permute-start.4 = (bf16[1296,128]{1,0:T(8,128)(2,1)S(1)}, bf16[1296,128]{1,0:T(8,128)(2,1)S(1)}, u32[]{:S(2)}, u32[]{:S(2)}) collective-permute-start(bf16[1296,128]{1,0:T(8,128)(2,1)S(1)} %pad_maximum_fusion.2.rest_1_.mixed_ref.refs_0_), channel_id=1, source_target_pairs={{0,4},{1,5},{2,6},{3,7},{4,0},{5,1},{6,2},{7,3},{8,12},{9,13},{10,... | collective-permute-start | bytes 995336 | tf_op jit(solution)/shard_map/ppermute | solution.py:33
  19.0 0.6 shard_map.69
  19.9 1.8 %collective-permute-start.3 = (bf16[2064,128]{1,0:T(8,128)(2,1)S(1)}, bf16[2064,128]{1,0:T(8,128)(2,1)S(1)}, u32[]{:S(2)}, u32[]{:S(2)}) collective-permute-start(bf16[2064,128]{1,0:T(8,128)(2,1)S(1)} %pad_maximum_fusion.1), channel_id=1, source_target_pairs={{0,1},{1,0},{2,3},{3,2},{4,5},{5,4},{6,7},{7,6},{8,9},{9,8},{10,11... | collective-permute-start | bytes 1585160 | tf_op jit(solution)/shard_map/ppermute | solution.py:33
  21.8 2.6 %collective-permute-start.7 = (bf16[768,128]{1,0:T(8,128)(2,1)S(1)}, bf16[768,128]{1,0:T(8,128)(2,1)S(1)}, u32[]{:S(2)}, u32[]{:S(2)}) collective-permute-start(bf16[768,128]{1,0:T(8,128)(2,1)S(1)} %bitcast.11), channel_id=1, source_target_pairs={{0,4},{1,5},{2,6},{3,7},{4,0},{5,1},{6,2},{7,3},{8,12},{9,13},{10,... | collective-permute-start | bytes 589832 | tf_op jit(solution)/shard_map/ppermute | solution.py:33
  24.4 14.5 %collective-permute-done.4.refs_2_ = bf16[1296,128]{1,0:T(8,128)(2,1)S(1)} collective-permute-done((bf16[1296,128]{1,0:T(8,128)(2,1)S(1)}, bf16[1296,128]{1,0:T(8,128)(2,1)S(1)}, u32[]{:S(2)}, u32[]{:S(2)}) %collective-permute-start.4) | collective-permute-done | bytes 331808 | tf_op jit(solution)/shard_map/ppermute | solution.py:33
  38.8 1.5 %collective-permute-start.5 = (bf16[1296,128]{1,0:T(8,128)(2,1)S(1)}, bf16[1296,128]{1,0:T(8,128)(2,1)S(1)}, u32[]{:S(2)}, u32[]{:S(2)}) collective-permute-start(bf16[1296,128]{1,0:T(8,128)(2,1)S(1)} %collective-permute-done.4.refs_2_), channel_id=1, source_target_pairs={{0,1},{1,0},{2,3},{3,2},{4,5},{5,4},{6,7},{7,6},{8,9},{9,8},{10,11... | collective-permute-start | bytes 995336 | tf_op jit(solution)/shard_map/ppermute | solution.py:33
  40.4 2.8 %shard_map.71.rest_0_.refs_6_ = f32[5,256,128]{2,1,0:T(8,128)S(1)} custom-call(bf16[1296,128]{1,0:T(8,128)(2,1)S(1)} %pad_maximum_fusion.2.rest_1_.mixed_ref.refs_0_, bf16[1792,128]{1,0:T(8,128)(2,1)S(1)} %get-tuple-element.12.rest_0_.hot_ref, bf16[256,3584]{1,0:T(8,128)(2,1)S(1)} %get-tuple-element.14.k_ref, bf16[768,128]{1,0:T(8,128)(2,1)S(1)} %bitcast.12), custom_call_target="tpu_custom_call" | custom-call | flops 2000000000 | bytes 3000000 | tf_op jit(solution)/shard_map/pallas_call | solution.py:285
  43.8 1.9 %shard_map.72.refs_7_.refs_6_ = f32[3,256,128]{2,1,0:T(8,128)S(1)} custom-call(bf16[768,128]{1,0:T(8,128)(2,1)S(1)} %bitcast.13, bf16[1792,128]{1,0:T(8,128)(2,1)S(1)} %get-tuple-element.12.rest_0_.hot_ref, bf16[256,3584]{1,0:T(8,128)(2,1)S(1)} %get-tuple-element.14.k_ref, f32[5,256,128]{2,1,0:T(8,128)S(1)} %shard_map.71.rest_0_.refs_6_), custom_call_target="tpu_custom_call" | custom-call | flops 2000000000 | bytes 3000000 | tf_op jit(solution)/shard_map/pallas_call | solution.py:285
  45.7 2.7 %collective-permute-done.5.refs_3_ = bf16[1296,128]{1,0:T(8,128)(2,1)S(1)} collective-permute-done((bf16[1296,128]{1,0:T(8,128)(2,1)S(1)}, bf16[1296,128]{1,0:T(8,128)(2,1)S(1)}, u32[]{:S(2)}, u32[]{:S(2)}) %collective-permute-start.5) | collective-permute-done | bytes 331808 | tf_op jit(solution)/shard_map/ppermute | solution.py:33
  48.5 2.3 %shard_map.73 = (f32[5,256,128]{2,1,0:T(8,128)S(1)}, bf16[5,256,128]{2,1,0:T(8,128)(2,1)S(1)}) custom-call(bf16[1296,128]{1,0:T(8,128)(2,1)S(1)} %pad_maximum_fusion.2.rest_1_.mixed_ref.refs_0_, bf16[2064,128]{1,0:T(8,128)(2,1)S(1)} %collective-permute-done.3.refs_1_, bf16[1296,128]{1,0:T(8,128)(2,1)S(1)} %collective-permute-done.4.refs_2_, ...), custom_call_target="tpu_custom_call" | custom-call | flops 1000000000 | bytes 3000000 | tf_op jit(solution)/shard_map/pallas_call | solution.py:352
  50.8 1.5 %shard_map.74 = (f32[3,256,128]{2,1,0:T(8,128)S(1)}, bf16[3,256,128]{2,1,0:T(8,128)(2,1)S(1)}) custom-call(bf16[768,128]{1,0:T(8,128)(2,1)S(1)} %bitcast.14, bf16[2064,128]{1,0:T(8,128)(2,1)S(1)} %collective-permute-done.3.refs_1_, bf16[768,128]{1,0:T(8,128)(2,1)S(1)} %collective-permute-done.7.refs_2_, bf16[768,128]{1,0:T(8,128)(2,1)S(1)} %collective-permute-done.8.refs_3_, ...), custom_call_target="tpu_custom_call" | custom-call | flops 1000000000 | bytes 3000000 | tf_op jit(solution)/shard_map/pallas_call | solution.py:352
  52.3 1.6 %collective-permute-start.9 = (bf16[3,256,128]{2,1,0:T(8,128)(2,1)S(1)}, bf16[3,256,128]{2,1,0:T(8,128)(2,1)S(1)}, u32[]{:S(2)}, u32[]{:S(2)}) collective-permute-start(bf16[3,256,128]{2,1,0:T(8,128)(2,1)S(1)} %get-tuple-element.18), channel_id=1, source_target_pairs={{0,2},{1,3},{2,0},{3,1},{4,6},{5,7},{6,4},{7,5},{8,10},{9,11},{10,... | collective-permute-start | bytes 589832 | tf_op jit(solution)/shard_map/ppermute | solution.py:33
  54.4 5.8 %collective-permute-done.9 = bf16[3,256,128]{2,1,0:T(8,128)(2,1)S(1)} collective-permute-done((bf16[3,256,128]{2,1,0:T(8,128)(2,1)S(1)}, bf16[3,256,128]{2,1,0:T(8,128)(2,1)S(1)}, u32[]{:S(2)}, u32[]{:S(2)}) %collective-permute-start.9) | collective-permute-done | bytes 196640 | tf_op jit(solution)/shard_map/ppermute | solution.py:33
  60.2 4.8 %collective-permute-done.6 = bf16[5,256,128]{2,1,0:T(8,128)(2,1)S(1)} collective-permute-done((bf16[5,256,128]{2,1,0:T(8,128)(2,1)S(1)}, bf16[5,256,128]{2,1,0:T(8,128)(2,1)S(1)}, u32[]{:S(2)}, u32[]{:S(2)}) %collective-permute-start.6) | collective-permute-done | bytes 327712 | tf_op jit(solution)/shard_map/ppermute | solution.py:33
  65.1 1.1 %pad_maximum_fusion = f32[8,256,128]{2,1,0:T(8,128)} fusion(f32[3,256,128]{2,1,0:T(8,128)S(1)} %convert_add_fusion.1, f32[5,256,128]{2,1,0:T(8,128)S(1)} %convert_add_fusion), kind=kLoop, calls=%fused_computation.1 | loop fusion | flops 262144 | bytes 2097152 | tf_op jit(solution)/shard_map/concatenate | solution.py:364
  (34 shorter events, 3.1 us)
Async XLA Ops:
  0.0 3.6 %copy-start.3 = (s32[128,16]{0,1:T(8,128)S(1)}, s32[128,16]{0,1:T(8,128)}, u32[]{:S(2)}) copy-start(s32[128,16]{0,1:T(8,128)} %param.11) | copy-start | bytes 24580
  0.0 3.6 %collective-permute-start = (bf16[8,256,128]{2,1,0:T(8,128)(2,1)}, bf16[8,256,128]{2,1,0:T(8,128)(2,1)S(1)}, u32[]{:S(2)}, u32[]{:S(2)}) collective-permute-start(bf16[8,256,128]{2,1,0:T(8,128)(2,1)} %bitcast.19), channel_id=1, source_target_pairs={{0,8},{8,0},{16,24},{24,16},{1,9},{9,1},{17,25},{25,17},{2,10},{10... | collective-permute-start | bytes 1572872 | tf_op jit(solution)/shard_map/ppermute | solution.py:33
  0.5 0.7 %copy-start = (f32[8,128]{1,0:T(8,128)S(1)}, f32[8,128]{1,0:T(8,128)}, u32[]{:S(2)}) copy-start(f32[8,128]{1,0:T(8,128)} %weight_hbm.1) | copy-start | bytes 12292
  1.1 0.7 copy-start.1
  1.8 0.7 copy-start.2
  2.5 1.2 %copy-start.5 = (bf16[8,16,16,128]{3,2,1,0:T(8,128)(2,1)S(1)}, bf16[8,16,16,128]{3,2,1,0:T(8,128)(2,1)}, u32[]{:S(2)}) copy-start(bf16[8,16,16,128]{3,2,1,0:T(8,128)(2,1)} %param.6) | copy-start | bytes 1572868
  3.8 3.4 %copy-start.4 = (bf16[16,16,16]{2,1,0:T(8,128)(2,1)S(1)}, bf16[16,16,16]{2,1,0:T(8,128)(2,1)}, u32[]{:S(2)}) copy-start(bf16[16,16,16]{2,1,0:T(8,128)(2,1)} %derivative_ref.1) | copy-start | bytes 24580
  4.7 11.1 %collective-permute-start.1 = (bf16[5,256,128]{2,1,0:T(8,128)(2,1)S(1)}, bf16[5,256,128]{2,1,0:T(8,128)(2,1)S(1)}, u32[]{:S(2)}, u32[]{:S(2)}) collective-permute-start(bf16[5,256,128]{2,1,0:T(8,128)(2,1)S(1)} %shard_map.65.after_ref), channel_id=1, source_target_pairs={{0,16},{8,24},{16,0},{24,8},{1,17},{9,25},{17,1},{25,9},{2,18},{10... | collective-permute-start | bytes 983048 | tf_op jit(solution)/shard_map/ppermute | solution.py:33
  12.0 7.8 %collective-permute-start.2 = (bf16[3,256,128]{2,1,0:T(8,128)(2,1)S(1)}, bf16[3,256,128]{2,1,0:T(8,128)(2,1)S(1)}, u32[]{:S(2)}, u32[]{:S(2)}) collective-permute-start(bf16[3,256,128]{2,1,0:T(8,128)(2,1)S(1)} %shard_map.68.rest_0_), channel_id=1, source_target_pairs={{0,16},{8,24},{16,0},{24,8},{1,17},{9,25},{17,1},{25,9},{2,18},{10... | collective-permute-start | bytes 589832 | tf_op jit(solution)/shard_map/ppermute | solution.py:33
  15.9 22.9 %collective-permute-start.4 = (bf16[1296,128]{1,0:T(8,128)(2,1)S(1)}, bf16[1296,128]{1,0:T(8,128)(2,1)S(1)}, u32[]{:S(2)}, u32[]{:S(2)}) collective-permute-start(bf16[1296,128]{1,0:T(8,128)(2,1)S(1)} %pad_maximum_fusion.2.rest_1_.mixed_ref.refs_0_), channel_id=1, source_target_pairs={{0,4},{1,5},{2,6},{3,7},{4,0},{5,1},{6,2},{7,3},{8,12},{9,13},{10,... | collective-permute-start | bytes 995336 | tf_op jit(solution)/shard_map/ppermute | solution.py:33
  19.9 25.8 %collective-permute-start.3 = (bf16[2064,128]{1,0:T(8,128)(2,1)S(1)}, bf16[2064,128]{1,0:T(8,128)(2,1)S(1)}, u32[]{:S(2)}, u32[]{:S(2)}) collective-permute-start(bf16[2064,128]{1,0:T(8,128)(2,1)S(1)} %pad_maximum_fusion.1), channel_id=1, source_target_pairs={{0,1},{1,0},{2,3},{3,2},{4,5},{5,4},{6,7},{7,6},{8,9},{9,8},{10,11... | collective-permute-start | bytes 1585160 | tf_op jit(solution)/shard_map/ppermute | solution.py:33
  21.8 21.5 %collective-permute-start.7 = (bf16[768,128]{1,0:T(8,128)(2,1)S(1)}, bf16[768,128]{1,0:T(8,128)(2,1)S(1)}, u32[]{:S(2)}, u32[]{:S(2)}) collective-permute-start(bf16[768,128]{1,0:T(8,128)(2,1)S(1)} %bitcast.11), channel_id=1, source_target_pairs={{0,4},{1,5},{2,6},{3,7},{4,0},{5,1},{6,2},{7,3},{8,12},{9,13},{10,... | collective-permute-start | bytes 589832 | tf_op jit(solution)/shard_map/ppermute | solution.py:33
  38.8 9.5 %collective-permute-start.5 = (bf16[1296,128]{1,0:T(8,128)(2,1)S(1)}, bf16[1296,128]{1,0:T(8,128)(2,1)S(1)}, u32[]{:S(2)}, u32[]{:S(2)}) collective-permute-start(bf16[1296,128]{1,0:T(8,128)(2,1)S(1)} %collective-permute-done.4.refs_2_), channel_id=1, source_target_pairs={{0,1},{1,0},{2,3},{3,2},{4,5},{5,4},{6,7},{7,6},{8,9},{9,8},{10,11... | collective-permute-start | bytes 995336 | tf_op jit(solution)/shard_map/ppermute | solution.py:33
  43.2 7.5 %collective-permute-start.8 = (bf16[768,128]{1,0:T(8,128)(2,1)S(1)}, bf16[768,128]{1,0:T(8,128)(2,1)S(1)}, u32[]{:S(2)}, u32[]{:S(2)}) collective-permute-start(bf16[768,128]{1,0:T(8,128)(2,1)S(1)} %collective-permute-done.7.refs_2_), channel_id=1, source_target_pairs={{0,1},{1,0},{2,3},{3,2},{4,5},{5,4},{6,7},{7,6},{8,9},{9,8},{10,11... | collective-permute-start | bytes 589832 | tf_op jit(solution)/shard_map/ppermute | solution.py:33
  52.3 7.9 %collective-permute-start.9 = (bf16[3,256,128]{2,1,0:T(8,128)(2,1)S(1)}, bf16[3,256,128]{2,1,0:T(8,128)(2,1)S(1)}, u32[]{:S(2)}, u32[]{:S(2)}) collective-permute-start(bf16[3,256,128]{2,1,0:T(8,128)(2,1)S(1)} %get-tuple-element.18), channel_id=1, source_target_pairs={{0,2},{1,3},{2,0},{3,1},{4,6},{5,7},{6,4},{7,5},{8,10},{9,11},{10,... | collective-permute-start | bytes 589832 | tf_op jit(solution)/shard_map/ppermute | solution.py:33
  53.8 11.2 %collective-permute-start.6 = (bf16[5,256,128]{2,1,0:T(8,128)(2,1)S(1)}, bf16[5,256,128]{2,1,0:T(8,128)(2,1)S(1)}, u32[]{:S(2)}, u32[]{:S(2)}) collective-permute-start(bf16[5,256,128]{2,1,0:T(8,128)(2,1)S(1)} %get-tuple-element.16), channel_id=1, source_target_pairs={{0,2},{1,3},{2,0},{3,1},{4,6},{5,7},{6,4},{7,5},{8,10},{9,11},{10,... | collective-permute-start | bytes 983048 | tf_op jit(solution)/shard_map/ppermute | solution.py:33

commit v3 on v2

--- a/solution.py
+++ b/solution.py
@@ -8,8 +8,8 @@
 from jax.sharding import PartitionSpec as P
 
 REMOTE_BONDS = 2
-CHUNKS = 2
 ID_ROWS = 16
+P_PART = 4
 COST = 1.0
 SUBLANES = 8
 VMEM_LIMIT = 48 * 1024 * 1024
@@ -41,22 +41,14 @@
     return lax.dot_general(left, right, (((1,), (1,)), ((), ())), preferred_element_type=F32)
 
 
-def table_kernel(
-    shift_hbm, occupation_hbm, weight_hbm, table_ref, shift_ref, occupation_ref, weight_ref, sems
-):
+def table_kernel(packed_ref, table_ref, scalar_ref, sem):
     groups, rows, spare = table_ref.shape[:3]
     span = spare - 1
-    modes = weight_ref.shape[0]
-    copies = [
-        pltpu.make_async_copy(shift_hbm, shift_ref, sems.at[0]),
-        pltpu.make_async_copy(occupation_hbm, occupation_ref, sems.at[1]),
-        pltpu.make_async_copy(weight_hbm, weight_ref, sems.at[2]),
-    ]
-    for copy in copies:
-        copy.start()
+    modes = packed_ref.shape[0] - SUBLANES
+    copy = pltpu.make_async_copy(packed_ref.at[pl.ds(modes, SUBLANES)], scalar_ref, sem)
+    copy.start()
     table_ref[...] = jnp.zeros_like(table_ref)
-    for copy in copies:
-        copy.wait()
+    copy.wait()
     me = lax.axis_index("energy")
     base = me // 2 * span
 
@@ -66,9 +58,9 @@
         table_ref[group, row, jnp.where(inside, slot, span)] = value
 
     for mode in range(modes):
-        shift = shift_ref[mode]
-        occupied = occupation_ref[mode]
-        weight = jnp.broadcast_to(weight_ref[mode : mode + 1, :], table_ref.shape[3:])
+        occupied = scalar_ref[0, mode]
+        shift = scalar_ref[1, mode].astype(jnp.int32)
+        weight = jnp.broadcast_to(packed_ref[mode : mode + 1, :], table_ref.shape[3:])
         emission = (weight * (occupied + 1.0)).astype(BF16).astype(F32)
         absorption = (weight * occupied).astype(BF16).astype(F32)
         for group in range(groups):
@@ -117,7 +109,7 @@
     return jnp.where(row == numbers, 1.0, 0.0).astype(BF16)
 
 
-def prepare_kernel(derivative_ref, columns_ref, after_ref, local_k_ref, remote_k_ref, local_hot_ref):
+def prepare_kernel(derivative_ref, columns_ref, after_ref, local_k_ref, remote_k_ref, local_hot_ref, ids_ref):
     bonds, orbital, _ = derivative_ref.shape
     square = orbital * orbital
     atoms = columns_ref.shape[1]
@@ -151,15 +143,29 @@
         local_hot_ref[bond * atoms : (bond + 1) * atoms, :] = hot(
             columns_ref[bond : bond + 1, :] - first, atoms
         )
-
-
-def remote_hot_kernel(bonds, flip, *refs):
-    id_refs, out_ref = refs[:-1], refs[-1]
+    rows = []
+    for bond in range(local_bonds, bonds):
+        number = columns_ref[bond : bond + 1, :]
+        rows += [number // atoms, number % atoms]
+    place = lax.broadcasted_iota(jnp.int32, ids_ref.shape, 0)
+    ids = jnp.zeros(ids_ref.shape, jnp.int32)
+    for at, row in enumerate(rows):
+        ids = jnp.where(place == at, row, ids)
+    ids_ref[...] = ids.astype(F32).astype(BF16)
+
+
+def pass_kernel(value_ref, after_ref, out_ref):
+    out_ref[...] = value_ref[...]
+
+
+def remote_hot_kernel(bonds, flips, *refs):
+    id_refs, out_ref = refs[:-2], refs[-1]
     atoms = id_refs[0].shape[1]
     me = lax.axis_index("atom")
     for place, ids_ref in enumerate(id_refs):
-        ids = ids_ref[...].astype(F32).astype(jnp.int32)
-        for which, slab in enumerate((me, me ^ flip)):
+        ids = ids_ref[ids_ref.shape[0] - ID_ROWS :, :].astype(F32).astype(jnp.int32)
+        for which, flip in enumerate(flips):
+            slab = me ^ flip
             for bond in range(bonds):
                 at = (which * bonds + bond) * atoms
                 number = (ids[2 * bond : 2 * bond + 1, :] - slab) * atoms + ids[
@@ -187,37 +193,55 @@
             out_ref[start + inner] = result[:, inner * atoms : (inner + 1) * atoms]
 
 
-def remote_kernel(offsets, *refs):
-    source_refs = refs[: len(offsets)]
-    hot_ref, k_ref, local_ref = refs[len(offsets) : len(offsets) + 3]
-    out_ref, away_ref = refs[-2:]
-    rows, square, atoms = local_ref.shape
+def remote_sums(source_refs, hot_ref, k_ref, rows, first, count, store):
+    atoms = source_refs[0].shape[1]
+    square = k_ref.shape[0]
     bonds = k_ref.shape[1] // square
-    for row in range(rows):
-        sources = jnp.concatenate(
-            [
-                ref[offset + row * square : offset + (row + 1) * square, :]
-                for offset, ref in zip(offsets, source_refs)
-            ],
-            axis=1,
-        )
-        summed = dot_nt(sources, hot_ref[...]).astype(BF16)
-        stacked = jnp.concatenate(
-            [
-                jnp.concatenate(
-                    [
-                        summed[:, (which * bonds + bond) * atoms : (which * bonds + bond + 1) * atoms]
-                        for which in range(2)
-                    ],
-                    axis=1,
-                )
-                for bond in range(bonds)
-            ],
-            axis=0,
-        )
+    width = bonds * atoms
+    group = max(1, 2 // count)
+    for start in range(0, rows, group):
+        inner = range(start, min(start + group, rows))
+        pieces = [[] for _ in range(bonds)]
+        for row in inner:
+            sources = jnp.concatenate(
+                [ref[row * square : (row + 1) * square, :] for ref in source_refs], axis=1
+            )
+            summed = dot_nt(sources, hot_ref[first * width : (first + count) * width, :])
+            summed = summed.astype(BF16)
+            for which in range(count):
+                for bond in range(bonds):
+                    at = which * width + bond * atoms
+                    pieces[bond].append(summed[:, at : at + atoms])
+        stacked = jnp.concatenate([jnp.concatenate(piece, axis=1) for piece in pieces], axis=0)
         result = dot(k_ref[...], stacked)
-        out_ref[row] = result[:, :atoms] + local_ref[row]
-        away_ref[row] = result[:, atoms:].astype(away_ref.dtype)
+        for place, row in enumerate(inner):
+            for which in range(count):
+                at = (place * count + which) * atoms
+                store(row, which, result[:, at : at + atoms])
+
+
+def away_kernel(source_count, *refs):
+    source_refs = refs[:source_count]
+    hot_ref, k_ref = refs[source_count : source_count + 2]
+    count = hot_ref.shape[0] // (k_ref.shape[1] // k_ref.shape[0] * source_refs[0].shape[1]) - 1
+    out_refs = refs[len(refs) - count :]
+    rows = out_refs[0].shape[0]
+
+    def store(row, which, value):
+        out_refs[which][row] = value.astype(BF16)
+
+    remote_sums(source_refs, hot_ref, k_ref, rows, 1, count, store)
+
+
+def stay_kernel(source_count, *refs):
+    source_refs = refs[:source_count]
+    hot_ref, k_ref, local_ref = refs[source_count : source_count + 3]
+    out_ref = refs[-1]
+
+    def store(row, which, value):
+        out_ref[row] = value + local_ref[row]
+
+    remote_sums(source_refs, hot_ref, k_ref, out_ref.shape[0], 0, 1, store)
 
 
 def per_device(green_blocks, derivative, phonon_weight, occupation, mode_shift, neighbours):
@@ -228,30 +252,30 @@
     local_bonds = bonds - REMOTE_BONDS
     pairs = lax.axis_size("energy") // 2
     slabs = lax.axis_size("atom")
-    flip = 2
-    high = [4 * i for i in range(slabs // 4)]
-    chunks = min(CHUNKS, rows)
-    last = max(1, 3 * rows // 8)
-    sizes = [rows - last, last] if chunks == 2 else [rows]
-    firsts = [sum(sizes[:chunk]) for chunk in range(chunks)]
+    high = [4 * i for i in range(1, slabs // 4)]
+    last = max(1, rows * P_PART // 8)
+    sizes = [rows - last, last]
+    firsts = [0, sizes[0]]
+    chunks = len(sizes)
     green = green_blocks.reshape(rows, square, atoms)
     columns = neighbours.T
 
     mate = swap(green, "energy", 1)
+
+    def lanes(row):
+        return jnp.pad(row.astype(F32), (0, atoms - modes))[None, :]
+
+    packed = jnp.concatenate([phonon_weight, lanes(occupation), lanes(mode_shift)], 0)
+    packed = jnp.pad(packed, ((0, SUBLANES - 2), (0, 0)))
     table = pl.pallas_call(
         table_kernel,
         out_shape=jax.ShapeDtypeStruct((pairs, rows, 2 * rows + 1, SUBLANES, atoms), F32),
-        in_specs=[HBM] * 3,
+        in_specs=[VMEM],
         out_specs=VMEM,
-        scratch_shapes=[
-            pltpu.SMEM((modes,), jnp.int32),
-            pltpu.SMEM((modes,), F32),
-            pltpu.VMEM((modes, atoms), F32),
-            pltpu.SemaphoreType.DMA((3,)),
-        ],
+        scratch_shapes=[pltpu.SMEM((SUBLANES, atoms), F32), pltpu.SemaphoreType.DMA],
         compiler_params=params(),
         cost_estimate=cost(1e6, 1e6),
-    )(mode_shift, occupation, phonon_weight)
+    )(packed)
     odd = lax.axis_index("energy") % 2 == 1
     pair = jnp.where(
         odd, jnp.concatenate([mate, green], 0), jnp.concatenate([green, mate], 0)
@@ -274,9 +298,10 @@
                 jax.ShapeDtypeStruct((square, local_bonds * square), BF16),
                 jax.ShapeDtypeStruct((square, REMOTE_BONDS * square), BF16),
                 jax.ShapeDtypeStruct((local_bonds * atoms, atoms), BF16),
+                jax.ShapeDtypeStruct((ID_ROWS, atoms), BF16),
             ),
             in_specs=[VMEM, VMEM, ANY],
-            out_specs=(VMEM, VMEM, VMEM),
+            out_specs=(VMEM,) * 4,
             compiler_params=params(),
             cost_estimate=cost(2e9, 3e6),
         )(derivative, columns, after)
@@ -294,77 +319,91 @@
             cost_estimate=cost(2e9, 3e6),
         )(mixed[chunk], local_hot, local_k, *after)
 
-    remote_ids = columns[local_bonds:, :]
-    ids = jnp.stack([remote_ids // atoms, remote_ids % atoms], 1).reshape(-1, atoms)
-    ids = jnp.pad(ids, ((0, ID_ROWS - ids.shape[0]), (0, 0))).astype(BF16)
-
     own, arrived = [], []
     after = []
     for chunk in range(chunks):
         away = [mix(group, chunk, BF16, after) for group in range(1, pairs)]
         arrived.append([swap(value, "energy", 2 * group) for group, value in enumerate(away, 1)])
         if chunk == 0:
-            local_k, remote_k, local_hot = prepare(away[0])
-            own.append(mix(0, chunk, F32, [local_hot]))
+            own.append(mix(0, chunk, F32, away[:1]))
             after = own[-1:]
         else:
-            after = away[:1]
-    mixed, local = [], []
+            local_k, remote_k, local_hot, ids = prepare(away[0])
+    mixed = []
     for chunk in range(chunks):
         if chunk > 0:
-            own.append(mix(0, chunk, F32, after + mixed[-1:] + local[-1:]))
+            own.append(mix(0, chunk, F32, mixed[-1:] + [local_hot]))
         total = own[chunk]
         for received in arrived[chunk]:
             total = total + received.astype(F32)
-        total = total.astype(BF16).reshape(-1, atoms)
-        mixed.append(jnp.concatenate([total, ids], 0) if chunk == 0 else total)
+        mixed.append(jnp.concatenate([total.astype(BF16).reshape(-1, atoms), ids], 0))
+
+    def ordered(value, after):
+        return pl.pallas_call(
+            pass_kernel,
+            out_shape=jax.ShapeDtypeStruct(value.shape, value.dtype),
+            in_specs=[VMEM, ANY],
+            out_specs=VMEM,
+            compiler_params=params(),
+            cost_estimate=cost(1e6, 1e6),
+        )(value, after)
+
+    plans = [([2], high), (high, [2])]
+    across = [[mixed[chunk]] + [swap(mixed[chunk], "atom", mask) for mask in masks]
+              for chunk, (masks, _) in enumerate(plans)]
+    local = [local_sum(0, mixed[-1:])]
+    after = local[0]
+    results, arrivals = [], []
+    for chunk, (_, flips) in enumerate(plans):
+        beside = across[chunk]
         if chunk > 0:
-            local.append(local_sum(chunk - 1, mixed[-1:]))
-    local.append(local_sum(chunks - 1, local[-1:]))
-
-    beside = swap(jnp.concatenate(mixed, 0), "atom", 1)
-    starts = [sum(value.shape[0] for value in mixed[:chunk]) for chunk in range(chunks)]
-
-    remote_hot = None
-    results = []
-    for chunk in range(chunks):
-        across = [swap(mixed[chunk], "atom", mask) for mask in high[1:]]
-        beyond = [swap(value, "atom", 1) for value in across]
-        sources = [mixed[chunk], beside] + across + beyond
-        offsets = [0, starts[chunk]] + [0] * (len(across) + len(beyond))
-        if remote_hot is None:
-            ends = sizes[0] * square
-            id_blocks = [
-                value[offset + ends : offset + ends + ID_ROWS]
-                for offset, value in zip(offsets, sources)
-            ]
-            remote_hot = pl.pallas_call(
-                functools.partial(remote_hot_kernel, REMOTE_BONDS, flip),
-                out_shape=jax.ShapeDtypeStruct(
-                    (2 * REMOTE_BONDS * atoms, len(sources) * atoms), BF16
-                ),
-                in_specs=[VMEM] * len(sources),
+            beside = beside[:1] + [ordered(value, after) for value in beside[1:]]
+            after = beside[1]
+            local.append(local_sum(chunk, [after]))
+            results.append(stay_sum(*waiting, after))
+            after = results[-1]
+        sources = across[chunk] + [swap(value, "atom", 1) for value in beside]
+        hots = pl.pallas_call(
+            functools.partial(remote_hot_kernel, REMOTE_BONDS, [0] + flips),
+            out_shape=jax.ShapeDtypeStruct(
+                ((1 + len(flips)) * REMOTE_BONDS * atoms, len(sources) * atoms), BF16
+            ),
+            in_specs=[VMEM] * len(sources) + [ANY],
+            out_specs=VMEM,
+            compiler_params=params(),
+            cost_estimate=cost(1e8, 1e6),
+        )(*sources, after)
+        block = jax.ShapeDtypeStruct((sizes[chunk], square, atoms), BF16)
+        away = pl.pallas_call(
+            functools.partial(away_kernel, len(sources)),
+            out_shape=(block,) * len(flips),
+            in_specs=[VMEM] * (len(sources) + 2) + [ANY],
+            out_specs=(VMEM,) * len(flips),
+            compiler_params=params(),
+            cost_estimate=cost(1e9, 3e6),
+        )(*sources, hots, remote_k, after)
+        received = [swap(value, "atom", flip) for value, flip in zip(away, flips)]
+
+        def stay_sum(chunk, sources, hots, after):
+            return pl.pallas_call(
+                functools.partial(stay_kernel, len(sources)),
+                out_shape=jax.ShapeDtypeStruct((sizes[chunk], square, atoms), F32),
+                in_specs=[VMEM] * (len(sources) + 3) + [ANY],
                 out_specs=VMEM,
                 compiler_params=params(),
-                cost_estimate=cost(1e8, 1e6),
-            )(*id_blocks)
-        after = local[-1:] + [partial for partial, _ in results[-1:]]
-        partial, away = pl.pallas_call(
-            functools.partial(remote_kernel, offsets),
-            out_shape=(
-                jax.ShapeDtypeStruct((sizes[chunk], square, atoms), F32),
-                jax.ShapeDtypeStruct((sizes[chunk], square, atoms), BF16),
-            ),
-            in_specs=[VMEM] * (len(sources) + 3) + [ANY] * len(after),
-            out_specs=(VMEM, VMEM),
-            compiler_params=params(),
-            cost_estimate=cost(1e9, 3e6),
-        )(*sources, remote_hot, remote_k, local[chunk], *after)
-        results.append((partial, swap(away, "atom", flip)))
-    combined = jnp.concatenate(
-        [partial + received.astype(F32) for partial, received in results], 0
-    )
-    return combined.reshape(rows, orbital, orbital, atoms)
+                cost_estimate=cost(1e9, 3e6),
+            )(*sources, hots, remote_k, local[chunk], after)
+
+        arrivals.append(received)
+        waiting = (chunk, sources, hots)
+        after = away[0]
+    results.append(stay_sum(*waiting, after))
+    combined = []
+    for stay, received in zip(results, arrivals):
+        for value in received:
+            stay = stay + value.astype(F32)
+        combined.append(stay)
+    return jnp.concatenate(combined, 0).reshape(rows, orbital, orbital, atoms)
 
 
 def solution(mesh):

time: 66.3 us -> 61.2 us (0.923)
  waiting for transfers between devices: 31.7 us -> 22.6 us
  other arithmetic: 1.55 us -> 4.1 us
  Pallas kernels: 15.9 us -> 17.4 us
  starting transfers between devices: 14.8 us -> 16.2 us
  local copies, waits for them, and re-layouts: 2.03 us -> 0.67 us
    ppermute x10 -> x11, waiting for transfers between devices: 31.7 us -> 22.6 us  [swap(): return lax.ppermute(value, axis, [(i, i ^ mask) for i in range(count)])]
    unnamed x12 -> x4, local copies, waits for them, and re-layouts: 2.01 us -> 0.01 us
    ppermute x10 -> x11, starting transfers between devices: 14.8 us -> 16.2 us  [swap(): return lax.ppermute(value, axis, [(i, i ^ mask) for i in range(count)])]
    select_n x1, other arithmetic: 0.16 us -> 1.43 us  [per_device(): jnp.where(odd, jnp.concatenate([mate, green], 0), jnp.concatenate([green,...]
    pallas_call x2, Pallas kernels: 4.71 us -> 5.58 us  [local_sum(): pl.pallas_call(local_kernel, out_shape=jax.ShapeDtypeStruct((sizes[chunk]...]
    concatenate x3 -> x4, other arithmetic: 1.12 us -> 1.77 us  [the longest x1 1.04 us: per_device(): return jnp.concatenate(combined, 0).reshape(rows, orbital, orbital, atoms)]
    pallas_call x3 -> x7, Pallas kernels: 3.88 us -> 4.26 us  [the longest x2 2.01 us: per_device(): pl.pallas_call(functools.partial(away_kernel, len(sources)), out_shape=(b...]
  transfers between devices with their start and end apart: 10 -> 11, of which waited for: 6 -> 7; matrix products, arithmetic and copies ran while one was open for 0% -> 4% of each run, Pallas kernels for 21% -> 27%
where the time goes in v3:
time: 61.2 us; the launch traced here: 61 us
  waiting for transfers between devices  22.6 us (37%)
  Pallas kernels  17.4 us (28%)
  starting transfers between devices  16.2 us (26%)
  other arithmetic  4.1 us (7%)
  local copies, waits for them, and re-layouts  0.67 us (1%)
    ppermute x11, waiting for transfers between devices, swap(): return lax.ppermute(value, axis, [(i, i ^ mask) for i in range(count)])  22.6 us
    ppermute x11, starting transfers between devices, swap(): return lax.ppermute(value, axis, [(i, i ^ mask) for i in range(count)])  16.2 us
    pallas_call x2, Pallas kernels, local_sum(): pl.pallas_call(local_kernel, out_shape=jax.ShapeDtypeStruct((sizes[chunk]...  5.58 us
    pallas_call x1, Pallas kernels, prepare(): pl.pallas_call(prepare_kernel, out_shape=(jax.ShapeDtypeStruct((square, l...  3.35 us
    pallas_call x4, Pallas kernels, mix(): pl.pallas_call(functools.partial(mix_kernel, group, firsts[chunk]), out_s...  2.96 us
    pallas_call x2, Pallas kernels, per_device(): pl.pallas_call(functools.partial(away_kernel, len(sources)), out_shape=(b...  2.01 us
    pallas_call x2, Pallas kernels, stay_sum(): pl.pallas_call(functools.partial(stay_kernel, len(sources)), out_shape=ja...  2 us
    select_n x1, other arithmetic, per_device(): jnp.where(odd, jnp.concatenate([mate, green], 0), jnp.concatenate([green,...  1.43 us
  transfers between devices with their start and end apart: 11, of which 7 were waited for; matrix products, arithmetic and copies ran while one was open for 4% of the time, Pallas kernels for 27%

profile of v3, /device:TPU:0, one launch (start us, length us, event | category | flops | bytes accessed | tf_op | source)
XLA Modules:
  0.0 61.0 jit_solution(15256858865465267628)
XLA Ops:
  2.5 1.2 %shard_map.64.table_ref = f32[2,8,17,8,128]{4,3,2,1,0:T(8,128)S(1)} custom-call(f32[16,128]{1,0:T(8,128)S(1)} %select_maximum_fusion.packed_ref), custom_call_target="tpu_custom_call" | custom-call | flops 1000000 | bytes 1000000 | tf_op jit(solution)/shard_map/pallas_call | solution.py:270
  3.7 1.4 %maximum_select_fusion.pair_ref = bf16[16,256,128]{2,1,0:T(8,128)(2,1)S(1)} fusion(bf16[8,256,128]{2,1,0:T(8,128)(2,1)} %bitcast.13, bf16[8,256,128]{2,1,0:T(8,128)(2,1)S(1)} %collective-permute-done, pred[]{:T(512)S(6)} %eq.5), kind=kLoop, calls=%fused_computation | loop fusion | flops 1572864 | bytes 2097153 | tf_op jit(solution)/shard_map/jit(_where)/select_n | solution.py:280
  5.9 2.6 %collective-permute-start.1 = (bf16[4,256,128]{2,1,0:T(8,128)(2,1)S(1)}, bf16[4,256,128]{2,1,0:T(8,128)(2,1)S(1)}, u32[]{:S(2)}, u32[]{:S(2)}) collective-permute-start(bf16[4,256,128]{2,1,0:T(8,128)(2,1)S(1)} %shard_map.65.rest_0_), channel_id=1, source_target_pairs={{0,16},{8,24},{16,0},{24,8},{1,17},{9,25},{17,1},{25,9},{2,18},{10... | collective-permute-start | bytes 786440 | tf_op jit(solution)/shard_map/ppermute | solution.py:33
  10.0 3.4 %shard_map.68 = (bf16[256,3584]{1,0:T(8,128)(2,1)S(1)}, bf16[256,512]{1,0:T(8,128)(2,1)S(1)}, bf16[1792,128]{1,0:T(8,128)(2,1)S(1)}, bf16[16,128]{1,0:T(8,128)(2,1)S(1)}) custom-call(bf16[16,16,16]{2,1,0:T(8,128)(2,1)S(1)} %copy-done, s32[16,128]{1,0:T(8,128)S(1)} %bitcast.9, bf16[4,256,128]{2,1,0:T(8,128)(2,1)S(1)} %shard_map.67.after_ref), custom_call_target="tpu_custom_call" | custom-call | flops 2000000000 | bytes 3000000 | tf_op jit(solution)/shard_map/pallas_call | solution.py:295
  13.4 2.2 %collective-permute-done.1 = bf16[4,256,128]{2,1,0:T(8,128)(2,1)S(1)} collective-permute-done((bf16[4,256,128]{2,1,0:T(8,128)(2,1)S(1)}, bf16[4,256,128]{2,1,0:T(8,128)(2,1)S(1)}, u32[]{:S(2)}, u32[]{:S(2)}) %collective-permute-start.1) | collective-permute-done | bytes 262176 | tf_op jit(solution)/shard_map/ppermute | solution.py:33
  15.7 2.1 %collective-permute-start.2 = (bf16[1040,128]{1,0:T(8,128)(2,1)S(1)}, bf16[1040,128]{1,0:T(8,128)(2,1)S(1)}, u32[]{:S(2)}, u32[]{:S(2)}) collective-permute-start(bf16[1040,128]{1,0:T(8,128)(2,1)S(1)} %pad_maximum_fusion.2.rest_0_.mixed_ref.refs_0_), channel_id=1, source_target_pairs={{0,2},{1,3},{2,0},{3,1},{4,6},{5,7},{6,4},{7,5},{8,10},{9,11},{10,... | collective-permute-start | bytes 798728 | tf_op jit(solution)/shard_map/ppermute | solution.py:33
  17.8 1.5 %collective-permute-start.3 = (bf16[1040,128]{1,0:T(8,128)(2,1)S(1)}, bf16[1040,128]{1,0:T(8,128)(2,1)S(1)}, u32[]{:S(2)}, u32[]{:S(2)}) collective-permute-start(bf16[1040,128]{1,0:T(8,128)(2,1)S(1)} %pad_maximum_fusion.2.rest_0_.mixed_ref.refs_0_), channel_id=1, source_target_pairs={{0,1},{1,0},{2,3},{3,2},{4,5},{5,4},{6,7},{7,6},{8,9},{9,8},{10,11... | collective-permute-start | bytes 798728 | tf_op jit(solution)/shard_map/ppermute | solution.py:33
  20.0 1.0 %collective-permute-done.5 = bf16[4,256,128]{2,1,0:T(8,128)(2,1)S(1)} collective-permute-done((bf16[4,256,128]{2,1,0:T(8,128)(2,1)S(1)}, bf16[4,256,128]{2,1,0:T(8,128)(2,1)S(1)}, u32[]{:S(2)}, u32[]{:S(2)}) %collective-permute-start.5) | collective-permute-done | bytes 262176 | tf_op jit(solution)/shard_map/ppermute | solution.py:33
  21.1 2.7 %collective-permute-done.2.refs_1_ = bf16[1040,128]{1,0:T(8,128)(2,1)S(1)} collective-permute-done((bf16[1040,128]{1,0:T(8,128)(2,1)S(1)}, bf16[1040,128]{1,0:T(8,128)(2,1)S(1)}, u32[]{:S(2)}, u32[]{:S(2)}) %collective-permute-start.2) | collective-permute-done | bytes 266272 | tf_op jit(solution)/shard_map/ppermute | solution.py:33
  23.8 1.6 %collective-permute-start.4 = (bf16[1040,128]{1,0:T(8,128)(2,1)S(1)}, bf16[1040,128]{1,0:T(8,128)(2,1)S(1)}, u32[]{:S(2)}, u32[]{:S(2)}) collective-permute-start(bf16[1040,128]{1,0:T(8,128)(2,1)S(1)} %collective-permute-done.2.refs_1_), channel_id=1, source_target_pairs={{0,1},{1,0},{2,3},{3,2},{4,5},{5,4},{6,7},{7,6},{8,9},{9,8},{10,11... | collective-permute-start | bytes 798728 | tf_op jit(solution)/shard_map/ppermute | solution.py:33
  25.4 2.7 %collective-permute-start.6 = (bf16[1040,128]{1,0:T(8,128)(2,1)S(1)}, bf16[1040,128]{1,0:T(8,128)(2,1)S(1)}, u32[]{:S(2)}, u32[]{:S(2)}) collective-permute-start(bf16[1040,128]{1,0:T(8,128)(2,1)S(1)} %pad_maximum_fusion.1.rest_0_.refs_0_.mixed_ref), channel_id=1, source_target_pairs={{0,4},{1,5},{2,6},{3,7},{4,0},{5,1},{6,2},{7,3},{8,12},{9,13},{10,... | collective-permute-start | bytes 798728 | tf_op jit(solution)/shard_map/ppermute | solution.py:33
  28.5 2.8 %shard_map.70.refs_4_.refs_6_ = f32[4,256,128]{2,1,0:T(8,128)S(1)} custom-call(bf16[1040,128]{1,0:T(8,128)(2,1)S(1)} %pad_maximum_fusion.2.rest_0_.mixed_ref.refs_0_, bf16[1792,128]{1,0:T(8,128)(2,1)S(1)} %get-tuple-element.10.rest_1_.hot_ref, bf16[256,3584]{1,0:T(8,128)(2,1)S(1)} %get-tuple-element.11.k_ref, ...), custom_call_target="tpu_custom_call" | custom-call | flops 2000000000 | bytes 3000000 | tf_op jit(solution)/shard_map/pallas_call | solution.py:310
  31.3 1.8 %collective-permute-done.4.refs_3_ = bf16[1040,128]{1,0:T(8,128)(2,1)S(1)} collective-permute-done((bf16[1040,128]{1,0:T(8,128)(2,1)S(1)}, bf16[1040,128]{1,0:T(8,128)(2,1)S(1)}, u32[]{:S(2)}, u32[]{:S(2)}) %collective-permute-start.4) | collective-permute-done | bytes 266272 | tf_op jit(solution)/shard_map/ppermute | solution.py:33
  33.2 1.0 %shard_map.72.after_ref = bf16[4,256,128]{2,1,0:T(8,128)(2,1)S(1)} custom-call(bf16[1040,128]{1,0:T(8,128)(2,1)S(1)} %pad_maximum_fusion.2.rest_0_.mixed_ref.refs_0_, bf16[1040,128]{1,0:T(8,128)(2,1)S(1)} %collective-permute-done.2.refs_1_, bf16[1040,128]{1,0:T(8,128)(2,1)S(1)} %collective-permute-done.3.refs_2_, ...), custom_call_target="tpu_custom_call" | custom-call | flops 1000000000 | bytes 3000000 | tf_op jit(solution)/shard_map/pallas_call | solution.py:377
  34.3 2.7 %collective-permute-start.7 = (bf16[4,256,128]{2,1,0:T(8,128)(2,1)S(1)}, bf16[4,256,128]{2,1,0:T(8,128)(2,1)S(1)}, u32[]{:S(2)}, u32[]{:S(2)}) collective-permute-start(bf16[4,256,128]{2,1,0:T(8,128)(2,1)S(1)} %shard_map.72.after_ref), channel_id=1, source_target_pairs={{0,4},{1,5},{2,6},{3,7},{4,0},{5,1},{6,2},{7,3},{8,12},{9,13},{10,... | collective-permute-start | bytes 786440 | tf_op jit(solution)/shard_map/ppermute | solution.py:33
  37.0 8.3 %collective-permute-done.6.value_ref.refs_1_ = bf16[1040,128]{1,0:T(8,128)(2,1)S(1)} collective-permute-done((bf16[1040,128]{1,0:T(8,128)(2,1)S(1)}, bf16[1040,128]{1,0:T(8,128)(2,1)S(1)}, u32[]{:S(2)}, u32[]{:S(2)}) %collective-permute-start.6) | collective-permute-done | bytes 266272 | tf_op jit(solution)/shard_map/ppermute | solution.py:33
  45.9 1.0 %shard_map.74.refs_4_.refs_6_ = f32[4,256,128]{2,1,0:T(8,128)S(1)} custom-call(bf16[1040,128]{1,0:T(8,128)(2,1)S(1)} %pad_maximum_fusion.2.rest_0_.mixed_ref.refs_0_, bf16[1040,128]{1,0:T(8,128)(2,1)S(1)} %collective-permute-done.2.refs_1_, bf16[1040,128]{1,0:T(8,128)(2,1)S(1)} %collective-permute-done.3.refs_2_, ...), custom_call_target="tpu_custom_call" | custom-call | flops 1000000000 | bytes 3000000 | tf_op jit(solution)/shard_map/pallas_call | solution.py:388
  46.9 2.8 %shard_map.76.refs_6_ = f32[4,256,128]{2,1,0:T(8,128)S(1)} custom-call(bf16[1040,128]{1,0:T(8,128)(2,1)S(1)} %pad_maximum_fusion.1.rest_0_.refs_0_.mixed_ref, bf16[1792,128]{1,0:T(8,128)(2,1)S(1)} %get-tuple-element.10.rest_1_.hot_ref, bf16[256,3584]{1,0:T(8,128)(2,1)S(1)} %get-tuple-element.11.k_ref, bf16[1040,128]{1,0:T(8,128)(2,1)S(1)} %shard_map.73.refs_7_.rest_0_), custom_call_target="tpu_custom_call" | custom-call | flops 2000000000 | bytes 3000000 | tf_op jit(solution)/shard_map/pallas_call | solution.py:310
  49.7 2.1 %collective-permute-done.9.refs_3_ = bf16[1040,128]{1,0:T(8,128)(2,1)S(1)} collective-permute-done((bf16[1040,128]{1,0:T(8,128)(2,1)S(1)}, bf16[1040,128]{1,0:T(8,128)(2,1)S(1)}, u32[]{:S(2)}, u32[]{:S(2)}) %collective-permute-start.9) | collective-permute-done | bytes 266272 | tf_op jit(solution)/shard_map/ppermute | solution.py:33
  51.9 1.0 %shard_map.77.refs_7_ = bf16[4,256,128]{2,1,0:T(8,128)(2,1)S(1)} custom-call(bf16[1040,128]{1,0:T(8,128)(2,1)S(1)} %pad_maximum_fusion.1.rest_0_.refs_0_.mixed_ref, bf16[1040,128]{1,0:T(8,128)(2,1)S(1)} %collective-permute-done.6.value_ref.refs_1_, bf16[1040,128]{1,0:T(8,128)(2,1)S(1)} %collective-permute-done.8.refs_2_, ...), custom_call_target="tpu_custom_call" | custom-call | flops 1000000000 | bytes 3000000 | tf_op jit(solution)/shard_map/pallas_call | solution.py:377
  52.9 1.5 %collective-permute-start.10 = (bf16[4,256,128]{2,1,0:T(8,128)(2,1)S(1)}, bf16[4,256,128]{2,1,0:T(8,128)(2,1)S(1)}, u32[]{:S(2)}, u32[]{:S(2)}) collective-permute-start(bf16[4,256,128]{2,1,0:T(8,128)(2,1)S(1)} %shard_map.77.refs_7_), channel_id=1, source_target_pairs={{0,2},{1,3},{2,0},{3,1},{4,6},{5,7},{6,4},{7,5},{8,10},{9,11},{10,... | collective-permute-start | bytes 786440 | tf_op jit(solution)/shard_map/ppermute | solution.py:33
  54.4 1.0 %shard_map.78 = f32[4,256,128]{2,1,0:T(8,128)S(1)} custom-call(bf16[1040,128]{1,0:T(8,128)(2,1)S(1)} %pad_maximum_fusion.1.rest_0_.refs_0_.mixed_ref, bf16[1040,128]{1,0:T(8,128)(2,1)S(1)} %collective-permute-done.6.value_ref.refs_1_, bf16[1040,128]{1,0:T(8,128)(2,1)S(1)} %collective-permute-done.8.refs_2_, ...), custom_call_target="tpu_custom_call" | custom-call | flops 1000000000 | bytes 3000000 | tf_op jit(solution)/shard_map/pallas_call | solution.py:388
  55.5 4.5 %collective-permute-done.10 = bf16[4,256,128]{2,1,0:T(8,128)(2,1)S(1)} collective-permute-done((bf16[4,256,128]{2,1,0:T(8,128)(2,1)S(1)}, bf16[4,256,128]{2,1,0:T(8,128)(2,1)S(1)}, u32[]{:S(2)}, u32[]{:S(2)}) %collective-permute-start.10) | collective-permute-done | bytes 262176 | tf_op jit(solution)/shard_map/ppermute | solution.py:33
  60.0 1.0 %pad_maximum_fusion = f32[8,256,128]{2,1,0:T(8,128)} fusion(f32[4,256,128]{2,1,0:T(8,128)S(1)} %convert_add_fusion, f32[4,256,128]{2,1,0:T(8,128)S(1)} %convert_add_fusion.1), kind=kLoop, calls=%fused_computation.1 | loop fusion | flops 262144 | bytes 2097152 | tf_op jit(solution)/shard_map/concatenate | solution.py:406
  (28 shorter events, 7.1 us)
Async XLA Ops:
  0.0 3.7 %collective-permute-start = (bf16[8,256,128]{2,1,0:T(8,128)(2,1)}, bf16[8,256,128]{2,1,0:T(8,128)(2,1)S(1)}, u32[]{:S(2)}, u32[]{:S(2)}) collective-permute-start(bf16[8,256,128]{2,1,0:T(8,128)(2,1)} %bitcast.12), channel_id=1, source_target_pairs={{0,8},{8,0},{16,24},{24,16},{1,9},{9,1},{17,25},{25,17},{2,10},{10... | collective-permute-start | bytes 1572872 | tf_op jit(solution)/shard_map/ppermute | solution.py:33
  5.9 9.7 %collective-permute-start.1 = (bf16[4,256,128]{2,1,0:T(8,128)(2,1)S(1)}, bf16[4,256,128]{2,1,0:T(8,128)(2,1)S(1)}, u32[]{:S(2)}, u32[]{:S(2)}) collective-permute-start(bf16[4,256,128]{2,1,0:T(8,128)(2,1)S(1)} %shard_map.65.rest_0_), channel_id=1, source_target_pairs={{0,16},{8,24},{16,0},{24,8},{1,17},{9,25},{17,1},{25,9},{2,18},{10... | collective-permute-start | bytes 786440 | tf_op jit(solution)/shard_map/ppermute | solution.py:33
  9.2 0.9 %copy-start = (bf16[16,16,16]{2,1,0:T(8,128)(2,1)S(1)}, bf16[16,16,16]{2,1,0:T(8,128)(2,1)}, u32[]{:S(2)}) copy-start(bf16[16,16,16]{2,1,0:T(8,128)(2,1)} %derivative_ref.1) | copy-start | bytes 24580
  9.2 0.8 %copy-start.1 = (s32[128,16]{0,1:T(8,128)S(1)}, s32[128,16]{0,1:T(8,128)}, u32[]{:S(2)}) copy-start(s32[128,16]{0,1:T(8,128)} %param.11) | copy-start | bytes 24580
  9.9 11.1 %collective-permute-start.5 = (bf16[4,256,128]{2,1,0:T(8,128)(2,1)S(1)}, bf16[4,256,128]{2,1,0:T(8,128)(2,1)S(1)}, u32[]{:S(2)}, u32[]{:S(2)}) collective-permute-start(bf16[4,256,128]{2,1,0:T(8,128)(2,1)S(1)} %shard_map.67.after_ref), channel_id=1, source_target_pairs={{0,16},{8,24},{16,0},{24,8},{1,17},{9,25},{17,1},{25,9},{2,18},{10... | collective-permute-start | bytes 786440 | tf_op jit(solution)/shard_map/ppermute | solution.py:33
  15.7 8.1 %collective-permute-start.2 = (bf16[1040,128]{1,0:T(8,128)(2,1)S(1)}, bf16[1040,128]{1,0:T(8,128)(2,1)S(1)}, u32[]{:S(2)}, u32[]{:S(2)}) collective-permute-start(bf16[1040,128]{1,0:T(8,128)(2,1)S(1)} %pad_maximum_fusion.2.rest_0_.mixed_ref.refs_0_), channel_id=1, source_target_pairs={{0,2},{1,3},{2,0},{3,1},{4,6},{5,7},{6,4},{7,5},{8,10},{9,11},{10,... | collective-permute-start | bytes 798728 | tf_op jit(solution)/shard_map/ppermute | solution.py:33
  17.8 13.6 %collective-permute-start.3 = (bf16[1040,128]{1,0:T(8,128)(2,1)S(1)}, bf16[1040,128]{1,0:T(8,128)(2,1)S(1)}, u32[]{:S(2)}, u32[]{:S(2)}) collective-permute-start(bf16[1040,128]{1,0:T(8,128)(2,1)S(1)} %pad_maximum_fusion.2.rest_0_.mixed_ref.refs_0_), channel_id=1, source_target_pairs={{0,1},{1,0},{2,3},{3,2},{4,5},{5,4},{6,7},{7,6},{8,9},{9,8},{10,11... | collective-permute-start | bytes 798728 | tf_op jit(solution)/shard_map/ppermute | solution.py:33
  23.8 9.3 %collective-permute-start.4 = (bf16[1040,128]{1,0:T(8,128)(2,1)S(1)}, bf16[1040,128]{1,0:T(8,128)(2,1)S(1)}, u32[]{:S(2)}, u32[]{:S(2)}) collective-permute-start(bf16[1040,128]{1,0:T(8,128)(2,1)S(1)} %collective-permute-done.2.refs_1_), channel_id=1, source_target_pairs={{0,1},{1,0},{2,3},{3,2},{4,5},{5,4},{6,7},{7,6},{8,9},{9,8},{10,11... | collective-permute-start | bytes 798728 | tf_op jit(solution)/shard_map/ppermute | solution.py:33
  25.4 19.9 %collective-permute-start.6 = (bf16[1040,128]{1,0:T(8,128)(2,1)S(1)}, bf16[1040,128]{1,0:T(8,128)(2,1)S(1)}, u32[]{:S(2)}, u32[]{:S(2)}) collective-permute-start(bf16[1040,128]{1,0:T(8,128)(2,1)S(1)} %pad_maximum_fusion.1.rest_0_.refs_0_.mixed_ref), channel_id=1, source_target_pairs={{0,4},{1,5},{2,6},{3,7},{4,0},{5,1},{6,2},{7,3},{8,12},{9,13},{10,... | collective-permute-start | bytes 798728 | tf_op jit(solution)/shard_map/ppermute | solution.py:33
  28.0 21.6 %collective-permute-start.8 = (bf16[1040,128]{1,0:T(8,128)(2,1)S(1)}, bf16[1040,128]{1,0:T(8,128)(2,1)S(1)}, u32[]{:S(2)}, u32[]{:S(2)}) collective-permute-start(bf16[1040,128]{1,0:T(8,128)(2,1)S(1)} %pad_maximum_fusion.1.rest_0_.refs_0_.mixed_ref), channel_id=1, source_target_pairs={{0,1},{1,0},{2,3},{3,2},{4,5},{5,4},{6,7},{7,6},{8,9},{9,8},{10,11... | collective-permute-start | bytes 798728 | tf_op jit(solution)/shard_map/ppermute | solution.py:33
  34.3 20.1 %collective-permute-start.7 = (bf16[4,256,128]{2,1,0:T(8,128)(2,1)S(1)}, bf16[4,256,128]{2,1,0:T(8,128)(2,1)S(1)}, u32[]{:S(2)}, u32[]{:S(2)}) collective-permute-start(bf16[4,256,128]{2,1,0:T(8,128)(2,1)S(1)} %shard_map.72.after_ref), channel_id=1, source_target_pairs={{0,4},{1,5},{2,6},{3,7},{4,0},{5,1},{6,2},{7,3},{8,12},{9,13},{10,... | collective-permute-start | bytes 786440 | tf_op jit(solution)/shard_map/ppermute | solution.py:33
  45.3 6.5 %collective-permute-start.9 = (bf16[1040,128]{1,0:T(8,128)(2,1)S(1)}, bf16[1040,128]{1,0:T(8,128)(2,1)S(1)}, u32[]{:S(2)}, u32[]{:S(2)}) collective-permute-start(bf16[1040,128]{1,0:T(8,128)(2,1)S(1)} %shard_map.73.refs_7_.rest_0_), channel_id=1, source_target_pairs={{0,1},{1,0},{2,3},{3,2},{4,5},{5,4},{6,7},{7,6},{8,9},{9,8},{10,11... | collective-permute-start | bytes 798728 | tf_op jit(solution)/shard_map/ppermute | solution.py:33
  52.9 7.0 %collective-permute-start.10 = (bf16[4,256,128]{2,1,0:T(8,128)(2,1)S(1)}, bf16[4,256,128]{2,1,0:T(8,128)(2,1)S(1)}, u32[]{:S(2)}, u32[]{:S(2)}) collective-permute-start(bf16[4,256,128]{2,1,0:T(8,128)(2,1)S(1)} %shard_map.77.refs_7_), channel_id=1, source_target_pairs={{0,2},{1,3},{2,0},{3,1},{4,6},{5,7},{6,4},{7,5},{8,10},{9,11},{10,... | collective-permute-start | bytes 786440 | tf_op jit(solution)/shard_map/ppermute | solution.py:33

commit v4 on v3

--- a/solution.py
+++ b/solution.py
@@ -15,7 +15,7 @@
 VMEM_LIMIT = 48 * 1024 * 1024
 
 VMEM = pl.BlockSpec(memory_space=pltpu.VMEM)
-HBM = pl.BlockSpec(memory_space=pltpu.HBM)
+SMEM = pl.BlockSpec(memory_space=pltpu.SMEM)
 ANY = pl.BlockSpec(memory_space=pl.ANY)
 F32, BF16 = jnp.float32, jnp.bfloat16
 
@@ -41,61 +41,53 @@
     return lax.dot_general(left, right, (((1,), (1,)), ((), ())), preferred_element_type=F32)
 
 
-def table_kernel(packed_ref, table_ref, scalar_ref, sem):
-    groups, rows, spare = table_ref.shape[:3]
-    span = spare - 1
-    modes = packed_ref.shape[0] - SUBLANES
-    copy = pltpu.make_async_copy(packed_ref.at[pl.ds(modes, SUBLANES)], scalar_ref, sem)
-    copy.start()
+def mix_kernel(group, first, shift_ref, coupling_ref, own_ref, mate_ref, *rest):
+    out_ref, table_ref = rest[-2:]
+    span, square, atoms = own_ref.shape
+    rows = out_ref.shape[0]
+    tile = table_ref.shape[2]
+    modes = coupling_ref.shape[0] // 2
+    me = lax.axis_index("energy")
+    base = me // 2 * 2 * span
+    move = me % 2 * span
+    target = me ^ (2 * group)
     table_ref[...] = jnp.zeros_like(table_ref)
-    copy.wait()
-    me = lax.axis_index("energy")
-    base = me // 2 * span
-
-    def put(group, row, source, value):
-        slot = source - base
-        inside = jnp.logical_and(slot >= 0, slot < span)
-        table_ref[group, row, jnp.where(inside, slot, span)] = value
+    couplings = coupling_ref[...].astype(F32)
+
+    def put(row, source, value):
+        place = source - base
+        slot = jnp.where(place < span, place + move, place - move)
+        inside = jnp.logical_and(place >= 0, place < 2 * span)
+        table_ref[row, jnp.where(inside, slot, 2 * span)] = value
 
     for mode in range(modes):
-        occupied = scalar_ref[0, mode]
-        shift = scalar_ref[1, mode].astype(jnp.int32)
-        weight = jnp.broadcast_to(packed_ref[mode : mode + 1, :], table_ref.shape[3:])
-        emission = (weight * (occupied + 1.0)).astype(BF16).astype(F32)
-        absorption = (weight * occupied).astype(BF16).astype(F32)
-        for group in range(groups):
-            target = me ^ (2 * group)
-            for row in range(rows):
-                energy = target * rows + row
-                if group == 0:
-                    put(group, row, energy - shift, emission)
-                    put(group, row, energy + shift, absorption)
-                else:
-                    above = target > me
-                    put(
-                        group,
-                        row,
-                        jnp.where(above, energy - shift, energy + shift),
-                        jnp.where(above, emission, absorption),
-                    )
-
-
-def mix_kernel(group, first, table_ref, pair_ref, *rest):
-    out_ref = rest[-1]
-    span, square, atoms = pair_ref.shape
-    rows = out_ref.shape[0]
-    tile = table_ref.shape[3]
+        shift = shift_ref[mode]
+        emission = jnp.broadcast_to(couplings[mode : mode + 1, :], (tile, atoms))
+        absorption = jnp.broadcast_to(couplings[modes + mode : modes + mode + 1, :], (tile, atoms))
+        if group > 0:
+            above = target > me
+            sign = jnp.where(above, -shift, shift)
+            coupling = jnp.where(above, emission, absorption)
+        for row in range(rows):
+            energy = target * span + first + row
+            if group == 0:
+                put(row, energy - shift, emission)
+                put(row, energy + shift, absorption)
+            else:
+                put(row, energy + sign, coupling)
+
     step = min(32, square)
 
     def body(block, carry):
         at = pl.multiple_of(block * step, step)
         totals = [None] * rows
-        for slot in range(span):
-            values = pair_ref[slot, pl.ds(at, step), :].astype(F32).reshape(
+        for slot in range(2 * span):
+            ref = own_ref if slot < span else mate_ref
+            values = ref[slot % span, pl.ds(at, step), :].astype(F32).reshape(
                 step // tile, tile, atoms
             )
             for row in range(rows):
-                term = table_ref[group, first + row, slot][None] * values
+                term = table_ref[row, slot][None] * values
                 totals[row] = term if totals[row] is None else totals[row] + term
         for row in range(rows):
             out_ref[row, pl.ds(at, step), :] = totals[row].reshape(step, atoms).astype(out_ref.dtype)
@@ -262,34 +254,21 @@
 
     mate = swap(green, "energy", 1)
 
-    def lanes(row):
-        return jnp.pad(row.astype(F32), (0, atoms - modes))[None, :]
-
-    packed = jnp.concatenate([phonon_weight, lanes(occupation), lanes(mode_shift)], 0)
-    packed = jnp.pad(packed, ((0, SUBLANES - 2), (0, 0)))
-    table = pl.pallas_call(
-        table_kernel,
-        out_shape=jax.ShapeDtypeStruct((pairs, rows, 2 * rows + 1, SUBLANES, atoms), F32),
-        in_specs=[VMEM],
-        out_specs=VMEM,
-        scratch_shapes=[pltpu.SMEM((SUBLANES, atoms), F32), pltpu.SemaphoreType.DMA],
-        compiler_params=params(),
-        cost_estimate=cost(1e6, 1e6),
-    )(packed)
-    odd = lax.axis_index("energy") % 2 == 1
-    pair = jnp.where(
-        odd, jnp.concatenate([mate, green], 0), jnp.concatenate([green, mate], 0)
-    )
+    occupied = occupation[:, None]
+    couplings = jnp.concatenate(
+        [phonon_weight * (occupied + 1.0), phonon_weight * occupied], 0
+    ).astype(BF16)
 
     def mix(group, chunk, kind, after):
         return pl.pallas_call(
             functools.partial(mix_kernel, group, firsts[chunk]),
             out_shape=jax.ShapeDtypeStruct((sizes[chunk], square, atoms), kind),
-            in_specs=[VMEM, VMEM] + [ANY] * len(after),
+            in_specs=[SMEM, VMEM, VMEM, VMEM] + [ANY] * len(after),
             out_specs=VMEM,
+            scratch_shapes=[pltpu.VMEM((sizes[chunk], 2 * rows + 1, SUBLANES, atoms), F32)],
             compiler_params=params(),
             cost_estimate=cost(5e8, 1e6),
-        )(table, pair, *after)
+        )(mode_shift, couplings, green, mate, *after)
 
     def prepare(after):
         return pl.pallas_call(
@@ -348,21 +327,22 @@
             cost_estimate=cost(1e6, 1e6),
         )(value, after)
 
-    plans = [([2], high), (high, [2])]
+    plans = [([2, 1, 3], high), (high, [2])]
     across = [[mixed[chunk]] + [swap(mixed[chunk], "atom", mask) for mask in masks]
               for chunk, (masks, _) in enumerate(plans)]
     local = [local_sum(0, mixed[-1:])]
     after = local[0]
     results, arrivals = [], []
     for chunk, (_, flips) in enumerate(plans):
-        beside = across[chunk]
-        if chunk > 0:
-            beside = beside[:1] + [ordered(value, after) for value in beside[1:]]
+        if chunk == 0:
+            sources = across[chunk]
+        else:
+            beside = [mixed[chunk]] + [ordered(value, after) for value in across[chunk][1:]]
+            sources = across[chunk] + [swap(value, "atom", 1) for value in beside]
             after = beside[1]
             local.append(local_sum(chunk, [after]))
             results.append(stay_sum(*waiting, after))
             after = results[-1]
-        sources = across[chunk] + [swap(value, "atom", 1) for value in beside]
         hots = pl.pallas_call(
             functools.partial(remote_hot_kernel, REMOTE_BONDS, [0] + flips),
             out_shape=jax.ShapeDtypeStruct(

time: 61.2 us -> 56.3 us (0.920)
  waiting for transfers between devices: 22.6 us -> 15.6 us
  Pallas kernels: 17.4 us -> 19 us
  other arithmetic: 4.1 us -> 2.76 us
  local copies, waits for them, and re-layouts: 0.67 us -> 1.72 us
    ppermute x11, waiting for transfers between devices: 22.6 us -> 15.6 us  [swap(): return lax.ppermute(value, axis, [(i, i ^ mask) for i in range(count)])]
    pallas_call x4, Pallas kernels: 2.96 us -> 5.79 us  [mix(): pl.pallas_call(functools.partial(mix_kernel, group, firsts[chunk]), out_s...]
    unnamed x4 -> x12, local copies, waits for them, and re-layouts: 0.01 us -> 1.72 us
    select_n x1 -> x0, other arithmetic: 1.43 us -> none  [per_device(): jnp.where(odd, jnp.concatenate([mate, green], 0), jnp.concatenate([green,...]
    pallas_call x1 -> x0, Pallas kernels: 1.2 us -> none  [per_device(): pl.pallas_call(table_kernel, out_shape=jax.ShapeDtypeStruct((pairs, rows,...]
    another operation x0 -> x1, other arithmetic: none -> 0.76 us
    concatenate x1, other arithmetic: 0.69 us -> 0.01 us  [per_device(): jnp.concatenate([phonon_weight * (occupied + 1.0), phonon_weight * occupi...]
    ppermute x11, starting transfers between devices: 16.2 us -> 16.8 us  [swap(): return lax.ppermute(value, axis, [(i, i ^ mask) for i in range(count)])]
  transfers between devices with their start and end apart: 11 -> 11, of which waited for: 7 -> 7; matrix products, arithmetic and copies ran while one was open for 4% -> 3% of each run, Pallas kernels for 27% -> 31%
where the time goes in v4:
time: 56.3 us; the launch traced here: 56.1 us
  Pallas kernels  19 us (34%)
  starting transfers between devices  16.8 us (30%)
  waiting for transfers between devices  15.6 us (28%)
  other arithmetic  2.76 us (5%)
  local copies, waits for them, and re-layouts  1.72 us (3%)
    ppermute x11, starting transfers between devices, swap(): return lax.ppermute(value, axis, [(i, i ^ mask) for i in range(count)])  16.8 us
    ppermute x11, waiting for transfers between devices, swap(): return lax.ppermute(value, axis, [(i, i ^ mask) for i in range(count)])  15.6 us
    pallas_call x4, Pallas kernels, mix(): pl.pallas_call(functools.partial(mix_kernel, group, firsts[chunk]), out_s...  5.79 us
    pallas_call x2, Pallas kernels, local_sum(): pl.pallas_call(local_kernel, out_shape=jax.ShapeDtypeStruct((sizes[chunk]...  5.58 us
    pallas_call x1, Pallas kernels, prepare(): pl.pallas_call(prepare_kernel, out_shape=(jax.ShapeDtypeStruct((square, l...  3.35 us
    pallas_call x2, Pallas kernels, per_device(): pl.pallas_call(functools.partial(away_kernel, len(sources)), out_shape=(b...  2 us
    pallas_call x2, Pallas kernels, stay_sum(): pl.pallas_call(functools.partial(stay_kernel, len(sources)), out_shape=ja...  1.99 us
    unnamed x12, local copies, waits for them, and re-layouts  1.72 us
  transfers between devices with their start and end apart: 11, of which 7 were waited for; matrix products, arithmetic and copies ran while one was open for 3% of the time, Pallas kernels for 31%

profile of v4, /device:TPU:0, one launch (start us, length us, event | category | flops | bytes accessed | tf_op | source)
XLA Modules:
  0.0 56.1 jit_solution(14786494376555225460)
XLA Ops:
  2.2 1.0 %copy-done = bf16[8,16,16,128]{3,2,1,0:T(8,128)(2,1)S(1)} copy-done((bf16[8,16,16,128]{3,2,1,0:T(8,128)(2,1)S(1)}, bf16[8,16,16,128]{3,2,1,0:T(8,128)(2,1)}, u32[]{:S(2)}) %copy-start) | copy-done | bytes 524312
  3.9 1.4 %shard_map.64.rest_0_ = bf16[4,256,128]{2,1,0:T(8,128)(2,1)S(1)} custom-call(s32[8]{0:T(128)S(1)} %copy-done.2, bf16[16,128]{1,0:T(8,128)(2,1)S(1)} %pad_maximum_fusion.3.coupling_ref, bf16[8,256,128]{2,1,0:T(8,128)(2,1)S(1)} %bitcast.6, bf16[8,256,128]{2,1,0:T(8,128)(2,1)S(1)} %collective-permute-done.mate_ref), custom_call_target="tpu_custom_call" | custom-call | flops 500000000 | bytes 1000000 | tf_op jit(solution)/shard_map/pallas_call | solution.py:263
  5.3 2.9 %collective-permute-start.1 = (bf16[4,256,128]{2,1,0:T(8,128)(2,1)S(1)}, bf16[4,256,128]{2,1,0:T(8,128)(2,1)S(1)}, u32[]{:S(2)}, u32[]{:S(2)}) collective-permute-start(bf16[4,256,128]{2,1,0:T(8,128)(2,1)S(1)} %shard_map.64.rest_0_), channel_id=1, source_target_pairs={{0,16},{8,24},{16,0},{24,8},{1,17},{9,25},{17,1},{25,9},{2,18},{10... | collective-permute-start | bytes 786440 | tf_op jit(solution)/shard_map/ppermute | solution.py:33
  8.2 1.5 %shard_map.65.rest_0_ = f32[4,256,128]{2,1,0:T(8,128)S(1)} custom-call(s32[8]{0:T(128)S(1)} %copy-done.2, bf16[16,128]{1,0:T(8,128)(2,1)S(1)} %pad_maximum_fusion.3.coupling_ref, bf16[8,256,128]{2,1,0:T(8,128)(2,1)S(1)} %bitcast.7, bf16[8,256,128]{2,1,0:T(8,128)(2,1)S(1)} %collective-permute-done.mate_ref, bf16[4,256,128]{2,1,0:T(8,128)(2,1)S(1)} %shard_map.64.rest_0_), custom_call_target="tpu_custom_call" | custom-call | flops 500000000 | bytes 1000000 | tf_op jit(solution)/shard_map/pallas_call | solution.py:263
  9.7 1.4 %shard_map.66.after_ref = bf16[4,256,128]{2,1,0:T(8,128)(2,1)S(1)} custom-call(s32[8]{0:T(128)S(1)} %copy-done.2, bf16[16,128]{1,0:T(8,128)(2,1)S(1)} %pad_maximum_fusion.3.coupling_ref, bf16[8,256,128]{2,1,0:T(8,128)(2,1)S(1)} %bitcast.8, bf16[8,256,128]{2,1,0:T(8,128)(2,1)S(1)} %collective-permute-done.mate_ref, f32[4,256,128]{2,1,0:T(8,128)S(1)} %shard_map.65.rest_0_), custom_call_target="tpu_custom_call" | custom-call | flops 500000000 | bytes 1000000 | tf_op jit(solution)/shard_map/pallas_call | solution.py:263
  11.2 3.4 %shard_map.67 = (bf16[256,3584]{1,0:T(8,128)(2,1)S(1)}, bf16[256,512]{1,0:T(8,128)(2,1)S(1)}, bf16[1792,128]{1,0:T(8,128)(2,1)S(1)}, bf16[16,128]{1,0:T(8,128)(2,1)S(1)}) custom-call(bf16[16,16,16]{2,1,0:T(8,128)(2,1)S(1)} %copy-done.4, s32[16,128]{1,0:T(8,128)S(1)} %bitcast.10, bf16[4,256,128]{2,1,0:T(8,128)(2,1)S(1)} %shard_map.66.after_ref), custom_call_target="tpu_custom_call" | custom-call | flops 2000000000 | bytes 3000000 | tf_op jit(solution)/shard_map/pallas_call | solution.py:274
  15.4 2.2 %collective-permute-start.2 = (bf16[1040,128]{1,0:T(8,128)(2,1)S(1)}, bf16[1040,128]{1,0:T(8,128)(2,1)S(1)}, u32[]{:S(2)}, u32[]{:S(2)}) collective-permute-start(bf16[1040,128]{1,0:T(8,128)(2,1)S(1)} %pad_maximum_fusion.2.rest_0_.mixed_ref.refs_0_), channel_id=1, source_target_pairs={{0,2},{1,3},{2,0},{3,1},{4,6},{5,7},{6,4},{7,5},{8,10},{9,11},{10,... | collective-permute-start | bytes 798728 | tf_op jit(solution)/shard_map/ppermute | solution.py:33
  17.6 1.5 %collective-permute-start.3 = (bf16[1040,128]{1,0:T(8,128)(2,1)S(1)}, bf16[1040,128]{1,0:T(8,128)(2,1)S(1)}, u32[]{:S(2)}, u32[]{:S(2)}) collective-permute-start(bf16[1040,128]{1,0:T(8,128)(2,1)S(1)} %pad_maximum_fusion.2.rest_0_.mixed_ref.refs_0_), channel_id=1, source_target_pairs={{0,1},{1,0},{2,3},{3,2},{4,5},{5,4},{6,7},{7,6},{8,9},{9,8},{10,11... | collective-permute-start | bytes 798728 | tf_op jit(solution)/shard_map/ppermute | solution.py:33
  19.2 1.5 %shard_map.68 = f32[4,256,128]{2,1,0:T(8,128)S(1)} custom-call(s32[8]{0:T(128)S(1)} %copy-done.3, bf16[16,128]{1,0:T(8,128)(2,1)S(1)} %pad_maximum_fusion.3.coupling_ref, bf16[8,256,128]{2,1,0:T(8,128)(2,1)S(1)} %bitcast.9, bf16[8,256,128]{2,1,0:T(8,128)(2,1)S(1)} %collective-permute-done.mate_ref, ...), custom_call_target="tpu_custom_call" | custom-call | flops 500000000 | bytes 1000000 | tf_op jit(solution)/shard_map/pallas_call | solution.py:263
  20.8 3.0 %collective-permute-start.6 = (bf16[1040,128]{1,0:T(8,128)(2,1)S(1)}, bf16[1040,128]{1,0:T(8,128)(2,1)S(1)}, u32[]{:S(2)}, u32[]{:S(2)}) collective-permute-start(bf16[1040,128]{1,0:T(8,128)(2,1)S(1)} %pad_maximum_fusion.1.rest_0_.refs_0_.mixed_ref), channel_id=1, source_target_pairs={{0,4},{1,5},{2,6},{3,7},{4,0},{5,1},{6,2},{7,3},{8,12},{9,13},{10,... | collective-permute-start | bytes 798728 | tf_op jit(solution)/shard_map/ppermute | solution.py:33
  23.8 1.5 %collective-permute-start.8 = (bf16[1040,128]{1,0:T(8,128)(2,1)S(1)}, bf16[1040,128]{1,0:T(8,128)(2,1)S(1)}, u32[]{:S(2)}, u32[]{:S(2)}) collective-permute-start(bf16[1040,128]{1,0:T(8,128)(2,1)S(1)} %pad_maximum_fusion.1.rest_0_.refs_0_.mixed_ref), channel_id=1, source_target_pairs={{0,1},{1,0},{2,3},{3,2},{4,5},{5,4},{6,7},{7,6},{8,9},{9,8},{10,11... | collective-permute-start | bytes 798728 | tf_op jit(solution)/shard_map/ppermute | solution.py:33
  25.4 2.8 %shard_map.69.refs_4_.refs_6_ = f32[4,256,128]{2,1,0:T(8,128)S(1)} custom-call(bf16[1040,128]{1,0:T(8,128)(2,1)S(1)} %pad_maximum_fusion.2.rest_0_.mixed_ref.refs_0_, bf16[1792,128]{1,0:T(8,128)(2,1)S(1)} %get-tuple-element.10.rest_1_.hot_ref, bf16[256,3584]{1,0:T(8,128)(2,1)S(1)} %get-tuple-element.11.k_ref, ...), custom_call_target="tpu_custom_call" | custom-call | flops 2000000000 | bytes 3000000 | tf_op jit(solution)/shard_map/pallas_call | solution.py:289
  28.2 2.5 %collective-permute-done.2.refs_1_ = bf16[1040,128]{1,0:T(8,128)(2,1)S(1)} collective-permute-done((bf16[1040,128]{1,0:T(8,128)(2,1)S(1)}, bf16[1040,128]{1,0:T(8,128)(2,1)S(1)}, u32[]{:S(2)}, u32[]{:S(2)}) %collective-permute-start.2) | collective-permute-done | bytes 266272 | tf_op jit(solution)/shard_map/ppermute | solution.py:33
  30.7 5.0 %collective-permute-done.4.refs_3_ = bf16[1040,128]{1,0:T(8,128)(2,1)S(1)} collective-permute-done((bf16[1040,128]{1,0:T(8,128)(2,1)S(1)}, bf16[1040,128]{1,0:T(8,128)(2,1)S(1)}, u32[]{:S(2)}, u32[]{:S(2)}) %collective-permute-start.4) | collective-permute-done | bytes 266272 | tf_op jit(solution)/shard_map/ppermute | solution.py:33
  35.8 1.0 %shard_map.71.after_ref = bf16[4,256,128]{2,1,0:T(8,128)(2,1)S(1)} custom-call(bf16[1040,128]{1,0:T(8,128)(2,1)S(1)} %pad_maximum_fusion.2.rest_0_.mixed_ref.refs_0_, bf16[1040,128]{1,0:T(8,128)(2,1)S(1)} %collective-permute-done.2.refs_1_, bf16[1040,128]{1,0:T(8,128)(2,1)S(1)} %collective-permute-done.3.refs_2_, ...), custom_call_target="tpu_custom_call" | custom-call | flops 1000000000 | bytes 3000000 | tf_op jit(solution)/shard_map/pallas_call | solution.py:357
  36.9 1.5 %collective-permute-start.9 = (bf16[1040,128]{1,0:T(8,128)(2,1)S(1)}, bf16[1040,128]{1,0:T(8,128)(2,1)S(1)}, u32[]{:S(2)}, u32[]{:S(2)}) collective-permute-start(bf16[1040,128]{1,0:T(8,128)(2,1)S(1)} %shard_map.72.refs_7_.rest_0_), channel_id=1, source_target_pairs={{0,1},{1,0},{2,3},{3,2},{4,5},{5,4},{6,7},{7,6},{8,9},{9,8},{10,11... | collective-permute-start | bytes 798728 | tf_op jit(solution)/shard_map/ppermute | solution.py:33
  39.4 2.8 %shard_map.75.refs_6_ = f32[4,256,128]{2,1,0:T(8,128)S(1)} custom-call(bf16[1040,128]{1,0:T(8,128)(2,1)S(1)} %pad_maximum_fusion.1.rest_0_.refs_0_.mixed_ref, bf16[1792,128]{1,0:T(8,128)(2,1)S(1)} %get-tuple-element.10.rest_1_.hot_ref, bf16[256,3584]{1,0:T(8,128)(2,1)S(1)} %get-tuple-element.11.k_ref, bf16[1040,128]{1,0:T(8,128)(2,1)S(1)} %shard_map.72.refs_7_.rest_0_), custom_call_target="tpu_custom_call" | custom-call | flops 2000000000 | bytes 3000000 | tf_op jit(solution)/shard_map/pallas_call | solution.py:289
  42.3 1.1 %collective-permute-done.9.refs_3_ = bf16[1040,128]{1,0:T(8,128)(2,1)S(1)} collective-permute-done((bf16[1040,128]{1,0:T(8,128)(2,1)S(1)}, bf16[1040,128]{1,0:T(8,128)(2,1)S(1)}, u32[]{:S(2)}, u32[]{:S(2)}) %collective-permute-start.9) | collective-permute-done | bytes 266272 | tf_op jit(solution)/shard_map/ppermute | solution.py:33
  43.5 1.0 %shard_map.76.refs_7_ = bf16[4,256,128]{2,1,0:T(8,128)(2,1)S(1)} custom-call(bf16[1040,128]{1,0:T(8,128)(2,1)S(1)} %pad_maximum_fusion.1.rest_0_.refs_0_.mixed_ref, bf16[1040,128]{1,0:T(8,128)(2,1)S(1)} %collective-permute-done.6.value_ref.refs_1_, bf16[1040,128]{1,0:T(8,128)(2,1)S(1)} %collective-permute-done.8.refs_2_, ...), custom_call_target="tpu_custom_call" | custom-call | flops 1000000000 | bytes 3000000 | tf_op jit(solution)/shard_map/pallas_call | solution.py:357
  44.5 3.5 %collective-permute-start.10 = (bf16[4,256,128]{2,1,0:T(8,128)(2,1)S(1)}, bf16[4,256,128]{2,1,0:T(8,128)(2,1)S(1)}, u32[]{:S(2)}, u32[]{:S(2)}) collective-permute-start(bf16[4,256,128]{2,1,0:T(8,128)(2,1)S(1)} %shard_map.76.refs_7_), channel_id=1, source_target_pairs={{0,2},{1,3},{2,0},{3,1},{4,6},{5,7},{6,4},{7,5},{8,10},{9,11},{10,... | collective-permute-start | bytes 786440 | tf_op jit(solution)/shard_map/ppermute | solution.py:33
  48.0 1.5 %collective-permute-done.7 = bf16[4,256,128]{2,1,0:T(8,128)(2,1)S(1)} collective-permute-done((bf16[4,256,128]{2,1,0:T(8,128)(2,1)S(1)}, bf16[4,256,128]{2,1,0:T(8,128)(2,1)S(1)}, u32[]{:S(2)}, u32[]{:S(2)}) %collective-permute-start.7) | collective-permute-done | bytes 262176 | tf_op jit(solution)/shard_map/ppermute | solution.py:33
  49.6 1.0 %shard_map.77 = f32[4,256,128]{2,1,0:T(8,128)S(1)} custom-call(bf16[1040,128]{1,0:T(8,128)(2,1)S(1)} %pad_maximum_fusion.1.rest_0_.refs_0_.mixed_ref, bf16[1040,128]{1,0:T(8,128)(2,1)S(1)} %collective-permute-done.6.value_ref.refs_1_, bf16[1040,128]{1,0:T(8,128)(2,1)S(1)} %collective-permute-done.8.refs_2_, ...), custom_call_target="tpu_custom_call" | custom-call | flops 1000000000 | bytes 3000000 | tf_op jit(solution)/shard_map/pallas_call | solution.py:368
  50.6 4.4 %collective-permute-done.10 = bf16[4,256,128]{2,1,0:T(8,128)(2,1)S(1)} collective-permute-done((bf16[4,256,128]{2,1,0:T(8,128)(2,1)S(1)}, bf16[4,256,128]{2,1,0:T(8,128)(2,1)S(1)}, u32[]{:S(2)}, u32[]{:S(2)}) %collective-permute-start.10) | collective-permute-done | bytes 262176 | tf_op jit(solution)/shard_map/ppermute | solution.py:33
  55.1 1.0 %pad_maximum_fusion = f32[8,256,128]{2,1,0:T(8,128)} fusion(f32[4,256,128]{2,1,0:T(8,128)S(1)} %convert_add_fusion, f32[4,256,128]{2,1,0:T(8,128)S(1)} %convert_add_fusion.1), kind=kLoop, calls=%fused_computation | loop fusion | flops 262144 | bytes 2097152 | tf_op jit(solution)/shard_map/concatenate | solution.py:386
  (34 shorter events, 5.3 us)
Async XLA Ops:
  0.0 2.2 %collective-permute-start = (bf16[8,256,128]{2,1,0:T(8,128)(2,1)}, bf16[8,256,128]{2,1,0:T(8,128)(2,1)S(1)}, u32[]{:S(2)}, u32[]{:S(2)}) collective-permute-start(bf16[8,256,128]{2,1,0:T(8,128)(2,1)} %bitcast.5), channel_id=1, source_target_pairs={{0,8},{8,0},{16,24},{24,16},{1,9},{9,1},{17,25},{25,17},{2,10},{10... | collective-permute-start | bytes 1572872 | tf_op jit(solution)/shard_map/ppermute | solution.py:33
  2.2 1.0 %copy-start = (bf16[8,16,16,128]{3,2,1,0:T(8,128)(2,1)S(1)}, bf16[8,16,16,128]{3,2,1,0:T(8,128)(2,1)}, u32[]{:S(2)}) copy-start(bf16[8,16,16,128]{3,2,1,0:T(8,128)(2,1)} %param.6) | copy-start | bytes 1572868
  3.2 0.7 %copy-start.2 = (s32[8]{0:T(128)S(1)}, s32[8]{0:T(128)}, u32[]{:S(2)}) copy-start(s32[8]{0:T(128)} %shift_ref.7) | copy-start | bytes 100
  5.3 5.9 %copy-start.4 = (bf16[16,16,16]{2,1,0:T(8,128)(2,1)S(1)}, bf16[16,16,16]{2,1,0:T(8,128)(2,1)}, u32[]{:S(2)}) copy-start(bf16[16,16,16]{2,1,0:T(8,128)(2,1)} %derivative_ref.1) | copy-start | bytes 24580
  5.3 5.9 %copy-start.5 = (s32[128,16]{0,1:T(8,128)S(1)}, s32[128,16]{0,1:T(8,128)}, u32[]{:S(2)}) copy-start(s32[128,16]{0,1:T(8,128)} %param.11) | copy-start | bytes 24580
  5.3 10.0 %collective-permute-start.1 = (bf16[4,256,128]{2,1,0:T(8,128)(2,1)S(1)}, bf16[4,256,128]{2,1,0:T(8,128)(2,1)S(1)}, u32[]{:S(2)}, u32[]{:S(2)}) collective-permute-start(bf16[4,256,128]{2,1,0:T(8,128)(2,1)S(1)} %shard_map.64.rest_0_), channel_id=1, source_target_pairs={{0,16},{8,24},{16,0},{24,8},{1,17},{9,25},{17,1},{25,9},{2,18},{10... | collective-permute-start | bytes 786440 | tf_op jit(solution)/shard_map/ppermute | solution.py:33
  11.1 9.6 %collective-permute-start.5 = (bf16[4,256,128]{2,1,0:T(8,128)(2,1)S(1)}, bf16[4,256,128]{2,1,0:T(8,128)(2,1)S(1)}, u32[]{:S(2)}, u32[]{:S(2)}) collective-permute-start(bf16[4,256,128]{2,1,0:T(8,128)(2,1)S(1)} %shard_map.66.after_ref), channel_id=1, source_target_pairs={{0,16},{8,24},{16,0},{24,8},{1,17},{9,25},{17,1},{25,9},{2,18},{10... | collective-permute-start | bytes 786440 | tf_op jit(solution)/shard_map/ppermute | solution.py:33
  11.2 7.9 %copy-start.3 = (s32[8]{0:T(128)S(1)}, s32[8]{0:T(128)}, u32[]{:S(2)}) copy-start(s32[8]{0:T(128)} %shift_ref.7) | copy-start | bytes 100
  14.6 4.6 %copy-start.1 = (bf16[8,16,16,128]{3,2,1,0:T(8,128)(2,1)S(1)}, bf16[8,16,16,128]{3,2,1,0:T(8,128)(2,1)}, u32[]{:S(2)}) copy-start(bf16[8,16,16,128]{3,2,1,0:T(8,128)(2,1)} %param.6) | copy-start | bytes 1572868
  15.4 15.2 %collective-permute-start.2 = (bf16[1040,128]{1,0:T(8,128)(2,1)S(1)}, bf16[1040,128]{1,0:T(8,128)(2,1)S(1)}, u32[]{:S(2)}, u32[]{:S(2)}) collective-permute-start(bf16[1040,128]{1,0:T(8,128)(2,1)S(1)} %pad_maximum_fusion.2.rest_0_.mixed_ref.refs_0_), channel_id=1, source_target_pairs={{0,2},{1,3},{2,0},{3,1},{4,6},{5,7},{6,4},{7,5},{8,10},{9,11},{10,... | collective-permute-start | bytes 798728 | tf_op jit(solution)/shard_map/ppermute | solution.py:33
  17.6 13.0 %collective-permute-start.3 = (bf16[1040,128]{1,0:T(8,128)(2,1)S(1)}, bf16[1040,128]{1,0:T(8,128)(2,1)S(1)}, u32[]{:S(2)}, u32[]{:S(2)}) collective-permute-start(bf16[1040,128]{1,0:T(8,128)(2,1)S(1)} %pad_maximum_fusion.2.rest_0_.mixed_ref.refs_0_), channel_id=1, source_target_pairs={{0,1},{1,0},{2,3},{3,2},{4,5},{5,4},{6,7},{7,6},{8,9},{9,8},{10,11... | collective-permute-start | bytes 798728 | tf_op jit(solution)/shard_map/ppermute | solution.py:33
  19.2 16.5 %collective-permute-start.4 = (bf16[1040,128]{1,0:T(8,128)(2,1)S(1)}, bf16[1040,128]{1,0:T(8,128)(2,1)S(1)}, u32[]{:S(2)}, u32[]{:S(2)}) collective-permute-start(bf16[1040,128]{1,0:T(8,128)(2,1)S(1)} %pad_maximum_fusion.2.rest_0_.mixed_ref.refs_0_), channel_id=1, source_target_pairs={{0,3},{1,2},{2,1},{3,0},{4,7},{5,6},{6,5},{7,4},{8,11},{9,10},{10,... | collective-permute-start | bytes 798728 | tf_op jit(solution)/shard_map/ppermute | solution.py:33
  20.8 16.0 %collective-permute-start.6 = (bf16[1040,128]{1,0:T(8,128)(2,1)S(1)}, bf16[1040,128]{1,0:T(8,128)(2,1)S(1)}, u32[]{:S(2)}, u32[]{:S(2)}) collective-permute-start(bf16[1040,128]{1,0:T(8,128)(2,1)S(1)} %pad_maximum_fusion.1.rest_0_.refs_0_.mixed_ref), channel_id=1, source_target_pairs={{0,4},{1,5},{2,6},{3,7},{4,0},{5,1},{6,2},{7,3},{8,12},{9,13},{10,... | collective-permute-start | bytes 798728 | tf_op jit(solution)/shard_map/ppermute | solution.py:33
  23.8 18.4 %collective-permute-start.8 = (bf16[1040,128]{1,0:T(8,128)(2,1)S(1)}, bf16[1040,128]{1,0:T(8,128)(2,1)S(1)}, u32[]{:S(2)}, u32[]{:S(2)}) collective-permute-start(bf16[1040,128]{1,0:T(8,128)(2,1)S(1)} %pad_maximum_fusion.1.rest_0_.refs_0_.mixed_ref), channel_id=1, source_target_pairs={{0,1},{1,0},{2,3},{3,2},{4,5},{5,4},{6,7},{7,6},{8,9},{9,8},{10,11... | collective-permute-start | bytes 798728 | tf_op jit(solution)/shard_map/ppermute | solution.py:33
  36.8 12.7 %collective-permute-start.7 = (bf16[4,256,128]{2,1,0:T(8,128)(2,1)S(1)}, bf16[4,256,128]{2,1,0:T(8,128)(2,1)S(1)}, u32[]{:S(2)}, u32[]{:S(2)}) collective-permute-start(bf16[4,256,128]{2,1,0:T(8,128)(2,1)S(1)} %shard_map.71.after_ref), channel_id=1, source_target_pairs={{0,4},{1,5},{2,6},{3,7},{4,0},{5,1},{6,2},{7,3},{8,12},{9,13},{10,... | collective-permute-start | bytes 786440 | tf_op jit(solution)/shard_map/ppermute | solution.py:33
  36.9 6.5 %collective-permute-start.9 = (bf16[1040,128]{1,0:T(8,128)(2,1)S(1)}, bf16[1040,128]{1,0:T(8,128)(2,1)S(1)}, u32[]{:S(2)}, u32[]{:S(2)}) collective-permute-start(bf16[1040,128]{1,0:T(8,128)(2,1)S(1)} %shard_map.72.refs_7_.rest_0_), channel_id=1, source_target_pairs={{0,1},{1,0},{2,3},{3,2},{4,5},{5,4},{6,7},{7,6},{8,9},{9,8},{10,11... | collective-permute-start | bytes 798728 | tf_op jit(solution)/shard_map/ppermute | solution.py:33
  44.5 10.5 %collective-permute-start.10 = (bf16[4,256,128]{2,1,0:T(8,128)(2,1)S(1)}, bf16[4,256,128]{2,1,0:T(8,128)(2,1)S(1)}, u32[]{:S(2)}, u32[]{:S(2)}) collective-permute-start(bf16[4,256,128]{2,1,0:T(8,128)(2,1)S(1)} %shard_map.76.refs_7_), channel_id=1, source_target_pairs={{0,2},{1,3},{2,0},{3,1},{4,6},{5,7},{6,4},{7,5},{8,10},{9,11},{10,... | collective-permute-start | bytes 786440 | tf_op jit(solution)/shard_map/ppermute | solution.py:33

commit v5 on v4

--- a/solution.py
+++ b/solution.py
@@ -254,10 +254,10 @@
 
     mate = swap(green, "energy", 1)
 
-    occupied = occupation[:, None]
-    couplings = jnp.concatenate(
-        [phonon_weight * (occupied + 1.0), phonon_weight * occupied], 0
-    ).astype(BF16)
+    kind = lax.broadcasted_iota(jnp.int32, (2, modes, atoms), 0)
+    occupied = jnp.broadcast_to(occupation[None, :, None], kind.shape)
+    couplings = phonon_weight[None] * jnp.where(kind == 0, occupied + 1.0, occupied)
+    couplings = couplings.reshape(2 * modes, atoms).astype(BF16)
 
     def mix(group, chunk, kind, after):
         return pl.pallas_call(
@@ -327,23 +327,8 @@
             cost_estimate=cost(1e6, 1e6),
         )(value, after)
 
-    plans = [([2, 1, 3], high), (high, [2])]
-    across = [[mixed[chunk]] + [swap(mixed[chunk], "atom", mask) for mask in masks]
-              for chunk, (masks, _) in enumerate(plans)]
-    local = [local_sum(0, mixed[-1:])]
-    after = local[0]
-    results, arrivals = [], []
-    for chunk, (_, flips) in enumerate(plans):
-        if chunk == 0:
-            sources = across[chunk]
-        else:
-            beside = [mixed[chunk]] + [ordered(value, after) for value in across[chunk][1:]]
-            sources = across[chunk] + [swap(value, "atom", 1) for value in beside]
-            after = beside[1]
-            local.append(local_sum(chunk, [after]))
-            results.append(stay_sum(*waiting, after))
-            after = results[-1]
-        hots = pl.pallas_call(
+    def one_hots(sources, flips, after):
+        return pl.pallas_call(
             functools.partial(remote_hot_kernel, REMOTE_BONDS, [0] + flips),
             out_shape=jax.ShapeDtypeStruct(
                 ((1 + len(flips)) * REMOTE_BONDS * atoms, len(sources) * atoms), BF16
@@ -353,8 +338,10 @@
             compiler_params=params(),
             cost_estimate=cost(1e8, 1e6),
         )(*sources, after)
+
+    def away_sums(chunk, sources, hots, flips, after):
         block = jax.ShapeDtypeStruct((sizes[chunk], square, atoms), BF16)
-        away = pl.pallas_call(
+        return pl.pallas_call(
             functools.partial(away_kernel, len(sources)),
             out_shape=(block,) * len(flips),
             in_specs=[VMEM] * (len(sources) + 2) + [ANY],
@@ -362,22 +349,36 @@
             compiler_params=params(),
             cost_estimate=cost(1e9, 3e6),
         )(*sources, hots, remote_k, after)
-        received = [swap(value, "atom", flip) for value, flip in zip(away, flips)]
-
-        def stay_sum(chunk, sources, hots, after):
-            return pl.pallas_call(
-                functools.partial(stay_kernel, len(sources)),
-                out_shape=jax.ShapeDtypeStruct((sizes[chunk], square, atoms), F32),
-                in_specs=[VMEM] * (len(sources) + 3) + [ANY],
-                out_specs=VMEM,
-                compiler_params=params(),
-                cost_estimate=cost(1e9, 3e6),
-            )(*sources, hots, remote_k, local[chunk], after)
-
-        arrivals.append(received)
-        waiting = (chunk, sources, hots)
-        after = away[0]
-    results.append(stay_sum(*waiting, after))
+
+    def stay_sum(chunk, sources, hots, local, after):
+        return pl.pallas_call(
+            functools.partial(stay_kernel, len(sources)),
+            out_shape=jax.ShapeDtypeStruct((sizes[chunk], square, atoms), F32),
+            in_specs=[VMEM] * (len(sources) + 3) + [ANY],
+            out_specs=VMEM,
+            compiler_params=params(),
+            cost_estimate=cost(1e9, 3e6),
+        )(*sources, hots, remote_k, local, after)
+
+    def send(values, masks):
+        return [swap(value, "atom", mask) for value, mask in zip(values, masks)]
+
+    outer, inner = mixed
+    far = send([outer] * len(high), high)
+    near = send([inner] * 3, [2, 1, 3])
+    local_outer = local_sum(0, [inner])
+    passed = [ordered(value, local_outer) for value in far]
+    outer_sources = [outer] + far + send([outer] + passed, [1] * (1 + len(passed)))
+    local_inner = local_sum(1, passed[:1])
+    inner_sources = [inner] + near
+    inner_hots = one_hots(inner_sources, high, local_inner)
+    inner_away = away_sums(1, inner_sources, inner_hots, high, local_inner)
+    outer_hots = one_hots(outer_sources, [2], inner_away[0])
+    outer_away = away_sums(0, outer_sources, outer_hots, [2], inner_away[0])
+    inner_stay = stay_sum(1, inner_sources, inner_hots, local_inner, outer_away[0])
+    outer_stay = stay_sum(0, outer_sources, outer_hots, local_outer, inner_stay)
+    results = [outer_stay, inner_stay]
+    arrivals = [send(outer_away, [2]), send(inner_away, high)]
     combined = []
     for stay, received in zip(results, arrivals):
         for value in received:

time: 56.3 us -> 60.2 us (1.069)
  waiting for transfers between devices: 15.6 us -> 20.1 us
  starting transfers between devices: 16.8 us -> 15.3 us
  local copies, waits for them, and re-layouts: 1.72 us -> 2.71 us
    ppermute x11, waiting for transfers between devices: 15.6 us -> 20.1 us  [swap(): return lax.ppermute(value, axis, [(i, i ^ mask) for i in range(count)])]
    ppermute x11, starting transfers between devices: 16.8 us -> 15.3 us  [swap(): return lax.ppermute(value, axis, [(i, i ^ mask) for i in range(count)])]
    broadcast_in_dim x0 -> x4, local copies, waits for them, and re-layouts: none -> 0.83 us  [per_device(): occupied = jnp.broadcast_to(occupation[None, :, None], kind.shape)]
    another operation x1 -> x0, other arithmetic: 0.76 us -> none
    convert_element_type x0 -> x1, other arithmetic: none -> 0.76 us  [per_device(): couplings = couplings.reshape(2 * modes, atoms).astype(BF16)]
  transfers between devices with their start and end apart: 11 -> 11, of which waited for: 7 -> 8; matrix products, arithmetic and copies ran while one was open for 3% -> 4% of each run, Pallas kernels for 31% -> 29%
where the time goes in v5:
time: 60.2 us; the launch traced here: 59.9 us
  waiting for transfers between devices  20.1 us (33%)
  Pallas kernels  18.9 us (31%)
  starting transfers between devices  15.3 us (25%)
  other arithmetic  2.75 us (5%)
  local copies, waits for them, and re-layouts  2.71 us (5%)
    ppermute x11, waiting for transfers between devices, swap(): return lax.ppermute(value, axis, [(i, i ^ mask) for i in range(count)])  20.1 us
    ppermute x11, starting transfers between devices, swap(): return lax.ppermute(value, axis, [(i, i ^ mask) for i in range(count)])  15.3 us
    pallas_call x4, Pallas kernels, mix(): pl.pallas_call(functools.partial(mix_kernel, group, firsts[chunk]), out_s...  5.74 us
    pallas_call x2, Pallas kernels, local_sum(): pl.pallas_call(local_kernel, out_shape=jax.ShapeDtypeStruct((sizes[chunk]...  5.56 us
    pallas_call x1, Pallas kernels, prepare(): pl.pallas_call(prepare_kernel, out_shape=(jax.ShapeDtypeStruct((square, l...  3.36 us
    pallas_call x2, Pallas kernels, stay_sum(): pl.pallas_call(functools.partial(stay_kernel, len(sources)), out_shape=ja...  1.98 us
    pallas_call x2, Pallas kernels, away_sums(): pl.pallas_call(functools.partial(away_kernel, len(sources)), out_shape=(b...  1.97 us
    unnamed x12, local copies, waits for them, and re-layouts  1.72 us
  transfers between devices with their start and end apart: 11, of which 8 were waited for; matrix products, arithmetic and copies ran while one was open for 4% of the time, Pallas kernels for 29%

profile of v5, /device:TPU:0, one launch (start us, length us, event | category | flops | bytes accessed | tf_op | source)
XLA Modules:
  0.0 59.9 jit_solution(15740402893735755492)
XLA Ops:
  2.9 1.0 %copy-done = bf16[8,16,16,128]{3,2,1,0:T(8,128)(2,1)S(1)} copy-done((bf16[8,16,16,128]{3,2,1,0:T(8,128)(2,1)S(1)}, bf16[8,16,16,128]{3,2,1,0:T(8,128)(2,1)}, u32[]{:S(2)}) %copy-start) | copy-done | bytes 524312
  4.6 1.4 %shard_map.64.rest_0_ = bf16[4,256,128]{2,1,0:T(8,128)(2,1)S(1)} custom-call(s32[8]{0:T(128)S(1)} %copy-done.2, bf16[16,128]{1,0:T(8,128)(2,1)S(1)} %fusion.coupling_ref, bf16[8,256,128]{2,1,0:T(8,128)(2,1)S(1)} %bitcast.10, bf16[8,256,128]{2,1,0:T(8,128)(2,1)S(1)} %collective-permute-done.mate_ref), custom_call_target="tpu_custom_call" | custom-call | flops 500000000 | bytes 1000000 | tf_op jit(solution)/shard_map/pallas_call | solution.py:263
  6.0 2.6 %collective-permute-start.1 = (bf16[4,256,128]{2,1,0:T(8,128)(2,1)S(1)}, bf16[4,256,128]{2,1,0:T(8,128)(2,1)S(1)}, u32[]{:S(2)}, u32[]{:S(2)}) collective-permute-start(bf16[4,256,128]{2,1,0:T(8,128)(2,1)S(1)} %shard_map.64.rest_0_), channel_id=1, source_target_pairs={{0,16},{8,24},{16,0},{24,8},{1,17},{9,25},{17,1},{25,9},{2,18},{10... | collective-permute-start | bytes 786440 | tf_op jit(solution)/shard_map/ppermute | solution.py:33
  8.5 1.5 %shard_map.65.rest_0_ = f32[4,256,128]{2,1,0:T(8,128)S(1)} custom-call(s32[8]{0:T(128)S(1)} %copy-done.2, bf16[16,128]{1,0:T(8,128)(2,1)S(1)} %fusion.coupling_ref, bf16[8,256,128]{2,1,0:T(8,128)(2,1)S(1)} %bitcast.11, bf16[8,256,128]{2,1,0:T(8,128)(2,1)S(1)} %collective-permute-done.mate_ref, bf16[4,256,128]{2,1,0:T(8,128)(2,1)S(1)} %shard_map.64.rest_0_), custom_call_target="tpu_custom_call" | custom-call | flops 500000000 | bytes 1000000 | tf_op jit(solution)/shard_map/pallas_call | solution.py:263
  10.0 1.4 %shard_map.66.after_ref = bf16[4,256,128]{2,1,0:T(8,128)(2,1)S(1)} custom-call(s32[8]{0:T(128)S(1)} %copy-done.2, bf16[16,128]{1,0:T(8,128)(2,1)S(1)} %fusion.coupling_ref, bf16[8,256,128]{2,1,0:T(8,128)(2,1)S(1)} %bitcast.12, bf16[8,256,128]{2,1,0:T(8,128)(2,1)S(1)} %collective-permute-done.mate_ref, f32[4,256,128]{2,1,0:T(8,128)S(1)} %shard_map.65.rest_0_), custom_call_target="tpu_custom_call" | custom-call | flops 500000000 | bytes 1000000 | tf_op jit(solution)/shard_map/pallas_call | solution.py:263
  11.5 3.4 %shard_map.67 = (bf16[256,3584]{1,0:T(8,128)(2,1)S(1)}, bf16[256,512]{1,0:T(8,128)(2,1)S(1)}, bf16[1792,128]{1,0:T(8,128)(2,1)S(1)}, bf16[16,128]{1,0:T(8,128)(2,1)S(1)}) custom-call(bf16[16,16,16]{2,1,0:T(8,128)(2,1)S(1)} %copy-done.4, s32[16,128]{1,0:T(8,128)S(1)} %bitcast.14, bf16[4,256,128]{2,1,0:T(8,128)(2,1)S(1)} %shard_map.66.after_ref), custom_call_target="tpu_custom_call" | custom-call | flops 2000000000 | bytes 3000000 | tf_op jit(solution)/shard_map/pallas_call | solution.py:274
  15.8 3.1 %collective-permute-start.2 = (bf16[1040,128]{1,0:T(8,128)(2,1)S(1)}, bf16[1040,128]{1,0:T(8,128)(2,1)S(1)}, u32[]{:S(2)}, u32[]{:S(2)}) collective-permute-start(bf16[1040,128]{1,0:T(8,128)(2,1)S(1)} %pad_maximum_fusion.2.rest_0_.mixed_ref.refs_0_), channel_id=1, source_target_pairs={{0,4},{1,5},{2,6},{3,7},{4,0},{5,1},{6,2},{7,3},{8,12},{9,13},{10,... | collective-permute-start | bytes 798728 | tf_op jit(solution)/shard_map/ppermute | solution.py:33
  18.9 1.5 %shard_map.68 = f32[4,256,128]{2,1,0:T(8,128)S(1)} custom-call(s32[8]{0:T(128)S(1)} %copy-done.3, bf16[16,128]{1,0:T(8,128)(2,1)S(1)} %fusion.coupling_ref, bf16[8,256,128]{2,1,0:T(8,128)(2,1)S(1)} %bitcast.13, bf16[8,256,128]{2,1,0:T(8,128)(2,1)S(1)} %collective-permute-done.mate_ref, bf16[1040,128]{1,0:T(8,128)(2,1)S(1)} %pad_maximum_fusion.2.rest_0_.mixed_ref.refs_0_, ...), custom_call_target="tpu_custom_call" | custom-call | flops 500000000 | bytes 1000000 | tf_op jit(solution)/shard_map/pallas_call | solution.py:263
  21.2 1.9 %collective-permute-start.6 = (bf16[1040,128]{1,0:T(8,128)(2,1)S(1)}, bf16[1040,128]{1,0:T(8,128)(2,1)S(1)}, u32[]{:S(2)}, u32[]{:S(2)}) collective-permute-start(bf16[1040,128]{1,0:T(8,128)(2,1)S(1)} %pad_maximum_fusion.1.rest_0_.mixed_ref.refs_0_), channel_id=1, source_target_pairs={{0,2},{1,3},{2,0},{3,1},{4,6},{5,7},{6,4},{7,5},{8,10},{9,11},{10,... | collective-permute-start | bytes 798728 | tf_op jit(solution)/shard_map/ppermute | solution.py:33
  23.1 1.5 %collective-permute-start.7 = (bf16[1040,128]{1,0:T(8,128)(2,1)S(1)}, bf16[1040,128]{1,0:T(8,128)(2,1)S(1)}, u32[]{:S(2)}, u32[]{:S(2)}) collective-permute-start(bf16[1040,128]{1,0:T(8,128)(2,1)S(1)} %pad_maximum_fusion.1.rest_0_.mixed_ref.refs_0_), channel_id=1, source_target_pairs={{0,1},{1,0},{2,3},{3,2},{4,5},{5,4},{6,7},{7,6},{8,9},{9,8},{10,11... | collective-permute-start | bytes 798728 | tf_op jit(solution)/shard_map/ppermute | solution.py:33
  24.8 1.8 %collective-permute-start.3 = (bf16[1040,128]{1,0:T(8,128)(2,1)S(1)}, bf16[1040,128]{1,0:T(8,128)(2,1)S(1)}, u32[]{:S(2)}, u32[]{:S(2)}) collective-permute-start(bf16[1040,128]{1,0:T(8,128)(2,1)S(1)} %pad_maximum_fusion.2.rest_0_.mixed_ref.refs_0_), channel_id=1, source_target_pairs={{0,1},{1,0},{2,3},{3,2},{4,5},{5,4},{6,7},{7,6},{8,9},{9,8},{10,11... | collective-permute-start | bytes 798728 | tf_op jit(solution)/shard_map/ppermute | solution.py:33
  26.6 2.8 %shard_map.69.after_ref.refs_6_ = f32[4,256,128]{2,1,0:T(8,128)S(1)} custom-call(bf16[1040,128]{1,0:T(8,128)(2,1)S(1)} %pad_maximum_fusion.2.rest_0_.mixed_ref.refs_0_, bf16[1792,128]{1,0:T(8,128)(2,1)S(1)} %get-tuple-element.10.rest_1_.hot_ref, bf16[256,3584]{1,0:T(8,128)(2,1)S(1)} %get-tuple-element.11.k_ref, ...), custom_call_target="tpu_custom_call" | custom-call | flops 2000000000 | bytes 3000000 | tf_op jit(solution)/shard_map/pallas_call | solution.py:289
  29.3 1.3 %collective-permute-done.2.value_ref.refs_1_ = bf16[1040,128]{1,0:T(8,128)(2,1)S(1)} collective-permute-done((bf16[1040,128]{1,0:T(8,128)(2,1)S(1)}, bf16[1040,128]{1,0:T(8,128)(2,1)S(1)}, u32[]{:S(2)}, u32[]{:S(2)}) %collective-permute-start.2) | collective-permute-done | bytes 266272 | tf_op jit(solution)/shard_map/ppermute | solution.py:33
  30.7 1.6 %collective-permute-start.5 = (bf16[1040,128]{1,0:T(8,128)(2,1)S(1)}, bf16[1040,128]{1,0:T(8,128)(2,1)S(1)}, u32[]{:S(2)}, u32[]{:S(2)}) collective-permute-start(bf16[1040,128]{1,0:T(8,128)(2,1)S(1)} %shard_map.70.rest_0_), channel_id=1, source_target_pairs={{0,1},{1,0},{2,3},{3,2},{4,5},{5,4},{6,7},{7,6},{8,9},{9,8},{10,11... | collective-permute-start | bytes 798728 | tf_op jit(solution)/shard_map/ppermute | solution.py:33
  32.3 2.8 %shard_map.71.refs_4_.refs_6_ = f32[4,256,128]{2,1,0:T(8,128)S(1)} custom-call(bf16[1040,128]{1,0:T(8,128)(2,1)S(1)} %pad_maximum_fusion.1.rest_0_.mixed_ref.refs_0_, bf16[1792,128]{1,0:T(8,128)(2,1)S(1)} %get-tuple-element.10.rest_1_.hot_ref, bf16[256,3584]{1,0:T(8,128)(2,1)S(1)} %get-tuple-element.11.k_ref, bf16[1040,128]{1,0:T(8,128)(2,1)S(1)} %shard_map.70.rest_0_), custom_call_target="tpu_custom_call" | custom-call | flops 2000000000 | bytes 3000000 | tf_op jit(solution)/shard_map/pallas_call | solution.py:289
  35.1 5.8 %collective-permute-done.8.refs_3_ = bf16[1040,128]{1,0:T(8,128)(2,1)S(1)} collective-permute-done((bf16[1040,128]{1,0:T(8,128)(2,1)S(1)}, bf16[1040,128]{1,0:T(8,128)(2,1)S(1)}, u32[]{:S(2)}, u32[]{:S(2)}) %collective-permute-start.8) | collective-permute-done | bytes 266272 | tf_op jit(solution)/shard_map/ppermute | solution.py:33
  42.0 1.7 %collective-permute-start.10 = (bf16[4,256,128]{2,1,0:T(8,128)(2,1)S(1)}, bf16[4,256,128]{2,1,0:T(8,128)(2,1)S(1)}, u32[]{:S(2)}, u32[]{:S(2)}) collective-permute-start(bf16[4,256,128]{2,1,0:T(8,128)(2,1)S(1)} %shard_map.73.refs_4_.refs_6_), channel_id=1, source_target_pairs={{0,4},{1,5},{2,6},{3,7},{4,0},{5,1},{6,2},{7,3},{8,12},{9,13},{10,... | collective-permute-start | bytes 786440 | tf_op jit(solution)/shard_map/ppermute | solution.py:33
  43.9 4.1 %collective-permute-done.5.refs_3_ = bf16[1040,128]{1,0:T(8,128)(2,1)S(1)} collective-permute-done((bf16[1040,128]{1,0:T(8,128)(2,1)S(1)}, bf16[1040,128]{1,0:T(8,128)(2,1)S(1)}, u32[]{:S(2)}, u32[]{:S(2)}) %collective-permute-start.5) | collective-permute-done | bytes 266272 | tf_op jit(solution)/shard_map/ppermute | solution.py:33
  48.1 1.0 %shard_map.75.refs_7_ = bf16[4,256,128]{2,1,0:T(8,128)(2,1)S(1)} custom-call(bf16[1040,128]{1,0:T(8,128)(2,1)S(1)} %pad_maximum_fusion.2.rest_0_.mixed_ref.refs_0_, bf16[1040,128]{1,0:T(8,128)(2,1)S(1)} %collective-permute-done.2.value_ref.refs_1_, bf16[1040,128]{1,0:T(8,128)(2,1)S(1)} %collective-permute-done.3.refs_2_, ...), custom_call_target="tpu_custom_call" | custom-call | flops 1000000000 | bytes 3000000 | tf_op jit(solution)/shard_map/pallas_call | solution.py:344
  49.6 1.0 %shard_map.76.refs_7_ = f32[4,256,128]{2,1,0:T(8,128)S(1)} custom-call(bf16[1040,128]{1,0:T(8,128)(2,1)S(1)} %pad_maximum_fusion.1.rest_0_.mixed_ref.refs_0_, bf16[1040,128]{1,0:T(8,128)(2,1)S(1)} %collective-permute-done.6.refs_1_, bf16[1040,128]{1,0:T(8,128)(2,1)S(1)} %collective-permute-done.7.refs_2_, ...), custom_call_target="tpu_custom_call" | custom-call | flops 1000000000 | bytes 3000000 | tf_op jit(solution)/shard_map/pallas_call | solution.py:354
  50.6 1.0 %shard_map.77 = f32[4,256,128]{2,1,0:T(8,128)S(1)} custom-call(bf16[1040,128]{1,0:T(8,128)(2,1)S(1)} %pad_maximum_fusion.2.rest_0_.mixed_ref.refs_0_, bf16[1040,128]{1,0:T(8,128)(2,1)S(1)} %collective-permute-done.2.value_ref.refs_1_, bf16[1040,128]{1,0:T(8,128)(2,1)S(1)} %collective-permute-done.3.refs_2_, ...), custom_call_target="tpu_custom_call" | custom-call | flops 1000000000 | bytes 3000000 | tf_op jit(solution)/shard_map/pallas_call | solution.py:354
  51.6 4.2 %collective-permute-done.10 = bf16[4,256,128]{2,1,0:T(8,128)(2,1)S(1)} collective-permute-done((bf16[4,256,128]{2,1,0:T(8,128)(2,1)S(1)}, bf16[4,256,128]{2,1,0:T(8,128)(2,1)S(1)}, u32[]{:S(2)}, u32[]{:S(2)}) %collective-permute-start.10) | collective-permute-done | bytes 262176 | tf_op jit(solution)/shard_map/ppermute | solution.py:33
  55.8 3.1 %collective-permute-done.9 = bf16[4,256,128]{2,1,0:T(8,128)(2,1)S(1)} collective-permute-done((bf16[4,256,128]{2,1,0:T(8,128)(2,1)S(1)}, bf16[4,256,128]{2,1,0:T(8,128)(2,1)S(1)}, u32[]{:S(2)}, u32[]{:S(2)}) %collective-permute-start.9) | collective-permute-done | bytes 262176 | tf_op jit(solution)/shard_map/ppermute | solution.py:33
  58.9 1.0 %pad_maximum_fusion = f32[8,256,128]{2,1,0:T(8,128)} fusion(f32[4,256,128]{2,1,0:T(8,128)S(1)} %convert_add_fusion, f32[4,256,128]{2,1,0:T(8,128)S(1)} %convert_add_fusion.1), kind=kLoop, calls=%fused_computation | loop fusion | flops 262144 | bytes 2097152 | tf_op jit(solution)/shard_map/concatenate | solution.py:387
  (40 shorter events, 7.4 us)
Async XLA Ops:
  0.0 2.9 %collective-permute-start = (bf16[8,256,128]{2,1,0:T(8,128)(2,1)}, bf16[8,256,128]{2,1,0:T(8,128)(2,1)S(1)}, u32[]{:S(2)}, u32[]{:S(2)}) collective-permute-start(bf16[8,256,128]{2,1,0:T(8,128)(2,1)} %bitcast.9), channel_id=1, source_target_pairs={{0,8},{8,0},{16,24},{24,16},{1,9},{9,1},{17,25},{25,17},{2,10},{10... | collective-permute-start | bytes 1572872 | tf_op jit(solution)/shard_map/ppermute | solution.py:33
  2.9 1.0 %copy-start = (bf16[8,16,16,128]{3,2,1,0:T(8,128)(2,1)S(1)}, bf16[8,16,16,128]{3,2,1,0:T(8,128)(2,1)}, u32[]{:S(2)}) copy-start(bf16[8,16,16,128]{3,2,1,0:T(8,128)(2,1)} %param.6) | copy-start | bytes 1572868
  3.9 0.7 %copy-start.2 = (s32[8]{0:T(128)S(1)}, s32[8]{0:T(128)}, u32[]{:S(2)}) copy-start(s32[8]{0:T(128)} %shift_ref.7) | copy-start | bytes 100
  6.0 5.5 %copy-start.4 = (bf16[16,16,16]{2,1,0:T(8,128)(2,1)S(1)}, bf16[16,16,16]{2,1,0:T(8,128)(2,1)}, u32[]{:S(2)}) copy-start(bf16[16,16,16]{2,1,0:T(8,128)(2,1)} %derivative_ref.1) | copy-start | bytes 24580
  6.0 5.5 %copy-start.5 = (s32[128,16]{0,1:T(8,128)S(1)}, s32[128,16]{0,1:T(8,128)}, u32[]{:S(2)}) copy-start(s32[128,16]{0,1:T(8,128)} %param.11) | copy-start | bytes 24580
  6.0 9.7 %collective-permute-start.1 = (bf16[4,256,128]{2,1,0:T(8,128)(2,1)S(1)}, bf16[4,256,128]{2,1,0:T(8,128)(2,1)S(1)}, u32[]{:S(2)}, u32[]{:S(2)}) collective-permute-start(bf16[4,256,128]{2,1,0:T(8,128)(2,1)S(1)} %shard_map.64.rest_0_), channel_id=1, source_target_pairs={{0,16},{8,24},{16,0},{24,8},{1,17},{9,25},{17,1},{25,9},{2,18},{10... | collective-permute-start | bytes 786440 | tf_op jit(solution)/shard_map/ppermute | solution.py:33
  11.4 9.7 %collective-permute-start.4 = (bf16[4,256,128]{2,1,0:T(8,128)(2,1)S(1)}, bf16[4,256,128]{2,1,0:T(8,128)(2,1)S(1)}, u32[]{:S(2)}, u32[]{:S(2)}) collective-permute-start(bf16[4,256,128]{2,1,0:T(8,128)(2,1)S(1)} %shard_map.66.after_ref), channel_id=1, source_target_pairs={{0,16},{8,24},{16,0},{24,8},{1,17},{9,25},{17,1},{25,9},{2,18},{10... | collective-permute-start | bytes 786440 | tf_op jit(solution)/shard_map/ppermute | solution.py:33
  11.5 7.4 %copy-start.3 = (s32[8]{0:T(128)S(1)}, s32[8]{0:T(128)}, u32[]{:S(2)}) copy-start(s32[8]{0:T(128)} %shift_ref.7) | copy-start | bytes 100
  14.9 4.0 %copy-start.1 = (bf16[8,16,16,128]{3,2,1,0:T(8,128)(2,1)S(1)}, bf16[8,16,16,128]{3,2,1,0:T(8,128)(2,1)}, u32[]{:S(2)}) copy-start(bf16[8,16,16,128]{3,2,1,0:T(8,128)(2,1)} %param.6) | copy-start | bytes 1572868
  15.8 14.8 %collective-permute-start.2 = (bf16[1040,128]{1,0:T(8,128)(2,1)S(1)}, bf16[1040,128]{1,0:T(8,128)(2,1)S(1)}, u32[]{:S(2)}, u32[]{:S(2)}) collective-permute-start(bf16[1040,128]{1,0:T(8,128)(2,1)S(1)} %pad_maximum_fusion.2.rest_0_.mixed_ref.refs_0_), channel_id=1, source_target_pairs={{0,4},{1,5},{2,6},{3,7},{4,0},{5,1},{6,2},{7,3},{8,12},{9,13},{10,... | collective-permute-start | bytes 798728 | tf_op jit(solution)/shard_map/ppermute | solution.py:33
  21.2 13.9 %collective-permute-start.6 = (bf16[1040,128]{1,0:T(8,128)(2,1)S(1)}, bf16[1040,128]{1,0:T(8,128)(2,1)S(1)}, u32[]{:S(2)}, u32[]{:S(2)}) collective-permute-start(bf16[1040,128]{1,0:T(8,128)(2,1)S(1)} %pad_maximum_fusion.1.rest_0_.mixed_ref.refs_0_), channel_id=1, source_target_pairs={{0,2},{1,3},{2,0},{3,1},{4,6},{5,7},{6,4},{7,5},{8,10},{9,11},{10,... | collective-permute-start | bytes 798728 | tf_op jit(solution)/shard_map/ppermute | solution.py:33
  23.1 12.0 %collective-permute-start.7 = (bf16[1040,128]{1,0:T(8,128)(2,1)S(1)}, bf16[1040,128]{1,0:T(8,128)(2,1)S(1)}, u32[]{:S(2)}, u32[]{:S(2)}) collective-permute-start(bf16[1040,128]{1,0:T(8,128)(2,1)S(1)} %pad_maximum_fusion.1.rest_0_.mixed_ref.refs_0_), channel_id=1, source_target_pairs={{0,1},{1,0},{2,3},{3,2},{4,5},{5,4},{6,7},{7,6},{8,9},{9,8},{10,11... | collective-permute-start | bytes 798728 | tf_op jit(solution)/shard_map/ppermute | solution.py:33
  24.6 16.3 %collective-permute-start.8 = (bf16[1040,128]{1,0:T(8,128)(2,1)S(1)}, bf16[1040,128]{1,0:T(8,128)(2,1)S(1)}, u32[]{:S(2)}, u32[]{:S(2)}) collective-permute-start(bf16[1040,128]{1,0:T(8,128)(2,1)S(1)} %pad_maximum_fusion.1.rest_0_.mixed_ref.refs_0_), channel_id=1, source_target_pairs={{0,3},{1,2},{2,1},{3,0},{4,7},{5,6},{6,5},{7,4},{8,11},{9,10},{10,... | collective-permute-start | bytes 798728 | tf_op jit(solution)/shard_map/ppermute | solution.py:33
  24.8 19.1 %collective-permute-start.3 = (bf16[1040,128]{1,0:T(8,128)(2,1)S(1)}, bf16[1040,128]{1,0:T(8,128)(2,1)S(1)}, u32[]{:S(2)}, u32[]{:S(2)}) collective-permute-start(bf16[1040,128]{1,0:T(8,128)(2,1)S(1)} %pad_maximum_fusion.2.rest_0_.mixed_ref.refs_0_), channel_id=1, source_target_pairs={{0,1},{1,0},{2,3},{3,2},{4,5},{5,4},{6,7},{7,6},{8,9},{9,8},{10,11... | collective-permute-start | bytes 798728 | tf_op jit(solution)/shard_map/ppermute | solution.py:33
  30.7 17.3 %collective-permute-start.5 = (bf16[1040,128]{1,0:T(8,128)(2,1)S(1)}, bf16[1040,128]{1,0:T(8,128)(2,1)S(1)}, u32[]{:S(2)}, u32[]{:S(2)}) collective-permute-start(bf16[1040,128]{1,0:T(8,128)(2,1)S(1)} %shard_map.70.rest_0_), channel_id=1, source_target_pairs={{0,1},{1,0},{2,3},{3,2},{4,5},{5,4},{6,7},{7,6},{8,9},{9,8},{10,11... | collective-permute-start | bytes 798728 | tf_op jit(solution)/shard_map/ppermute | solution.py:33
  42.0 13.7 %collective-permute-start.10 = (bf16[4,256,128]{2,1,0:T(8,128)(2,1)S(1)}, bf16[4,256,128]{2,1,0:T(8,128)(2,1)S(1)}, u32[]{:S(2)}, u32[]{:S(2)}) collective-permute-start(bf16[4,256,128]{2,1,0:T(8,128)(2,1)S(1)} %shard_map.73.refs_4_.refs_6_), channel_id=1, source_target_pairs={{0,4},{1,5},{2,6},{3,7},{4,0},{5,1},{6,2},{7,3},{8,12},{9,13},{10,... | collective-permute-start | bytes 786440 | tf_op jit(solution)/shard_map/ppermute | solution.py:33
  49.1 9.7 %collective-permute-start.9 = (bf16[4,256,128]{2,1,0:T(8,128)(2,1)S(1)}, bf16[4,256,128]{2,1,0:T(8,128)(2,1)S(1)}, u32[]{:S(2)}, u32[]{:S(2)}) collective-permute-start(bf16[4,256,128]{2,1,0:T(8,128)(2,1)S(1)} %shard_map.75.refs_7_), channel_id=1, source_target_pairs={{0,2},{1,3},{2,0},{3,1},{4,6},{5,7},{6,4},{7,5},{8,10},{9,11},{10,... | collective-permute-start | bytes 786440 | tf_op jit(solution)/shard_map/ppermute | solution.py:33

commit v6 on v5

--- a/solution.py
+++ b/solution.py
@@ -146,8 +146,17 @@
     ids_ref[...] = ids.astype(F32).astype(BF16)
 
 
-def pass_kernel(value_ref, after_ref, out_ref):
-    out_ref[...] = value_ref[...]
+def stage_kernel(green_ref, shift_ref, green_out, shift_out):
+    green_out[...] = green_ref[...]
+    for mode in range(shift_ref.shape[0]):
+        shift_out[mode] = shift_ref[mode]
+
+
+def pass_kernel(pieces, value_ref, after_ref, *out_refs):
+    for index, ((first, end), out_ref) in enumerate(zip(pieces, out_refs)):
+        out_ref[: end - first, :] = value_ref[first:end, :]
+        if index == 0:
+            out_ref[end - first :, :] = value_ref[value_ref.shape[0] - ID_ROWS :, :]
 
 
 def remote_hot_kernel(bonds, flips, *refs):
@@ -185,7 +194,7 @@
             out_ref[start + inner] = result[:, inner * atoms : (inner + 1) * atoms]
 
 
-def remote_sums(source_refs, hot_ref, k_ref, rows, first, count, store):
+def remote_sums(source_refs, offsets, hot_ref, k_ref, rows, first, count, store):
     atoms = source_refs[0].shape[1]
     square = k_ref.shape[0]
     bonds = k_ref.shape[1] // square
@@ -196,7 +205,11 @@
         pieces = [[] for _ in range(bonds)]
         for row in inner:
             sources = jnp.concatenate(
-                [ref[row * square : (row + 1) * square, :] for ref in source_refs], axis=1
+                [
+                    ref[at + row * square : at + (row + 1) * square, :]
+                    for at, ref in zip(offsets, source_refs)
+                ],
+                axis=1,
             )
             summed = dot_nt(sources, hot_ref[first * width : (first + count) * width, :])
             summed = summed.astype(BF16)
@@ -212,7 +225,8 @@
                 store(row, which, result[:, at : at + atoms])
 
 
-def away_kernel(source_count, *refs):
+def away_kernel(offsets, *refs):
+    source_count = len(offsets)
     source_refs = refs[:source_count]
     hot_ref, k_ref = refs[source_count : source_count + 2]
     count = hot_ref.shape[0] // (k_ref.shape[1] // k_ref.shape[0] * source_refs[0].shape[1]) - 1
@@ -222,18 +236,19 @@
     def store(row, which, value):
         out_refs[which][row] = value.astype(BF16)
 
-    remote_sums(source_refs, hot_ref, k_ref, rows, 1, count, store)
-
-
-def stay_kernel(source_count, *refs):
+    remote_sums(source_refs, offsets, hot_ref, k_ref, rows, 1, count, store)
+
+
+def stay_kernel(offsets, skip, *refs):
+    source_count = len(offsets)
     source_refs = refs[:source_count]
     hot_ref, k_ref, local_ref = refs[source_count : source_count + 3]
     out_ref = refs[-1]
 
     def store(row, which, value):
-        out_ref[row] = value + local_ref[row]
-
-    remote_sums(source_refs, hot_ref, k_ref, out_ref.shape[0], 0, 1, store)
+        out_ref[row] = value + local_ref[skip + row]
+
+    remote_sums(source_refs, offsets, hot_ref, k_ref, out_ref.shape[0], 0, 1, store)
 
 
 def per_device(green_blocks, derivative, phonon_weight, occupation, mode_shift, neighbours):
@@ -254,10 +269,19 @@
 
     mate = swap(green, "energy", 1)
 
-    kind = lax.broadcasted_iota(jnp.int32, (2, modes, atoms), 0)
-    occupied = jnp.broadcast_to(occupation[None, :, None], kind.shape)
-    couplings = phonon_weight[None] * jnp.where(kind == 0, occupied + 1.0, occupied)
-    couplings = couplings.reshape(2 * modes, atoms).astype(BF16)
+    absorption = phonon_weight * occupation[:, None]
+    couplings = jnp.concatenate([absorption + phonon_weight, absorption], 0).astype(BF16)
+    green_near, shift_near = pl.pallas_call(
+        stage_kernel,
+        out_shape=(
+            jax.ShapeDtypeStruct(green.shape, green.dtype),
+            jax.ShapeDtypeStruct(mode_shift.shape, mode_shift.dtype),
+        ),
+        in_specs=[VMEM, SMEM],
+        out_specs=(VMEM, SMEM),
+        compiler_params=params(),
+        cost_estimate=cost(1e6, 1e6),
+    )(green, mode_shift)
 
     def mix(group, chunk, kind, after):
         return pl.pallas_call(
@@ -268,7 +292,7 @@
             scratch_shapes=[pltpu.VMEM((sizes[chunk], 2 * rows + 1, SUBLANES, atoms), F32)],
             compiler_params=params(),
             cost_estimate=cost(5e8, 1e6),
-        )(mode_shift, couplings, green, mate, *after)
+        )(shift_near, couplings, green_near, mate, *after)
 
     def prepare(after):
         return pl.pallas_call(
@@ -317,12 +341,15 @@
             total = total + received.astype(F32)
         mixed.append(jnp.concatenate([total.astype(BF16).reshape(-1, atoms), ids], 0))
 
-    def ordered(value, after):
-        return pl.pallas_call(
-            pass_kernel,
-            out_shape=jax.ShapeDtypeStruct(value.shape, value.dtype),
+    def ordered(value, pieces, after):
+        return pl.pallas_call(
+            functools.partial(pass_kernel, pieces),
+            out_shape=tuple(
+                jax.ShapeDtypeStruct((end - first + (ID_ROWS if first == 0 else 0), atoms), BF16)
+                for first, end in pieces
+            ),
             in_specs=[VMEM, ANY],
-            out_specs=VMEM,
+            out_specs=(VMEM,) * len(pieces),
             compiler_params=params(),
             cost_estimate=cost(1e6, 1e6),
         )(value, after)
@@ -339,10 +366,10 @@
             cost_estimate=cost(1e8, 1e6),
         )(*sources, after)
 
-    def away_sums(chunk, sources, hots, flips, after):
-        block = jax.ShapeDtypeStruct((sizes[chunk], square, atoms), BF16)
-        return pl.pallas_call(
-            functools.partial(away_kernel, len(sources)),
+    def away_sums(count, sources, offsets, hots, flips, after):
+        block = jax.ShapeDtypeStruct((count, square, atoms), BF16)
+        return pl.pallas_call(
+            functools.partial(away_kernel, offsets),
             out_shape=(block,) * len(flips),
             in_specs=[VMEM] * (len(sources) + 2) + [ANY],
             out_specs=(VMEM,) * len(flips),
@@ -350,35 +377,63 @@
             cost_estimate=cost(1e9, 3e6),
         )(*sources, hots, remote_k, after)
 
-    def stay_sum(chunk, sources, hots, local, after):
-        return pl.pallas_call(
-            functools.partial(stay_kernel, len(sources)),
-            out_shape=jax.ShapeDtypeStruct((sizes[chunk], square, atoms), F32),
-            in_specs=[VMEM] * (len(sources) + 3) + [ANY],
+    def stay_sum(count, skip, sources, offsets, hots, local, after):
+        return pl.pallas_call(
+            functools.partial(stay_kernel, offsets, skip),
+            out_shape=jax.ShapeDtypeStruct((count, square, atoms), F32),
+            in_specs=[VMEM] * (len(sources) + 3) + [ANY] * len(after),
             out_specs=VMEM,
             compiler_params=params(),
-            cost_estimate=cost(1e9, 3e6),
-        )(*sources, hots, remote_k, local, after)
+            cost_estimate=cost(4e9, 3e6),
+        )(*sources, hots, remote_k, local, *after)
 
     def send(values, masks):
         return [swap(value, "atom", mask) for value, mask in zip(values, masks)]
 
-    outer, inner = mixed
-    far = send([outer] * len(high), high)
-    near = send([inner] * 3, [2, 1, 3])
-    local_outer = local_sum(0, [inner])
-    passed = [ordered(value, local_outer) for value in far]
-    outer_sources = [outer] + far + send([outer] + passed, [1] * (1 + len(passed)))
-    local_inner = local_sum(1, passed[:1])
-    inner_sources = [inner] + near
-    inner_hots = one_hots(inner_sources, high, local_inner)
-    inner_away = away_sums(1, inner_sources, inner_hots, high, local_inner)
-    outer_hots = one_hots(outer_sources, [2], inner_away[0])
-    outer_away = away_sums(0, outer_sources, outer_hots, [2], inner_away[0])
-    inner_stay = stay_sum(1, inner_sources, inner_hots, local_inner, outer_away[0])
-    outer_stay = stay_sum(0, outer_sources, outer_hots, local_outer, inner_stay)
-    results = [outer_stay, inner_stay]
-    arrivals = [send(outer_away, [2]), send(inner_away, high)]
+    inner, outer = mixed
+    near = [inner] + send([inner] * 3, [2, 1, 3])
+    far = [outer] + send([outer] * len(high), high)
+    far_beside = send([outer], [1])
+    local_inner = local_sum(0, [outer])
+    local_outer = local_sum(1, [local_inner])
+    straight = [0] * len(near)
+    near_hots = one_hots(near, high, local_outer)
+    near_away = away_sums(sizes[0], near, straight, near_hots, high, local_outer)
+    near_back = send(near_away, high)
+    counts = [sizes[1] - sizes[1] // 2, sizes[1] // 2]
+    skips = [0, counts[0]]
+    pieces = [(skip * square, (skip + count) * square) for skip, count in zip(skips, counts)]
+    passed = [ordered(value, pieces, near_away[0]) for value in far[1:]]
+    far_next = [[value[index] for value in passed] for index in range(len(pieces))]
+    far_next = [send(values, [1] * len(values)) for values in far_next]
+    stay_inner = stay_sum(
+        sizes[0], 0, near, straight, near_hots, local_inner, passed[0][-1:]
+    )
+    after = stay_inner
+    far_hots = None
+    far_away, far_lists = [], []
+    for index, (first, _) in enumerate(pieces):
+        sources = far + far_beside + far_next[index]
+        offsets = [first] * (len(far) + 1) + [0] * len(far_next[index])
+        if far_hots is None:
+            far_hots = one_hots(sources, [2], after)
+        away = away_sums(counts[index], sources, offsets, far_hots, [2], after)
+        after = away[0]
+        far_away.append(swap(away[0], "atom", 2))
+        far_lists.append((sources, offsets))
+    results, arrivals = [stay_inner], [near_back]
+    for index, (sources, offsets) in enumerate(far_lists):
+        after = stay_sum(
+            counts[index],
+            skips[index],
+            sources,
+            offsets,
+            far_hots,
+            local_outer,
+            near_back + [after],
+        )
+        results.append(after)
+        arrivals.append([far_away[index]])
     combined = []
     for stay, received in zip(results, arrivals):
         for value in received:

time: 60.2 us -> 56.7 us (0.942)
  waiting for transfers between devices: 20.1 us -> 14.9 us
  Pallas kernels: 18.9 us -> 20.7 us
  starting transfers between devices: 15.3 us -> 16.9 us
  local copies, waits for them, and re-layouts: 2.71 us -> 1.71 us
  other arithmetic: 2.75 us -> 2.11 us
    ppermute x11 -> x13, waiting for transfers between devices: 20.1 us -> 14.9 us  [swap(): return lax.ppermute(value, axis, [(i, i ^ mask) for i in range(count)])]
    pallas_call x5 -> x8, Pallas kernels: 3.97 us -> 5.75 us  [the longest x3 2.3 us: away_sums(): pl.pallas_call(functools.partial(away_kernel, offsets), out_shape=(block,...]
    ppermute x11 -> x13, starting transfers between devices: 15.3 us -> 16.9 us  [swap(): return lax.ppermute(value, axis, [(i, i ^ mask) for i in range(count)])]
    broadcast_in_dim x4 -> x0, local copies, waits for them, and re-layouts: 0.83 us -> none  [per_device(): occupied = jnp.broadcast_to(occupation[None, :, None], kind.shape)]
    another operation x0 -> x1, other arithmetic: none -> 0.76 us
    convert_element_type x1 -> x0, other arithmetic: 0.76 us -> none  [per_device(): couplings = couplings.reshape(2 * modes, atoms).astype(BF16)]
    add x1 -> x0, other arithmetic: 0.66 us -> none  [per_device(): occupied + 1.0]
    unnamed x12 -> x8, local copies, waits for them, and re-layouts: 1.72 us -> 1.71 us
  transfers between devices with their start and end apart: 11 -> 13, of which waited for: 8 -> 7; matrix products, arithmetic and copies ran while one was open for 4% -> 2% of each run, Pallas kernels for 29% -> 34%
where the time goes in v6:
time: 56.7 us; the launch traced here: 56.6 us
  Pallas kernels  20.7 us (37%)
  starting transfers between devices  16.9 us (30%)
  waiting for transfers between devices  14.9 us (26%)
  other arithmetic  2.11 us (4%)
  local copies, waits for them, and re-layouts  1.71 us (3%)
    ppermute x13, starting transfers between devices, swap(): return lax.ppermute(value, axis, [(i, i ^ mask) for i in range(count)])  16.9 us
    ppermute x13, waiting for transfers between devices, swap(): return lax.ppermute(value, axis, [(i, i ^ mask) for i in range(count)])  14.9 us
    pallas_call x4, Pallas kernels, mix(): pl.pallas_call(functools.partial(mix_kernel, group, firsts[chunk]), out_s...  5.79 us
    pallas_call x2, Pallas kernels, local_sum(): pl.pallas_call(local_kernel, out_shape=jax.ShapeDtypeStruct((sizes[chunk]...  5.57 us
    pallas_call x1, Pallas kernels, prepare(): pl.pallas_call(prepare_kernel, out_shape=(jax.ShapeDtypeStruct((square, l...  3.35 us
    pallas_call x3, Pallas kernels, away_sums(): pl.pallas_call(functools.partial(away_kernel, offsets), out_shape=(block,...  2.3 us
    pallas_call x3, Pallas kernels, stay_sum(): pl.pallas_call(functools.partial(stay_kernel, offsets, skip), out_shape=j...  2.3 us
    unnamed x8, local copies, waits for them, and re-layouts  1.71 us
  transfers between devices with their start and end apart: 13, of which 7 were waited for; matrix products, arithmetic and copies ran while one was open for 2% of the time, Pallas kernels for 34%

profile of v6, /device:TPU:0, one launch (start us, length us, event | category | flops | bytes accessed | tf_op | source)
XLA Modules:
  0.0 56.6 jit_solution(18379006761542427305)
XLA Ops:
  0.5 1.0 %copy-done = bf16[8,16,16,128]{3,2,1,0:T(8,128)(2,1)S(1)} copy-done((bf16[8,16,16,128]{3,2,1,0:T(8,128)(2,1)S(1)}, bf16[8,16,16,128]{3,2,1,0:T(8,128)(2,1)}, u32[]{:S(2)}) %copy-start) | copy-done | bytes 524312
  2.2 1.1 %shard_map.64 = (bf16[8,256,128]{2,1,0:T(8,128)(2,1)S(1)}, s32[8]{0:T(128)S(1)}) custom-call(bf16[8,256,128]{2,1,0:T(8,128)(2,1)S(1)} %bitcast.6, s32[8]{0:T(128)S(1)} %copy-done.1), custom_call_target="tpu_custom_call" | custom-call | flops 1000000 | bytes 1000000 | tf_op jit(solution)/shard_map/pallas_call | solution.py:274
  4.1 1.4 %shard_map.65.rest_0_ = bf16[4,256,128]{2,1,0:T(8,128)(2,1)S(1)} custom-call(s32[8]{0:T(128)S(1)} %get-tuple-element.13.shift_ref, bf16[16,128]{1,0:T(8,128)(2,1)S(1)} %pad_maximum_fusion.3.coupling_ref, bf16[8,256,128]{2,1,0:T(8,128)(2,1)S(1)} %get-tuple-element.14.own_ref, bf16[8,256,128]{2,1,0:T(8,128)(2,1)S(1)} %collective-permute-done.mate_ref), custom_call_target="tpu_custom_call" | custom-call | flops 500000000 | bytes 1000000 | tf_op jit(solution)/shard_map/pallas_call | solution.py:287
  5.5 2.6 %collective-permute-start.1 = (bf16[4,256,128]{2,1,0:T(8,128)(2,1)S(1)}, bf16[4,256,128]{2,1,0:T(8,128)(2,1)S(1)}, u32[]{:S(2)}, u32[]{:S(2)}) collective-permute-start(bf16[4,256,128]{2,1,0:T(8,128)(2,1)S(1)} %shard_map.65.rest_0_), channel_id=1, source_target_pairs={{0,16},{8,24},{16,0},{24,8},{1,17},{9,25},{17,1},{25,9},{2,18},{10... | collective-permute-start | bytes 786440 | tf_op jit(solution)/shard_map/ppermute | solution.py:33
  8.0 1.5 %shard_map.66.rest_0_ = f32[4,256,128]{2,1,0:T(8,128)S(1)} custom-call(s32[8]{0:T(128)S(1)} %get-tuple-element.13.shift_ref, bf16[16,128]{1,0:T(8,128)(2,1)S(1)} %pad_maximum_fusion.3.coupling_ref, bf16[8,256,128]{2,1,0:T(8,128)(2,1)S(1)} %get-tuple-element.14.own_ref, bf16[8,256,128]{2,1,0:T(8,128)(2,1)S(1)} %collective-permute-done.mate_ref, ...), custom_call_target="tpu_custom_call" | custom-call | flops 500000000 | bytes 1000000 | tf_op jit(solution)/shard_map/pallas_call | solution.py:287
  9.6 1.4 %shard_map.67.after_ref = bf16[4,256,128]{2,1,0:T(8,128)(2,1)S(1)} custom-call(s32[8]{0:T(128)S(1)} %get-tuple-element.13.shift_ref, bf16[16,128]{1,0:T(8,128)(2,1)S(1)} %pad_maximum_fusion.3.coupling_ref, bf16[8,256,128]{2,1,0:T(8,128)(2,1)S(1)} %get-tuple-element.14.own_ref, bf16[8,256,128]{2,1,0:T(8,128)(2,1)S(1)} %collective-permute-done.mate_ref, ...), custom_call_target="tpu_custom_call" | custom-call | flops 500000000 | bytes 1000000 | tf_op jit(solution)/shard_map/pallas_call | solution.py:287
  11.0 3.4 %shard_map.68 = (bf16[256,3584]{1,0:T(8,128)(2,1)S(1)}, bf16[256,512]{1,0:T(8,128)(2,1)S(1)}, bf16[1792,128]{1,0:T(8,128)(2,1)S(1)}, bf16[16,128]{1,0:T(8,128)(2,1)S(1)}) custom-call(bf16[16,16,16]{2,1,0:T(8,128)(2,1)S(1)} %copy-done.2, s32[16,128]{1,0:T(8,128)S(1)} %bitcast.7, bf16[4,256,128]{2,1,0:T(8,128)(2,1)S(1)} %shard_map.67.after_ref), custom_call_target="tpu_custom_call" | custom-call | flops 2000000000 | bytes 3000000 | tf_op jit(solution)/shard_map/pallas_call | solution.py:298
  15.3 2.1 %collective-permute-start.2 = (bf16[1040,128]{1,0:T(8,128)(2,1)S(1)}, bf16[1040,128]{1,0:T(8,128)(2,1)S(1)}, u32[]{:S(2)}, u32[]{:S(2)}) collective-permute-start(bf16[1040,128]{1,0:T(8,128)(2,1)S(1)} %pad_maximum_fusion.2.rest_0_.mixed_ref.refs_0_), channel_id=1, source_target_pairs={{0,2},{1,3},{2,0},{3,1},{4,6},{5,7},{6,4},{7,5},{8,10},{9,11},{10,... | collective-permute-start | bytes 798728 | tf_op jit(solution)/shard_map/ppermute | solution.py:33
  17.4 1.5 %collective-permute-start.3 = (bf16[1040,128]{1,0:T(8,128)(2,1)S(1)}, bf16[1040,128]{1,0:T(8,128)(2,1)S(1)}, u32[]{:S(2)}, u32[]{:S(2)}) collective-permute-start(bf16[1040,128]{1,0:T(8,128)(2,1)S(1)} %pad_maximum_fusion.2.rest_0_.mixed_ref.refs_0_), channel_id=1, source_target_pairs={{0,1},{1,0},{2,3},{3,2},{4,5},{5,4},{6,7},{7,6},{8,9},{9,8},{10,11... | collective-permute-start | bytes 798728 | tf_op jit(solution)/shard_map/ppermute | solution.py:33
  18.9 1.5 %shard_map.69 = f32[4,256,128]{2,1,0:T(8,128)S(1)} custom-call(s32[8]{0:T(128)S(1)} %get-tuple-element.13.shift_ref, bf16[16,128]{1,0:T(8,128)(2,1)S(1)} %pad_maximum_fusion.3.coupling_ref, bf16[8,256,128]{2,1,0:T(8,128)(2,1)S(1)} %get-tuple-element.14.own_ref, bf16[8,256,128]{2,1,0:T(8,128)(2,1)S(1)} %collective-permute-done.mate_ref, ...), custom_call_target="tpu_custom_call" | custom-call | flops 500000000 | bytes 1000000 | tf_op jit(solution)/shard_map/pallas_call | solution.py:287
  20.7 2.9 %collective-permute-start.6 = (bf16[1040,128]{1,0:T(8,128)(2,1)S(1)}, bf16[1040,128]{1,0:T(8,128)(2,1)S(1)}, u32[]{:S(2)}, u32[]{:S(2)}) collective-permute-start(bf16[1040,128]{1,0:T(8,128)(2,1)S(1)} %pad_maximum_fusion.1.rest_0_.mixed_ref.refs_0_), channel_id=1, source_target_pairs={{0,4},{1,5},{2,6},{3,7},{4,0},{5,1},{6,2},{7,3},{8,12},{9,13},{10,... | collective-permute-start | bytes 798728 | tf_op jit(solution)/shard_map/ppermute | solution.py:33
  23.6 1.5 %collective-permute-start.8 = (bf16[1040,128]{1,0:T(8,128)(2,1)S(1)}, bf16[1040,128]{1,0:T(8,128)(2,1)S(1)}, u32[]{:S(2)}, u32[]{:S(2)}) collective-permute-start(bf16[1040,128]{1,0:T(8,128)(2,1)S(1)} %pad_maximum_fusion.1.rest_0_.mixed_ref.refs_0_), channel_id=1, source_target_pairs={{0,1},{1,0},{2,3},{3,2},{4,5},{5,4},{6,7},{7,6},{8,9},{9,8},{10,11... | collective-permute-start | bytes 798728 | tf_op jit(solution)/shard_map/ppermute | solution.py:33
  25.2 2.8 %shard_map.70.rest_0_.refs_6_ = f32[4,256,128]{2,1,0:T(8,128)S(1)} custom-call(bf16[1040,128]{1,0:T(8,128)(2,1)S(1)} %pad_maximum_fusion.2.rest_0_.mixed_ref.refs_0_, bf16[1792,128]{1,0:T(8,128)(2,1)S(1)} %get-tuple-element.16.rest_1_.hot_ref, bf16[256,3584]{1,0:T(8,128)(2,1)S(1)} %get-tuple-element.17.k_ref, ...), custom_call_target="tpu_custom_call" | custom-call | flops 2000000000 | bytes 3000000 | tf_op jit(solution)/shard_map/pallas_call | solution.py:313
  27.9 2.8 %shard_map.71.refs_4_.refs_6_ = f32[4,256,128]{2,1,0:T(8,128)S(1)} custom-call(bf16[1040,128]{1,0:T(8,128)(2,1)S(1)} %pad_maximum_fusion.1.rest_0_.mixed_ref.refs_0_, bf16[1792,128]{1,0:T(8,128)(2,1)S(1)} %get-tuple-element.16.rest_1_.hot_ref, bf16[256,3584]{1,0:T(8,128)(2,1)S(1)} %get-tuple-element.17.k_ref, f32[4,256,128]{2,1,0:T(8,128)S(1)} %shard_map.70.rest_0_.refs_6_), custom_call_target="tpu_custom_call" | custom-call | flops 2000000000 | bytes 3000000 | tf_op jit(solution)/shard_map/pallas_call | solution.py:313
  30.8 5.2 %collective-permute-done.4.refs_3_ = bf16[1040,128]{1,0:T(8,128)(2,1)S(1)} collective-permute-done((bf16[1040,128]{1,0:T(8,128)(2,1)S(1)}, bf16[1040,128]{1,0:T(8,128)(2,1)S(1)}, u32[]{:S(2)}, u32[]{:S(2)}) %collective-permute-start.4) | collective-permute-done | bytes 266272 | tf_op jit(solution)/shard_map/ppermute | solution.py:33
  36.0 1.0 %shard_map.73.after_ref = bf16[4,256,128]{2,1,0:T(8,128)(2,1)S(1)} custom-call(bf16[1040,128]{1,0:T(8,128)(2,1)S(1)} %pad_maximum_fusion.2.rest_0_.mixed_ref.refs_0_, bf16[1040,128]{1,0:T(8,128)(2,1)S(1)} %collective-permute-done.2.refs_1_, bf16[1040,128]{1,0:T(8,128)(2,1)S(1)} %collective-permute-done.3.refs_2_, ...), custom_call_target="tpu_custom_call" | custom-call | flops 1000000000 | bytes 3000000 | tf_op jit(solution)/shard_map/pallas_call | solution.py:371
  37.2 1.2 %collective-permute-start.9 = (bf16[528,128]{1,0:T(8,128)(2,1)S(1)}, bf16[528,128]{1,0:T(8,128)(2,1)S(1)}, u32[]{:S(2)}, u32[]{:S(2)}) collective-permute-start(bf16[528,128]{1,0:T(8,128)(2,1)S(1)} %get-tuple-element.20), channel_id=1, source_target_pairs={{0,1},{1,0},{2,3},{3,2},{4,5},{5,4},{6,7},{7,6},{8,9},{9,8},{10,11... | collective-permute-start | bytes 405512 | tf_op jit(solution)/shard_map/ppermute | solution.py:33
  39.3 1.0 %shard_map.75.refs_4_.refs_6_ = f32[4,256,128]{2,1,0:T(8,128)S(1)} custom-call(bf16[1040,128]{1,0:T(8,128)(2,1)S(1)} %pad_maximum_fusion.2.rest_0_.mixed_ref.refs_0_, bf16[1040,128]{1,0:T(8,128)(2,1)S(1)} %collective-permute-done.2.refs_1_, bf16[1040,128]{1,0:T(8,128)(2,1)S(1)} %collective-permute-done.3.refs_2_, ...), custom_call_target="tpu_custom_call" | custom-call | flops 4000000000 | bytes 3000000 | tf_op jit(solution)/shard_map/pallas_call | solution.py:381
  40.3 2.2 %collective-permute-done.9.refs_3_ = bf16[528,128]{1,0:T(8,128)(2,1)S(1)} collective-permute-done((bf16[528,128]{1,0:T(8,128)(2,1)S(1)}, bf16[528,128]{1,0:T(8,128)(2,1)S(1)}, u32[]{:S(2)}, u32[]{:S(2)}) %collective-permute-start.9) | collective-permute-done | bytes 135200 | tf_op jit(solution)/shard_map/ppermute | solution.py:33
  43.3 3.0 %collective-permute-start.11 = (bf16[2,256,128]{2,1,0:T(8,128)(2,1)S(1)}, bf16[2,256,128]{2,1,0:T(8,128)(2,1)S(1)}, u32[]{:S(2)}, u32[]{:S(2)}) collective-permute-start(bf16[2,256,128]{2,1,0:T(8,128)(2,1)S(1)} %shard_map.77.refs_6_), channel_id=1, source_target_pairs={{0,2},{1,3},{2,0},{3,1},{4,6},{5,7},{6,4},{7,5},{8,10},{9,11},{10,... | collective-permute-start | bytes 393224 | tf_op jit(solution)/shard_map/ppermute | solution.py:33
  47.5 2.7 %collective-permute-done.7.refs_7_ = bf16[4,256,128]{2,1,0:T(8,128)(2,1)S(1)} collective-permute-done((bf16[4,256,128]{2,1,0:T(8,128)(2,1)S(1)}, bf16[4,256,128]{2,1,0:T(8,128)(2,1)S(1)}, u32[]{:S(2)}, u32[]{:S(2)}) %collective-permute-start.7) | collective-permute-done | bytes 262176 | tf_op jit(solution)/shard_map/ppermute | solution.py:33
  51.7 1.5 %collective-permute-done.11 = bf16[2,256,128]{2,1,0:T(8,128)(2,1)S(1)} collective-permute-done((bf16[2,256,128]{2,1,0:T(8,128)(2,1)S(1)}, bf16[2,256,128]{2,1,0:T(8,128)(2,1)S(1)}, u32[]{:S(2)}, u32[]{:S(2)}) %collective-permute-start.11) | collective-permute-done | bytes 131104 | tf_op jit(solution)/shard_map/ppermute | solution.py:33
  53.2 2.3 %collective-permute-done.12 = bf16[2,256,128]{2,1,0:T(8,128)(2,1)S(1)} collective-permute-done((bf16[2,256,128]{2,1,0:T(8,128)(2,1)S(1)}, bf16[2,256,128]{2,1,0:T(8,128)(2,1)S(1)}, u32[]{:S(2)}, u32[]{:S(2)}) %collective-permute-start.12) | collective-permute-done | bytes 131104 | tf_op jit(solution)/shard_map/ppermute | solution.py:33
  55.5 1.1 %pad_maximum_fusion = f32[8,256,128]{2,1,0:T(8,128)} fusion(f32[2,256,128]{2,1,0:T(8,128)S(1)} %convert_add_fusion.1, f32[2,256,128]{2,1,0:T(8,128)S(1)} %convert_add_fusion.2, f32[4,256,128]{2,1,0:T(8,128)S(1)} %convert_add_fusion), kind=kLoop, calls=%fused_computation | loop fusion | flops 524288 | bytes 2097152 | tf_op jit(solution)/shard_map/concatenate | solution.py:442
  (37 shorter events, 7.7 us)
Async XLA Ops:
  0.0 4.1 %collective-permute-start = (bf16[8,256,128]{2,1,0:T(8,128)(2,1)}, bf16[8,256,128]{2,1,0:T(8,128)(2,1)S(1)}, u32[]{:S(2)}, u32[]{:S(2)}) collective-permute-start(bf16[8,256,128]{2,1,0:T(8,128)(2,1)} %bitcast.5), channel_id=1, source_target_pairs={{0,8},{8,0},{16,24},{24,16},{1,9},{9,1},{17,25},{25,17},{2,10},{10... | collective-permute-start | bytes 1572872 | tf_op jit(solution)/shard_map/ppermute | solution.py:33
  0.5 1.0 %copy-start = (bf16[8,16,16,128]{3,2,1,0:T(8,128)(2,1)S(1)}, bf16[8,16,16,128]{3,2,1,0:T(8,128)(2,1)}, u32[]{:S(2)}) copy-start(bf16[8,16,16,128]{3,2,1,0:T(8,128)(2,1)} %param.6) | copy-start | bytes 1572868
  1.5 0.7 %copy-start.1 = (s32[8]{0:T(128)S(1)}, s32[8]{0:T(128)}, u32[]{:S(2)}) copy-start(s32[8]{0:T(128)} %shift_ref.1) | copy-start | bytes 100
  5.5 5.6 %copy-start.2 = (bf16[16,16,16]{2,1,0:T(8,128)(2,1)S(1)}, bf16[16,16,16]{2,1,0:T(8,128)(2,1)}, u32[]{:S(2)}) copy-start(bf16[16,16,16]{2,1,0:T(8,128)(2,1)} %derivative_ref.1) | copy-start | bytes 24580
  5.5 5.6 %copy-start.3 = (s32[128,16]{0,1:T(8,128)S(1)}, s32[128,16]{0,1:T(8,128)}, u32[]{:S(2)}) copy-start(s32[128,16]{0,1:T(8,128)} %param.11) | copy-start | bytes 24580
  5.5 9.7 %collective-permute-start.1 = (bf16[4,256,128]{2,1,0:T(8,128)(2,1)S(1)}, bf16[4,256,128]{2,1,0:T(8,128)(2,1)S(1)}, u32[]{:S(2)}, u32[]{:S(2)}) collective-permute-start(bf16[4,256,128]{2,1,0:T(8,128)(2,1)S(1)} %shard_map.65.rest_0_), channel_id=1, source_target_pairs={{0,16},{8,24},{16,0},{24,8},{1,17},{9,25},{17,1},{25,9},{2,18},{10... | collective-permute-start | bytes 786440 | tf_op jit(solution)/shard_map/ppermute | solution.py:33
  10.9 9.7 %collective-permute-start.5 = (bf16[4,256,128]{2,1,0:T(8,128)(2,1)S(1)}, bf16[4,256,128]{2,1,0:T(8,128)(2,1)S(1)}, u32[]{:S(2)}, u32[]{:S(2)}) collective-permute-start(bf16[4,256,128]{2,1,0:T(8,128)(2,1)S(1)} %shard_map.67.after_ref), channel_id=1, source_target_pairs={{0,16},{8,24},{16,0},{24,8},{1,17},{9,25},{17,1},{25,9},{2,18},{10... | collective-permute-start | bytes 786440 | tf_op jit(solution)/shard_map/ppermute | solution.py:33
  15.3 15.5 %collective-permute-start.2 = (bf16[1040,128]{1,0:T(8,128)(2,1)S(1)}, bf16[1040,128]{1,0:T(8,128)(2,1)S(1)}, u32[]{:S(2)}, u32[]{:S(2)}) collective-permute-start(bf16[1040,128]{1,0:T(8,128)(2,1)S(1)} %pad_maximum_fusion.2.rest_0_.mixed_ref.refs_0_), channel_id=1, source_target_pairs={{0,2},{1,3},{2,0},{3,1},{4,6},{5,7},{6,4},{7,5},{8,10},{9,11},{10,... | collective-permute-start | bytes 798728 | tf_op jit(solution)/shard_map/ppermute | solution.py:33
  17.4 13.4 %collective-permute-start.3 = (bf16[1040,128]{1,0:T(8,128)(2,1)S(1)}, bf16[1040,128]{1,0:T(8,128)(2,1)S(1)}, u32[]{:S(2)}, u32[]{:S(2)}) collective-permute-start(bf16[1040,128]{1,0:T(8,128)(2,1)S(1)} %pad_maximum_fusion.2.rest_0_.mixed_ref.refs_0_), channel_id=1, source_target_pairs={{0,1},{1,0},{2,3},{3,2},{4,5},{5,4},{6,7},{7,6},{8,9},{9,8},{10,11... | collective-permute-start | bytes 798728 | tf_op jit(solution)/shard_map/ppermute | solution.py:33
  18.9 17.0 %collective-permute-start.4 = (bf16[1040,128]{1,0:T(8,128)(2,1)S(1)}, bf16[1040,128]{1,0:T(8,128)(2,1)S(1)}, u32[]{:S(2)}, u32[]{:S(2)}) collective-permute-start(bf16[1040,128]{1,0:T(8,128)(2,1)S(1)} %pad_maximum_fusion.2.rest_0_.mixed_ref.refs_0_), channel_id=1, source_target_pairs={{0,3},{1,2},{2,1},{3,0},{4,7},{5,6},{6,5},{7,4},{8,11},{9,10},{10,... | collective-permute-start | bytes 798728 | tf_op jit(solution)/shard_map/ppermute | solution.py:33
  20.7 16.4 %collective-permute-start.6 = (bf16[1040,128]{1,0:T(8,128)(2,1)S(1)}, bf16[1040,128]{1,0:T(8,128)(2,1)S(1)}, u32[]{:S(2)}, u32[]{:S(2)}) collective-permute-start(bf16[1040,128]{1,0:T(8,128)(2,1)S(1)} %pad_maximum_fusion.1.rest_0_.mixed_ref.refs_0_), channel_id=1, source_target_pairs={{0,4},{1,5},{2,6},{3,7},{4,0},{5,1},{6,2},{7,3},{8,12},{9,13},{10,... | collective-permute-start | bytes 798728 | tf_op jit(solution)/shard_map/ppermute | solution.py:33
  23.6 16.6 %collective-permute-start.8 = (bf16[1040,128]{1,0:T(8,128)(2,1)S(1)}, bf16[1040,128]{1,0:T(8,128)(2,1)S(1)}, u32[]{:S(2)}, u32[]{:S(2)}) collective-permute-start(bf16[1040,128]{1,0:T(8,128)(2,1)S(1)} %pad_maximum_fusion.1.rest_0_.mixed_ref.refs_0_), channel_id=1, source_target_pairs={{0,1},{1,0},{2,3},{3,2},{4,5},{5,4},{6,7},{7,6},{8,9},{9,8},{10,11... | collective-permute-start | bytes 798728 | tf_op jit(solution)/shard_map/ppermute | solution.py:33
  37.0 13.2 %collective-permute-start.7 = (bf16[4,256,128]{2,1,0:T(8,128)(2,1)S(1)}, bf16[4,256,128]{2,1,0:T(8,128)(2,1)S(1)}, u32[]{:S(2)}, u32[]{:S(2)}) collective-permute-start(bf16[4,256,128]{2,1,0:T(8,128)(2,1)S(1)} %shard_map.73.after_ref), channel_id=1, source_target_pairs={{0,4},{1,5},{2,6},{3,7},{4,0},{5,1},{6,2},{7,3},{8,12},{9,13},{10,... | collective-permute-start | bytes 786440 | tf_op jit(solution)/shard_map/ppermute | solution.py:33
  37.2 5.3 %collective-permute-start.9 = (bf16[528,128]{1,0:T(8,128)(2,1)S(1)}, bf16[528,128]{1,0:T(8,128)(2,1)S(1)}, u32[]{:S(2)}, u32[]{:S(2)}) collective-permute-start(bf16[528,128]{1,0:T(8,128)(2,1)S(1)} %get-tuple-element.20), channel_id=1, source_target_pairs={{0,1},{1,0},{2,3},{3,2},{4,5},{5,4},{6,7},{7,6},{8,9},{9,8},{10,11... | collective-permute-start | bytes 405512 | tf_op jit(solution)/shard_map/ppermute | solution.py:33
  38.4 7.9 %collective-permute-start.10 = (bf16[512,128]{1,0:T(8,128)(2,1)S(1)}, bf16[512,128]{1,0:T(8,128)(2,1)S(1)}, u32[]{:S(2)}, u32[]{:S(2)}) collective-permute-start(bf16[512,128]{1,0:T(8,128)(2,1)S(1)} %get-tuple-element.19.refs_7_), channel_id=1, source_target_pairs={{0,1},{1,0},{2,3},{3,2},{4,5},{5,4},{6,7},{7,6},{8,9},{9,8},{10,11... | collective-permute-start | bytes 393224 | tf_op jit(solution)/shard_map/ppermute | solution.py:33
  43.3 9.9 %collective-permute-start.11 = (bf16[2,256,128]{2,1,0:T(8,128)(2,1)S(1)}, bf16[2,256,128]{2,1,0:T(8,128)(2,1)S(1)}, u32[]{:S(2)}, u32[]{:S(2)}) collective-permute-start(bf16[2,256,128]{2,1,0:T(8,128)(2,1)S(1)} %shard_map.77.refs_6_), channel_id=1, source_target_pairs={{0,2},{1,3},{2,0},{3,1},{4,6},{5,7},{6,4},{7,5},{8,10},{9,11},{10,... | collective-permute-start | bytes 393224 | tf_op jit(solution)/shard_map/ppermute | solution.py:33
  46.9 8.5 %collective-permute-start.12 = (bf16[2,256,128]{2,1,0:T(8,128)(2,1)S(1)}, bf16[2,256,128]{2,1,0:T(8,128)(2,1)S(1)}, u32[]{:S(2)}, u32[]{:S(2)}) collective-permute-start(bf16[2,256,128]{2,1,0:T(8,128)(2,1)S(1)} %shard_map.78.refs_8_), channel_id=1, source_target_pairs={{0,2},{1,3},{2,0},{3,1},{4,6},{5,7},{6,4},{7,5},{8,10},{9,11},{10,... | collective-permute-start | bytes 393224 | tf_op jit(solution)/shard_map/ppermute | solution.py:33

commit v7 on v6

--- a/solution.py
+++ b/solution.py
@@ -9,7 +9,7 @@
 
 REMOTE_BONDS = 2
 ID_ROWS = 16
-P_PART = 4
+P_PART = 3
 COST = 1.0
 SUBLANES = 8
 VMEM_LIMIT = 48 * 1024 * 1024
@@ -144,12 +144,6 @@
     for at, row in enumerate(rows):
         ids = jnp.where(place == at, row, ids)
     ids_ref[...] = ids.astype(F32).astype(BF16)
-
-
-def stage_kernel(green_ref, shift_ref, green_out, shift_out):
-    green_out[...] = green_ref[...]
-    for mode in range(shift_ref.shape[0]):
-        shift_out[mode] = shift_ref[mode]
 
 
 def pass_kernel(pieces, value_ref, after_ref, *out_refs):
@@ -271,17 +265,6 @@
 
     absorption = phonon_weight * occupation[:, None]
     couplings = jnp.concatenate([absorption + phonon_weight, absorption], 0).astype(BF16)
-    green_near, shift_near = pl.pallas_call(
-        stage_kernel,
-        out_shape=(
-            jax.ShapeDtypeStruct(green.shape, green.dtype),
-            jax.ShapeDtypeStruct(mode_shift.shape, mode_shift.dtype),
-        ),
-        in_specs=[VMEM, SMEM],
-        out_specs=(VMEM, SMEM),
-        compiler_params=params(),
-        cost_estimate=cost(1e6, 1e6),
-    )(green, mode_shift)
 
     def mix(group, chunk, kind, after):
         return pl.pallas_call(
@@ -292,7 +275,7 @@
             scratch_shapes=[pltpu.VMEM((sizes[chunk], 2 * rows + 1, SUBLANES, atoms), F32)],
             compiler_params=params(),
             cost_estimate=cost(5e8, 1e6),
-        )(shift_near, couplings, green_near, mate, *after)
+        )(mode_shift, couplings, green, mate, *after)
 
     def prepare(after):
         return pl.pallas_call(
@@ -400,8 +383,7 @@
     near_hots = one_hots(near, high, local_outer)
     near_away = away_sums(sizes[0], near, straight, near_hots, high, local_outer)
     near_back = send(near_away, high)
-    counts = [sizes[1] - sizes[1] // 2, sizes[1] // 2]
-    skips = [0, counts[0]]
+    counts, skips = [sizes[1]], [0]
     pieces = [(skip * square, (skip + count) * square) for skip, count in zip(skips, counts)]
     passed = [ordered(value, pieces, near_away[0]) for value in far[1:]]
     far_next = [[value[index] for value in passed] for index in range(len(pieces))]
@@ -430,7 +412,7 @@
             offsets,
             far_hots,
             local_outer,
-            near_back + [after],
+            [after],
         )
         results.append(after)
         arrivals.append([far_away[index]])

time: 56.7 us -> 59.1 us (1.042)
  waiting for transfers between devices: 14.9 us -> 19.7 us
  Pallas kernels: 20.7 us -> 17.7 us
  starting transfers between devices: 16.9 us -> 17.5 us
    ppermute x13 -> x11, waiting for transfers between devices: 14.9 us -> 19.7 us  [swap(): return lax.ppermute(value, axis, [(i, i ^ mask) for i in range(count)])]
    pallas_call x1 -> x0, Pallas kernels: 1.14 us -> none  [per_device(): pl.pallas_call(stage_kernel, out_shape=(jax.ShapeDtypeStruct(green.shape,...]
    pallas_call x2, Pallas kernels: 5.57 us -> 4.75 us  [local_sum(): pl.pallas_call(local_kernel, out_shape=jax.ShapeDtypeStruct((sizes[chunk]...]
    ppermute x13 -> x11, starting transfers between devices: 16.9 us -> 17.5 us  [swap(): return lax.ppermute(value, axis, [(i, i ^ mask) for i in range(count)])]
    pallas_call x3 -> x2, Pallas kernels: 2.3 us -> 1.8 us  [away_sums(): pl.pallas_call(functools.partial(away_kernel, offsets), out_shape=(block,...]
    pallas_call x3 -> x2, Pallas kernels: 2.3 us -> 1.81 us  [stay_sum(): pl.pallas_call(functools.partial(stay_kernel, offsets, skip), out_shape=j...]
    unnamed x8 -> x10, local copies, waits for them, and re-layouts: 1.71 us -> 1.71 us
  transfers between devices with their start and end apart: 13 -> 11, of which waited for: 7 -> 7; matrix products, arithmetic and copies ran while one was open for 2% -> 2% of each run, Pallas kernels for 34% -> 27%
where the time goes in v7:
time: 59.1 us; the launch traced here: 58.9 us
  waiting for transfers between devices  19.7 us (33%)
  Pallas kernels  17.7 us (30%)
  starting transfers between devices  17.5 us (30%)
  other arithmetic  2.08 us (4%)
  local copies, waits for them, and re-layouts  1.71 us (3%)
    ppermute x11, waiting for transfers between devices, swap(): return lax.ppermute(value, axis, [(i, i ^ mask) for i in range(count)])  19.7 us
    ppermute x11, starting transfers between devices, swap(): return lax.ppermute(value, axis, [(i, i ^ mask) for i in range(count)])  17.5 us
    pallas_call x4, Pallas kernels, mix(): pl.pallas_call(functools.partial(mix_kernel, group, firsts[chunk]), out_s...  5.76 us
    pallas_call x2, Pallas kernels, local_sum(): pl.pallas_call(local_kernel, out_shape=jax.ShapeDtypeStruct((sizes[chunk]...  4.75 us
    pallas_call x1, Pallas kernels, prepare(): pl.pallas_call(prepare_kernel, out_shape=(jax.ShapeDtypeStruct((square, l...  3.35 us
    pallas_call x2, Pallas kernels, stay_sum(): pl.pallas_call(functools.partial(stay_kernel, offsets, skip), out_shape=j...  1.81 us
    pallas_call x2, Pallas kernels, away_sums(): pl.pallas_call(functools.partial(away_kernel, offsets), out_shape=(block,...  1.8 us
    unnamed x10, local copies, waits for them, and re-layouts  1.71 us
  transfers between devices with their start and end apart: 11, of which 7 were waited for; matrix products, arithmetic and copies ran while one was open for 2% of the time, Pallas kernels for 27%

profile of v7, /device:TPU:0, one launch (start us, length us, event | category | flops | bytes accessed | tf_op | source)
XLA Modules:
  0.0 58.9 jit_solution(13072830282533008731)
XLA Ops:
  1.2 1.0 %collective-permute-done.mate_ref = bf16[8,256,128]{2,1,0:T(8,128)(2,1)S(1)} collective-permute-done((bf16[8,256,128]{2,1,0:T(8,128)(2,1)}, bf16[8,256,128]{2,1,0:T(8,128)(2,1)S(1)}, u32[]{:S(2)}, u32[]{:S(2)}) %collective-permute-start) | collective-permute-done | bytes 524320 | tf_op jit(solution)/shard_map/ppermute | solution.py:33
  2.2 1.0 %copy-done = bf16[8,16,16,128]{3,2,1,0:T(8,128)(2,1)S(1)} copy-done((bf16[8,16,16,128]{3,2,1,0:T(8,128)(2,1)S(1)}, bf16[8,16,16,128]{3,2,1,0:T(8,128)(2,1)}, u32[]{:S(2)}) %copy-start) | copy-done | bytes 524312
  3.9 1.5 %shard_map.64.rest_0_ = bf16[5,256,128]{2,1,0:T(8,128)(2,1)S(1)} custom-call(s32[8]{0:T(128)S(1)} %copy-done.2, bf16[16,128]{1,0:T(8,128)(2,1)S(1)} %pad_maximum_fusion.3.coupling_ref, bf16[8,256,128]{2,1,0:T(8,128)(2,1)S(1)} %bitcast.6, bf16[8,256,128]{2,1,0:T(8,128)(2,1)S(1)} %collective-permute-done.mate_ref), custom_call_target="tpu_custom_call" | custom-call | flops 500000000 | bytes 1000000 | tf_op jit(solution)/shard_map/pallas_call | solution.py:270
  5.5 2.9 %collective-permute-start.1 = (bf16[5,256,128]{2,1,0:T(8,128)(2,1)S(1)}, bf16[5,256,128]{2,1,0:T(8,128)(2,1)S(1)}, u32[]{:S(2)}, u32[]{:S(2)}) collective-permute-start(bf16[5,256,128]{2,1,0:T(8,128)(2,1)S(1)} %shard_map.64.rest_0_), channel_id=1, source_target_pairs={{0,16},{8,24},{16,0},{24,8},{1,17},{9,25},{17,1},{25,9},{2,18},{10... | collective-permute-start | bytes 983048 | tf_op jit(solution)/shard_map/ppermute | solution.py:33
  8.4 1.7 %shard_map.65.rest_0_ = f32[5,256,128]{2,1,0:T(8,128)S(1)} custom-call(s32[8]{0:T(128)S(1)} %copy-done.2, bf16[16,128]{1,0:T(8,128)(2,1)S(1)} %pad_maximum_fusion.3.coupling_ref, bf16[8,256,128]{2,1,0:T(8,128)(2,1)S(1)} %bitcast.7, bf16[8,256,128]{2,1,0:T(8,128)(2,1)S(1)} %collective-permute-done.mate_ref, bf16[5,256,128]{2,1,0:T(8,128)(2,1)S(1)} %shard_map.64.rest_0_), custom_call_target="tpu_custom_call" | custom-call | flops 500000000 | bytes 1000000 | tf_op jit(solution)/shard_map/pallas_call | solution.py:270
  10.1 1.2 %shard_map.66.after_ref = bf16[3,256,128]{2,1,0:T(8,128)(2,1)S(1)} custom-call(s32[8]{0:T(128)S(1)} %copy-done.2, bf16[16,128]{1,0:T(8,128)(2,1)S(1)} %pad_maximum_fusion.3.coupling_ref, bf16[8,256,128]{2,1,0:T(8,128)(2,1)S(1)} %bitcast.8, bf16[8,256,128]{2,1,0:T(8,128)(2,1)S(1)} %collective-permute-done.mate_ref, f32[5,256,128]{2,1,0:T(8,128)S(1)} %shard_map.65.rest_0_), custom_call_target="tpu_custom_call" | custom-call | flops 500000000 | bytes 1000000 | tf_op jit(solution)/shard_map/pallas_call | solution.py:270
  11.4 3.3 %shard_map.67 = (bf16[256,3584]{1,0:T(8,128)(2,1)S(1)}, bf16[256,512]{1,0:T(8,128)(2,1)S(1)}, bf16[1792,128]{1,0:T(8,128)(2,1)S(1)}, bf16[16,128]{1,0:T(8,128)(2,1)S(1)}) custom-call(bf16[16,16,16]{2,1,0:T(8,128)(2,1)S(1)} %copy-done.3, s32[16,128]{1,0:T(8,128)S(1)} %bitcast.10, bf16[3,256,128]{2,1,0:T(8,128)(2,1)S(1)} %shard_map.66.after_ref), custom_call_target="tpu_custom_call" | custom-call | flops 2000000000 | bytes 3000000 | tf_op jit(solution)/shard_map/pallas_call | solution.py:281
  14.8 2.1 %collective-permute-done.1 = bf16[5,256,128]{2,1,0:T(8,128)(2,1)S(1)} collective-permute-done((bf16[5,256,128]{2,1,0:T(8,128)(2,1)S(1)}, bf16[5,256,128]{2,1,0:T(8,128)(2,1)S(1)}, u32[]{:S(2)}, u32[]{:S(2)}) %collective-permute-start.1) | collective-permute-done | bytes 327712 | tf_op jit(solution)/shard_map/ppermute | solution.py:33
  17.0 2.2 %collective-permute-start.2 = (bf16[1296,128]{1,0:T(8,128)(2,1)S(1)}, bf16[1296,128]{1,0:T(8,128)(2,1)S(1)}, u32[]{:S(2)}, u32[]{:S(2)}) collective-permute-start(bf16[1296,128]{1,0:T(8,128)(2,1)S(1)} %pad_maximum_fusion.1.rest_0_.mixed_ref.refs_0_), channel_id=1, source_target_pairs={{0,2},{1,3},{2,0},{3,1},{4,6},{5,7},{6,4},{7,5},{8,10},{9,11},{10,... | collective-permute-start | bytes 995336 | tf_op jit(solution)/shard_map/ppermute | solution.py:33
  19.2 1.5 %collective-permute-start.3 = (bf16[1296,128]{1,0:T(8,128)(2,1)S(1)}, bf16[1296,128]{1,0:T(8,128)(2,1)S(1)}, u32[]{:S(2)}, u32[]{:S(2)}) collective-permute-start(bf16[1296,128]{1,0:T(8,128)(2,1)S(1)} %pad_maximum_fusion.1.rest_0_.mixed_ref.refs_0_), channel_id=1, source_target_pairs={{0,1},{1,0},{2,3},{3,2},{4,5},{5,4},{6,7},{7,6},{8,9},{9,8},{10,11... | collective-permute-start | bytes 995336 | tf_op jit(solution)/shard_map/ppermute | solution.py:33
  20.7 1.3 %shard_map.68 = f32[3,256,128]{2,1,0:T(8,128)S(1)} custom-call(s32[8]{0:T(128)S(1)} %copy-done.2, bf16[16,128]{1,0:T(8,128)(2,1)S(1)} %pad_maximum_fusion.3.coupling_ref, bf16[8,256,128]{2,1,0:T(8,128)(2,1)S(1)} %bitcast.9, bf16[8,256,128]{2,1,0:T(8,128)(2,1)S(1)} %collective-permute-done.mate_ref, ...), custom_call_target="tpu_custom_call" | custom-call | flops 500000000 | bytes 1000000 | tf_op jit(solution)/shard_map/pallas_call | solution.py:270
  22.1 3.0 %collective-permute-start.6 = (bf16[784,128]{1,0:T(8,128)(2,1)S(1)}, bf16[784,128]{1,0:T(8,128)(2,1)S(1)}, u32[]{:S(2)}, u32[]{:S(2)}) collective-permute-start(bf16[784,128]{1,0:T(8,128)(2,1)S(1)} %pad_maximum_fusion.2.rest_0_.mixed_ref.refs_0_), channel_id=1, source_target_pairs={{0,4},{1,5},{2,6},{3,7},{4,0},{5,1},{6,2},{7,3},{8,12},{9,13},{10,... | collective-permute-start | bytes 602120 | tf_op jit(solution)/shard_map/ppermute | solution.py:33
  25.2 1.5 %collective-permute-start.8 = (bf16[784,128]{1,0:T(8,128)(2,1)S(1)}, bf16[784,128]{1,0:T(8,128)(2,1)S(1)}, u32[]{:S(2)}, u32[]{:S(2)}) collective-permute-start(bf16[784,128]{1,0:T(8,128)(2,1)S(1)} %pad_maximum_fusion.2.rest_0_.mixed_ref.refs_0_), channel_id=1, source_target_pairs={{0,1},{1,0},{2,3},{3,2},{4,5},{5,4},{6,7},{7,6},{8,9},{9,8},{10,11... | collective-permute-start | bytes 602120 | tf_op jit(solution)/shard_map/ppermute | solution.py:33
  26.7 2.9 %shard_map.69.rest_0_.refs_6_ = f32[5,256,128]{2,1,0:T(8,128)S(1)} custom-call(bf16[1296,128]{1,0:T(8,128)(2,1)S(1)} %pad_maximum_fusion.1.rest_0_.mixed_ref.refs_0_, bf16[1792,128]{1,0:T(8,128)(2,1)S(1)} %get-tuple-element.10.rest_1_.hot_ref, bf16[256,3584]{1,0:T(8,128)(2,1)S(1)} %get-tuple-element.11.k_ref, ...), custom_call_target="tpu_custom_call" | custom-call | flops 2000000000 | bytes 3000000 | tf_op jit(solution)/shard_map/pallas_call | solution.py:296
  29.6 1.9 %shard_map.70.refs_4_.refs_6_ = f32[3,256,128]{2,1,0:T(8,128)S(1)} custom-call(bf16[784,128]{1,0:T(8,128)(2,1)S(1)} %pad_maximum_fusion.2.rest_0_.mixed_ref.refs_0_, bf16[1792,128]{1,0:T(8,128)(2,1)S(1)} %get-tuple-element.10.rest_1_.hot_ref, bf16[256,3584]{1,0:T(8,128)(2,1)S(1)} %get-tuple-element.11.k_ref, f32[5,256,128]{2,1,0:T(8,128)S(1)} %shard_map.69.rest_0_.refs_6_), custom_call_target="tpu_custom_call" | custom-call | flops 2000000000 | bytes 3000000 | tf_op jit(solution)/shard_map/pallas_call | solution.py:296
  32.2 6.1 %collective-permute-done.4.refs_3_ = bf16[1296,128]{1,0:T(8,128)(2,1)S(1)} collective-permute-done((bf16[1296,128]{1,0:T(8,128)(2,1)S(1)}, bf16[1296,128]{1,0:T(8,128)(2,1)S(1)}, u32[]{:S(2)}, u32[]{:S(2)}) %collective-permute-start.4) | collective-permute-done | bytes 331808 | tf_op jit(solution)/shard_map/ppermute | solution.py:33
  38.4 1.1 %shard_map.72.after_ref = bf16[5,256,128]{2,1,0:T(8,128)(2,1)S(1)} custom-call(bf16[1296,128]{1,0:T(8,128)(2,1)S(1)} %pad_maximum_fusion.1.rest_0_.mixed_ref.refs_0_, bf16[1296,128]{1,0:T(8,128)(2,1)S(1)} %collective-permute-done.2.refs_1_, bf16[1296,128]{1,0:T(8,128)(2,1)S(1)} %collective-permute-done.3.refs_2_, ...), custom_call_target="tpu_custom_call" | custom-call | flops 1000000000 | bytes 3000000 | tf_op jit(solution)/shard_map/pallas_call | solution.py:354
  40.3 1.6 %collective-permute-start.9 = (bf16[784,128]{1,0:T(8,128)(2,1)S(1)}, bf16[784,128]{1,0:T(8,128)(2,1)S(1)}, u32[]{:S(2)}, u32[]{:S(2)}) collective-permute-start(bf16[784,128]{1,0:T(8,128)(2,1)S(1)} %shard_map.73.refs_7_), channel_id=1, source_target_pairs={{0,1},{1,0},{2,3},{3,2},{4,5},{5,4},{6,7},{7,6},{8,9},{9,8},{10,11... | collective-permute-start | bytes 602120 | tf_op jit(solution)/shard_map/ppermute | solution.py:33
  41.9 1.1 %shard_map.74.refs_4_.refs_6_ = f32[5,256,128]{2,1,0:T(8,128)S(1)} custom-call(bf16[1296,128]{1,0:T(8,128)(2,1)S(1)} %pad_maximum_fusion.1.rest_0_.mixed_ref.refs_0_, bf16[1296,128]{1,0:T(8,128)(2,1)S(1)} %collective-permute-done.2.refs_1_, bf16[1296,128]{1,0:T(8,128)(2,1)S(1)} %collective-permute-done.3.refs_2_, ...), custom_call_target="tpu_custom_call" | custom-call | flops 4000000000 | bytes 3000000 | tf_op jit(solution)/shard_map/pallas_call | solution.py:364
  43.1 3.0 %collective-permute-done.9.refs_3_ = bf16[784,128]{1,0:T(8,128)(2,1)S(1)} collective-permute-done((bf16[784,128]{1,0:T(8,128)(2,1)S(1)}, bf16[784,128]{1,0:T(8,128)(2,1)S(1)}, u32[]{:S(2)}, u32[]{:S(2)}) %collective-permute-start.9) | collective-permute-done | bytes 200736 | tf_op jit(solution)/shard_map/ppermute | solution.py:33
  46.9 3.4 %collective-permute-start.10 = (bf16[3,256,128]{2,1,0:T(8,128)(2,1)S(1)}, bf16[3,256,128]{2,1,0:T(8,128)(2,1)S(1)}, u32[]{:S(2)}, u32[]{:S(2)}) collective-permute-start(bf16[3,256,128]{2,1,0:T(8,128)(2,1)S(1)} %shard_map.76.refs_7_), channel_id=1, source_target_pairs={{0,2},{1,3},{2,0},{3,1},{4,6},{5,7},{6,4},{7,5},{8,10},{9,11},{10,... | collective-permute-start | bytes 589832 | tf_op jit(solution)/shard_map/ppermute | solution.py:33
  51.0 3.8 %collective-permute-done.7 = bf16[5,256,128]{2,1,0:T(8,128)(2,1)S(1)} collective-permute-done((bf16[5,256,128]{2,1,0:T(8,128)(2,1)S(1)}, bf16[5,256,128]{2,1,0:T(8,128)(2,1)S(1)}, u32[]{:S(2)}, u32[]{:S(2)}) %collective-permute-start.7) | collective-permute-done | bytes 327712 | tf_op jit(solution)/shard_map/ppermute | solution.py:33
  54.9 2.9 %collective-permute-done.10 = bf16[3,256,128]{2,1,0:T(8,128)(2,1)S(1)} collective-permute-done((bf16[3,256,128]{2,1,0:T(8,128)(2,1)S(1)}, bf16[3,256,128]{2,1,0:T(8,128)(2,1)S(1)}, u32[]{:S(2)}, u32[]{:S(2)}) %collective-permute-start.10) | collective-permute-done | bytes 196640 | tf_op jit(solution)/shard_map/ppermute | solution.py:33
  57.9 1.0 %pad_maximum_fusion = f32[8,256,128]{2,1,0:T(8,128)} fusion(f32[3,256,128]{2,1,0:T(8,128)S(1)} %convert_add_fusion.1, f32[5,256,128]{2,1,0:T(8,128)S(1)} %convert_add_fusion), kind=kLoop, calls=%fused_computation | loop fusion | flops 262144 | bytes 2097152 | tf_op jit(solution)/shard_map/concatenate | solution.py:424
  (31 shorter events, 5.4 us)
Async XLA Ops:
  0.0 2.2 %collective-permute-start = (bf16[8,256,128]{2,1,0:T(8,128)(2,1)}, bf16[8,256,128]{2,1,0:T(8,128)(2,1)S(1)}, u32[]{:S(2)}, u32[]{:S(2)}) collective-permute-start(bf16[8,256,128]{2,1,0:T(8,128)(2,1)} %bitcast.5), channel_id=1, source_target_pairs={{0,8},{8,0},{16,24},{24,16},{1,9},{9,1},{17,25},{25,17},{2,10},{10... | collective-permute-start | bytes 1572872 | tf_op jit(solution)/shard_map/ppermute | solution.py:33
  2.2 1.0 %copy-start = (bf16[8,16,16,128]{3,2,1,0:T(8,128)(2,1)S(1)}, bf16[8,16,16,128]{3,2,1,0:T(8,128)(2,1)}, u32[]{:S(2)}) copy-start(bf16[8,16,16,128]{3,2,1,0:T(8,128)(2,1)} %param.6) | copy-start | bytes 1572868
  3.2 0.7 %copy-start.2 = (s32[8]{0:T(128)S(1)}, s32[8]{0:T(128)}, u32[]{:S(2)}) copy-start(s32[8]{0:T(128)} %shift_ref.7) | copy-start | bytes 100
  5.4 6.0 %copy-start.3 = (bf16[16,16,16]{2,1,0:T(8,128)(2,1)S(1)}, bf16[16,16,16]{2,1,0:T(8,128)(2,1)}, u32[]{:S(2)}) copy-start(bf16[16,16,16]{2,1,0:T(8,128)(2,1)} %derivative_ref.1) | copy-start | bytes 24580
  5.5 5.9 %copy-start.4 = (s32[128,16]{0,1:T(8,128)S(1)}, s32[128,16]{0,1:T(8,128)}, u32[]{:S(2)}) copy-start(s32[128,16]{0,1:T(8,128)} %param.11) | copy-start | bytes 24580
  5.5 11.4 %collective-permute-start.1 = (bf16[5,256,128]{2,1,0:T(8,128)(2,1)S(1)}, bf16[5,256,128]{2,1,0:T(8,128)(2,1)S(1)}, u32[]{:S(2)}, u32[]{:S(2)}) collective-permute-start(bf16[5,256,128]{2,1,0:T(8,128)(2,1)S(1)} %shard_map.64.rest_0_), channel_id=1, source_target_pairs={{0,16},{8,24},{16,0},{24,8},{1,17},{9,25},{17,1},{25,9},{2,18},{10... | collective-permute-start | bytes 983048 | tf_op jit(solution)/shard_map/ppermute | solution.py:33
  11.3 10.7 %collective-permute-start.5 = (bf16[3,256,128]{2,1,0:T(8,128)(2,1)S(1)}, bf16[3,256,128]{2,1,0:T(8,128)(2,1)S(1)}, u32[]{:S(2)}, u32[]{:S(2)}) collective-permute-start(bf16[3,256,128]{2,1,0:T(8,128)(2,1)S(1)} %shard_map.66.after_ref), channel_id=1, source_target_pairs={{0,16},{8,24},{16,0},{24,8},{1,17},{9,25},{17,1},{25,9},{2,18},{10... | collective-permute-start | bytes 589832 | tf_op jit(solution)/shard_map/ppermute | solution.py:33
  14.8 6.0 %copy-start.1 = (bf16[8,16,16,128]{3,2,1,0:T(8,128)(2,1)S(1)}, bf16[8,16,16,128]{3,2,1,0:T(8,128)(2,1)}, u32[]{:S(2)}) copy-start(bf16[8,16,16,128]{3,2,1,0:T(8,128)(2,1)} %param.6) | copy-start | bytes 1572868
  17.0 15.2 %collective-permute-start.2 = (bf16[1296,128]{1,0:T(8,128)(2,1)S(1)}, bf16[1296,128]{1,0:T(8,128)(2,1)S(1)}, u32[]{:S(2)}, u32[]{:S(2)}) collective-permute-start(bf16[1296,128]{1,0:T(8,128)(2,1)S(1)} %pad_maximum_fusion.1.rest_0_.mixed_ref.refs_0_), channel_id=1, source_target_pairs={{0,2},{1,3},{2,0},{3,1},{4,6},{5,7},{6,4},{7,5},{8,10},{9,11},{10,... | collective-permute-start | bytes 995336 | tf_op jit(solution)/shard_map/ppermute | solution.py:33
  19.2 13.0 %collective-permute-start.3 = (bf16[1296,128]{1,0:T(8,128)(2,1)S(1)}, bf16[1296,128]{1,0:T(8,128)(2,1)S(1)}, u32[]{:S(2)}, u32[]{:S(2)}) collective-permute-start(bf16[1296,128]{1,0:T(8,128)(2,1)S(1)} %pad_maximum_fusion.1.rest_0_.mixed_ref.refs_0_), channel_id=1, source_target_pairs={{0,1},{1,0},{2,3},{3,2},{4,5},{5,4},{6,7},{7,6},{8,9},{9,8},{10,11... | collective-permute-start | bytes 995336 | tf_op jit(solution)/shard_map/ppermute | solution.py:33
  20.7 17.6 %collective-permute-start.4 = (bf16[1296,128]{1,0:T(8,128)(2,1)S(1)}, bf16[1296,128]{1,0:T(8,128)(2,1)S(1)}, u32[]{:S(2)}, u32[]{:S(2)}) collective-permute-start(bf16[1296,128]{1,0:T(8,128)(2,1)S(1)} %pad_maximum_fusion.1.rest_0_.mixed_ref.refs_0_), channel_id=1, source_target_pairs={{0,3},{1,2},{2,1},{3,0},{4,7},{5,6},{6,5},{7,4},{8,11},{9,10},{10,... | collective-permute-start | bytes 995336 | tf_op jit(solution)/shard_map/ppermute | solution.py:33
  22.1 18.2 %collective-permute-start.6 = (bf16[784,128]{1,0:T(8,128)(2,1)S(1)}, bf16[784,128]{1,0:T(8,128)(2,1)S(1)}, u32[]{:S(2)}, u32[]{:S(2)}) collective-permute-start(bf16[784,128]{1,0:T(8,128)(2,1)S(1)} %pad_maximum_fusion.2.rest_0_.mixed_ref.refs_0_), channel_id=1, source_target_pairs={{0,4},{1,5},{2,6},{3,7},{4,0},{5,1},{6,2},{7,3},{8,12},{9,13},{10,... | collective-permute-start | bytes 602120 | tf_op jit(solution)/shard_map/ppermute | solution.py:33
  25.2 17.9 %collective-permute-start.8 = (bf16[784,128]{1,0:T(8,128)(2,1)S(1)}, bf16[784,128]{1,0:T(8,128)(2,1)S(1)}, u32[]{:S(2)}, u32[]{:S(2)}) collective-permute-start(bf16[784,128]{1,0:T(8,128)(2,1)S(1)} %pad_maximum_fusion.2.rest_0_.mixed_ref.refs_0_), channel_id=1, source_target_pairs={{0,1},{1,0},{2,3},{3,2},{4,5},{5,4},{6,7},{7,6},{8,9},{9,8},{10,11... | collective-permute-start | bytes 602120 | tf_op jit(solution)/shard_map/ppermute | solution.py:33
  39.6 15.2 %collective-permute-start.7 = (bf16[5,256,128]{2,1,0:T(8,128)(2,1)S(1)}, bf16[5,256,128]{2,1,0:T(8,128)(2,1)S(1)}, u32[]{:S(2)}, u32[]{:S(2)}) collective-permute-start(bf16[5,256,128]{2,1,0:T(8,128)(2,1)S(1)} %shard_map.72.after_ref), channel_id=1, source_target_pairs={{0,4},{1,5},{2,6},{3,7},{4,0},{5,1},{6,2},{7,3},{8,12},{9,13},{10,... | collective-permute-start | bytes 983048 | tf_op jit(solution)/shard_map/ppermute | solution.py:33
  40.3 5.8 %collective-permute-start.9 = (bf16[784,128]{1,0:T(8,128)(2,1)S(1)}, bf16[784,128]{1,0:T(8,128)(2,1)S(1)}, u32[]{:S(2)}, u32[]{:S(2)}) collective-permute-start(bf16[784,128]{1,0:T(8,128)(2,1)S(1)} %shard_map.73.refs_7_), channel_id=1, source_target_pairs={{0,1},{1,0},{2,3},{3,2},{4,5},{5,4},{6,7},{7,6},{8,9},{9,8},{10,11... | collective-permute-start | bytes 602120 | tf_op jit(solution)/shard_map/ppermute | solution.py:33
  46.9 10.9 %collective-permute-start.10 = (bf16[3,256,128]{2,1,0:T(8,128)(2,1)S(1)}, bf16[3,256,128]{2,1,0:T(8,128)(2,1)S(1)}, u32[]{:S(2)}, u32[]{:S(2)}) collective-permute-start(bf16[3,256,128]{2,1,0:T(8,128)(2,1)S(1)} %shard_map.76.refs_7_), channel_id=1, source_target_pairs={{0,2},{1,3},{2,0},{3,1},{4,6},{5,7},{6,4},{7,5},{8,10},{9,11},{10,... | collective-permute-start | bytes 589832 | tf_op jit(solution)/shard_map/ppermute | solution.py:33

commit v8 on v7

--- a/solution.py
+++ b/solution.py
@@ -9,7 +9,7 @@
 
 REMOTE_BONDS = 2
 ID_ROWS = 16
-P_PART = 3
+P_PART = 4
 COST = 1.0
 SUBLANES = 8
 VMEM_LIMIT = 48 * 1024 * 1024
@@ -374,29 +374,35 @@
         return [swap(value, "atom", mask) for value, mask in zip(values, masks)]
 
     inner, outer = mixed
-    near = [inner] + send([inner] * 3, [2, 1, 3])
+    across, beside = send([inner] * 2, [2, 1])
     far = [outer] + send([outer] * len(high), high)
-    far_beside = send([outer], [1])
+    [turned] = ordered(across, [(0, sizes[0] * square)], outer)
+    near = [inner, across, beside] + send([turned], [1])
     local_inner = local_sum(0, [outer])
     local_outer = local_sum(1, [local_inner])
+    far_beside = send(ordered(outer, [(0, sizes[1] * square)], local_inner), [1])
     straight = [0] * len(near)
-    near_hots = one_hots(near, high, local_outer)
-    near_away = away_sums(sizes[0], near, straight, near_hots, high, local_outer)
+    counts = [sizes[1] - sizes[1] // 2, sizes[1] // 2]
+    skips = [0, counts[0]]
+    pieces = [(skip * square, (skip + count) * square) for skip, count in zip(skips, counts)]
+
+    def pass_far(after):
+        passed = [ordered(value, pieces, after) for value in far[1:]]
+        steps = [[value[index] for value in passed] for index in range(len(pieces))]
+        return passed[0][-1], [send(values, [1] * len(values)) for values in steps]
+
+    behind = local_outer
+    near_hots = one_hots(near, high, behind)
+    near_away = away_sums(sizes[0], near, straight, near_hots, high, behind)
     near_back = send(near_away, high)
-    counts, skips = [sizes[1]], [0]
-    pieces = [(skip * square, (skip + count) * square) for skip, count in zip(skips, counts)]
-    passed = [ordered(value, pieces, near_away[0]) for value in far[1:]]
-    far_next = [[value[index] for value in passed] for index in range(len(pieces))]
-    far_next = [send(values, [1] * len(values)) for values in far_next]
-    stay_inner = stay_sum(
-        sizes[0], 0, near, straight, near_hots, local_inner, passed[0][-1:]
-    )
+    behind, far_next = pass_far(near_away[0])
+    stay_inner = stay_sum(sizes[0], 0, near, straight, near_hots, local_inner, [behind])
     after = stay_inner
     far_hots = None
     far_away, far_lists = [], []
     for index, (first, _) in enumerate(pieces):
         sources = far + far_beside + far_next[index]
-        offsets = [first] * (len(far) + 1) + [0] * len(far_next[index])
+        offsets = [first] * len(far) + [first] + [0] * len(far_next[index])
         if far_hots is None:
             far_hots = one_hots(sources, [2], after)
         away = away_sums(counts[index], sources, offsets, far_hots, [2], after)
@@ -406,12 +412,7 @@
     results, arrivals = [stay_inner], [near_back]
     for index, (sources, offsets) in enumerate(far_lists):
         after = stay_sum(
-            counts[index],
-            skips[index],
-            sources,
-            offsets,
-            far_hots,
-            local_outer,
+            counts[index], skips[index], sources, offsets, far_hots, local_outer,
             [after],
         )
         results.append(after)

time: 59.1 us -> 53.3 us (0.902)
  waiting for transfers between devices: 19.7 us -> 9.9 us
  Pallas kernels: 17.7 us -> 19.7 us
  starting transfers between devices: 17.5 us -> 19.5 us
    ppermute x11 -> x13, waiting for transfers between devices: 19.7 us -> 9.9 us  [swap(): return lax.ppermute(value, axis, [(i, i ^ mask) for i in range(count)])]
    ppermute x11 -> x13, starting transfers between devices: 17.5 us -> 19.5 us  [swap(): return lax.ppermute(value, axis, [(i, i ^ mask) for i in range(count)])]
    pallas_call x2, Pallas kernels: 4.75 us -> 5.59 us  [local_sum(): pl.pallas_call(local_kernel, out_shape=jax.ShapeDtypeStruct((sizes[chunk]...]
    pallas_call x2 -> x3, Pallas kernels: 1.8 us -> 2.32 us  [away_sums(): pl.pallas_call(functools.partial(away_kernel, offsets), out_shape=(block,...]
    pallas_call x2 -> x3, Pallas kernels: 1.81 us -> 2.31 us  [stay_sum(): pl.pallas_call(functools.partial(stay_kernel, offsets, skip), out_shape=j...]
    unnamed x10 -> x12, local copies, waits for them, and re-layouts: 1.71 us -> 1.72 us
  transfers between devices with their start and end apart: 11 -> 13, of which waited for: 7 -> 7; matrix products, arithmetic and copies ran while one was open for 2% -> 2% of each run, Pallas kernels for 27% -> 34%
where the time goes in v8:
time: 53.3 us; the launch traced here: 53.1 us
  Pallas kernels  19.7 us (37%)
  starting transfers between devices  19.5 us (37%)
  waiting for transfers between devices  9.9 us (19%)
  other arithmetic  2.08 us (4%)
  local copies, waits for them, and re-layouts  1.72 us (3%)
    ppermute x13, starting transfers between devices, swap(): return lax.ppermute(value, axis, [(i, i ^ mask) for i in range(count)])  19.5 us
    ppermute x13, waiting for transfers between devices, swap(): return lax.ppermute(value, axis, [(i, i ^ mask) for i in range(count)])  9.9 us
    pallas_call x4, Pallas kernels, mix(): pl.pallas_call(functools.partial(mix_kernel, group, firsts[chunk]), out_s...  5.79 us
    pallas_call x2, Pallas kernels, local_sum(): pl.pallas_call(local_kernel, out_shape=jax.ShapeDtypeStruct((sizes[chunk]...  5.59 us
    pallas_call x1, Pallas kernels, prepare(): pl.pallas_call(prepare_kernel, out_shape=(jax.ShapeDtypeStruct((square, l...  3.35 us
    pallas_call x3, Pallas kernels, away_sums(): pl.pallas_call(functools.partial(away_kernel, offsets), out_shape=(block,...  2.32 us
    pallas_call x3, Pallas kernels, stay_sum(): pl.pallas_call(functools.partial(stay_kernel, offsets, skip), out_shape=j...  2.31 us
    unnamed x12, local copies, waits for them, and re-layouts  1.72 us
  transfers between devices with their start and end apart: 13, of which 7 were waited for; matrix products, arithmetic and copies ran while one was open for 2% of the time, Pallas kernels for 34%

profile of v8, /device:TPU:0, one launch (start us, length us, event | category | flops | bytes accessed | tf_op | source)
XLA Modules:
  0.0 53.1 jit_solution(16729980233032119390)
XLA Ops:
  2.2 1.0 %copy-done = bf16[8,16,16,128]{3,2,1,0:T(8,128)(2,1)S(1)} copy-done((bf16[8,16,16,128]{3,2,1,0:T(8,128)(2,1)S(1)}, bf16[8,16,16,128]{3,2,1,0:T(8,128)(2,1)}, u32[]{:S(2)}) %copy-start) | copy-done | bytes 524312
  3.9 1.4 %shard_map.64.rest_0_ = bf16[4,256,128]{2,1,0:T(8,128)(2,1)S(1)} custom-call(s32[8]{0:T(128)S(1)} %copy-done.2, bf16[16,128]{1,0:T(8,128)(2,1)S(1)} %pad_maximum_fusion.3.coupling_ref, bf16[8,256,128]{2,1,0:T(8,128)(2,1)S(1)} %bitcast.6, bf16[8,256,128]{2,1,0:T(8,128)(2,1)S(1)} %collective-permute-done.mate_ref), custom_call_target="tpu_custom_call" | custom-call | flops 500000000 | bytes 1000000 | tf_op jit(solution)/shard_map/pallas_call | solution.py:270
  5.3 2.9 %collective-permute-start.1 = (bf16[4,256,128]{2,1,0:T(8,128)(2,1)S(1)}, bf16[4,256,128]{2,1,0:T(8,128)(2,1)S(1)}, u32[]{:S(2)}, u32[]{:S(2)}) collective-permute-start(bf16[4,256,128]{2,1,0:T(8,128)(2,1)S(1)} %shard_map.64.rest_0_), channel_id=1, source_target_pairs={{0,16},{8,24},{16,0},{24,8},{1,17},{9,25},{17,1},{25,9},{2,18},{10... | collective-permute-start | bytes 786440 | tf_op jit(solution)/shard_map/ppermute | solution.py:33
  8.2 1.5 %shard_map.65.rest_0_ = f32[4,256,128]{2,1,0:T(8,128)S(1)} custom-call(s32[8]{0:T(128)S(1)} %copy-done.2, bf16[16,128]{1,0:T(8,128)(2,1)S(1)} %pad_maximum_fusion.3.coupling_ref, bf16[8,256,128]{2,1,0:T(8,128)(2,1)S(1)} %bitcast.7, bf16[8,256,128]{2,1,0:T(8,128)(2,1)S(1)} %collective-permute-done.mate_ref, bf16[4,256,128]{2,1,0:T(8,128)(2,1)S(1)} %shard_map.64.rest_0_), custom_call_target="tpu_custom_call" | custom-call | flops 500000000 | bytes 1000000 | tf_op jit(solution)/shard_map/pallas_call | solution.py:270
  9.7 1.4 %shard_map.66.after_ref = bf16[4,256,128]{2,1,0:T(8,128)(2,1)S(1)} custom-call(s32[8]{0:T(128)S(1)} %copy-done.2, bf16[16,128]{1,0:T(8,128)(2,1)S(1)} %pad_maximum_fusion.3.coupling_ref, bf16[8,256,128]{2,1,0:T(8,128)(2,1)S(1)} %bitcast.8, bf16[8,256,128]{2,1,0:T(8,128)(2,1)S(1)} %collective-permute-done.mate_ref, f32[4,256,128]{2,1,0:T(8,128)S(1)} %shard_map.65.rest_0_), custom_call_target="tpu_custom_call" | custom-call | flops 500000000 | bytes 1000000 | tf_op jit(solution)/shard_map/pallas_call | solution.py:270
  11.2 3.4 %shard_map.67 = (bf16[256,3584]{1,0:T(8,128)(2,1)S(1)}, bf16[256,512]{1,0:T(8,128)(2,1)S(1)}, bf16[1792,128]{1,0:T(8,128)(2,1)S(1)}, bf16[16,128]{1,0:T(8,128)(2,1)S(1)}) custom-call(bf16[16,16,16]{2,1,0:T(8,128)(2,1)S(1)} %copy-done.4, s32[16,128]{1,0:T(8,128)S(1)} %bitcast.10, bf16[4,256,128]{2,1,0:T(8,128)(2,1)S(1)} %shard_map.66.after_ref), custom_call_target="tpu_custom_call" | custom-call | flops 2000000000 | bytes 3000000 | tf_op jit(solution)/shard_map/pallas_call | solution.py:281
  15.4 2.2 %collective-permute-start.2 = (bf16[1040,128]{1,0:T(8,128)(2,1)S(1)}, bf16[1040,128]{1,0:T(8,128)(2,1)S(1)}, u32[]{:S(2)}, u32[]{:S(2)}) collective-permute-start(bf16[1040,128]{1,0:T(8,128)(2,1)S(1)} %pad_maximum_fusion.2.rest_0_.mixed_ref.refs_0_), channel_id=1, source_target_pairs={{0,2},{1,3},{2,0},{3,1},{4,6},{5,7},{6,4},{7,5},{8,10},{9,11},{10,... | collective-permute-start | bytes 798728 | tf_op jit(solution)/shard_map/ppermute | solution.py:33
  17.6 1.5 %collective-permute-start.3 = (bf16[1040,128]{1,0:T(8,128)(2,1)S(1)}, bf16[1040,128]{1,0:T(8,128)(2,1)S(1)}, u32[]{:S(2)}, u32[]{:S(2)}) collective-permute-start(bf16[1040,128]{1,0:T(8,128)(2,1)S(1)} %pad_maximum_fusion.2.rest_0_.mixed_ref.refs_0_), channel_id=1, source_target_pairs={{0,1},{1,0},{2,3},{3,2},{4,5},{5,4},{6,7},{7,6},{8,9},{9,8},{10,11... | collective-permute-start | bytes 798728 | tf_op jit(solution)/shard_map/ppermute | solution.py:33
  19.2 1.5 %shard_map.68 = f32[4,256,128]{2,1,0:T(8,128)S(1)} custom-call(s32[8]{0:T(128)S(1)} %copy-done.3, bf16[16,128]{1,0:T(8,128)(2,1)S(1)} %pad_maximum_fusion.3.coupling_ref, bf16[8,256,128]{2,1,0:T(8,128)(2,1)S(1)} %bitcast.9, bf16[8,256,128]{2,1,0:T(8,128)(2,1)S(1)} %collective-permute-done.mate_ref, ...), custom_call_target="tpu_custom_call" | custom-call | flops 500000000 | bytes 1000000 | tf_op jit(solution)/shard_map/pallas_call | solution.py:270
  20.8 2.7 %collective-permute-start.6 = (bf16[1040,128]{1,0:T(8,128)(2,1)S(1)}, bf16[1040,128]{1,0:T(8,128)(2,1)S(1)}, u32[]{:S(2)}, u32[]{:S(2)}) collective-permute-start(bf16[1040,128]{1,0:T(8,128)(2,1)S(1)} %pad_maximum_fusion.1.after_ref.rest_0_.mixed_ref.value_ref.refs_0_), channel_id=1, source_target_pairs={{0,4},{1,5},{2,6},{3,7},{4,0},{5,1},{6,2},{7,3},{8,12},{9,13},{10,... | collective-permute-start | bytes 798728 | tf_op jit(solution)/shard_map/ppermute | solution.py:33
  23.5 1.6 %collective-permute-start.5 = (bf16[1040,128]{1,0:T(8,128)(2,1)S(1)}, bf16[1040,128]{1,0:T(8,128)(2,1)S(1)}, u32[]{:S(2)}, u32[]{:S(2)}) collective-permute-start(bf16[1040,128]{1,0:T(8,128)(2,1)S(1)} %shard_map.69), channel_id=1, source_target_pairs={{0,1},{1,0},{2,3},{3,2},{4,5},{5,4},{6,7},{7,6},{8,9},{9,8},{10,11... | collective-permute-start | bytes 798728 | tf_op jit(solution)/shard_map/ppermute | solution.py:33
  25.1 2.8 %shard_map.70.rest_0_.refs_6_.after_ref = f32[4,256,128]{2,1,0:T(8,128)S(1)} custom-call(bf16[1040,128]{1,0:T(8,128)(2,1)S(1)} %pad_maximum_fusion.2.rest_0_.mixed_ref.refs_0_, bf16[1792,128]{1,0:T(8,128)(2,1)S(1)} %get-tuple-element.12.rest_1_.hot_ref, bf16[256,3584]{1,0:T(8,128)(2,1)S(1)} %get-tuple-element.13.k_ref, ...), custom_call_target="tpu_custom_call" | custom-call | flops 2000000000 | bytes 3000000 | tf_op jit(solution)/shard_map/pallas_call | solution.py:296
  28.5 2.8 %shard_map.71.refs_4_.refs_6_ = f32[4,256,128]{2,1,0:T(8,128)S(1)} custom-call(bf16[1040,128]{1,0:T(8,128)(2,1)S(1)} %pad_maximum_fusion.1.after_ref.rest_0_.mixed_ref.value_ref.refs_0_, bf16[1792,128]{1,0:T(8,128)(2,1)S(1)} %get-tuple-element.12.rest_1_.hot_ref, bf16[256,3584]{1,0:T(8,128)(2,1)S(1)} %get-tuple-element.13.k_ref, ...), custom_call_target="tpu_custom_call" | custom-call | flops 2000000000 | bytes 3000000 | tf_op jit(solution)/shard_map/pallas_call | solution.py:296
  31.3 1.1 %collective-permute-done.5.refs_3_ = bf16[1040,128]{1,0:T(8,128)(2,1)S(1)} collective-permute-done((bf16[1040,128]{1,0:T(8,128)(2,1)S(1)}, bf16[1040,128]{1,0:T(8,128)(2,1)S(1)}, u32[]{:S(2)}, u32[]{:S(2)}) %collective-permute-start.5) | collective-permute-done | bytes 266272 | tf_op jit(solution)/shard_map/ppermute | solution.py:33
  32.5 1.0 %shard_map.73.after_ref = bf16[4,256,128]{2,1,0:T(8,128)(2,1)S(1)} custom-call(bf16[1040,128]{1,0:T(8,128)(2,1)S(1)} %pad_maximum_fusion.2.rest_0_.mixed_ref.refs_0_, bf16[1040,128]{1,0:T(8,128)(2,1)S(1)} %collective-permute-done.2.value_ref.refs_1_, bf16[1040,128]{1,0:T(8,128)(2,1)S(1)} %collective-permute-done.3.refs_2_, ...), custom_call_target="tpu_custom_call" | custom-call | flops 1000000000 | bytes 3000000 | tf_op jit(solution)/shard_map/pallas_call | solution.py:354
  33.5 2.8 %collective-permute-start.7 = (bf16[4,256,128]{2,1,0:T(8,128)(2,1)S(1)}, bf16[4,256,128]{2,1,0:T(8,128)(2,1)S(1)}, u32[]{:S(2)}, u32[]{:S(2)}) collective-permute-start(bf16[4,256,128]{2,1,0:T(8,128)(2,1)S(1)} %shard_map.73.after_ref), channel_id=1, source_target_pairs={{0,4},{1,5},{2,6},{3,7},{4,0},{5,1},{6,2},{7,3},{8,12},{9,13},{10,... | collective-permute-start | bytes 786440 | tf_op jit(solution)/shard_map/ppermute | solution.py:33
  36.3 2.3 %collective-permute-done.6.value_ref.refs_1_ = bf16[1040,128]{1,0:T(8,128)(2,1)S(1)} collective-permute-done((bf16[1040,128]{1,0:T(8,128)(2,1)S(1)}, bf16[1040,128]{1,0:T(8,128)(2,1)S(1)}, u32[]{:S(2)}, u32[]{:S(2)}) %collective-permute-start.6) | collective-permute-done | bytes 266272 | tf_op jit(solution)/shard_map/ppermute | solution.py:33
  38.6 1.4 %collective-permute-start.9 = (bf16[528,128]{1,0:T(8,128)(2,1)S(1)}, bf16[528,128]{1,0:T(8,128)(2,1)S(1)}, u32[]{:S(2)}, u32[]{:S(2)}) collective-permute-start(bf16[528,128]{1,0:T(8,128)(2,1)S(1)} %get-tuple-element.16), channel_id=1, source_target_pairs={{0,1},{1,0},{2,3},{3,2},{4,5},{5,4},{6,7},{7,6},{8,9},{9,8},{10,11... | collective-permute-start | bytes 405512 | tf_op jit(solution)/shard_map/ppermute | solution.py:33
  40.7 1.0 %shard_map.75.refs_4_.refs_6_ = f32[4,256,128]{2,1,0:T(8,128)S(1)} custom-call(bf16[1040,128]{1,0:T(8,128)(2,1)S(1)} %pad_maximum_fusion.2.rest_0_.mixed_ref.refs_0_, bf16[1040,128]{1,0:T(8,128)(2,1)S(1)} %collective-permute-done.2.value_ref.refs_1_, bf16[1040,128]{1,0:T(8,128)(2,1)S(1)} %collective-permute-done.3.refs_2_, ...), custom_call_target="tpu_custom_call" | custom-call | flops 4000000000 | bytes 3000000 | tf_op jit(solution)/shard_map/pallas_call | solution.py:364
  41.7 2.0 %collective-permute-done.9.refs_3_ = bf16[528,128]{1,0:T(8,128)(2,1)S(1)} collective-permute-done((bf16[528,128]{1,0:T(8,128)(2,1)S(1)}, bf16[528,128]{1,0:T(8,128)(2,1)S(1)}, u32[]{:S(2)}, u32[]{:S(2)}) %collective-permute-start.9) | collective-permute-done | bytes 135200 | tf_op jit(solution)/shard_map/ppermute | solution.py:33
  44.5 1.6 %collective-permute-start.11 = (bf16[2,256,128]{2,1,0:T(8,128)(2,1)S(1)}, bf16[2,256,128]{2,1,0:T(8,128)(2,1)S(1)}, u32[]{:S(2)}, u32[]{:S(2)}) collective-permute-start(bf16[2,256,128]{2,1,0:T(8,128)(2,1)S(1)} %shard_map.78.refs_6_), channel_id=1, source_target_pairs={{0,2},{1,3},{2,0},{3,1},{4,6},{5,7},{6,4},{7,5},{8,10},{9,11},{10,... | collective-permute-start | bytes 393224 | tf_op jit(solution)/shard_map/ppermute | solution.py:33
  49.1 1.5 %collective-permute-done.11 = bf16[2,256,128]{2,1,0:T(8,128)(2,1)S(1)} collective-permute-done((bf16[2,256,128]{2,1,0:T(8,128)(2,1)S(1)}, bf16[2,256,128]{2,1,0:T(8,128)(2,1)S(1)}, u32[]{:S(2)}, u32[]{:S(2)}) %collective-permute-start.11) | collective-permute-done | bytes 131104 | tf_op jit(solution)/shard_map/ppermute | solution.py:33
  50.6 1.4 %collective-permute-done.12 = bf16[2,256,128]{2,1,0:T(8,128)(2,1)S(1)} collective-permute-done((bf16[2,256,128]{2,1,0:T(8,128)(2,1)S(1)}, bf16[2,256,128]{2,1,0:T(8,128)(2,1)S(1)}, u32[]{:S(2)}, u32[]{:S(2)}) %collective-permute-start.12) | collective-permute-done | bytes 131104 | tf_op jit(solution)/shard_map/ppermute | solution.py:33
  52.0 1.0 %pad_maximum_fusion = f32[8,256,128]{2,1,0:T(8,128)} fusion(f32[2,256,128]{2,1,0:T(8,128)S(1)} %convert_add_fusion.1, f32[2,256,128]{2,1,0:T(8,128)S(1)} %convert_add_fusion.2, f32[4,256,128]{2,1,0:T(8,128)S(1)} %convert_add_fusion), kind=kLoop, calls=%fused_computation | loop fusion | flops 524288 | bytes 2097152 | tf_op jit(solution)/shard_map/concatenate | solution.py:425
  (42 shorter events, 9.1 us)
Async XLA Ops:
  0.0 2.2 %collective-permute-start = (bf16[8,256,128]{2,1,0:T(8,128)(2,1)}, bf16[8,256,128]{2,1,0:T(8,128)(2,1)S(1)}, u32[]{:S(2)}, u32[]{:S(2)}) collective-permute-start(bf16[8,256,128]{2,1,0:T(8,128)(2,1)} %bitcast.5), channel_id=1, source_target_pairs={{0,8},{8,0},{16,24},{24,16},{1,9},{9,1},{17,25},{25,17},{2,10},{10... | collective-permute-start | bytes 1572872 | tf_op jit(solution)/shard_map/ppermute | solution.py:33
  2.2 1.0 %copy-start = (bf16[8,16,16,128]{3,2,1,0:T(8,128)(2,1)S(1)}, bf16[8,16,16,128]{3,2,1,0:T(8,128)(2,1)}, u32[]{:S(2)}) copy-start(bf16[8,16,16,128]{3,2,1,0:T(8,128)(2,1)} %param.6) | copy-start | bytes 1572868
  3.2 0.7 %copy-start.2 = (s32[8]{0:T(128)S(1)}, s32[8]{0:T(128)}, u32[]{:S(2)}) copy-start(s32[8]{0:T(128)} %shift_ref.7) | copy-start | bytes 100
  5.3 5.9 %copy-start.4 = (bf16[16,16,16]{2,1,0:T(8,128)(2,1)S(1)}, bf16[16,16,16]{2,1,0:T(8,128)(2,1)}, u32[]{:S(2)}) copy-start(bf16[16,16,16]{2,1,0:T(8,128)(2,1)} %derivative_ref.1) | copy-start | bytes 24580
  5.3 5.9 %copy-start.5 = (s32[128,16]{0,1:T(8,128)S(1)}, s32[128,16]{0,1:T(8,128)}, u32[]{:S(2)}) copy-start(s32[128,16]{0,1:T(8,128)} %param.11) | copy-start | bytes 24580
  5.3 10.0 %collective-permute-start.1 = (bf16[4,256,128]{2,1,0:T(8,128)(2,1)S(1)}, bf16[4,256,128]{2,1,0:T(8,128)(2,1)S(1)}, u32[]{:S(2)}, u32[]{:S(2)}) collective-permute-start(bf16[4,256,128]{2,1,0:T(8,128)(2,1)S(1)} %shard_map.64.rest_0_), channel_id=1, source_target_pairs={{0,16},{8,24},{16,0},{24,8},{1,17},{9,25},{17,1},{25,9},{2,18},{10... | collective-permute-start | bytes 786440 | tf_op jit(solution)/shard_map/ppermute | solution.py:33
  11.1 9.5 %collective-permute-start.4 = (bf16[4,256,128]{2,1,0:T(8,128)(2,1)S(1)}, bf16[4,256,128]{2,1,0:T(8,128)(2,1)S(1)}, u32[]{:S(2)}, u32[]{:S(2)}) collective-permute-start(bf16[4,256,128]{2,1,0:T(8,128)(2,1)S(1)} %shard_map.66.after_ref), channel_id=1, source_target_pairs={{0,16},{8,24},{16,0},{24,8},{1,17},{9,25},{17,1},{25,9},{2,18},{10... | collective-permute-start | bytes 786440 | tf_op jit(solution)/shard_map/ppermute | solution.py:33
  11.2 7.9 %copy-start.3 = (s32[8]{0:T(128)S(1)}, s32[8]{0:T(128)}, u32[]{:S(2)}) copy-start(s32[8]{0:T(128)} %shift_ref.7) | copy-start | bytes 100
  14.6 4.6 %copy-start.1 = (bf16[8,16,16,128]{3,2,1,0:T(8,128)(2,1)S(1)}, bf16[8,16,16,128]{3,2,1,0:T(8,128)(2,1)}, u32[]{:S(2)}) copy-start(bf16[8,16,16,128]{3,2,1,0:T(8,128)(2,1)} %param.6) | copy-start | bytes 1572868
  15.4 8.0 %collective-permute-start.2 = (bf16[1040,128]{1,0:T(8,128)(2,1)S(1)}, bf16[1040,128]{1,0:T(8,128)(2,1)S(1)}, u32[]{:S(2)}, u32[]{:S(2)}) collective-permute-start(bf16[1040,128]{1,0:T(8,128)(2,1)S(1)} %pad_maximum_fusion.2.rest_0_.mixed_ref.refs_0_), channel_id=1, source_target_pairs={{0,2},{1,3},{2,0},{3,1},{4,6},{5,7},{6,4},{7,5},{8,10},{9,11},{10,... | collective-permute-start | bytes 798728 | tf_op jit(solution)/shard_map/ppermute | solution.py:33
  17.6 13.6 %collective-permute-start.3 = (bf16[1040,128]{1,0:T(8,128)(2,1)S(1)}, bf16[1040,128]{1,0:T(8,128)(2,1)S(1)}, u32[]{:S(2)}, u32[]{:S(2)}) collective-permute-start(bf16[1040,128]{1,0:T(8,128)(2,1)S(1)} %pad_maximum_fusion.2.rest_0_.mixed_ref.refs_0_), channel_id=1, source_target_pairs={{0,1},{1,0},{2,3},{3,2},{4,5},{5,4},{6,7},{7,6},{8,9},{9,8},{10,11... | collective-permute-start | bytes 798728 | tf_op jit(solution)/shard_map/ppermute | solution.py:33
  20.8 17.8 %collective-permute-start.6 = (bf16[1040,128]{1,0:T(8,128)(2,1)S(1)}, bf16[1040,128]{1,0:T(8,128)(2,1)S(1)}, u32[]{:S(2)}, u32[]{:S(2)}) collective-permute-start(bf16[1040,128]{1,0:T(8,128)(2,1)S(1)} %pad_maximum_fusion.1.after_ref.rest_0_.mixed_ref.value_ref.refs_0_), channel_id=1, source_target_pairs={{0,4},{1,5},{2,6},{3,7},{4,0},{5,1},{6,2},{7,3},{8,12},{9,13},{10,... | collective-permute-start | bytes 798728 | tf_op jit(solution)/shard_map/ppermute | solution.py:33
  23.5 8.9 %collective-permute-start.5 = (bf16[1040,128]{1,0:T(8,128)(2,1)S(1)}, bf16[1040,128]{1,0:T(8,128)(2,1)S(1)}, u32[]{:S(2)}, u32[]{:S(2)}) collective-permute-start(bf16[1040,128]{1,0:T(8,128)(2,1)S(1)} %shard_map.69), channel_id=1, source_target_pairs={{0,1},{1,0},{2,3},{3,2},{4,5},{5,4},{6,7},{7,6},{8,9},{9,8},{10,11... | collective-permute-start | bytes 798728 | tf_op jit(solution)/shard_map/ppermute | solution.py:33
  27.9 13.8 %collective-permute-start.8 = (bf16[1040,128]{1,0:T(8,128)(2,1)S(1)}, bf16[1040,128]{1,0:T(8,128)(2,1)S(1)}, u32[]{:S(2)}, u32[]{:S(2)}) collective-permute-start(bf16[1040,128]{1,0:T(8,128)(2,1)S(1)} %shard_map.76), channel_id=1, source_target_pairs={{0,1},{1,0},{2,3},{3,2},{4,5},{5,4},{6,7},{7,6},{8,9},{9,8},{10,11... | collective-permute-start | bytes 798728 | tf_op jit(solution)/shard_map/ppermute | solution.py:33
  33.5 15.5 %collective-permute-start.7 = (bf16[4,256,128]{2,1,0:T(8,128)(2,1)S(1)}, bf16[4,256,128]{2,1,0:T(8,128)(2,1)S(1)}, u32[]{:S(2)}, u32[]{:S(2)}) collective-permute-start(bf16[4,256,128]{2,1,0:T(8,128)(2,1)S(1)} %shard_map.73.after_ref), channel_id=1, source_target_pairs={{0,4},{1,5},{2,6},{3,7},{4,0},{5,1},{6,2},{7,3},{8,12},{9,13},{10,... | collective-permute-start | bytes 786440 | tf_op jit(solution)/shard_map/ppermute | solution.py:33
  38.6 5.1 %collective-permute-start.9 = (bf16[528,128]{1,0:T(8,128)(2,1)S(1)}, bf16[528,128]{1,0:T(8,128)(2,1)S(1)}, u32[]{:S(2)}, u32[]{:S(2)}) collective-permute-start(bf16[528,128]{1,0:T(8,128)(2,1)S(1)} %get-tuple-element.16), channel_id=1, source_target_pairs={{0,1},{1,0},{2,3},{3,2},{4,5},{5,4},{6,7},{7,6},{8,9},{9,8},{10,11... | collective-permute-start | bytes 405512 | tf_op jit(solution)/shard_map/ppermute | solution.py:33
  40.0 6.0 %collective-permute-start.10 = (bf16[512,128]{1,0:T(8,128)(2,1)S(1)}, bf16[512,128]{1,0:T(8,128)(2,1)S(1)}, u32[]{:S(2)}, u32[]{:S(2)}) collective-permute-start(bf16[512,128]{1,0:T(8,128)(2,1)S(1)} %get-tuple-element.15.refs_7_), channel_id=1, source_target_pairs={{0,1},{1,0},{2,3},{3,2},{4,5},{5,4},{6,7},{7,6},{8,9},{9,8},{10,11... | collective-permute-start | bytes 393224 | tf_op jit(solution)/shard_map/ppermute | solution.py:33
  44.5 6.1 %collective-permute-start.11 = (bf16[2,256,128]{2,1,0:T(8,128)(2,1)S(1)}, bf16[2,256,128]{2,1,0:T(8,128)(2,1)S(1)}, u32[]{:S(2)}, u32[]{:S(2)}) collective-permute-start(bf16[2,256,128]{2,1,0:T(8,128)(2,1)S(1)} %shard_map.78.refs_6_), channel_id=1, source_target_pairs={{0,2},{1,3},{2,0},{3,1},{4,6},{5,7},{6,4},{7,5},{8,10},{9,11},{10,... | collective-permute-start | bytes 393224 | tf_op jit(solution)/shard_map/ppermute | solution.py:33
  46.7 5.3 %collective-permute-start.12 = (bf16[2,256,128]{2,1,0:T(8,128)(2,1)S(1)}, bf16[2,256,128]{2,1,0:T(8,128)(2,1)S(1)}, u32[]{:S(2)}, u32[]{:S(2)}) collective-permute-start(bf16[2,256,128]{2,1,0:T(8,128)(2,1)S(1)} %shard_map.79.refs_7_), channel_id=1, source_target_pairs={{0,2},{1,3},{2,0},{3,1},{4,6},{5,7},{6,4},{7,5},{8,10},{9,11},{10,... | collective-permute-start | bytes 393224 | tf_op jit(solution)/shard_map/ppermute | solution.py:33

commit v9 on v8

--- a/solution.py
+++ b/solution.py
@@ -15,7 +15,6 @@
 VMEM_LIMIT = 48 * 1024 * 1024
 
 VMEM = pl.BlockSpec(memory_space=pltpu.VMEM)
-SMEM = pl.BlockSpec(memory_space=pltpu.SMEM)
 ANY = pl.BlockSpec(memory_space=pl.ANY)
 F32, BF16 = jnp.float32, jnp.bfloat16
 
@@ -41,8 +40,10 @@
     return lax.dot_general(left, right, (((1,), (1,)), ((), ())), preferred_element_type=F32)
 
 
-def mix_kernel(group, first, shift_ref, coupling_ref, own_ref, mate_ref, *rest):
-    out_ref, table_ref = rest[-2:]
+def mix_kernel(group, first, shift_rows_ref, coupling_ref, own_ref, mate_ref, *rest):
+    out_ref, table_ref, shift_ref, sem = rest[-4:]
+    copy = pltpu.make_async_copy(shift_rows_ref, shift_ref, sem)
+    copy.start()
     span, square, atoms = own_ref.shape
     rows = out_ref.shape[0]
     tile = table_ref.shape[2]
@@ -53,6 +54,7 @@
     target = me ^ (2 * group)
     table_ref[...] = jnp.zeros_like(table_ref)
     couplings = coupling_ref[...].astype(F32)
+    copy.wait()
 
     def put(row, source, value):
         place = source - base
@@ -61,7 +63,7 @@
         table_ref[row, jnp.where(inside, slot, 2 * span)] = value
 
     for mode in range(modes):
-        shift = shift_ref[mode]
+        shift = shift_ref[mode, 0]
         emission = jnp.broadcast_to(couplings[mode : mode + 1, :], (tile, atoms))
         absorption = jnp.broadcast_to(couplings[modes + mode : modes + mode + 1, :], (tile, atoms))
         if group > 0:
@@ -144,6 +146,10 @@
     for at, row in enumerate(rows):
         ids = jnp.where(place == at, row, ids)
     ids_ref[...] = ids.astype(F32).astype(BF16)
+
+
+def copy_kernel(value_ref, *rest):
+    rest[-1][...] = value_ref[...]
 
 
 def pass_kernel(pieces, value_ref, after_ref, *out_refs):
@@ -265,17 +271,30 @@
 
     absorption = phonon_weight * occupation[:, None]
     couplings = jnp.concatenate([absorption + phonon_weight, absorption], 0).astype(BF16)
+    shift_rows = jnp.broadcast_to(mode_shift[:, None], (modes, atoms))
+    green_near = pl.pallas_call(
+        copy_kernel,
+        out_shape=jax.ShapeDtypeStruct(green.shape, green.dtype),
+        in_specs=[VMEM],
+        out_specs=VMEM,
+        compiler_params=params(),
+        cost_estimate=cost(1e6, 1e6),
+    )(green)
 
     def mix(group, chunk, kind, after):
         return pl.pallas_call(
             functools.partial(mix_kernel, group, firsts[chunk]),
             out_shape=jax.ShapeDtypeStruct((sizes[chunk], square, atoms), kind),
-            in_specs=[SMEM, VMEM, VMEM, VMEM] + [ANY] * len(after),
+            in_specs=[VMEM] * 4 + [ANY] * len(after),
             out_specs=VMEM,
-            scratch_shapes=[pltpu.VMEM((sizes[chunk], 2 * rows + 1, SUBLANES, atoms), F32)],
+            scratch_shapes=[
+                pltpu.VMEM((sizes[chunk], 2 * rows + 1, SUBLANES, atoms), F32),
+                pltpu.SMEM((modes, atoms), jnp.int32),
+                pltpu.SemaphoreType.DMA,
+            ],
             compiler_params=params(),
             cost_estimate=cost(5e8, 1e6),
-        )(mode_shift, couplings, green, mate, *after)
+        )(shift_rows, couplings, green_near, mate, *after)
 
     def prepare(after):
         return pl.pallas_call(
@@ -394,8 +413,19 @@
     behind = local_outer
     near_hots = one_hots(near, high, behind)
     near_away = away_sums(sizes[0], near, straight, near_hots, high, behind)
-    near_back = send(near_away, high)
-    behind, far_next = pass_far(near_away[0])
+    held = [
+        pl.pallas_call(
+            copy_kernel,
+            out_shape=jax.ShapeDtypeStruct(value.shape, value.dtype),
+            in_specs=[VMEM, ANY],
+            out_specs=VMEM,
+            compiler_params=params(),
+            cost_estimate=cost(1e6, 1e6),
+        )(value, far[-1])
+        for value in near_away
+    ]
+    near_back = send(held, high)
+    behind, far_next = pass_far(held[0])
     stay_inner = stay_sum(sizes[0], 0, near, straight, near_hots, local_inner, [behind])
     after = stay_inner
     far_hots = None

time: 53.3 us -> 54.9 us (1.030)
  starting transfers between devices: 19.5 us -> 20.5 us
    ppermute x13, starting transfers between devices: 19.5 us -> 20.5 us  [swap(): return lax.ppermute(value, axis, [(i, i ^ mask) for i in range(count)])]
    broadcast_in_dim x0 -> x1, local copies, waits for them, and re-layouts: none -> 0.72 us  [per_device(): shift_rows = jnp.broadcast_to(mode_shift[:, None], (modes, atoms))]
    unnamed x12 -> x6, local copies, waits for them, and re-layouts: 1.72 us -> 1.05 us
  transfers between devices with their start and end apart: 13 -> 13, of which waited for: 7 -> 6; matrix products, arithmetic and copies ran while one was open for 2% -> 2% of each run, Pallas kernels for 34% -> 34%
where the time goes in v9:
time: 54.9 us; the launch traced here: 54.7 us
  starting transfers between devices  20.5 us (37%)
  Pallas kernels  19.9 us (36%)
  waiting for transfers between devices  10.2 us (19%)
  other arithmetic  2.12 us (4%)
  local copies, waits for them, and re-layouts  1.78 us (3%)
    ppermute x13, starting transfers between devices, swap(): return lax.ppermute(value, axis, [(i, i ^ mask) for i in range(count)])  20.5 us
    ppermute x13, waiting for transfers between devices, swap(): return lax.ppermute(value, axis, [(i, i ^ mask) for i in range(count)])  10.2 us
    pallas_call x4, Pallas kernels, mix(): pl.pallas_call(functools.partial(mix_kernel, group, firsts[chunk]), out_s...  6.01 us
    pallas_call x2, Pallas kernels, local_sum(): pl.pallas_call(local_kernel, out_shape=jax.ShapeDtypeStruct((sizes[chunk]...  5.56 us
    pallas_call x1, Pallas kernels, prepare(): pl.pallas_call(prepare_kernel, out_shape=(jax.ShapeDtypeStruct((square, l...  3.36 us
    pallas_call x3, Pallas kernels, away_sums(): pl.pallas_call(functools.partial(away_kernel, offsets), out_shape=(block,...  2.29 us
    pallas_call x3, Pallas kernels, stay_sum(): pl.pallas_call(functools.partial(stay_kernel, offsets, skip), out_shape=j...  2.28 us
  transfers between devices with their start and end apart: 13, of which 6 were waited for; matrix products, arithmetic and copies ran while one was open for 2% of the time, Pallas kernels for 34%

profile of v9, /device:TPU:0, one launch (start us, length us, event | category | flops | bytes accessed | tf_op | source)
XLA Modules:
  0.0 54.7 jit_solution(787505922241003023)
XLA Ops:
  0.5 1.0 %copy-done = bf16[8,16,16,128]{3,2,1,0:T(8,128)(2,1)S(1)} copy-done((bf16[8,16,16,128]{3,2,1,0:T(8,128)(2,1)S(1)}, bf16[8,16,16,128]{3,2,1,0:T(8,128)(2,1)}, u32[]{:S(2)}) %copy-start) | copy-done | bytes 524312
  3.0 1.4 %shard_map.65.rest_0_ = bf16[4,256,128]{2,1,0:T(8,128)(2,1)S(1)} custom-call(s32[8,128]{1,0:T(8,128)S(1)} %broadcast_in_dim.2.shift_rows_ref, bf16[16,128]{1,0:T(8,128)(2,1)S(1)} %pad_maximum_fusion.3.coupling_ref, bf16[8,256,128]{2,1,0:T(8,128)(2,1)S(1)} %shard_map.64.own_ref, bf16[8,256,128]{2,1,0:T(8,128)(2,1)S(1)} %collective-permute-done.mate_ref), custom_call_target="tpu_custom_call" | custom-call | flops 500000000 | bytes 1000000 | tf_op jit(solution)/shard_map/pallas_call | solution.py:285
  4.5 2.8 %collective-permute-start.1 = (bf16[4,256,128]{2,1,0:T(8,128)(2,1)S(1)}, bf16[4,256,128]{2,1,0:T(8,128)(2,1)S(1)}, u32[]{:S(2)}, u32[]{:S(2)}) collective-permute-start(bf16[4,256,128]{2,1,0:T(8,128)(2,1)S(1)} %shard_map.65.rest_0_), channel_id=1, source_target_pairs={{0,16},{8,24},{16,0},{24,8},{1,17},{9,25},{17,1},{25,9},{2,18},{10... | collective-permute-start | bytes 786440 | tf_op jit(solution)/shard_map/ppermute | solution.py:32
  7.3 1.6 %shard_map.66.rest_0_ = f32[4,256,128]{2,1,0:T(8,128)S(1)} custom-call(s32[8,128]{1,0:T(8,128)S(1)} %broadcast_in_dim.2.shift_rows_ref, bf16[16,128]{1,0:T(8,128)(2,1)S(1)} %pad_maximum_fusion.3.coupling_ref, bf16[8,256,128]{2,1,0:T(8,128)(2,1)S(1)} %shard_map.64.own_ref, bf16[8,256,128]{2,1,0:T(8,128)(2,1)S(1)} %collective-permute-done.mate_ref, ...), custom_call_target="tpu_custom_call" | custom-call | flops 500000000 | bytes 1000000 | tf_op jit(solution)/shard_map/pallas_call | solution.py:285
  8.9 1.4 %shard_map.67.after_ref = bf16[4,256,128]{2,1,0:T(8,128)(2,1)S(1)} custom-call(s32[8,128]{1,0:T(8,128)S(1)} %broadcast_in_dim.2.shift_rows_ref, bf16[16,128]{1,0:T(8,128)(2,1)S(1)} %pad_maximum_fusion.3.coupling_ref, bf16[8,256,128]{2,1,0:T(8,128)(2,1)S(1)} %shard_map.64.own_ref, bf16[8,256,128]{2,1,0:T(8,128)(2,1)S(1)} %collective-permute-done.mate_ref, ...), custom_call_target="tpu_custom_call" | custom-call | flops 500000000 | bytes 1000000 | tf_op jit(solution)/shard_map/pallas_call | solution.py:285
  10.4 3.4 %shard_map.68 = (bf16[256,3584]{1,0:T(8,128)(2,1)S(1)}, bf16[256,512]{1,0:T(8,128)(2,1)S(1)}, bf16[1792,128]{1,0:T(8,128)(2,1)S(1)}, bf16[16,128]{1,0:T(8,128)(2,1)S(1)}) custom-call(bf16[16,16,16]{2,1,0:T(8,128)(2,1)S(1)} %copy-done.1, s32[16,128]{1,0:T(8,128)S(1)} %bitcast.7, bf16[4,256,128]{2,1,0:T(8,128)(2,1)S(1)} %shard_map.67.after_ref), custom_call_target="tpu_custom_call" | custom-call | flops 2000000000 | bytes 3000000 | tf_op jit(solution)/shard_map/pallas_call | solution.py:300
  14.5 2.2 %collective-permute-start.2 = (bf16[1040,128]{1,0:T(8,128)(2,1)S(1)}, bf16[1040,128]{1,0:T(8,128)(2,1)S(1)}, u32[]{:S(2)}, u32[]{:S(2)}) collective-permute-start(bf16[1040,128]{1,0:T(8,128)(2,1)S(1)} %pad_maximum_fusion.2.rest_0_.mixed_ref.refs_0_), channel_id=1, source_target_pairs={{0,2},{1,3},{2,0},{3,1},{4,6},{5,7},{6,4},{7,5},{8,10},{9,11},{10,... | collective-permute-start | bytes 798728 | tf_op jit(solution)/shard_map/ppermute | solution.py:32
  16.7 1.5 %collective-permute-start.3 = (bf16[1040,128]{1,0:T(8,128)(2,1)S(1)}, bf16[1040,128]{1,0:T(8,128)(2,1)S(1)}, u32[]{:S(2)}, u32[]{:S(2)}) collective-permute-start(bf16[1040,128]{1,0:T(8,128)(2,1)S(1)} %pad_maximum_fusion.2.rest_0_.mixed_ref.refs_0_), channel_id=1, source_target_pairs={{0,1},{1,0},{2,3},{3,2},{4,5},{5,4},{6,7},{7,6},{8,9},{9,8},{10,11... | collective-permute-start | bytes 798728 | tf_op jit(solution)/shard_map/ppermute | solution.py:32
  18.2 1.6 %shard_map.69 = f32[4,256,128]{2,1,0:T(8,128)S(1)} custom-call(s32[8,128]{1,0:T(8,128)S(1)} %broadcast_in_dim.2.shift_rows_ref, bf16[16,128]{1,0:T(8,128)(2,1)S(1)} %pad_maximum_fusion.3.coupling_ref, bf16[8,256,128]{2,1,0:T(8,128)(2,1)S(1)} %shard_map.64.own_ref, bf16[8,256,128]{2,1,0:T(8,128)(2,1)S(1)} %collective-permute-done.mate_ref, ...), custom_call_target="tpu_custom_call" | custom-call | flops 500000000 | bytes 1000000 | tf_op jit(solution)/shard_map/pallas_call | solution.py:285
  19.9 2.7 %collective-permute-start.6 = (bf16[1040,128]{1,0:T(8,128)(2,1)S(1)}, bf16[1040,128]{1,0:T(8,128)(2,1)S(1)}, u32[]{:S(2)}, u32[]{:S(2)}) collective-permute-start(bf16[1040,128]{1,0:T(8,128)(2,1)S(1)} %pad_maximum_fusion.1.after_ref.rest_0_.mixed_ref.value_ref.refs_0_), channel_id=1, source_target_pairs={{0,4},{1,5},{2,6},{3,7},{4,0},{5,1},{6,2},{7,3},{8,12},{9,13},{10,... | collective-permute-start | bytes 798728 | tf_op jit(solution)/shard_map/ppermute | solution.py:32
  22.7 1.6 %collective-permute-start.5 = (bf16[1040,128]{1,0:T(8,128)(2,1)S(1)}, bf16[1040,128]{1,0:T(8,128)(2,1)S(1)}, u32[]{:S(2)}, u32[]{:S(2)}) collective-permute-start(bf16[1040,128]{1,0:T(8,128)(2,1)S(1)} %shard_map.70), channel_id=1, source_target_pairs={{0,1},{1,0},{2,3},{3,2},{4,5},{5,4},{6,7},{7,6},{8,9},{9,8},{10,11... | collective-permute-start | bytes 798728 | tf_op jit(solution)/shard_map/ppermute | solution.py:32
  24.3 2.8 %shard_map.71.rest_0_.refs_6_.after_ref = f32[4,256,128]{2,1,0:T(8,128)S(1)} custom-call(bf16[1040,128]{1,0:T(8,128)(2,1)S(1)} %pad_maximum_fusion.2.rest_0_.mixed_ref.refs_0_, bf16[1792,128]{1,0:T(8,128)(2,1)S(1)} %get-tuple-element.12.rest_1_.hot_ref, bf16[256,3584]{1,0:T(8,128)(2,1)S(1)} %get-tuple-element.13.k_ref, ...), custom_call_target="tpu_custom_call" | custom-call | flops 2000000000 | bytes 3000000 | tf_op jit(solution)/shard_map/pallas_call | solution.py:315
  27.7 2.8 %shard_map.72.refs_4_.refs_6_ = f32[4,256,128]{2,1,0:T(8,128)S(1)} custom-call(bf16[1040,128]{1,0:T(8,128)(2,1)S(1)} %pad_maximum_fusion.1.after_ref.rest_0_.mixed_ref.value_ref.refs_0_, bf16[1792,128]{1,0:T(8,128)(2,1)S(1)} %get-tuple-element.12.rest_1_.hot_ref, bf16[256,3584]{1,0:T(8,128)(2,1)S(1)} %get-tuple-element.13.k_ref, ...), custom_call_target="tpu_custom_call" | custom-call | flops 2000000000 | bytes 3000000 | tf_op jit(solution)/shard_map/pallas_call | solution.py:315
  30.5 1.3 %collective-permute-done.5.refs_3_ = bf16[1040,128]{1,0:T(8,128)(2,1)S(1)} collective-permute-done((bf16[1040,128]{1,0:T(8,128)(2,1)S(1)}, bf16[1040,128]{1,0:T(8,128)(2,1)S(1)}, u32[]{:S(2)}, u32[]{:S(2)}) %collective-permute-start.5) | collective-permute-done | bytes 266272 | tf_op jit(solution)/shard_map/ppermute | solution.py:32
  31.8 1.0 %shard_map.74.value_ref = bf16[4,256,128]{2,1,0:T(8,128)(2,1)S(1)} custom-call(bf16[1040,128]{1,0:T(8,128)(2,1)S(1)} %pad_maximum_fusion.2.rest_0_.mixed_ref.refs_0_, bf16[1040,128]{1,0:T(8,128)(2,1)S(1)} %collective-permute-done.2.value_ref.refs_1_, bf16[1040,128]{1,0:T(8,128)(2,1)S(1)} %collective-permute-done.3.refs_2_, ...), custom_call_target="tpu_custom_call" | custom-call | flops 1000000000 | bytes 3000000 | tf_op jit(solution)/shard_map/pallas_call | solution.py:373
  32.8 1.6 %collective-permute-done.6.rest_0_.value_ref.refs_1_ = bf16[1040,128]{1,0:T(8,128)(2,1)S(1)} collective-permute-done((bf16[1040,128]{1,0:T(8,128)(2,1)S(1)}, bf16[1040,128]{1,0:T(8,128)(2,1)S(1)}, u32[]{:S(2)}, u32[]{:S(2)}) %collective-permute-start.6) | collective-permute-done | bytes 266272 | tf_op jit(solution)/shard_map/ppermute | solution.py:32
  34.5 0.9 %collective-permute-start.7 = (bf16[4,256,128]{2,1,0:T(8,128)(2,1)S(1)}, bf16[4,256,128]{2,1,0:T(8,128)(2,1)S(1)}, u32[]{:S(2)}, u32[]{:S(2)}) collective-permute-start(bf16[4,256,128]{2,1,0:T(8,128)(2,1)S(1)} %shard_map.75.after_ref), channel_id=1, source_target_pairs={{0,4},{1,5},{2,6},{3,7},{4,0},{5,1},{6,2},{7,3},{8,12},{9,13},{10,... | collective-permute-start | bytes 786440 | tf_op jit(solution)/shard_map/ppermute | solution.py:32
  35.4 2.3 %collective-permute-start.9 = (bf16[528,128]{1,0:T(8,128)(2,1)S(1)}, bf16[528,128]{1,0:T(8,128)(2,1)S(1)}, u32[]{:S(2)}, u32[]{:S(2)}) collective-permute-start(bf16[528,128]{1,0:T(8,128)(2,1)S(1)} %get-tuple-element.16), channel_id=1, source_target_pairs={{0,1},{1,0},{2,3},{3,2},{4,5},{5,4},{6,7},{7,6},{8,9},{9,8},{10,11... | collective-permute-start | bytes 405512 | tf_op jit(solution)/shard_map/ppermute | solution.py:32
  37.8 1.0 %shard_map.77.refs_4_.refs_6_ = f32[4,256,128]{2,1,0:T(8,128)S(1)} custom-call(bf16[1040,128]{1,0:T(8,128)(2,1)S(1)} %pad_maximum_fusion.2.rest_0_.mixed_ref.refs_0_, bf16[1040,128]{1,0:T(8,128)(2,1)S(1)} %collective-permute-done.2.value_ref.refs_1_, bf16[1040,128]{1,0:T(8,128)(2,1)S(1)} %collective-permute-done.3.refs_2_, ...), custom_call_target="tpu_custom_call" | custom-call | flops 4000000000 | bytes 3000000 | tf_op jit(solution)/shard_map/pallas_call | solution.py:383
  38.8 1.9 %collective-permute-done.9.refs_3_ = bf16[528,128]{1,0:T(8,128)(2,1)S(1)} collective-permute-done((bf16[528,128]{1,0:T(8,128)(2,1)S(1)}, bf16[528,128]{1,0:T(8,128)(2,1)S(1)}, u32[]{:S(2)}, u32[]{:S(2)}) %collective-permute-start.9) | collective-permute-done | bytes 135200 | tf_op jit(solution)/shard_map/ppermute | solution.py:32
  41.5 4.5 %collective-permute-start.11 = (bf16[2,256,128]{2,1,0:T(8,128)(2,1)S(1)}, bf16[2,256,128]{2,1,0:T(8,128)(2,1)S(1)}, u32[]{:S(2)}, u32[]{:S(2)}) collective-permute-start(bf16[2,256,128]{2,1,0:T(8,128)(2,1)S(1)} %shard_map.80.refs_6_), channel_id=1, source_target_pairs={{0,2},{1,3},{2,0},{3,1},{4,6},{5,7},{6,4},{7,5},{8,10},{9,11},{10,... | collective-permute-start | bytes 393224 | tf_op jit(solution)/shard_map/ppermute | solution.py:32
  48.8 2.3 %collective-permute-done.11 = bf16[2,256,128]{2,1,0:T(8,128)(2,1)S(1)} collective-permute-done((bf16[2,256,128]{2,1,0:T(8,128)(2,1)S(1)}, bf16[2,256,128]{2,1,0:T(8,128)(2,1)S(1)}, u32[]{:S(2)}, u32[]{:S(2)}) %collective-permute-start.11) | collective-permute-done | bytes 131104 | tf_op jit(solution)/shard_map/ppermute | solution.py:32
  51.1 2.5 %collective-permute-done.12 = bf16[2,256,128]{2,1,0:T(8,128)(2,1)S(1)} collective-permute-done((bf16[2,256,128]{2,1,0:T(8,128)(2,1)S(1)}, bf16[2,256,128]{2,1,0:T(8,128)(2,1)S(1)}, u32[]{:S(2)}, u32[]{:S(2)}) %collective-permute-start.12) | collective-permute-done | bytes 131104 | tf_op jit(solution)/shard_map/ppermute | solution.py:32
  53.6 1.0 %pad_maximum_fusion = f32[8,256,128]{2,1,0:T(8,128)} fusion(f32[2,256,128]{2,1,0:T(8,128)S(1)} %convert_add_fusion.1, f32[2,256,128]{2,1,0:T(8,128)S(1)} %convert_add_fusion.2, f32[4,256,128]{2,1,0:T(8,128)S(1)} %convert_add_fusion), kind=kLoop, calls=%fused_computation | loop fusion | flops 524288 | bytes 2097152 | tf_op jit(solution)/shard_map/concatenate | solution.py:455
  (39 shorter events, 7.3 us)
Async XLA Ops:
  0.0 2.3 %collective-permute-start = (bf16[8,256,128]{2,1,0:T(8,128)(2,1)}, bf16[8,256,128]{2,1,0:T(8,128)(2,1)S(1)}, u32[]{:S(2)}, u32[]{:S(2)}) collective-permute-start(bf16[8,256,128]{2,1,0:T(8,128)(2,1)} %bitcast.5), channel_id=1, source_target_pairs={{0,8},{8,0},{16,24},{24,16},{1,9},{9,1},{17,25},{25,17},{2,10},{10... | collective-permute-start | bytes 1572872 | tf_op jit(solution)/shard_map/ppermute | solution.py:32
  0.5 1.0 %copy-start = (bf16[8,16,16,128]{3,2,1,0:T(8,128)(2,1)S(1)}, bf16[8,16,16,128]{3,2,1,0:T(8,128)(2,1)}, u32[]{:S(2)}) copy-start(bf16[8,16,16,128]{3,2,1,0:T(8,128)(2,1)} %param.6) | copy-start | bytes 1572868
  4.5 5.9 %copy-start.1 = (bf16[16,16,16]{2,1,0:T(8,128)(2,1)S(1)}, bf16[16,16,16]{2,1,0:T(8,128)(2,1)}, u32[]{:S(2)}) copy-start(bf16[16,16,16]{2,1,0:T(8,128)(2,1)} %derivative_ref.1) | copy-start | bytes 24580
  4.5 5.9 %copy-start.2 = (s32[128,16]{0,1:T(8,128)S(1)}, s32[128,16]{0,1:T(8,128)}, u32[]{:S(2)}) copy-start(s32[128,16]{0,1:T(8,128)} %param.11) | copy-start | bytes 24580
  4.5 9.9 %collective-permute-start.1 = (bf16[4,256,128]{2,1,0:T(8,128)(2,1)S(1)}, bf16[4,256,128]{2,1,0:T(8,128)(2,1)S(1)}, u32[]{:S(2)}, u32[]{:S(2)}) collective-permute-start(bf16[4,256,128]{2,1,0:T(8,128)(2,1)S(1)} %shard_map.65.rest_0_), channel_id=1, source_target_pairs={{0,16},{8,24},{16,0},{24,8},{1,17},{9,25},{17,1},{25,9},{2,18},{10... | collective-permute-start | bytes 786440 | tf_op jit(solution)/shard_map/ppermute | solution.py:32
  10.3 9.5 %collective-permute-start.4 = (bf16[4,256,128]{2,1,0:T(8,128)(2,1)S(1)}, bf16[4,256,128]{2,1,0:T(8,128)(2,1)S(1)}, u32[]{:S(2)}, u32[]{:S(2)}) collective-permute-start(bf16[4,256,128]{2,1,0:T(8,128)(2,1)S(1)} %shard_map.67.after_ref), channel_id=1, source_target_pairs={{0,16},{8,24},{16,0},{24,8},{1,17},{9,25},{17,1},{25,9},{2,18},{10... | collective-permute-start | bytes 786440 | tf_op jit(solution)/shard_map/ppermute | solution.py:32
  14.5 8.2 %collective-permute-start.2 = (bf16[1040,128]{1,0:T(8,128)(2,1)S(1)}, bf16[1040,128]{1,0:T(8,128)(2,1)S(1)}, u32[]{:S(2)}, u32[]{:S(2)}) collective-permute-start(bf16[1040,128]{1,0:T(8,128)(2,1)S(1)} %pad_maximum_fusion.2.rest_0_.mixed_ref.refs_0_), channel_id=1, source_target_pairs={{0,2},{1,3},{2,0},{3,1},{4,6},{5,7},{6,4},{7,5},{8,10},{9,11},{10,... | collective-permute-start | bytes 798728 | tf_op jit(solution)/shard_map/ppermute | solution.py:32
  16.7 13.7 %collective-permute-start.3 = (bf16[1040,128]{1,0:T(8,128)(2,1)S(1)}, bf16[1040,128]{1,0:T(8,128)(2,1)S(1)}, u32[]{:S(2)}, u32[]{:S(2)}) collective-permute-start(bf16[1040,128]{1,0:T(8,128)(2,1)S(1)} %pad_maximum_fusion.2.rest_0_.mixed_ref.refs_0_), channel_id=1, source_target_pairs={{0,1},{1,0},{2,3},{3,2},{4,5},{5,4},{6,7},{7,6},{8,9},{9,8},{10,11... | collective-permute-start | bytes 798728 | tf_op jit(solution)/shard_map/ppermute | solution.py:32
  19.9 14.5 %collective-permute-start.6 = (bf16[1040,128]{1,0:T(8,128)(2,1)S(1)}, bf16[1040,128]{1,0:T(8,128)(2,1)S(1)}, u32[]{:S(2)}, u32[]{:S(2)}) collective-permute-start(bf16[1040,128]{1,0:T(8,128)(2,1)S(1)} %pad_maximum_fusion.1.after_ref.rest_0_.mixed_ref.value_ref.refs_0_), channel_id=1, source_target_pairs={{0,4},{1,5},{2,6},{3,7},{4,0},{5,1},{6,2},{7,3},{8,12},{9,13},{10,... | collective-permute-start | bytes 798728 | tf_op jit(solution)/shard_map/ppermute | solution.py:32
  22.7 9.0 %collective-permute-start.5 = (bf16[1040,128]{1,0:T(8,128)(2,1)S(1)}, bf16[1040,128]{1,0:T(8,128)(2,1)S(1)}, u32[]{:S(2)}, u32[]{:S(2)}) collective-permute-start(bf16[1040,128]{1,0:T(8,128)(2,1)S(1)} %shard_map.70), channel_id=1, source_target_pairs={{0,1},{1,0},{2,3},{3,2},{4,5},{5,4},{6,7},{7,6},{8,9},{9,8},{10,11... | collective-permute-start | bytes 798728 | tf_op jit(solution)/shard_map/ppermute | solution.py:32
  27.1 11.7 %collective-permute-start.8 = (bf16[1040,128]{1,0:T(8,128)(2,1)S(1)}, bf16[1040,128]{1,0:T(8,128)(2,1)S(1)}, u32[]{:S(2)}, u32[]{:S(2)}) collective-permute-start(bf16[1040,128]{1,0:T(8,128)(2,1)S(1)} %shard_map.78), channel_id=1, source_target_pairs={{0,1},{1,0},{2,3},{3,2},{4,5},{5,4},{6,7},{7,6},{8,9},{9,8},{10,11... | collective-permute-start | bytes 798728 | tf_op jit(solution)/shard_map/ppermute | solution.py:32
  34.5 14.2 %collective-permute-start.7 = (bf16[4,256,128]{2,1,0:T(8,128)(2,1)S(1)}, bf16[4,256,128]{2,1,0:T(8,128)(2,1)S(1)}, u32[]{:S(2)}, u32[]{:S(2)}) collective-permute-start(bf16[4,256,128]{2,1,0:T(8,128)(2,1)S(1)} %shard_map.75.after_ref), channel_id=1, source_target_pairs={{0,4},{1,5},{2,6},{3,7},{4,0},{5,1},{6,2},{7,3},{8,12},{9,13},{10,... | collective-permute-start | bytes 786440 | tf_op jit(solution)/shard_map/ppermute | solution.py:32
  35.4 5.3 %collective-permute-start.9 = (bf16[528,128]{1,0:T(8,128)(2,1)S(1)}, bf16[528,128]{1,0:T(8,128)(2,1)S(1)}, u32[]{:S(2)}, u32[]{:S(2)}) collective-permute-start(bf16[528,128]{1,0:T(8,128)(2,1)S(1)} %get-tuple-element.16), channel_id=1, source_target_pairs={{0,1},{1,0},{2,3},{3,2},{4,5},{5,4},{6,7},{7,6},{8,9},{9,8},{10,11... | collective-permute-start | bytes 405512 | tf_op jit(solution)/shard_map/ppermute | solution.py:32
  37.7 8.2 %collective-permute-start.10 = (bf16[512,128]{1,0:T(8,128)(2,1)S(1)}, bf16[512,128]{1,0:T(8,128)(2,1)S(1)}, u32[]{:S(2)}, u32[]{:S(2)}) collective-permute-start(bf16[512,128]{1,0:T(8,128)(2,1)S(1)} %get-tuple-element.15.refs_7_), channel_id=1, source_target_pairs={{0,1},{1,0},{2,3},{3,2},{4,5},{5,4},{6,7},{7,6},{8,9},{9,8},{10,11... | collective-permute-start | bytes 393224 | tf_op jit(solution)/shard_map/ppermute | solution.py:32
  41.5 9.6 %collective-permute-start.11 = (bf16[2,256,128]{2,1,0:T(8,128)(2,1)S(1)}, bf16[2,256,128]{2,1,0:T(8,128)(2,1)S(1)}, u32[]{:S(2)}, u32[]{:S(2)}) collective-permute-start(bf16[2,256,128]{2,1,0:T(8,128)(2,1)S(1)} %shard_map.80.refs_6_), channel_id=1, source_target_pairs={{0,2},{1,3},{2,0},{3,1},{4,6},{5,7},{6,4},{7,5},{8,10},{9,11},{10,... | collective-permute-start | bytes 393224 | tf_op jit(solution)/shard_map/ppermute | solution.py:32
  46.6 7.0 %collective-permute-start.12 = (bf16[2,256,128]{2,1,0:T(8,128)(2,1)S(1)}, bf16[2,256,128]{2,1,0:T(8,128)(2,1)S(1)}, u32[]{:S(2)}, u32[]{:S(2)}) collective-permute-start(bf16[2,256,128]{2,1,0:T(8,128)(2,1)S(1)} %shard_map.81.refs_7_), channel_id=1, source_target_pairs={{0,2},{1,3},{2,0},{3,1},{4,6},{5,7},{6,4},{7,5},{8,10},{9,11},{10,... | collective-permute-start | bytes 393224 | tf_op jit(solution)/shard_map/ppermute | solution.py:32

commit v10 on v9

--- a/solution.py
+++ b/solution.py
@@ -413,19 +413,8 @@
     behind = local_outer
     near_hots = one_hots(near, high, behind)
     near_away = away_sums(sizes[0], near, straight, near_hots, high, behind)
-    held = [
-        pl.pallas_call(
-            copy_kernel,
-            out_shape=jax.ShapeDtypeStruct(value.shape, value.dtype),
-            in_specs=[VMEM, ANY],
-            out_specs=VMEM,
-            compiler_params=params(),
-            cost_estimate=cost(1e6, 1e6),
-        )(value, far[-1])
-        for value in near_away
-    ]
-    near_back = send(held, high)
-    behind, far_next = pass_far(held[0])
+    near_back = send(near_away, high)
+    behind, far_next = pass_far(near_away[0])
     stay_inner = stay_sum(sizes[0], 0, near, straight, near_hots, local_inner, [behind])
     after = stay_inner
     far_hots = None

time: 54.9 us -> 52.6 us (0.958)
  starting transfers between devices: 20.5 us -> 19.2 us
  waiting for transfers between devices: 10.2 us -> 9.22 us
    ppermute x13, starting transfers between devices: 20.5 us -> 19.2 us  [swap(): return lax.ppermute(value, axis, [(i, i ^ mask) for i in range(count)])]
    ppermute x13, waiting for transfers between devices: 10.2 us -> 9.22 us  [swap(): return lax.ppermute(value, axis, [(i, i ^ mask) for i in range(count)])]
  transfers between devices with their start and end apart: 13 -> 13, of which waited for: 6 -> 6; matrix products, arithmetic and copies ran while one was open for 2% -> 2% of each run, Pallas kernels for 34% -> 35%
where the time goes in v10:
time: 52.6 us; the launch traced here: 52.4 us
  Pallas kernels  19.9 us (38%)
  starting transfers between devices  19.2 us (37%)
  waiting for transfers between devices  9.22 us (18%)
  other arithmetic  2.1 us (4%)
  local copies, waits for them, and re-layouts  1.78 us (3%)
    ppermute x13, starting transfers between devices, swap(): return lax.ppermute(value, axis, [(i, i ^ mask) for i in range(count)])  19.2 us
    ppermute x13, waiting for transfers between devices, swap(): return lax.ppermute(value, axis, [(i, i ^ mask) for i in range(count)])  9.22 us
    pallas_call x4, Pallas kernels, mix(): pl.pallas_call(functools.partial(mix_kernel, group, firsts[chunk]), out_s...  6.01 us
    pallas_call x2, Pallas kernels, local_sum(): pl.pallas_call(local_kernel, out_shape=jax.ShapeDtypeStruct((sizes[chunk]...  5.59 us
    pallas_call x1, Pallas kernels, prepare(): pl.pallas_call(prepare_kernel, out_shape=(jax.ShapeDtypeStruct((square, l...  3.36 us
    pallas_call x3, Pallas kernels, stay_sum(): pl.pallas_call(functools.partial(stay_kernel, offsets, skip), out_shape=j...  2.31 us
    pallas_call x3, Pallas kernels, away_sums(): pl.pallas_call(functools.partial(away_kernel, offsets), out_shape=(block,...  2.31 us
    unnamed x6, local copies, waits for them, and re-layouts  1.05 us
  transfers between devices with their start and end apart: 13, of which 6 were waited for; matrix products, arithmetic and copies ran while one was open for 2% of the time, Pallas kernels for 35%

profile of v10, /device:TPU:0, one launch (start us, length us, event | category | flops | bytes accessed | tf_op | source)
XLA Modules:
  0.0 52.4 jit_solution(17860619198796544641)
XLA Ops:
  0.5 1.0 %copy-done = bf16[8,16,16,128]{3,2,1,0:T(8,128)(2,1)S(1)} copy-done((bf16[8,16,16,128]{3,2,1,0:T(8,128)(2,1)S(1)}, bf16[8,16,16,128]{3,2,1,0:T(8,128)(2,1)}, u32[]{:S(2)}) %copy-start) | copy-done | bytes 524312
  3.0 1.4 %shard_map.65.rest_0_ = bf16[4,256,128]{2,1,0:T(8,128)(2,1)S(1)} custom-call(s32[8,128]{1,0:T(8,128)S(1)} %broadcast_in_dim.2.shift_rows_ref, bf16[16,128]{1,0:T(8,128)(2,1)S(1)} %pad_maximum_fusion.3.coupling_ref, bf16[8,256,128]{2,1,0:T(8,128)(2,1)S(1)} %shard_map.64.own_ref, bf16[8,256,128]{2,1,0:T(8,128)(2,1)S(1)} %collective-permute-done.mate_ref), custom_call_target="tpu_custom_call" | custom-call | flops 500000000 | bytes 1000000 | tf_op jit(solution)/shard_map/pallas_call | solution.py:285
  4.5 2.8 %collective-permute-start.1 = (bf16[4,256,128]{2,1,0:T(8,128)(2,1)S(1)}, bf16[4,256,128]{2,1,0:T(8,128)(2,1)S(1)}, u32[]{:S(2)}, u32[]{:S(2)}) collective-permute-start(bf16[4,256,128]{2,1,0:T(8,128)(2,1)S(1)} %shard_map.65.rest_0_), channel_id=1, source_target_pairs={{0,16},{8,24},{16,0},{24,8},{1,17},{9,25},{17,1},{25,9},{2,18},{10... | collective-permute-start | bytes 786440 | tf_op jit(solution)/shard_map/ppermute | solution.py:32
  7.3 1.6 %shard_map.66.rest_0_ = f32[4,256,128]{2,1,0:T(8,128)S(1)} custom-call(s32[8,128]{1,0:T(8,128)S(1)} %broadcast_in_dim.2.shift_rows_ref, bf16[16,128]{1,0:T(8,128)(2,1)S(1)} %pad_maximum_fusion.3.coupling_ref, bf16[8,256,128]{2,1,0:T(8,128)(2,1)S(1)} %shard_map.64.own_ref, bf16[8,256,128]{2,1,0:T(8,128)(2,1)S(1)} %collective-permute-done.mate_ref, ...), custom_call_target="tpu_custom_call" | custom-call | flops 500000000 | bytes 1000000 | tf_op jit(solution)/shard_map/pallas_call | solution.py:285
  8.9 1.4 %shard_map.67.after_ref = bf16[4,256,128]{2,1,0:T(8,128)(2,1)S(1)} custom-call(s32[8,128]{1,0:T(8,128)S(1)} %broadcast_in_dim.2.shift_rows_ref, bf16[16,128]{1,0:T(8,128)(2,1)S(1)} %pad_maximum_fusion.3.coupling_ref, bf16[8,256,128]{2,1,0:T(8,128)(2,1)S(1)} %shard_map.64.own_ref, bf16[8,256,128]{2,1,0:T(8,128)(2,1)S(1)} %collective-permute-done.mate_ref, ...), custom_call_target="tpu_custom_call" | custom-call | flops 500000000 | bytes 1000000 | tf_op jit(solution)/shard_map/pallas_call | solution.py:285
  10.4 3.4 %shard_map.68 = (bf16[256,3584]{1,0:T(8,128)(2,1)S(1)}, bf16[256,512]{1,0:T(8,128)(2,1)S(1)}, bf16[1792,128]{1,0:T(8,128)(2,1)S(1)}, bf16[16,128]{1,0:T(8,128)(2,1)S(1)}) custom-call(bf16[16,16,16]{2,1,0:T(8,128)(2,1)S(1)} %copy-done.1, s32[16,128]{1,0:T(8,128)S(1)} %bitcast.7, bf16[4,256,128]{2,1,0:T(8,128)(2,1)S(1)} %shard_map.67.after_ref), custom_call_target="tpu_custom_call" | custom-call | flops 2000000000 | bytes 3000000 | tf_op jit(solution)/shard_map/pallas_call | solution.py:300
  14.5 2.2 %collective-permute-start.2 = (bf16[1040,128]{1,0:T(8,128)(2,1)S(1)}, bf16[1040,128]{1,0:T(8,128)(2,1)S(1)}, u32[]{:S(2)}, u32[]{:S(2)}) collective-permute-start(bf16[1040,128]{1,0:T(8,128)(2,1)S(1)} %pad_maximum_fusion.2.rest_0_.mixed_ref.refs_0_), channel_id=1, source_target_pairs={{0,2},{1,3},{2,0},{3,1},{4,6},{5,7},{6,4},{7,5},{8,10},{9,11},{10,... | collective-permute-start | bytes 798728 | tf_op jit(solution)/shard_map/ppermute | solution.py:32
  16.7 1.5 %collective-permute-start.3 = (bf16[1040,128]{1,0:T(8,128)(2,1)S(1)}, bf16[1040,128]{1,0:T(8,128)(2,1)S(1)}, u32[]{:S(2)}, u32[]{:S(2)}) collective-permute-start(bf16[1040,128]{1,0:T(8,128)(2,1)S(1)} %pad_maximum_fusion.2.rest_0_.mixed_ref.refs_0_), channel_id=1, source_target_pairs={{0,1},{1,0},{2,3},{3,2},{4,5},{5,4},{6,7},{7,6},{8,9},{9,8},{10,11... | collective-permute-start | bytes 798728 | tf_op jit(solution)/shard_map/ppermute | solution.py:32
  18.2 1.6 %shard_map.69 = f32[4,256,128]{2,1,0:T(8,128)S(1)} custom-call(s32[8,128]{1,0:T(8,128)S(1)} %broadcast_in_dim.2.shift_rows_ref, bf16[16,128]{1,0:T(8,128)(2,1)S(1)} %pad_maximum_fusion.3.coupling_ref, bf16[8,256,128]{2,1,0:T(8,128)(2,1)S(1)} %shard_map.64.own_ref, bf16[8,256,128]{2,1,0:T(8,128)(2,1)S(1)} %collective-permute-done.mate_ref, ...), custom_call_target="tpu_custom_call" | custom-call | flops 500000000 | bytes 1000000 | tf_op jit(solution)/shard_map/pallas_call | solution.py:285
  19.9 2.7 %collective-permute-start.6 = (bf16[1040,128]{1,0:T(8,128)(2,1)S(1)}, bf16[1040,128]{1,0:T(8,128)(2,1)S(1)}, u32[]{:S(2)}, u32[]{:S(2)}) collective-permute-start(bf16[1040,128]{1,0:T(8,128)(2,1)S(1)} %pad_maximum_fusion.1.after_ref.rest_0_.mixed_ref.value_ref.refs_0_), channel_id=1, source_target_pairs={{0,4},{1,5},{2,6},{3,7},{4,0},{5,1},{6,2},{7,3},{8,12},{9,13},{10,... | collective-permute-start | bytes 798728 | tf_op jit(solution)/shard_map/ppermute | solution.py:32
  22.7 1.6 %collective-permute-start.5 = (bf16[1040,128]{1,0:T(8,128)(2,1)S(1)}, bf16[1040,128]{1,0:T(8,128)(2,1)S(1)}, u32[]{:S(2)}, u32[]{:S(2)}) collective-permute-start(bf16[1040,128]{1,0:T(8,128)(2,1)S(1)} %shard_map.70), channel_id=1, source_target_pairs={{0,1},{1,0},{2,3},{3,2},{4,5},{5,4},{6,7},{7,6},{8,9},{9,8},{10,11... | collective-permute-start | bytes 798728 | tf_op jit(solution)/shard_map/ppermute | solution.py:32
  24.3 2.8 %shard_map.71.rest_0_.refs_6_.after_ref = f32[4,256,128]{2,1,0:T(8,128)S(1)} custom-call(bf16[1040,128]{1,0:T(8,128)(2,1)S(1)} %pad_maximum_fusion.2.rest_0_.mixed_ref.refs_0_, bf16[1792,128]{1,0:T(8,128)(2,1)S(1)} %get-tuple-element.12.rest_1_.hot_ref, bf16[256,3584]{1,0:T(8,128)(2,1)S(1)} %get-tuple-element.13.k_ref, ...), custom_call_target="tpu_custom_call" | custom-call | flops 2000000000 | bytes 3000000 | tf_op jit(solution)/shard_map/pallas_call | solution.py:315
  27.7 2.8 %shard_map.72.refs_4_.refs_6_ = f32[4,256,128]{2,1,0:T(8,128)S(1)} custom-call(bf16[1040,128]{1,0:T(8,128)(2,1)S(1)} %pad_maximum_fusion.1.after_ref.rest_0_.mixed_ref.value_ref.refs_0_, bf16[1792,128]{1,0:T(8,128)(2,1)S(1)} %get-tuple-element.12.rest_1_.hot_ref, bf16[256,3584]{1,0:T(8,128)(2,1)S(1)} %get-tuple-element.13.k_ref, ...), custom_call_target="tpu_custom_call" | custom-call | flops 2000000000 | bytes 3000000 | tf_op jit(solution)/shard_map/pallas_call | solution.py:315
  30.5 1.2 %collective-permute-done.5.refs_3_ = bf16[1040,128]{1,0:T(8,128)(2,1)S(1)} collective-permute-done((bf16[1040,128]{1,0:T(8,128)(2,1)S(1)}, bf16[1040,128]{1,0:T(8,128)(2,1)S(1)}, u32[]{:S(2)}, u32[]{:S(2)}) %collective-permute-start.5) | collective-permute-done | bytes 266272 | tf_op jit(solution)/shard_map/ppermute | solution.py:32
  31.8 1.0 %shard_map.74.after_ref = bf16[4,256,128]{2,1,0:T(8,128)(2,1)S(1)} custom-call(bf16[1040,128]{1,0:T(8,128)(2,1)S(1)} %pad_maximum_fusion.2.rest_0_.mixed_ref.refs_0_, bf16[1040,128]{1,0:T(8,128)(2,1)S(1)} %collective-permute-done.2.value_ref.refs_1_, bf16[1040,128]{1,0:T(8,128)(2,1)S(1)} %collective-permute-done.3.refs_2_, ...), custom_call_target="tpu_custom_call" | custom-call | flops 1000000000 | bytes 3000000 | tf_op jit(solution)/shard_map/pallas_call | solution.py:373
  32.8 2.5 %collective-permute-start.7 = (bf16[4,256,128]{2,1,0:T(8,128)(2,1)S(1)}, bf16[4,256,128]{2,1,0:T(8,128)(2,1)S(1)}, u32[]{:S(2)}, u32[]{:S(2)}) collective-permute-start(bf16[4,256,128]{2,1,0:T(8,128)(2,1)S(1)} %shard_map.74.after_ref), channel_id=1, source_target_pairs={{0,4},{1,5},{2,6},{3,7},{4,0},{5,1},{6,2},{7,3},{8,12},{9,13},{10,... | collective-permute-start | bytes 786440 | tf_op jit(solution)/shard_map/ppermute | solution.py:32
  35.4 2.5 %collective-permute-done.6.value_ref.refs_1_ = bf16[1040,128]{1,0:T(8,128)(2,1)S(1)} collective-permute-done((bf16[1040,128]{1,0:T(8,128)(2,1)S(1)}, bf16[1040,128]{1,0:T(8,128)(2,1)S(1)}, u32[]{:S(2)}, u32[]{:S(2)}) %collective-permute-start.6) | collective-permute-done | bytes 266272 | tf_op jit(solution)/shard_map/ppermute | solution.py:32
  37.9 1.4 %collective-permute-start.9 = (bf16[528,128]{1,0:T(8,128)(2,1)S(1)}, bf16[528,128]{1,0:T(8,128)(2,1)S(1)}, u32[]{:S(2)}, u32[]{:S(2)}) collective-permute-start(bf16[528,128]{1,0:T(8,128)(2,1)S(1)} %get-tuple-element.16), channel_id=1, source_target_pairs={{0,1},{1,0},{2,3},{3,2},{4,5},{5,4},{6,7},{7,6},{8,9},{9,8},{10,11... | collective-permute-start | bytes 405512 | tf_op jit(solution)/shard_map/ppermute | solution.py:32
  40.0 1.0 %shard_map.76.refs_4_.refs_6_ = f32[4,256,128]{2,1,0:T(8,128)S(1)} custom-call(bf16[1040,128]{1,0:T(8,128)(2,1)S(1)} %pad_maximum_fusion.2.rest_0_.mixed_ref.refs_0_, bf16[1040,128]{1,0:T(8,128)(2,1)S(1)} %collective-permute-done.2.value_ref.refs_1_, bf16[1040,128]{1,0:T(8,128)(2,1)S(1)} %collective-permute-done.3.refs_2_, ...), custom_call_target="tpu_custom_call" | custom-call | flops 4000000000 | bytes 3000000 | tf_op jit(solution)/shard_map/pallas_call | solution.py:383
  41.0 2.0 %collective-permute-done.9.refs_3_ = bf16[528,128]{1,0:T(8,128)(2,1)S(1)} collective-permute-done((bf16[528,128]{1,0:T(8,128)(2,1)S(1)}, bf16[528,128]{1,0:T(8,128)(2,1)S(1)}, u32[]{:S(2)}, u32[]{:S(2)}) %collective-permute-start.9) | collective-permute-done | bytes 135200 | tf_op jit(solution)/shard_map/ppermute | solution.py:32
  43.8 1.6 %collective-permute-start.11 = (bf16[2,256,128]{2,1,0:T(8,128)(2,1)S(1)}, bf16[2,256,128]{2,1,0:T(8,128)(2,1)S(1)}, u32[]{:S(2)}, u32[]{:S(2)}) collective-permute-start(bf16[2,256,128]{2,1,0:T(8,128)(2,1)S(1)} %shard_map.79.refs_6_), channel_id=1, source_target_pairs={{0,2},{1,3},{2,0},{3,1},{4,6},{5,7},{6,4},{7,5},{8,10},{9,11},{10,... | collective-permute-start | bytes 393224 | tf_op jit(solution)/shard_map/ppermute | solution.py:32
  48.4 1.5 %collective-permute-done.11 = bf16[2,256,128]{2,1,0:T(8,128)(2,1)S(1)} collective-permute-done((bf16[2,256,128]{2,1,0:T(8,128)(2,1)S(1)}, bf16[2,256,128]{2,1,0:T(8,128)(2,1)S(1)}, u32[]{:S(2)}, u32[]{:S(2)}) %collective-permute-start.11) | collective-permute-done | bytes 131104 | tf_op jit(solution)/shard_map/ppermute | solution.py:32
  50.0 1.4 %collective-permute-done.12 = bf16[2,256,128]{2,1,0:T(8,128)(2,1)S(1)} collective-permute-done((bf16[2,256,128]{2,1,0:T(8,128)(2,1)S(1)}, bf16[2,256,128]{2,1,0:T(8,128)(2,1)S(1)}, u32[]{:S(2)}, u32[]{:S(2)}) %collective-permute-start.12) | collective-permute-done | bytes 131104 | tf_op jit(solution)/shard_map/ppermute | solution.py:32
  51.4 1.0 %pad_maximum_fusion = f32[8,256,128]{2,1,0:T(8,128)} fusion(f32[2,256,128]{2,1,0:T(8,128)S(1)} %convert_add_fusion.1, f32[2,256,128]{2,1,0:T(8,128)S(1)} %convert_add_fusion.2, f32[4,256,128]{2,1,0:T(8,128)S(1)} %convert_add_fusion), kind=kLoop, calls=%fused_computation | loop fusion | flops 524288 | bytes 2097152 | tf_op jit(solution)/shard_map/concatenate | solution.py:444
  (38 shorter events, 8.1 us)
Async XLA Ops:
  0.0 2.3 %collective-permute-start = (bf16[8,256,128]{2,1,0:T(8,128)(2,1)}, bf16[8,256,128]{2,1,0:T(8,128)(2,1)S(1)}, u32[]{:S(2)}, u32[]{:S(2)}) collective-permute-start(bf16[8,256,128]{2,1,0:T(8,128)(2,1)} %bitcast.5), channel_id=1, source_target_pairs={{0,8},{8,0},{16,24},{24,16},{1,9},{9,1},{17,25},{25,17},{2,10},{10... | collective-permute-start | bytes 1572872 | tf_op jit(solution)/shard_map/ppermute | solution.py:32
  0.5 1.0 %copy-start = (bf16[8,16,16,128]{3,2,1,0:T(8,128)(2,1)S(1)}, bf16[8,16,16,128]{3,2,1,0:T(8,128)(2,1)}, u32[]{:S(2)}) copy-start(bf16[8,16,16,128]{3,2,1,0:T(8,128)(2,1)} %param.6) | copy-start | bytes 1572868
  4.5 5.9 %copy-start.1 = (bf16[16,16,16]{2,1,0:T(8,128)(2,1)S(1)}, bf16[16,16,16]{2,1,0:T(8,128)(2,1)}, u32[]{:S(2)}) copy-start(bf16[16,16,16]{2,1,0:T(8,128)(2,1)} %derivative_ref.1) | copy-start | bytes 24580
  4.5 5.9 %copy-start.2 = (s32[128,16]{0,1:T(8,128)S(1)}, s32[128,16]{0,1:T(8,128)}, u32[]{:S(2)}) copy-start(s32[128,16]{0,1:T(8,128)} %param.11) | copy-start | bytes 24580
  4.5 9.9 %collective-permute-start.1 = (bf16[4,256,128]{2,1,0:T(8,128)(2,1)S(1)}, bf16[4,256,128]{2,1,0:T(8,128)(2,1)S(1)}, u32[]{:S(2)}, u32[]{:S(2)}) collective-permute-start(bf16[4,256,128]{2,1,0:T(8,128)(2,1)S(1)} %shard_map.65.rest_0_), channel_id=1, source_target_pairs={{0,16},{8,24},{16,0},{24,8},{1,17},{9,25},{17,1},{25,9},{2,18},{10... | collective-permute-start | bytes 786440 | tf_op jit(solution)/shard_map/ppermute | solution.py:32
  10.3 9.5 %collective-permute-start.4 = (bf16[4,256,128]{2,1,0:T(8,128)(2,1)S(1)}, bf16[4,256,128]{2,1,0:T(8,128)(2,1)S(1)}, u32[]{:S(2)}, u32[]{:S(2)}) collective-permute-start(bf16[4,256,128]{2,1,0:T(8,128)(2,1)S(1)} %shard_map.67.after_ref), channel_id=1, source_target_pairs={{0,16},{8,24},{16,0},{24,8},{1,17},{9,25},{17,1},{25,9},{2,18},{10... | collective-permute-start | bytes 786440 | tf_op jit(solution)/shard_map/ppermute | solution.py:32
  14.5 8.2 %collective-permute-start.2 = (bf16[1040,128]{1,0:T(8,128)(2,1)S(1)}, bf16[1040,128]{1,0:T(8,128)(2,1)S(1)}, u32[]{:S(2)}, u32[]{:S(2)}) collective-permute-start(bf16[1040,128]{1,0:T(8,128)(2,1)S(1)} %pad_maximum_fusion.2.rest_0_.mixed_ref.refs_0_), channel_id=1, source_target_pairs={{0,2},{1,3},{2,0},{3,1},{4,6},{5,7},{6,4},{7,5},{8,10},{9,11},{10,... | collective-permute-start | bytes 798728 | tf_op jit(solution)/shard_map/ppermute | solution.py:32
  16.7 13.8 %collective-permute-start.3 = (bf16[1040,128]{1,0:T(8,128)(2,1)S(1)}, bf16[1040,128]{1,0:T(8,128)(2,1)S(1)}, u32[]{:S(2)}, u32[]{:S(2)}) collective-permute-start(bf16[1040,128]{1,0:T(8,128)(2,1)S(1)} %pad_maximum_fusion.2.rest_0_.mixed_ref.refs_0_), channel_id=1, source_target_pairs={{0,1},{1,0},{2,3},{3,2},{4,5},{5,4},{6,7},{7,6},{8,9},{9,8},{10,11... | collective-permute-start | bytes 798728 | tf_op jit(solution)/shard_map/ppermute | solution.py:32
  19.9 18.0 %collective-permute-start.6 = (bf16[1040,128]{1,0:T(8,128)(2,1)S(1)}, bf16[1040,128]{1,0:T(8,128)(2,1)S(1)}, u32[]{:S(2)}, u32[]{:S(2)}) collective-permute-start(bf16[1040,128]{1,0:T(8,128)(2,1)S(1)} %pad_maximum_fusion.1.after_ref.rest_0_.mixed_ref.value_ref.refs_0_), channel_id=1, source_target_pairs={{0,4},{1,5},{2,6},{3,7},{4,0},{5,1},{6,2},{7,3},{8,12},{9,13},{10,... | collective-permute-start | bytes 798728 | tf_op jit(solution)/shard_map/ppermute | solution.py:32
  22.7 9.0 %collective-permute-start.5 = (bf16[1040,128]{1,0:T(8,128)(2,1)S(1)}, bf16[1040,128]{1,0:T(8,128)(2,1)S(1)}, u32[]{:S(2)}, u32[]{:S(2)}) collective-permute-start(bf16[1040,128]{1,0:T(8,128)(2,1)S(1)} %shard_map.70), channel_id=1, source_target_pairs={{0,1},{1,0},{2,3},{3,2},{4,5},{5,4},{6,7},{7,6},{8,9},{9,8},{10,11... | collective-permute-start | bytes 798728 | tf_op jit(solution)/shard_map/ppermute | solution.py:32
  27.1 13.9 %collective-permute-start.8 = (bf16[1040,128]{1,0:T(8,128)(2,1)S(1)}, bf16[1040,128]{1,0:T(8,128)(2,1)S(1)}, u32[]{:S(2)}, u32[]{:S(2)}) collective-permute-start(bf16[1040,128]{1,0:T(8,128)(2,1)S(1)} %shard_map.77), channel_id=1, source_target_pairs={{0,1},{1,0},{2,3},{3,2},{4,5},{5,4},{6,7},{7,6},{8,9},{9,8},{10,11... | collective-permute-start | bytes 798728 | tf_op jit(solution)/shard_map/ppermute | solution.py:32
  32.8 15.5 %collective-permute-start.7 = (bf16[4,256,128]{2,1,0:T(8,128)(2,1)S(1)}, bf16[4,256,128]{2,1,0:T(8,128)(2,1)S(1)}, u32[]{:S(2)}, u32[]{:S(2)}) collective-permute-start(bf16[4,256,128]{2,1,0:T(8,128)(2,1)S(1)} %shard_map.74.after_ref), channel_id=1, source_target_pairs={{0,4},{1,5},{2,6},{3,7},{4,0},{5,1},{6,2},{7,3},{8,12},{9,13},{10,... | collective-permute-start | bytes 786440 | tf_op jit(solution)/shard_map/ppermute | solution.py:32
  37.9 5.1 %collective-permute-start.9 = (bf16[528,128]{1,0:T(8,128)(2,1)S(1)}, bf16[528,128]{1,0:T(8,128)(2,1)S(1)}, u32[]{:S(2)}, u32[]{:S(2)}) collective-permute-start(bf16[528,128]{1,0:T(8,128)(2,1)S(1)} %get-tuple-element.16), channel_id=1, source_target_pairs={{0,1},{1,0},{2,3},{3,2},{4,5},{5,4},{6,7},{7,6},{8,9},{9,8},{10,11... | collective-permute-start | bytes 405512 | tf_op jit(solution)/shard_map/ppermute | solution.py:32
  39.4 6.0 %collective-permute-start.10 = (bf16[512,128]{1,0:T(8,128)(2,1)S(1)}, bf16[512,128]{1,0:T(8,128)(2,1)S(1)}, u32[]{:S(2)}, u32[]{:S(2)}) collective-permute-start(bf16[512,128]{1,0:T(8,128)(2,1)S(1)} %get-tuple-element.15.refs_7_), channel_id=1, source_target_pairs={{0,1},{1,0},{2,3},{3,2},{4,5},{5,4},{6,7},{7,6},{8,9},{9,8},{10,11... | collective-permute-start | bytes 393224 | tf_op jit(solution)/shard_map/ppermute | solution.py:32
  43.8 6.1 %collective-permute-start.11 = (bf16[2,256,128]{2,1,0:T(8,128)(2,1)S(1)}, bf16[2,256,128]{2,1,0:T(8,128)(2,1)S(1)}, u32[]{:S(2)}, u32[]{:S(2)}) collective-permute-start(bf16[2,256,128]{2,1,0:T(8,128)(2,1)S(1)} %shard_map.79.refs_6_), channel_id=1, source_target_pairs={{0,2},{1,3},{2,0},{3,1},{4,6},{5,7},{6,4},{7,5},{8,10},{9,11},{10,... | collective-permute-start | bytes 393224 | tf_op jit(solution)/shard_map/ppermute | solution.py:32
  46.0 5.3 %collective-permute-start.12 = (bf16[2,256,128]{2,1,0:T(8,128)(2,1)S(1)}, bf16[2,256,128]{2,1,0:T(8,128)(2,1)S(1)}, u32[]{:S(2)}, u32[]{:S(2)}) collective-permute-start(bf16[2,256,128]{2,1,0:T(8,128)(2,1)S(1)} %shard_map.80.refs_7_), channel_id=1, source_target_pairs={{0,2},{1,3},{2,0},{3,1},{4,6},{5,7},{6,4},{7,5},{8,10},{9,11},{10,... | collective-permute-start | bytes 393224 | tf_op jit(solution)/shard_map/ppermute | solution.py:32

commit v11 on v10

--- a/solution.py
+++ b/solution.py
@@ -103,7 +103,7 @@
     return jnp.where(row == numbers, 1.0, 0.0).astype(BF16)
 
 
-def prepare_kernel(derivative_ref, columns_ref, after_ref, local_k_ref, remote_k_ref, local_hot_ref, ids_ref):
+def prepare_kernel(derivative_ref, columns_ref, after_ref, local_k_ref, remote_k_ref, local_hot_ref):
     bonds, orbital, _ = derivative_ref.shape
     square = orbital * orbital
     atoms = columns_ref.shape[1]
@@ -137,8 +137,12 @@
         local_hot_ref[bond * atoms : (bond + 1) * atoms, :] = hot(
             columns_ref[bond : bond + 1, :] - first, atoms
         )
+
+
+def ids_kernel(columns_ref, ids_ref):
+    bonds, atoms = columns_ref.shape
     rows = []
-    for bond in range(local_bonds, bonds):
+    for bond in range(bonds - REMOTE_BONDS, bonds):
         number = columns_ref[bond : bond + 1, :]
         rows += [number // atoms, number % atoms]
     place = lax.broadcasted_iota(jnp.int32, ids_ref.shape, 0)
@@ -303,15 +307,14 @@
                 jax.ShapeDtypeStruct((square, local_bonds * square), BF16),
                 jax.ShapeDtypeStruct((square, REMOTE_BONDS * square), BF16),
                 jax.ShapeDtypeStruct((local_bonds * atoms, atoms), BF16),
-                jax.ShapeDtypeStruct((ID_ROWS, atoms), BF16),
             ),
             in_specs=[VMEM, VMEM, ANY],
-            out_specs=(VMEM,) * 4,
+            out_specs=(VMEM,) * 3,
             compiler_params=params(),
             cost_estimate=cost(2e9, 3e6),
         )(derivative, columns, after)
 
-    def local_sum(chunk, after):
+    def local_sum(chunk, after, flops=2e9):
         return pl.pallas_call(
             local_kernel,
             out_shape=jax.ShapeDtypeStruct((sizes[chunk], square, atoms), F32),
@@ -321,7 +324,7 @@
                 pltpu.VMEM((local_bonds * square, min(2, sizes[chunk]) * atoms), BF16)
             ],
             compiler_params=params(),
-            cost_estimate=cost(2e9, 3e6),
+            cost_estimate=cost(flops, 3e6),
         )(mixed[chunk], local_hot, local_k, *after)
 
     own, arrived = [], []
@@ -329,16 +332,28 @@
     for chunk in range(chunks):
         away = [mix(group, chunk, BF16, after) for group in range(1, pairs)]
         arrived.append([swap(value, "energy", 2 * group) for group, value in enumerate(away, 1)])
-        if chunk == 0:
-            own.append(mix(0, chunk, F32, away[:1]))
-            after = own[-1:]
-        else:
-            local_k, remote_k, local_hot, ids = prepare(away[0])
+        own.append(mix(0, chunk, F32, away[:1]))
+        after = own[-1:]
+    ids = pl.pallas_call(
+        ids_kernel,
+        out_shape=jax.ShapeDtypeStruct((ID_ROWS, atoms), BF16),
+        in_specs=[VMEM],
+        out_specs=VMEM,
+        compiler_params=params(),
+        cost_estimate=cost(1e6, 1e6),
+    )(columns)
     mixed = []
     for chunk in range(chunks):
+        total = own[chunk]
         if chunk > 0:
-            own.append(mix(0, chunk, F32, mixed[-1:] + [local_hot]))
-        total = own[chunk]
+            total = pl.pallas_call(
+                copy_kernel,
+                out_shape=jax.ShapeDtypeStruct(total.shape, total.dtype),
+                in_specs=[VMEM, ANY],
+                out_specs=VMEM,
+                compiler_params=params(),
+                cost_estimate=cost(1e6, 1e6),
+            )(total, mixed[-1])
         for received in arrived[chunk]:
             total = total + received.astype(F32)
         mixed.append(jnp.concatenate([total.astype(BF16).reshape(-1, atoms), ids], 0))
@@ -379,14 +394,14 @@
             cost_estimate=cost(1e9, 3e6),
         )(*sources, hots, remote_k, after)
 
-    def stay_sum(count, skip, sources, offsets, hots, local, after):
+    def stay_sum(count, skip, sources, offsets, hots, local, after, flops):
         return pl.pallas_call(
             functools.partial(stay_kernel, offsets, skip),
             out_shape=jax.ShapeDtypeStruct((count, square, atoms), F32),
             in_specs=[VMEM] * (len(sources) + 3) + [ANY] * len(after),
             out_specs=VMEM,
             compiler_params=params(),
-            cost_estimate=cost(4e9, 3e6),
+            cost_estimate=cost(flops, 3e6),
         )(*sources, hots, remote_k, local, *after)
 
     def send(values, masks):
@@ -397,8 +412,8 @@
     far = [outer] + send([outer] * len(high), high)
     [turned] = ordered(across, [(0, sizes[0] * square)], outer)
     near = [inner, across, beside] + send([turned], [1])
-    local_inner = local_sum(0, [outer])
-    local_outer = local_sum(1, [local_inner])
+    local_k, remote_k, local_hot = prepare(turned)
+    local_inner = local_sum(0, [])
     far_beside = send(ordered(outer, [(0, sizes[1] * square)], local_inner), [1])
     straight = [0] * len(near)
     counts = [sizes[1] - sizes[1] // 2, sizes[1] // 2]
@@ -410,12 +425,12 @@
         steps = [[value[index] for value in passed] for index in range(len(pieces))]
         return passed[0][-1], [send(values, [1] * len(values)) for values in steps]
 
-    behind = local_outer
+    behind = local_inner
     near_hots = one_hots(near, high, behind)
     near_away = away_sums(sizes[0], near, straight, near_hots, high, behind)
     near_back = send(near_away, high)
     behind, far_next = pass_far(near_away[0])
-    stay_inner = stay_sum(sizes[0], 0, near, straight, near_hots, local_inner, [behind])
+    stay_inner = stay_sum(sizes[0], 0, near, straight, near_hots, local_inner, [behind], 4e9)
     after = stay_inner
     far_hots = None
     far_away, far_lists = [], []
@@ -428,11 +443,13 @@
         after = away[0]
         far_away.append(swap(away[0], "atom", 2))
         far_lists.append((sources, offsets))
+    local_outer = local_sum(1, [after], 1e6)
     results, arrivals = [stay_inner], [near_back]
     for index, (sources, offsets) in enumerate(far_lists):
         after = stay_sum(
             counts[index], skips[index], sources, offsets, far_hots, local_outer,
             [after],
+            1e6,
         )
         results.append(after)
         arrivals.append([far_away[index]])

time: 52.6 us -> 55.1 us (1.048)
  starting transfers between devices: 19.2 us -> 22.8 us
  waiting for transfers between devices: 9.22 us -> 8.2 us
    ppermute x13, starting transfers between devices: 19.2 us -> 22.8 us  [swap(): return lax.ppermute(value, axis, [(i, i ^ mask) for i in range(count)])]
    ppermute x13, waiting for transfers between devices: 9.22 us -> 8.2 us  [swap(): return lax.ppermute(value, axis, [(i, i ^ mask) for i in range(count)])]
  transfers between devices with their start and end apart: 13 -> 13, of which waited for: 6 -> 5; matrix products, arithmetic and copies ran while one was open for 2% -> 2% of each run, Pallas kernels for 35% -> 34%
where the time goes in v11:
time: 55.1 us; the launch traced here: 54.9 us
  starting transfers between devices  22.8 us (41%)
  Pallas kernels  19.8 us (36%)
  waiting for transfers between devices  8.2 us (15%)
  other arithmetic  2.07 us (4%)
  local copies, waits for them, and re-layouts  1.78 us (3%)
    ppermute x13, starting transfers between devices, swap(): return lax.ppermute(value, axis, [(i, i ^ mask) for i in range(count)])  22.8 us
    ppermute x13, waiting for transfers between devices, swap(): return lax.ppermute(value, axis, [(i, i ^ mask) for i in range(count)])  8.2 us
    pallas_call x4, Pallas kernels, mix(): pl.pallas_call(functools.partial(mix_kernel, group, firsts[chunk]), out_s...  5.98 us
    pallas_call x2, Pallas kernels, local_sum(): pl.pallas_call(local_kernel, out_shape=jax.ShapeDtypeStruct((sizes[chunk]...  5.54 us
    pallas_call x1, Pallas kernels, prepare(): pl.pallas_call(prepare_kernel, out_shape=(jax.ShapeDtypeStruct((square, l...  3.35 us
    pallas_call x3, Pallas kernels, stay_sum(): pl.pallas_call(functools.partial(stay_kernel, offsets, skip), out_shape=j...  2.3 us
    pallas_call x3, Pallas kernels, away_sums(): pl.pallas_call(functools.partial(away_kernel, offsets), out_shape=(block,...  2.29 us
  transfers between devices with their start and end apart: 13, of which 5 were waited for; matrix products, arithmetic and copies ran while one was open for 2% of the time, Pallas kernels for 34%

profile of v11, /device:TPU:0, one launch (start us, length us, event | category | flops | bytes accessed | tf_op | source)
XLA Modules:
  0.0 54.9 jit_solution(744098191316368268)
XLA Ops:
  0.5 1.0 %copy-done = bf16[8,16,16,128]{3,2,1,0:T(8,128)(2,1)S(1)} copy-done((bf16[8,16,16,128]{3,2,1,0:T(8,128)(2,1)S(1)}, bf16[8,16,16,128]{3,2,1,0:T(8,128)(2,1)}, u32[]{:S(2)}) %copy-start) | copy-done | bytes 524312
  3.0 1.4 %shard_map.65.rest_0_ = bf16[4,256,128]{2,1,0:T(8,128)(2,1)S(1)} custom-call(s32[8,128]{1,0:T(8,128)S(1)} %broadcast_in_dim.2.shift_rows_ref, bf16[16,128]{1,0:T(8,128)(2,1)S(1)} %pad_maximum_fusion.3.coupling_ref, bf16[8,256,128]{2,1,0:T(8,128)(2,1)S(1)} %shard_map.64.own_ref, bf16[8,256,128]{2,1,0:T(8,128)(2,1)S(1)} %collective-permute-done.mate_ref), custom_call_target="tpu_custom_call" | custom-call | flops 500000000 | bytes 1000000 | tf_op jit(solution)/shard_map/pallas_call | solution.py:289
  4.5 2.8 %collective-permute-start.1 = (bf16[4,256,128]{2,1,0:T(8,128)(2,1)S(1)}, bf16[4,256,128]{2,1,0:T(8,128)(2,1)S(1)}, u32[]{:S(2)}, u32[]{:S(2)}) collective-permute-start(bf16[4,256,128]{2,1,0:T(8,128)(2,1)S(1)} %shard_map.65.rest_0_), channel_id=1, source_target_pairs={{0,16},{8,24},{16,0},{24,8},{1,17},{9,25},{17,1},{25,9},{2,18},{10... | collective-permute-start | bytes 786440 | tf_op jit(solution)/shard_map/ppermute | solution.py:32
  7.3 1.5 %shard_map.66.rest_0_ = f32[4,256,128]{2,1,0:T(8,128)S(1)} custom-call(s32[8,128]{1,0:T(8,128)S(1)} %broadcast_in_dim.2.shift_rows_ref, bf16[16,128]{1,0:T(8,128)(2,1)S(1)} %pad_maximum_fusion.3.coupling_ref, bf16[8,256,128]{2,1,0:T(8,128)(2,1)S(1)} %shard_map.64.own_ref, bf16[8,256,128]{2,1,0:T(8,128)(2,1)S(1)} %collective-permute-done.mate_ref, ...), custom_call_target="tpu_custom_call" | custom-call | flops 500000000 | bytes 1000000 | tf_op jit(solution)/shard_map/pallas_call | solution.py:289
  8.9 1.4 %shard_map.68.rest_0_ = bf16[4,256,128]{2,1,0:T(8,128)(2,1)S(1)} custom-call(s32[8,128]{1,0:T(8,128)S(1)} %broadcast_in_dim.2.shift_rows_ref, bf16[16,128]{1,0:T(8,128)(2,1)S(1)} %pad_maximum_fusion.3.coupling_ref, bf16[8,256,128]{2,1,0:T(8,128)(2,1)S(1)} %shard_map.64.own_ref, bf16[8,256,128]{2,1,0:T(8,128)(2,1)S(1)} %collective-permute-done.mate_ref, ...), custom_call_target="tpu_custom_call" | custom-call | flops 500000000 | bytes 1000000 | tf_op jit(solution)/shard_map/pallas_call | solution.py:289
  10.4 1.6 %shard_map.69.value_ref = f32[4,256,128]{2,1,0:T(8,128)S(1)} custom-call(s32[8,128]{1,0:T(8,128)S(1)} %broadcast_in_dim.2.shift_rows_ref, bf16[16,128]{1,0:T(8,128)(2,1)S(1)} %pad_maximum_fusion.3.coupling_ref, bf16[8,256,128]{2,1,0:T(8,128)(2,1)S(1)} %shard_map.64.own_ref, bf16[8,256,128]{2,1,0:T(8,128)(2,1)S(1)} %collective-permute-done.mate_ref, ...), custom_call_target="tpu_custom_call" | custom-call | flops 500000000 | bytes 1000000 | tf_op jit(solution)/shard_map/pallas_call | solution.py:289
  12.0 2.4 %collective-permute-done.1 = bf16[4,256,128]{2,1,0:T(8,128)(2,1)S(1)} collective-permute-done((bf16[4,256,128]{2,1,0:T(8,128)(2,1)S(1)}, bf16[4,256,128]{2,1,0:T(8,128)(2,1)S(1)}, u32[]{:S(2)}, u32[]{:S(2)}) %collective-permute-start.1) | collective-permute-done | bytes 262176 | tf_op jit(solution)/shard_map/ppermute | solution.py:32
  14.5 2.2 %collective-permute-start.2 = (bf16[1040,128]{1,0:T(8,128)(2,1)S(1)}, bf16[1040,128]{1,0:T(8,128)(2,1)S(1)}, u32[]{:S(2)}, u32[]{:S(2)}) collective-permute-start(bf16[1040,128]{1,0:T(8,128)(2,1)S(1)} %pad_maximum_fusion.2.rest_0_.mixed_ref.refs_0_), channel_id=1, source_target_pairs={{0,2},{1,3},{2,0},{3,1},{4,6},{5,7},{6,4},{7,5},{8,10},{9,11},{10,... | collective-permute-start | bytes 798728 | tf_op jit(solution)/shard_map/ppermute | solution.py:32
  16.7 1.5 %collective-permute-start.3 = (bf16[1040,128]{1,0:T(8,128)(2,1)S(1)}, bf16[1040,128]{1,0:T(8,128)(2,1)S(1)}, u32[]{:S(2)}, u32[]{:S(2)}) collective-permute-start(bf16[1040,128]{1,0:T(8,128)(2,1)S(1)} %pad_maximum_fusion.2.rest_0_.mixed_ref.refs_0_), channel_id=1, source_target_pairs={{0,1},{1,0},{2,3},{3,2},{4,5},{5,4},{6,7},{7,6},{8,9},{9,8},{10,11... | collective-permute-start | bytes 798728 | tf_op jit(solution)/shard_map/ppermute | solution.py:32
  18.2 1.4 %collective-permute-done.4 = bf16[4,256,128]{2,1,0:T(8,128)(2,1)S(1)} collective-permute-done((bf16[4,256,128]{2,1,0:T(8,128)(2,1)S(1)}, bf16[4,256,128]{2,1,0:T(8,128)(2,1)S(1)}, u32[]{:S(2)}, u32[]{:S(2)}) %collective-permute-start.4) | collective-permute-done | bytes 262176 | tf_op jit(solution)/shard_map/ppermute | solution.py:32
  19.7 2.9 %collective-permute-start.6 = (bf16[1040,128]{1,0:T(8,128)(2,1)S(1)}, bf16[1040,128]{1,0:T(8,128)(2,1)S(1)}, u32[]{:S(2)}, u32[]{:S(2)}) collective-permute-start(bf16[1040,128]{1,0:T(8,128)(2,1)S(1)} %pad_maximum_fusion.1.after_ref.value_ref.refs_0_.mixed_ref), channel_id=1, source_target_pairs={{0,4},{1,5},{2,6},{3,7},{4,0},{5,1},{6,2},{7,3},{8,12},{9,13},{10,... | collective-permute-start | bytes 798728 | tf_op jit(solution)/shard_map/ppermute | solution.py:32
  22.7 1.6 %collective-permute-start.5 = (bf16[1040,128]{1,0:T(8,128)(2,1)S(1)}, bf16[1040,128]{1,0:T(8,128)(2,1)S(1)}, u32[]{:S(2)}, u32[]{:S(2)}) collective-permute-start(bf16[1040,128]{1,0:T(8,128)(2,1)S(1)} %shard_map.71.after_ref), channel_id=1, source_target_pairs={{0,1},{1,0},{2,3},{3,2},{4,5},{5,4},{6,7},{7,6},{8,9},{9,8},{10,11... | collective-permute-start | bytes 798728 | tf_op jit(solution)/shard_map/ppermute | solution.py:32
  24.2 3.3 %shard_map.72 = (bf16[256,3584]{1,0:T(8,128)(2,1)S(1)}, bf16[256,512]{1,0:T(8,128)(2,1)S(1)}, bf16[1792,128]{1,0:T(8,128)(2,1)S(1)}) custom-call(bf16[16,16,16]{2,1,0:T(8,128)(2,1)S(1)} %copy-done.2, s32[16,128]{1,0:T(8,128)S(1)} %bitcast.8, bf16[1040,128]{1,0:T(8,128)(2,1)S(1)} %shard_map.71.after_ref), custom_call_target="tpu_custom_call" | custom-call | flops 2000000000 | bytes 3000000 | tf_op jit(solution)/shard_map/pallas_call | solution.py:304
  27.6 2.8 %shard_map.73.refs_4_.refs_6_.after_ref = f32[4,256,128]{2,1,0:T(8,128)S(1)} custom-call(bf16[1040,128]{1,0:T(8,128)(2,1)S(1)} %pad_maximum_fusion.2.rest_0_.mixed_ref.refs_0_, bf16[1792,128]{1,0:T(8,128)(2,1)S(1)} %get-tuple-element.10.hot_ref, bf16[256,3584]{1,0:T(8,128)(2,1)S(1)} %get-tuple-element.11.k_ref), custom_call_target="tpu_custom_call" | custom-call | flops 2000000000 | bytes 3000000 | tf_op jit(solution)/shard_map/pallas_call | solution.py:318
  31.1 1.0 %shard_map.75.after_ref = bf16[4,256,128]{2,1,0:T(8,128)(2,1)S(1)} custom-call(bf16[1040,128]{1,0:T(8,128)(2,1)S(1)} %pad_maximum_fusion.2.rest_0_.mixed_ref.refs_0_, bf16[1040,128]{1,0:T(8,128)(2,1)S(1)} %collective-permute-done.2.value_ref.refs_1_, bf16[1040,128]{1,0:T(8,128)(2,1)S(1)} %collective-permute-done.3.refs_2_, ...), custom_call_target="tpu_custom_call" | custom-call | flops 1000000000 | bytes 3000000 | tf_op jit(solution)/shard_map/pallas_call | solution.py:388
  32.1 2.3 %collective-permute-start.7 = (bf16[4,256,128]{2,1,0:T(8,128)(2,1)S(1)}, bf16[4,256,128]{2,1,0:T(8,128)(2,1)S(1)}, u32[]{:S(2)}, u32[]{:S(2)}) collective-permute-start(bf16[4,256,128]{2,1,0:T(8,128)(2,1)S(1)} %shard_map.75.after_ref), channel_id=1, source_target_pairs={{0,4},{1,5},{2,6},{3,7},{4,0},{5,1},{6,2},{7,3},{8,12},{9,13},{10,... | collective-permute-start | bytes 786440 | tf_op jit(solution)/shard_map/ppermute | solution.py:32
  34.6 1.5 %collective-permute-start.9 = (bf16[528,128]{1,0:T(8,128)(2,1)S(1)}, bf16[528,128]{1,0:T(8,128)(2,1)S(1)}, u32[]{:S(2)}, u32[]{:S(2)}) collective-permute-start(bf16[528,128]{1,0:T(8,128)(2,1)S(1)} %get-tuple-element.14), channel_id=1, source_target_pairs={{0,1},{1,0},{2,3},{3,2},{4,5},{5,4},{6,7},{7,6},{8,9},{9,8},{10,11... | collective-permute-start | bytes 405512 | tf_op jit(solution)/shard_map/ppermute | solution.py:32
  36.7 1.0 %shard_map.77.refs_4_.refs_6_ = f32[4,256,128]{2,1,0:T(8,128)S(1)} custom-call(bf16[1040,128]{1,0:T(8,128)(2,1)S(1)} %pad_maximum_fusion.2.rest_0_.mixed_ref.refs_0_, bf16[1040,128]{1,0:T(8,128)(2,1)S(1)} %collective-permute-done.2.value_ref.refs_1_, bf16[1040,128]{1,0:T(8,128)(2,1)S(1)} %collective-permute-done.3.refs_2_, ...), custom_call_target="tpu_custom_call" | custom-call | flops 4000000000 | bytes 3000000 | tf_op jit(solution)/shard_map/pallas_call | solution.py:398
  37.7 1.4 %collective-permute-done.8.refs_2_ = bf16[1040,128]{1,0:T(8,128)(2,1)S(1)} collective-permute-done((bf16[1040,128]{1,0:T(8,128)(2,1)S(1)}, bf16[1040,128]{1,0:T(8,128)(2,1)S(1)}, u32[]{:S(2)}, u32[]{:S(2)}) %collective-permute-start.8) | collective-permute-done | bytes 266272 | tf_op jit(solution)/shard_map/ppermute | solution.py:32
  39.1 2.8 %collective-permute-done.9.refs_3_ = bf16[528,128]{1,0:T(8,128)(2,1)S(1)} collective-permute-done((bf16[528,128]{1,0:T(8,128)(2,1)S(1)}, bf16[528,128]{1,0:T(8,128)(2,1)S(1)}, u32[]{:S(2)}, u32[]{:S(2)}) %collective-permute-start.9) | collective-permute-done | bytes 135200 | tf_op jit(solution)/shard_map/ppermute | solution.py:32
  42.7 5.5 %collective-permute-start.11 = (bf16[2,256,128]{2,1,0:T(8,128)(2,1)S(1)}, bf16[2,256,128]{2,1,0:T(8,128)(2,1)S(1)}, u32[]{:S(2)}, u32[]{:S(2)}) collective-permute-start(bf16[2,256,128]{2,1,0:T(8,128)(2,1)S(1)} %shard_map.80.refs_6_), channel_id=1, source_target_pairs={{0,2},{1,3},{2,0},{3,1},{4,6},{5,7},{6,4},{7,5},{8,10},{9,11},{10,... | collective-permute-start | bytes 393224 | tf_op jit(solution)/shard_map/ppermute | solution.py:32
  48.8 0.8 %collective-permute-start.12 = (bf16[2,256,128]{2,1,0:T(8,128)(2,1)S(1)}, bf16[2,256,128]{2,1,0:T(8,128)(2,1)S(1)}, u32[]{:S(2)}, u32[]{:S(2)}) collective-permute-start(bf16[2,256,128]{2,1,0:T(8,128)(2,1)S(1)} %shard_map.81.rest_0_.refs_7_), channel_id=1, source_target_pairs={{0,2},{1,3},{2,0},{3,1},{4,6},{5,7},{6,4},{7,5},{8,10},{9,11},{10,... | collective-permute-start | bytes 393224 | tf_op jit(solution)/shard_map/ppermute | solution.py:32
  49.6 2.8 %shard_map.82.refs_6_ = f32[4,256,128]{2,1,0:T(8,128)S(1)} custom-call(bf16[1040,128]{1,0:T(8,128)(2,1)S(1)} %pad_maximum_fusion.1.after_ref.value_ref.refs_0_.mixed_ref, bf16[1792,128]{1,0:T(8,128)(2,1)S(1)} %get-tuple-element.10.hot_ref, bf16[256,3584]{1,0:T(8,128)(2,1)S(1)} %get-tuple-element.11.k_ref, bf16[2,256,128]{2,1,0:T(8,128)(2,1)S(1)} %shard_map.81.rest_0_.refs_7_), custom_call_target="tpu_custom_call" | custom-call | flops 1000000 | bytes 3000000 | tf_op jit(solution)/shard_map/pallas_call | solution.py:318
  53.9 1.0 %pad_maximum_fusion = f32[8,256,128]{2,1,0:T(8,128)} fusion(f32[2,256,128]{2,1,0:T(8,128)S(1)} %convert_add_fusion.1, f32[2,256,128]{2,1,0:T(8,128)S(1)} %convert_add_fusion.2, f32[4,256,128]{2,1,0:T(8,128)S(1)} %convert_add_fusion), kind=kLoop, calls=%fused_computation | loop fusion | flops 524288 | bytes 2097152 | tf_op jit(solution)/shard_map/concatenate | solution.py:461
  (40 shorter events, 6.6 us)
Async XLA Ops:
  0.0 2.3 %collective-permute-start = (bf16[8,256,128]{2,1,0:T(8,128)(2,1)}, bf16[8,256,128]{2,1,0:T(8,128)(2,1)S(1)}, u32[]{:S(2)}, u32[]{:S(2)}) collective-permute-start(bf16[8,256,128]{2,1,0:T(8,128)(2,1)} %bitcast.5), channel_id=1, source_target_pairs={{0,8},{8,0},{16,24},{24,16},{1,9},{9,1},{17,25},{25,17},{2,10},{10... | collective-permute-start | bytes 1572872 | tf_op jit(solution)/shard_map/ppermute | solution.py:32
  0.5 1.0 %copy-start = (bf16[8,16,16,128]{3,2,1,0:T(8,128)(2,1)S(1)}, bf16[8,16,16,128]{3,2,1,0:T(8,128)(2,1)}, u32[]{:S(2)}) copy-start(bf16[8,16,16,128]{3,2,1,0:T(8,128)(2,1)} %param.6) | copy-start | bytes 1572868
  1.5 5.8 %copy-start.1 = (s32[128,16]{0,1:T(8,128)S(1)}, s32[128,16]{0,1:T(8,128)}, u32[]{:S(2)}) copy-start(s32[128,16]{0,1:T(8,128)} %param.11) | copy-start | bytes 24580
  4.5 9.9 %collective-permute-start.1 = (bf16[4,256,128]{2,1,0:T(8,128)(2,1)S(1)}, bf16[4,256,128]{2,1,0:T(8,128)(2,1)S(1)}, u32[]{:S(2)}, u32[]{:S(2)}) collective-permute-start(bf16[4,256,128]{2,1,0:T(8,128)(2,1)S(1)} %shard_map.65.rest_0_), channel_id=1, source_target_pairs={{0,16},{8,24},{16,0},{24,8},{1,17},{9,25},{17,1},{25,9},{2,18},{10... | collective-permute-start | bytes 786440 | tf_op jit(solution)/shard_map/ppermute | solution.py:32
  10.3 9.3 %collective-permute-start.4 = (bf16[4,256,128]{2,1,0:T(8,128)(2,1)S(1)}, bf16[4,256,128]{2,1,0:T(8,128)(2,1)S(1)}, u32[]{:S(2)}, u32[]{:S(2)}) collective-permute-start(bf16[4,256,128]{2,1,0:T(8,128)(2,1)S(1)} %shard_map.68.rest_0_), channel_id=1, source_target_pairs={{0,16},{8,24},{16,0},{24,8},{1,17},{9,25},{17,1},{25,9},{2,18},{10... | collective-permute-start | bytes 786440 | tf_op jit(solution)/shard_map/ppermute | solution.py:32
  14.5 9.8 %copy-start.2 = (bf16[16,16,16]{2,1,0:T(8,128)(2,1)S(1)}, bf16[16,16,16]{2,1,0:T(8,128)(2,1)}, u32[]{:S(2)}) copy-start(bf16[16,16,16]{2,1,0:T(8,128)(2,1)} %derivative_ref.1) | copy-start | bytes 24580
  14.5 8.2 %collective-permute-start.2 = (bf16[1040,128]{1,0:T(8,128)(2,1)S(1)}, bf16[1040,128]{1,0:T(8,128)(2,1)S(1)}, u32[]{:S(2)}, u32[]{:S(2)}) collective-permute-start(bf16[1040,128]{1,0:T(8,128)(2,1)S(1)} %pad_maximum_fusion.2.rest_0_.mixed_ref.refs_0_), channel_id=1, source_target_pairs={{0,2},{1,3},{2,0},{3,1},{4,6},{5,7},{6,4},{7,5},{8,10},{9,11},{10,... | collective-permute-start | bytes 798728 | tf_op jit(solution)/shard_map/ppermute | solution.py:32
  16.7 14.3 %collective-permute-start.3 = (bf16[1040,128]{1,0:T(8,128)(2,1)S(1)}, bf16[1040,128]{1,0:T(8,128)(2,1)S(1)}, u32[]{:S(2)}, u32[]{:S(2)}) collective-permute-start(bf16[1040,128]{1,0:T(8,128)(2,1)S(1)} %pad_maximum_fusion.2.rest_0_.mixed_ref.refs_0_), channel_id=1, source_target_pairs={{0,1},{1,0},{2,3},{3,2},{4,5},{5,4},{6,7},{7,6},{8,9},{9,8},{10,11... | collective-permute-start | bytes 798728 | tf_op jit(solution)/shard_map/ppermute | solution.py:32
  19.7 14.8 %collective-permute-start.6 = (bf16[1040,128]{1,0:T(8,128)(2,1)S(1)}, bf16[1040,128]{1,0:T(8,128)(2,1)S(1)}, u32[]{:S(2)}, u32[]{:S(2)}) collective-permute-start(bf16[1040,128]{1,0:T(8,128)(2,1)S(1)} %pad_maximum_fusion.1.after_ref.value_ref.refs_0_.mixed_ref), channel_id=1, source_target_pairs={{0,4},{1,5},{2,6},{3,7},{4,0},{5,1},{6,2},{7,3},{8,12},{9,13},{10,... | collective-permute-start | bytes 798728 | tf_op jit(solution)/shard_map/ppermute | solution.py:32
  22.7 8.3 %collective-permute-start.5 = (bf16[1040,128]{1,0:T(8,128)(2,1)S(1)}, bf16[1040,128]{1,0:T(8,128)(2,1)S(1)}, u32[]{:S(2)}, u32[]{:S(2)}) collective-permute-start(bf16[1040,128]{1,0:T(8,128)(2,1)S(1)} %shard_map.71.after_ref), channel_id=1, source_target_pairs={{0,1},{1,0},{2,3},{3,2},{4,5},{5,4},{6,7},{7,6},{8,9},{9,8},{10,11... | collective-permute-start | bytes 798728 | tf_op jit(solution)/shard_map/ppermute | solution.py:32
  30.4 8.7 %collective-permute-start.8 = (bf16[1040,128]{1,0:T(8,128)(2,1)S(1)}, bf16[1040,128]{1,0:T(8,128)(2,1)S(1)}, u32[]{:S(2)}, u32[]{:S(2)}) collective-permute-start(bf16[1040,128]{1,0:T(8,128)(2,1)S(1)} %shard_map.78), channel_id=1, source_target_pairs={{0,1},{1,0},{2,3},{3,2},{4,5},{5,4},{6,7},{7,6},{8,9},{9,8},{10,11... | collective-permute-start | bytes 798728 | tf_op jit(solution)/shard_map/ppermute | solution.py:32
  32.1 21.6 %collective-permute-start.7 = (bf16[4,256,128]{2,1,0:T(8,128)(2,1)S(1)}, bf16[4,256,128]{2,1,0:T(8,128)(2,1)S(1)}, u32[]{:S(2)}, u32[]{:S(2)}) collective-permute-start(bf16[4,256,128]{2,1,0:T(8,128)(2,1)S(1)} %shard_map.75.after_ref), channel_id=1, source_target_pairs={{0,4},{1,5},{2,6},{3,7},{4,0},{5,1},{6,2},{7,3},{8,12},{9,13},{10,... | collective-permute-start | bytes 786440 | tf_op jit(solution)/shard_map/ppermute | solution.py:32
  34.6 7.4 %collective-permute-start.9 = (bf16[528,128]{1,0:T(8,128)(2,1)S(1)}, bf16[528,128]{1,0:T(8,128)(2,1)S(1)}, u32[]{:S(2)}, u32[]{:S(2)}) collective-permute-start(bf16[528,128]{1,0:T(8,128)(2,1)S(1)} %get-tuple-element.14), channel_id=1, source_target_pairs={{0,1},{1,0},{2,3},{3,2},{4,5},{5,4},{6,7},{7,6},{8,9},{9,8},{10,11... | collective-permute-start | bytes 405512 | tf_op jit(solution)/shard_map/ppermute | solution.py:32
  36.0 12.1 %collective-permute-start.10 = (bf16[512,128]{1,0:T(8,128)(2,1)S(1)}, bf16[512,128]{1,0:T(8,128)(2,1)S(1)}, u32[]{:S(2)}, u32[]{:S(2)}) collective-permute-start(bf16[512,128]{1,0:T(8,128)(2,1)S(1)} %get-tuple-element.13.refs_7_), channel_id=1, source_target_pairs={{0,1},{1,0},{2,3},{3,2},{4,5},{5,4},{6,7},{7,6},{8,9},{9,8},{10,11... | collective-permute-start | bytes 393224 | tf_op jit(solution)/shard_map/ppermute | solution.py:32
  42.7 11.1 %collective-permute-start.11 = (bf16[2,256,128]{2,1,0:T(8,128)(2,1)S(1)}, bf16[2,256,128]{2,1,0:T(8,128)(2,1)S(1)}, u32[]{:S(2)}, u32[]{:S(2)}) collective-permute-start(bf16[2,256,128]{2,1,0:T(8,128)(2,1)S(1)} %shard_map.80.refs_6_), channel_id=1, source_target_pairs={{0,2},{1,3},{2,0},{3,1},{4,6},{5,7},{6,4},{7,5},{8,10},{9,11},{10,... | collective-permute-start | bytes 393224 | tf_op jit(solution)/shard_map/ppermute | solution.py:32
  48.8 5.0 %collective-permute-start.12 = (bf16[2,256,128]{2,1,0:T(8,128)(2,1)S(1)}, bf16[2,256,128]{2,1,0:T(8,128)(2,1)S(1)}, u32[]{:S(2)}, u32[]{:S(2)}) collective-permute-start(bf16[2,256,128]{2,1,0:T(8,128)(2,1)S(1)} %shard_map.81.rest_0_.refs_7_), channel_id=1, source_target_pairs={{0,2},{1,3},{2,0},{3,1},{4,6},{5,7},{6,4},{7,5},{8,10},{9,11},{10,... | collective-permute-start | bytes 393224 | tf_op jit(solution)/shard_map/ppermute | solution.py:32

commit v12 on v10

--- a/solution.py
+++ b/solution.py
@@ -410,11 +410,11 @@
         steps = [[value[index] for value in passed] for index in range(len(pieces))]
         return passed[0][-1], [send(values, [1] * len(values)) for values in steps]
 
-    behind = local_outer
+    behind, far_next = pass_far(local_outer)
     near_hots = one_hots(near, high, behind)
     near_away = away_sums(sizes[0], near, straight, near_hots, high, behind)
     near_back = send(near_away, high)
-    behind, far_next = pass_far(near_away[0])
+    behind = near_away[0]
     stay_inner = stay_sum(sizes[0], 0, near, straight, near_hots, local_inner, [behind])
     after = stay_inner
     far_hots = None

time: 52.6 us -> 54.3 us (1.032)
  waiting for transfers between devices: 9.22 us -> 13.4 us
  starting transfers between devices: 19.2 us -> 16.8 us
    ppermute x13, waiting for transfers between devices: 9.22 us -> 13.4 us  [swap(): return lax.ppermute(value, axis, [(i, i ^ mask) for i in range(count)])]
    ppermute x13, starting transfers between devices: 19.2 us -> 16.8 us  [swap(): return lax.ppermute(value, axis, [(i, i ^ mask) for i in range(count)])]
  transfers between devices with their start and end apart: 13 -> 13, of which waited for: 6 -> 5; matrix products, arithmetic and copies ran while one was open for 2% -> 2% of each run, Pallas kernels for 35% -> 34%
where the time goes in v12:
time: 54.3 us; the launch traced here: 54.1 us
  Pallas kernels  19.9 us (37%)
  starting transfers between devices  16.8 us (31%)
  waiting for transfers between devices  13.4 us (25%)
  other arithmetic  2.12 us (4%)
  local copies, waits for them, and re-layouts  1.78 us (3%)
    ppermute x13, starting transfers between devices, swap(): return lax.ppermute(value, axis, [(i, i ^ mask) for i in range(count)])  16.8 us
    ppermute x13, waiting for transfers between devices, swap(): return lax.ppermute(value, axis, [(i, i ^ mask) for i in range(count)])  13.4 us
    pallas_call x4, Pallas kernels, mix(): pl.pallas_call(functools.partial(mix_kernel, group, firsts[chunk]), out_s...  6.01 us
    pallas_call x2, Pallas kernels, local_sum(): pl.pallas_call(local_kernel, out_shape=jax.ShapeDtypeStruct((sizes[chunk]...  5.56 us
    pallas_call x1, Pallas kernels, prepare(): pl.pallas_call(prepare_kernel, out_shape=(jax.ShapeDtypeStruct((square, l...  3.36 us
    pallas_call x3, Pallas kernels, away_sums(): pl.pallas_call(functools.partial(away_kernel, offsets), out_shape=(block,...  2.3 us
    pallas_call x3, Pallas kernels, stay_sum(): pl.pallas_call(functools.partial(stay_kernel, offsets, skip), out_shape=j...  2.3 us
  transfers between devices with their start and end apart: 13, of which 5 were waited for; matrix products, arithmetic and copies ran while one was open for 2% of the time, Pallas kernels for 34%

profile of v12, /device:TPU:0, one launch (start us, length us, event | category | flops | bytes accessed | tf_op | source)
XLA Modules:
  0.0 54.1 jit_solution(2543782625860291093)
XLA Ops:
  0.5 1.0 %copy-done = bf16[8,16,16,128]{3,2,1,0:T(8,128)(2,1)S(1)} copy-done((bf16[8,16,16,128]{3,2,1,0:T(8,128)(2,1)S(1)}, bf16[8,16,16,128]{3,2,1,0:T(8,128)(2,1)}, u32[]{:S(2)}) %copy-start) | copy-done | bytes 524312
  1.5 0.8 %fusion = (bf16[8,128]{1,0:T(8,128)(2,1)S(1)}, bf16[8,128]{1,0:T(8,128)(2,1)S(1)}) fusion(f32[8,128]{1,0:T(8,128)} %param.8, f32[8]{0:T(128)} %param.9), kind=kLoop, calls=%fused_computation.10 | loop fusion | flops 4096 | bytes 8224 | tf_op jit(solution)/shard_map/convert
  2.3 0.7 %broadcast_in_dim.2.shift_rows_ref = s32[8,128]{1,0:T(8,128)S(1)} broadcast(s32[8]{0:T(128)} %param.10), dimensions={0} | broadcast | bytes 4128 | tf_op jit(solution)/shard_map/broadcast_in_dim | solution.py:274
  3.0 1.4 %shard_map.65.rest_0_ = bf16[4,256,128]{2,1,0:T(8,128)(2,1)S(1)} custom-call(s32[8,128]{1,0:T(8,128)S(1)} %broadcast_in_dim.2.shift_rows_ref, bf16[16,128]{1,0:T(8,128)(2,1)S(1)} %pad_maximum_fusion.3.coupling_ref, bf16[8,256,128]{2,1,0:T(8,128)(2,1)S(1)} %shard_map.64.own_ref, bf16[8,256,128]{2,1,0:T(8,128)(2,1)S(1)} %collective-permute-done.mate_ref), custom_call_target="tpu_custom_call" | custom-call | flops 500000000 | bytes 1000000 | tf_op jit(solution)/shard_map/pallas_call | solution.py:285
  4.5 2.8 %collective-permute-start.1 = (bf16[4,256,128]{2,1,0:T(8,128)(2,1)S(1)}, bf16[4,256,128]{2,1,0:T(8,128)(2,1)S(1)}, u32[]{:S(2)}, u32[]{:S(2)}) collective-permute-start(bf16[4,256,128]{2,1,0:T(8,128)(2,1)S(1)} %shard_map.65.rest_0_), channel_id=1, source_target_pairs={{0,16},{8,24},{16,0},{24,8},{1,17},{9,25},{17,1},{25,9},{2,18},{10... | collective-permute-start | bytes 786440 | tf_op jit(solution)/shard_map/ppermute | solution.py:32
  7.3 1.6 %shard_map.66.rest_0_ = f32[4,256,128]{2,1,0:T(8,128)S(1)} custom-call(s32[8,128]{1,0:T(8,128)S(1)} %broadcast_in_dim.2.shift_rows_ref, bf16[16,128]{1,0:T(8,128)(2,1)S(1)} %pad_maximum_fusion.3.coupling_ref, bf16[8,256,128]{2,1,0:T(8,128)(2,1)S(1)} %shard_map.64.own_ref, bf16[8,256,128]{2,1,0:T(8,128)(2,1)S(1)} %collective-permute-done.mate_ref, ...), custom_call_target="tpu_custom_call" | custom-call | flops 500000000 | bytes 1000000 | tf_op jit(solution)/shard_map/pallas_call | solution.py:285
  8.9 1.4 %shard_map.67.after_ref = bf16[4,256,128]{2,1,0:T(8,128)(2,1)S(1)} custom-call(s32[8,128]{1,0:T(8,128)S(1)} %broadcast_in_dim.2.shift_rows_ref, bf16[16,128]{1,0:T(8,128)(2,1)S(1)} %pad_maximum_fusion.3.coupling_ref, bf16[8,256,128]{2,1,0:T(8,128)(2,1)S(1)} %shard_map.64.own_ref, bf16[8,256,128]{2,1,0:T(8,128)(2,1)S(1)} %collective-permute-done.mate_ref, ...), custom_call_target="tpu_custom_call" | custom-call | flops 500000000 | bytes 1000000 | tf_op jit(solution)/shard_map/pallas_call | solution.py:285
  10.4 3.4 %shard_map.68 = (bf16[256,3584]{1,0:T(8,128)(2,1)S(1)}, bf16[256,512]{1,0:T(8,128)(2,1)S(1)}, bf16[1792,128]{1,0:T(8,128)(2,1)S(1)}, bf16[16,128]{1,0:T(8,128)(2,1)S(1)}) custom-call(bf16[16,16,16]{2,1,0:T(8,128)(2,1)S(1)} %copy-done.1, s32[16,128]{1,0:T(8,128)S(1)} %bitcast.7, bf16[4,256,128]{2,1,0:T(8,128)(2,1)S(1)} %shard_map.67.after_ref), custom_call_target="tpu_custom_call" | custom-call | flops 2000000000 | bytes 3000000 | tf_op jit(solution)/shard_map/pallas_call | solution.py:300
  14.5 2.2 %collective-permute-start.2 = (bf16[1040,128]{1,0:T(8,128)(2,1)S(1)}, bf16[1040,128]{1,0:T(8,128)(2,1)S(1)}, u32[]{:S(2)}, u32[]{:S(2)}) collective-permute-start(bf16[1040,128]{1,0:T(8,128)(2,1)S(1)} %pad_maximum_fusion.2.rest_0_.mixed_ref.refs_0_), channel_id=1, source_target_pairs={{0,2},{1,3},{2,0},{3,1},{4,6},{5,7},{6,4},{7,5},{8,10},{9,11},{10,... | collective-permute-start | bytes 798728 | tf_op jit(solution)/shard_map/ppermute | solution.py:32
  16.7 1.5 %collective-permute-start.3 = (bf16[1040,128]{1,0:T(8,128)(2,1)S(1)}, bf16[1040,128]{1,0:T(8,128)(2,1)S(1)}, u32[]{:S(2)}, u32[]{:S(2)}) collective-permute-start(bf16[1040,128]{1,0:T(8,128)(2,1)S(1)} %pad_maximum_fusion.2.rest_0_.mixed_ref.refs_0_), channel_id=1, source_target_pairs={{0,1},{1,0},{2,3},{3,2},{4,5},{5,4},{6,7},{7,6},{8,9},{9,8},{10,11... | collective-permute-start | bytes 798728 | tf_op jit(solution)/shard_map/ppermute | solution.py:32
  18.2 1.6 %shard_map.69 = f32[4,256,128]{2,1,0:T(8,128)S(1)} custom-call(s32[8,128]{1,0:T(8,128)S(1)} %broadcast_in_dim.2.shift_rows_ref, bf16[16,128]{1,0:T(8,128)(2,1)S(1)} %pad_maximum_fusion.3.coupling_ref, bf16[8,256,128]{2,1,0:T(8,128)(2,1)S(1)} %shard_map.64.own_ref, bf16[8,256,128]{2,1,0:T(8,128)(2,1)S(1)} %collective-permute-done.mate_ref, ...), custom_call_target="tpu_custom_call" | custom-call | flops 500000000 | bytes 1000000 | tf_op jit(solution)/shard_map/pallas_call | solution.py:285
  19.9 2.7 %collective-permute-start.6 = (bf16[1040,128]{1,0:T(8,128)(2,1)S(1)}, bf16[1040,128]{1,0:T(8,128)(2,1)S(1)}, u32[]{:S(2)}, u32[]{:S(2)}) collective-permute-start(bf16[1040,128]{1,0:T(8,128)(2,1)S(1)} %pad_maximum_fusion.1.after_ref.rest_0_.mixed_ref.value_ref.refs_0_), channel_id=1, source_target_pairs={{0,4},{1,5},{2,6},{3,7},{4,0},{5,1},{6,2},{7,3},{8,12},{9,13},{10,... | collective-permute-start | bytes 798728 | tf_op jit(solution)/shard_map/ppermute | solution.py:32
  22.7 1.6 %collective-permute-start.5 = (bf16[1040,128]{1,0:T(8,128)(2,1)S(1)}, bf16[1040,128]{1,0:T(8,128)(2,1)S(1)}, u32[]{:S(2)}, u32[]{:S(2)}) collective-permute-start(bf16[1040,128]{1,0:T(8,128)(2,1)S(1)} %shard_map.70), channel_id=1, source_target_pairs={{0,1},{1,0},{2,3},{3,2},{4,5},{5,4},{6,7},{7,6},{8,9},{9,8},{10,11... | collective-permute-start | bytes 798728 | tf_op jit(solution)/shard_map/ppermute | solution.py:32
  24.3 2.8 %shard_map.71.rest_0_.refs_6_.after_ref = f32[4,256,128]{2,1,0:T(8,128)S(1)} custom-call(bf16[1040,128]{1,0:T(8,128)(2,1)S(1)} %pad_maximum_fusion.2.rest_0_.mixed_ref.refs_0_, bf16[1792,128]{1,0:T(8,128)(2,1)S(1)} %get-tuple-element.12.rest_1_.hot_ref, bf16[256,3584]{1,0:T(8,128)(2,1)S(1)} %get-tuple-element.13.k_ref, ...), custom_call_target="tpu_custom_call" | custom-call | flops 2000000000 | bytes 3000000 | tf_op jit(solution)/shard_map/pallas_call | solution.py:315
  27.7 2.8 %shard_map.72.after_ref.refs_6_ = f32[4,256,128]{2,1,0:T(8,128)S(1)} custom-call(bf16[1040,128]{1,0:T(8,128)(2,1)S(1)} %pad_maximum_fusion.1.after_ref.rest_0_.mixed_ref.value_ref.refs_0_, bf16[1792,128]{1,0:T(8,128)(2,1)S(1)} %get-tuple-element.12.rest_1_.hot_ref, bf16[256,3584]{1,0:T(8,128)(2,1)S(1)} %get-tuple-element.13.k_ref, ...), custom_call_target="tpu_custom_call" | custom-call | flops 2000000000 | bytes 3000000 | tf_op jit(solution)/shard_map/pallas_call | solution.py:315
  30.4 4.0 %collective-permute-done.6.value_ref.refs_1_ = bf16[1040,128]{1,0:T(8,128)(2,1)S(1)} collective-permute-done((bf16[1040,128]{1,0:T(8,128)(2,1)S(1)}, bf16[1040,128]{1,0:T(8,128)(2,1)S(1)}, u32[]{:S(2)}, u32[]{:S(2)}) %collective-permute-start.6) | collective-permute-done | bytes 266272 | tf_op jit(solution)/shard_map/ppermute | solution.py:32
  34.5 1.5 %collective-permute-start.9 = (bf16[528,128]{1,0:T(8,128)(2,1)S(1)}, bf16[528,128]{1,0:T(8,128)(2,1)S(1)}, u32[]{:S(2)}, u32[]{:S(2)}) collective-permute-start(bf16[528,128]{1,0:T(8,128)(2,1)S(1)} %get-tuple-element.16), channel_id=1, source_target_pairs={{0,1},{1,0},{2,3},{3,2},{4,5},{5,4},{6,7},{7,6},{8,9},{9,8},{10,11... | collective-permute-start | bytes 405512 | tf_op jit(solution)/shard_map/ppermute | solution.py:32
  36.7 1.0 %shard_map.75.refs_7_ = bf16[4,256,128]{2,1,0:T(8,128)(2,1)S(1)} custom-call(bf16[1040,128]{1,0:T(8,128)(2,1)S(1)} %pad_maximum_fusion.2.rest_0_.mixed_ref.refs_0_, bf16[1040,128]{1,0:T(8,128)(2,1)S(1)} %collective-permute-done.2.value_ref.refs_1_, bf16[1040,128]{1,0:T(8,128)(2,1)S(1)} %collective-permute-done.3.refs_2_, ...), custom_call_target="tpu_custom_call" | custom-call | flops 1000000000 | bytes 3000000 | tf_op jit(solution)/shard_map/pallas_call | solution.py:373
  37.8 1.0 %shard_map.76.refs_4_.refs_6_ = f32[4,256,128]{2,1,0:T(8,128)S(1)} custom-call(bf16[1040,128]{1,0:T(8,128)(2,1)S(1)} %pad_maximum_fusion.2.rest_0_.mixed_ref.refs_0_, bf16[1040,128]{1,0:T(8,128)(2,1)S(1)} %collective-permute-done.2.value_ref.refs_1_, bf16[1040,128]{1,0:T(8,128)(2,1)S(1)} %collective-permute-done.3.refs_2_, ...), custom_call_target="tpu_custom_call" | custom-call | flops 4000000000 | bytes 3000000 | tf_op jit(solution)/shard_map/pallas_call | solution.py:383
  38.8 1.5 %collective-permute-done.9.refs_3_ = bf16[528,128]{1,0:T(8,128)(2,1)S(1)} collective-permute-done((bf16[528,128]{1,0:T(8,128)(2,1)S(1)}, bf16[528,128]{1,0:T(8,128)(2,1)S(1)}, u32[]{:S(2)}, u32[]{:S(2)}) %collective-permute-start.9) | collective-permute-done | bytes 135200 | tf_op jit(solution)/shard_map/ppermute | solution.py:32
  41.1 2.5 %collective-permute-start.11 = (bf16[2,256,128]{2,1,0:T(8,128)(2,1)S(1)}, bf16[2,256,128]{2,1,0:T(8,128)(2,1)S(1)}, u32[]{:S(2)}, u32[]{:S(2)}) collective-permute-start(bf16[2,256,128]{2,1,0:T(8,128)(2,1)S(1)} %shard_map.79.refs_6_), channel_id=1, source_target_pairs={{0,2},{1,3},{2,0},{3,1},{4,6},{5,7},{6,4},{7,5},{8,10},{9,11},{10,... | collective-permute-start | bytes 393224 | tf_op jit(solution)/shard_map/ppermute | solution.py:32
  45.7 5.2 %collective-permute-done.11 = bf16[2,256,128]{2,1,0:T(8,128)(2,1)S(1)} collective-permute-done((bf16[2,256,128]{2,1,0:T(8,128)(2,1)S(1)}, bf16[2,256,128]{2,1,0:T(8,128)(2,1)S(1)}, u32[]{:S(2)}, u32[]{:S(2)}) %collective-permute-start.11) | collective-permute-done | bytes 131104 | tf_op jit(solution)/shard_map/ppermute | solution.py:32
  51.0 2.0 %collective-permute-done.12 = bf16[2,256,128]{2,1,0:T(8,128)(2,1)S(1)} collective-permute-done((bf16[2,256,128]{2,1,0:T(8,128)(2,1)S(1)}, bf16[2,256,128]{2,1,0:T(8,128)(2,1)S(1)}, u32[]{:S(2)}, u32[]{:S(2)}) %collective-permute-start.12) | collective-permute-done | bytes 131104 | tf_op jit(solution)/shard_map/ppermute | solution.py:32
  53.1 1.0 %pad_maximum_fusion = f32[8,256,128]{2,1,0:T(8,128)} fusion(f32[2,256,128]{2,1,0:T(8,128)S(1)} %convert_add_fusion.1, f32[2,256,128]{2,1,0:T(8,128)S(1)} %convert_add_fusion.2, f32[4,256,128]{2,1,0:T(8,128)S(1)} %convert_add_fusion), kind=kLoop, calls=%fused_computation | loop fusion | flops 524288 | bytes 2097152 | tf_op jit(solution)/shard_map/concatenate | solution.py:444
  (38 shorter events, 5.7 us)
Async XLA Ops:
  0.0 2.3 %collective-permute-start = (bf16[8,256,128]{2,1,0:T(8,128)(2,1)}, bf16[8,256,128]{2,1,0:T(8,128)(2,1)S(1)}, u32[]{:S(2)}, u32[]{:S(2)}) collective-permute-start(bf16[8,256,128]{2,1,0:T(8,128)(2,1)} %bitcast.5), channel_id=1, source_target_pairs={{0,8},{8,0},{16,24},{24,16},{1,9},{9,1},{17,25},{25,17},{2,10},{10... | collective-permute-start | bytes 1572872 | tf_op jit(solution)/shard_map/ppermute | solution.py:32
  0.5 1.0 %copy-start = (bf16[8,16,16,128]{3,2,1,0:T(8,128)(2,1)S(1)}, bf16[8,16,16,128]{3,2,1,0:T(8,128)(2,1)}, u32[]{:S(2)}) copy-start(bf16[8,16,16,128]{3,2,1,0:T(8,128)(2,1)} %param.6) | copy-start | bytes 1572868
  4.5 5.9 %copy-start.1 = (bf16[16,16,16]{2,1,0:T(8,128)(2,1)S(1)}, bf16[16,16,16]{2,1,0:T(8,128)(2,1)}, u32[]{:S(2)}) copy-start(bf16[16,16,16]{2,1,0:T(8,128)(2,1)} %derivative_ref.1) | copy-start | bytes 24580
  4.5 5.9 %copy-start.2 = (s32[128,16]{0,1:T(8,128)S(1)}, s32[128,16]{0,1:T(8,128)}, u32[]{:S(2)}) copy-start(s32[128,16]{0,1:T(8,128)} %param.11) | copy-start | bytes 24580
  4.5 9.9 %collective-permute-start.1 = (bf16[4,256,128]{2,1,0:T(8,128)(2,1)S(1)}, bf16[4,256,128]{2,1,0:T(8,128)(2,1)S(1)}, u32[]{:S(2)}, u32[]{:S(2)}) collective-permute-start(bf16[4,256,128]{2,1,0:T(8,128)(2,1)S(1)} %shard_map.65.rest_0_), channel_id=1, source_target_pairs={{0,16},{8,24},{16,0},{24,8},{1,17},{9,25},{17,1},{25,9},{2,18},{10... | collective-permute-start | bytes 786440 | tf_op jit(solution)/shard_map/ppermute | solution.py:32
  10.3 9.5 %collective-permute-start.4 = (bf16[4,256,128]{2,1,0:T(8,128)(2,1)S(1)}, bf16[4,256,128]{2,1,0:T(8,128)(2,1)S(1)}, u32[]{:S(2)}, u32[]{:S(2)}) collective-permute-start(bf16[4,256,128]{2,1,0:T(8,128)(2,1)S(1)} %shard_map.67.after_ref), channel_id=1, source_target_pairs={{0,16},{8,24},{16,0},{24,8},{1,17},{9,25},{17,1},{25,9},{2,18},{10... | collective-permute-start | bytes 786440 | tf_op jit(solution)/shard_map/ppermute | solution.py:32
  14.5 8.2 %collective-permute-start.2 = (bf16[1040,128]{1,0:T(8,128)(2,1)S(1)}, bf16[1040,128]{1,0:T(8,128)(2,1)S(1)}, u32[]{:S(2)}, u32[]{:S(2)}) collective-permute-start(bf16[1040,128]{1,0:T(8,128)(2,1)S(1)} %pad_maximum_fusion.2.rest_0_.mixed_ref.refs_0_), channel_id=1, source_target_pairs={{0,2},{1,3},{2,0},{3,1},{4,6},{5,7},{6,4},{7,5},{8,10},{9,11},{10,... | collective-permute-start | bytes 798728 | tf_op jit(solution)/shard_map/ppermute | solution.py:32
  16.7 19.9 %collective-permute-start.3 = (bf16[1040,128]{1,0:T(8,128)(2,1)S(1)}, bf16[1040,128]{1,0:T(8,128)(2,1)S(1)}, u32[]{:S(2)}, u32[]{:S(2)}) collective-permute-start(bf16[1040,128]{1,0:T(8,128)(2,1)S(1)} %pad_maximum_fusion.2.rest_0_.mixed_ref.refs_0_), channel_id=1, source_target_pairs={{0,1},{1,0},{2,3},{3,2},{4,5},{5,4},{6,7},{7,6},{8,9},{9,8},{10,11... | collective-permute-start | bytes 798728 | tf_op jit(solution)/shard_map/ppermute | solution.py:32
  19.9 14.5 %collective-permute-start.6 = (bf16[1040,128]{1,0:T(8,128)(2,1)S(1)}, bf16[1040,128]{1,0:T(8,128)(2,1)S(1)}, u32[]{:S(2)}, u32[]{:S(2)}) collective-permute-start(bf16[1040,128]{1,0:T(8,128)(2,1)S(1)} %pad_maximum_fusion.1.after_ref.rest_0_.mixed_ref.value_ref.refs_0_), channel_id=1, source_target_pairs={{0,4},{1,5},{2,6},{3,7},{4,0},{5,1},{6,2},{7,3},{8,12},{9,13},{10,... | collective-permute-start | bytes 798728 | tf_op jit(solution)/shard_map/ppermute | solution.py:32
  22.7 13.9 %collective-permute-start.5 = (bf16[1040,128]{1,0:T(8,128)(2,1)S(1)}, bf16[1040,128]{1,0:T(8,128)(2,1)S(1)}, u32[]{:S(2)}, u32[]{:S(2)}) collective-permute-start(bf16[1040,128]{1,0:T(8,128)(2,1)S(1)} %shard_map.70), channel_id=1, source_target_pairs={{0,1},{1,0},{2,3},{3,2},{4,5},{5,4},{6,7},{7,6},{8,9},{9,8},{10,11... | collective-permute-start | bytes 798728 | tf_op jit(solution)/shard_map/ppermute | solution.py:32
  27.1 11.7 %collective-permute-start.8 = (bf16[1040,128]{1,0:T(8,128)(2,1)S(1)}, bf16[1040,128]{1,0:T(8,128)(2,1)S(1)}, u32[]{:S(2)}, u32[]{:S(2)}) collective-permute-start(bf16[1040,128]{1,0:T(8,128)(2,1)S(1)} %shard_map.77), channel_id=1, source_target_pairs={{0,1},{1,0},{2,3},{3,2},{4,5},{5,4},{6,7},{7,6},{8,9},{9,8},{10,11... | collective-permute-start | bytes 798728 | tf_op jit(solution)/shard_map/ppermute | solution.py:32
  34.5 5.8 %collective-permute-start.9 = (bf16[528,128]{1,0:T(8,128)(2,1)S(1)}, bf16[528,128]{1,0:T(8,128)(2,1)S(1)}, u32[]{:S(2)}, u32[]{:S(2)}) collective-permute-start(bf16[528,128]{1,0:T(8,128)(2,1)S(1)} %get-tuple-element.16), channel_id=1, source_target_pairs={{0,1},{1,0},{2,3},{3,2},{4,5},{5,4},{6,7},{7,6},{8,9},{9,8},{10,11... | collective-permute-start | bytes 405512 | tf_op jit(solution)/shard_map/ppermute | solution.py:32
  36.0 7.6 %collective-permute-start.10 = (bf16[512,128]{1,0:T(8,128)(2,1)S(1)}, bf16[512,128]{1,0:T(8,128)(2,1)S(1)}, u32[]{:S(2)}, u32[]{:S(2)}) collective-permute-start(bf16[512,128]{1,0:T(8,128)(2,1)S(1)} %get-tuple-element.14.refs_4_.refs_6_), channel_id=1, source_target_pairs={{0,1},{1,0},{2,3},{3,2},{4,5},{5,4},{6,7},{7,6},{8,9},{9,8},{10,11... | collective-permute-start | bytes 393224 | tf_op jit(solution)/shard_map/ppermute | solution.py:32
  37.7 15.3 %collective-permute-start.7 = (bf16[4,256,128]{2,1,0:T(8,128)(2,1)S(1)}, bf16[4,256,128]{2,1,0:T(8,128)(2,1)S(1)}, u32[]{:S(2)}, u32[]{:S(2)}) collective-permute-start(bf16[4,256,128]{2,1,0:T(8,128)(2,1)S(1)} %shard_map.75.refs_7_), channel_id=1, source_target_pairs={{0,4},{1,5},{2,6},{3,7},{4,0},{5,1},{6,2},{7,3},{8,12},{9,13},{10,... | collective-permute-start | bytes 786440 | tf_op jit(solution)/shard_map/ppermute | solution.py:32
  41.1 9.9 %collective-permute-start.11 = (bf16[2,256,128]{2,1,0:T(8,128)(2,1)S(1)}, bf16[2,256,128]{2,1,0:T(8,128)(2,1)S(1)}, u32[]{:S(2)}, u32[]{:S(2)}) collective-permute-start(bf16[2,256,128]{2,1,0:T(8,128)(2,1)S(1)} %shard_map.79.refs_6_), channel_id=1, source_target_pairs={{0,2},{1,3},{2,0},{3,1},{4,6},{5,7},{6,4},{7,5},{8,10},{9,11},{10,... | collective-permute-start | bytes 393224 | tf_op jit(solution)/shard_map/ppermute | solution.py:32
  44.3 8.7 %collective-permute-start.12 = (bf16[2,256,128]{2,1,0:T(8,128)(2,1)S(1)}, bf16[2,256,128]{2,1,0:T(8,128)(2,1)S(1)}, u32[]{:S(2)}, u32[]{:S(2)}) collective-permute-start(bf16[2,256,128]{2,1,0:T(8,128)(2,1)S(1)} %shard_map.80.refs_7_), channel_id=1, source_target_pairs={{0,2},{1,3},{2,0},{3,1},{4,6},{5,7},{6,4},{7,5},{8,10},{9,11},{10,... | collective-permute-start | bytes 393224 | tf_op jit(solution)/shard_map/ppermute | solution.py:32

commit v13 on v10

--- a/solution.py
+++ b/solution.py
@@ -401,7 +401,7 @@
     local_outer = local_sum(1, [local_inner])
     far_beside = send(ordered(outer, [(0, sizes[1] * square)], local_inner), [1])
     straight = [0] * len(near)
-    counts = [sizes[1] - sizes[1] // 2, sizes[1] // 2]
+    counts = [sizes[1] // 4, sizes[1] - sizes[1] // 4]
     skips = [0, counts[0]]
     pieces = [(skip * square, (skip + count) * square) for skip, count in zip(skips, counts)]
 

time: 52.6 us -> 53 us (level)
  waiting for transfers between devices: 9.22 us -> 10.1 us
    ppermute x13, waiting for transfers between devices: 9.22 us -> 10.1 us  [swap(): return lax.ppermute(value, axis, [(i, i ^ mask) for i in range(count)])]
where the time goes in v13:
time: 53 us; the launch traced here: 52.8 us
  Pallas kernels  19.7 us (37%)
  starting transfers between devices  18.8 us (35%)
  waiting for transfers between devices  10.1 us (19%)
  other arithmetic  2.11 us (4%)
  local copies, waits for them, and re-layouts  1.78 us (3%)
    ppermute x13, starting transfers between devices, swap(): return lax.ppermute(value, axis, [(i, i ^ mask) for i in range(count)])  18.8 us
    ppermute x13, waiting for transfers between devices, swap(): return lax.ppermute(value, axis, [(i, i ^ mask) for i in range(count)])  10.1 us
    pallas_call x4, Pallas kernels, mix(): pl.pallas_call(functools.partial(mix_kernel, group, firsts[chunk]), out_s...  6.01 us
    pallas_call x2, Pallas kernels, local_sum(): pl.pallas_call(local_kernel, out_shape=jax.ShapeDtypeStruct((sizes[chunk]...  5.56 us
    pallas_call x1, Pallas kernels, prepare(): pl.pallas_call(prepare_kernel, out_shape=(jax.ShapeDtypeStruct((square, l...  3.36 us
    pallas_call x3, Pallas kernels, away_sums(): pl.pallas_call(functools.partial(away_kernel, offsets), out_shape=(block,...  2.24 us
    pallas_call x3, Pallas kernels, stay_sum(): pl.pallas_call(functools.partial(stay_kernel, offsets, skip), out_shape=j...  2.23 us
  transfers between devices with their start and end apart: 13, of which 6 were waited for; matrix products, arithmetic and copies ran while one was open for 2% of the time, Pallas kernels for 35%

profile of v13, /device:TPU:0, one launch (start us, length us, event | category | flops | bytes accessed | tf_op | source)
XLA Modules:
  0.0 52.8 jit_solution(1734829796563941266)
XLA Ops:
  0.5 1.0 %copy-done = bf16[8,16,16,128]{3,2,1,0:T(8,128)(2,1)S(1)} copy-done((bf16[8,16,16,128]{3,2,1,0:T(8,128)(2,1)S(1)}, bf16[8,16,16,128]{3,2,1,0:T(8,128)(2,1)}, u32[]{:S(2)}) %copy-start) | copy-done | bytes 524312
  3.0 1.4 %shard_map.65.rest_0_ = bf16[4,256,128]{2,1,0:T(8,128)(2,1)S(1)} custom-call(s32[8,128]{1,0:T(8,128)S(1)} %broadcast_in_dim.2.shift_rows_ref, bf16[16,128]{1,0:T(8,128)(2,1)S(1)} %pad_maximum_fusion.3.coupling_ref, bf16[8,256,128]{2,1,0:T(8,128)(2,1)S(1)} %shard_map.64.own_ref, bf16[8,256,128]{2,1,0:T(8,128)(2,1)S(1)} %collective-permute-done.mate_ref), custom_call_target="tpu_custom_call" | custom-call | flops 500000000 | bytes 1000000 | tf_op jit(solution)/shard_map/pallas_call | solution.py:285
  4.5 2.8 %collective-permute-start.1 = (bf16[4,256,128]{2,1,0:T(8,128)(2,1)S(1)}, bf16[4,256,128]{2,1,0:T(8,128)(2,1)S(1)}, u32[]{:S(2)}, u32[]{:S(2)}) collective-permute-start(bf16[4,256,128]{2,1,0:T(8,128)(2,1)S(1)} %shard_map.65.rest_0_), channel_id=1, source_target_pairs={{0,16},{8,24},{16,0},{24,8},{1,17},{9,25},{17,1},{25,9},{2,18},{10... | collective-permute-start | bytes 786440 | tf_op jit(solution)/shard_map/ppermute | solution.py:32
  7.3 1.6 %shard_map.66.rest_0_ = f32[4,256,128]{2,1,0:T(8,128)S(1)} custom-call(s32[8,128]{1,0:T(8,128)S(1)} %broadcast_in_dim.2.shift_rows_ref, bf16[16,128]{1,0:T(8,128)(2,1)S(1)} %pad_maximum_fusion.3.coupling_ref, bf16[8,256,128]{2,1,0:T(8,128)(2,1)S(1)} %shard_map.64.own_ref, bf16[8,256,128]{2,1,0:T(8,128)(2,1)S(1)} %collective-permute-done.mate_ref, ...), custom_call_target="tpu_custom_call" | custom-call | flops 500000000 | bytes 1000000 | tf_op jit(solution)/shard_map/pallas_call | solution.py:285
  8.9 1.4 %shard_map.67.after_ref = bf16[4,256,128]{2,1,0:T(8,128)(2,1)S(1)} custom-call(s32[8,128]{1,0:T(8,128)S(1)} %broadcast_in_dim.2.shift_rows_ref, bf16[16,128]{1,0:T(8,128)(2,1)S(1)} %pad_maximum_fusion.3.coupling_ref, bf16[8,256,128]{2,1,0:T(8,128)(2,1)S(1)} %shard_map.64.own_ref, bf16[8,256,128]{2,1,0:T(8,128)(2,1)S(1)} %collective-permute-done.mate_ref, ...), custom_call_target="tpu_custom_call" | custom-call | flops 500000000 | bytes 1000000 | tf_op jit(solution)/shard_map/pallas_call | solution.py:285
  10.4 3.4 %shard_map.68 = (bf16[256,3584]{1,0:T(8,128)(2,1)S(1)}, bf16[256,512]{1,0:T(8,128)(2,1)S(1)}, bf16[1792,128]{1,0:T(8,128)(2,1)S(1)}, bf16[16,128]{1,0:T(8,128)(2,1)S(1)}) custom-call(bf16[16,16,16]{2,1,0:T(8,128)(2,1)S(1)} %copy-done.1, s32[16,128]{1,0:T(8,128)S(1)} %bitcast.7, bf16[4,256,128]{2,1,0:T(8,128)(2,1)S(1)} %shard_map.67.after_ref), custom_call_target="tpu_custom_call" | custom-call | flops 2000000000 | bytes 3000000 | tf_op jit(solution)/shard_map/pallas_call | solution.py:300
  14.5 2.2 %collective-permute-start.2 = (bf16[1040,128]{1,0:T(8,128)(2,1)S(1)}, bf16[1040,128]{1,0:T(8,128)(2,1)S(1)}, u32[]{:S(2)}, u32[]{:S(2)}) collective-permute-start(bf16[1040,128]{1,0:T(8,128)(2,1)S(1)} %pad_maximum_fusion.2.rest_0_.mixed_ref.refs_0_), channel_id=1, source_target_pairs={{0,2},{1,3},{2,0},{3,1},{4,6},{5,7},{6,4},{7,5},{8,10},{9,11},{10,... | collective-permute-start | bytes 798728 | tf_op jit(solution)/shard_map/ppermute | solution.py:32
  16.7 1.5 %collective-permute-start.3 = (bf16[1040,128]{1,0:T(8,128)(2,1)S(1)}, bf16[1040,128]{1,0:T(8,128)(2,1)S(1)}, u32[]{:S(2)}, u32[]{:S(2)}) collective-permute-start(bf16[1040,128]{1,0:T(8,128)(2,1)S(1)} %pad_maximum_fusion.2.rest_0_.mixed_ref.refs_0_), channel_id=1, source_target_pairs={{0,1},{1,0},{2,3},{3,2},{4,5},{5,4},{6,7},{7,6},{8,9},{9,8},{10,11... | collective-permute-start | bytes 798728 | tf_op jit(solution)/shard_map/ppermute | solution.py:32
  18.2 1.6 %shard_map.69 = f32[4,256,128]{2,1,0:T(8,128)S(1)} custom-call(s32[8,128]{1,0:T(8,128)S(1)} %broadcast_in_dim.2.shift_rows_ref, bf16[16,128]{1,0:T(8,128)(2,1)S(1)} %pad_maximum_fusion.3.coupling_ref, bf16[8,256,128]{2,1,0:T(8,128)(2,1)S(1)} %shard_map.64.own_ref, bf16[8,256,128]{2,1,0:T(8,128)(2,1)S(1)} %collective-permute-done.mate_ref, ...), custom_call_target="tpu_custom_call" | custom-call | flops 500000000 | bytes 1000000 | tf_op jit(solution)/shard_map/pallas_call | solution.py:285
  19.9 2.7 %collective-permute-start.6 = (bf16[1040,128]{1,0:T(8,128)(2,1)S(1)}, bf16[1040,128]{1,0:T(8,128)(2,1)S(1)}, u32[]{:S(2)}, u32[]{:S(2)}) collective-permute-start(bf16[1040,128]{1,0:T(8,128)(2,1)S(1)} %pad_maximum_fusion.1.after_ref.rest_0_.mixed_ref.value_ref.refs_0_), channel_id=1, source_target_pairs={{0,4},{1,5},{2,6},{3,7},{4,0},{5,1},{6,2},{7,3},{8,12},{9,13},{10,... | collective-permute-start | bytes 798728 | tf_op jit(solution)/shard_map/ppermute | solution.py:32
  22.7 1.6 %collective-permute-start.5 = (bf16[1040,128]{1,0:T(8,128)(2,1)S(1)}, bf16[1040,128]{1,0:T(8,128)(2,1)S(1)}, u32[]{:S(2)}, u32[]{:S(2)}) collective-permute-start(bf16[1040,128]{1,0:T(8,128)(2,1)S(1)} %shard_map.70), channel_id=1, source_target_pairs={{0,1},{1,0},{2,3},{3,2},{4,5},{5,4},{6,7},{7,6},{8,9},{9,8},{10,11... | collective-permute-start | bytes 798728 | tf_op jit(solution)/shard_map/ppermute | solution.py:32
  24.3 2.8 %shard_map.71.rest_0_.refs_6_.after_ref = f32[4,256,128]{2,1,0:T(8,128)S(1)} custom-call(bf16[1040,128]{1,0:T(8,128)(2,1)S(1)} %pad_maximum_fusion.2.rest_0_.mixed_ref.refs_0_, bf16[1792,128]{1,0:T(8,128)(2,1)S(1)} %get-tuple-element.12.rest_1_.hot_ref, bf16[256,3584]{1,0:T(8,128)(2,1)S(1)} %get-tuple-element.13.k_ref, ...), custom_call_target="tpu_custom_call" | custom-call | flops 2000000000 | bytes 3000000 | tf_op jit(solution)/shard_map/pallas_call | solution.py:315
  27.7 2.8 %shard_map.72.refs_4_.refs_6_ = f32[4,256,128]{2,1,0:T(8,128)S(1)} custom-call(bf16[1040,128]{1,0:T(8,128)(2,1)S(1)} %pad_maximum_fusion.1.after_ref.rest_0_.mixed_ref.value_ref.refs_0_, bf16[1792,128]{1,0:T(8,128)(2,1)S(1)} %get-tuple-element.12.rest_1_.hot_ref, bf16[256,3584]{1,0:T(8,128)(2,1)S(1)} %get-tuple-element.13.k_ref, ...), custom_call_target="tpu_custom_call" | custom-call | flops 2000000000 | bytes 3000000 | tf_op jit(solution)/shard_map/pallas_call | solution.py:315
  30.5 1.3 %collective-permute-done.5.refs_3_ = bf16[1040,128]{1,0:T(8,128)(2,1)S(1)} collective-permute-done((bf16[1040,128]{1,0:T(8,128)(2,1)S(1)}, bf16[1040,128]{1,0:T(8,128)(2,1)S(1)}, u32[]{:S(2)}, u32[]{:S(2)}) %collective-permute-start.5) | collective-permute-done | bytes 266272 | tf_op jit(solution)/shard_map/ppermute | solution.py:32
  31.8 1.0 %shard_map.74.after_ref = bf16[4,256,128]{2,1,0:T(8,128)(2,1)S(1)} custom-call(bf16[1040,128]{1,0:T(8,128)(2,1)S(1)} %pad_maximum_fusion.2.rest_0_.mixed_ref.refs_0_, bf16[1040,128]{1,0:T(8,128)(2,1)S(1)} %collective-permute-done.2.value_ref.refs_1_, bf16[1040,128]{1,0:T(8,128)(2,1)S(1)} %collective-permute-done.3.refs_2_, ...), custom_call_target="tpu_custom_call" | custom-call | flops 1000000000 | bytes 3000000 | tf_op jit(solution)/shard_map/pallas_call | solution.py:373
  32.9 2.5 %collective-permute-start.7 = (bf16[4,256,128]{2,1,0:T(8,128)(2,1)S(1)}, bf16[4,256,128]{2,1,0:T(8,128)(2,1)S(1)}, u32[]{:S(2)}, u32[]{:S(2)}) collective-permute-start(bf16[4,256,128]{2,1,0:T(8,128)(2,1)S(1)} %shard_map.74.after_ref), channel_id=1, source_target_pairs={{0,4},{1,5},{2,6},{3,7},{4,0},{5,1},{6,2},{7,3},{8,12},{9,13},{10,... | collective-permute-start | bytes 786440 | tf_op jit(solution)/shard_map/ppermute | solution.py:32
  35.4 2.6 %collective-permute-done.6.value_ref.refs_1_ = bf16[1040,128]{1,0:T(8,128)(2,1)S(1)} collective-permute-done((bf16[1040,128]{1,0:T(8,128)(2,1)S(1)}, bf16[1040,128]{1,0:T(8,128)(2,1)S(1)}, u32[]{:S(2)}, u32[]{:S(2)}) %collective-permute-start.6) | collective-permute-done | bytes 266272 | tf_op jit(solution)/shard_map/ppermute | solution.py:32
  38.0 1.4 %collective-permute-start.9 = (bf16[272,128]{1,0:T(8,128)(2,1)S(1)}, bf16[272,128]{1,0:T(8,128)(2,1)S(1)}, u32[]{:S(2)}, u32[]{:S(2)}) collective-permute-start(bf16[272,128]{1,0:T(8,128)(2,1)S(1)} %get-tuple-element.16), channel_id=1, source_target_pairs={{0,1},{1,0},{2,3},{3,2},{4,5},{5,4},{6,7},{7,6},{8,9},{9,8},{10,11... | collective-permute-start | bytes 208904 | tf_op jit(solution)/shard_map/ppermute | solution.py:32
  40.1 1.0 %shard_map.76.refs_4_.refs_6_ = f32[4,256,128]{2,1,0:T(8,128)S(1)} custom-call(bf16[1040,128]{1,0:T(8,128)(2,1)S(1)} %pad_maximum_fusion.2.rest_0_.mixed_ref.refs_0_, bf16[1040,128]{1,0:T(8,128)(2,1)S(1)} %collective-permute-done.2.value_ref.refs_1_, bf16[1040,128]{1,0:T(8,128)(2,1)S(1)} %collective-permute-done.3.refs_2_, ...), custom_call_target="tpu_custom_call" | custom-call | flops 4000000000 | bytes 3000000 | tf_op jit(solution)/shard_map/pallas_call | solution.py:383
  41.1 1.3 %collective-permute-done.9.refs_3_ = bf16[272,128]{1,0:T(8,128)(2,1)S(1)} collective-permute-done((bf16[272,128]{1,0:T(8,128)(2,1)S(1)}, bf16[272,128]{1,0:T(8,128)(2,1)S(1)}, u32[]{:S(2)}, u32[]{:S(2)}) %collective-permute-start.9) | collective-permute-done | bytes 69664 | tf_op jit(solution)/shard_map/ppermute | solution.py:32
  43.7 1.4 %collective-permute-done.10.refs_3_ = bf16[768,128]{1,0:T(8,128)(2,1)S(1)} collective-permute-done((bf16[768,128]{1,0:T(8,128)(2,1)S(1)}, bf16[768,128]{1,0:T(8,128)(2,1)S(1)}, u32[]{:S(2)}, u32[]{:S(2)}) %collective-permute-start.10) | collective-permute-done | bytes 196640 | tf_op jit(solution)/shard_map/ppermute | solution.py:32
  45.8 1.6 %collective-permute-start.12 = (bf16[3,256,128]{2,1,0:T(8,128)(2,1)S(1)}, bf16[3,256,128]{2,1,0:T(8,128)(2,1)S(1)}, u32[]{:S(2)}, u32[]{:S(2)}) collective-permute-start(bf16[3,256,128]{2,1,0:T(8,128)(2,1)S(1)} %shard_map.80.refs_7_), channel_id=1, source_target_pairs={{0,2},{1,3},{2,0},{3,1},{4,6},{5,7},{6,4},{7,5},{8,10},{9,11},{10,... | collective-permute-start | bytes 589832 | tf_op jit(solution)/shard_map/ppermute | solution.py:32
  48.7 3.0 %collective-permute-done.12 = bf16[3,256,128]{2,1,0:T(8,128)(2,1)S(1)} collective-permute-done((bf16[3,256,128]{2,1,0:T(8,128)(2,1)S(1)}, bf16[3,256,128]{2,1,0:T(8,128)(2,1)S(1)}, u32[]{:S(2)}, u32[]{:S(2)}) %collective-permute-start.12) | collective-permute-done | bytes 196640 | tf_op jit(solution)/shard_map/ppermute | solution.py:32
  51.7 1.0 %pad_maximum_fusion = f32[8,256,128]{2,1,0:T(8,128)} fusion(f32[3,256,128]{2,1,0:T(8,128)S(1)} %convert_add_fusion.1, f32[1,256,128]{2,1,0:T(8,128)S(1)} %convert_add_fusion.2, f32[4,256,128]{2,1,0:T(8,128)S(1)} %convert_add_fusion), kind=kLoop, calls=%fused_computation | loop fusion | flops 524288 | bytes 2097152 | tf_op jit(solution)/shard_map/concatenate | solution.py:444
  (38 shorter events, 7.6 us)
Async XLA Ops:
  0.0 2.3 %collective-permute-start = (bf16[8,256,128]{2,1,0:T(8,128)(2,1)}, bf16[8,256,128]{2,1,0:T(8,128)(2,1)S(1)}, u32[]{:S(2)}, u32[]{:S(2)}) collective-permute-start(bf16[8,256,128]{2,1,0:T(8,128)(2,1)} %bitcast.5), channel_id=1, source_target_pairs={{0,8},{8,0},{16,24},{24,16},{1,9},{9,1},{17,25},{25,17},{2,10},{10... | collective-permute-start | bytes 1572872 | tf_op jit(solution)/shard_map/ppermute | solution.py:32
  0.5 1.0 %copy-start = (bf16[8,16,16,128]{3,2,1,0:T(8,128)(2,1)S(1)}, bf16[8,16,16,128]{3,2,1,0:T(8,128)(2,1)}, u32[]{:S(2)}) copy-start(bf16[8,16,16,128]{3,2,1,0:T(8,128)(2,1)} %param.6) | copy-start | bytes 1572868
  4.5 5.9 %copy-start.1 = (bf16[16,16,16]{2,1,0:T(8,128)(2,1)S(1)}, bf16[16,16,16]{2,1,0:T(8,128)(2,1)}, u32[]{:S(2)}) copy-start(bf16[16,16,16]{2,1,0:T(8,128)(2,1)} %derivative_ref.1) | copy-start | bytes 24580
  4.5 5.9 %copy-start.2 = (s32[128,16]{0,1:T(8,128)S(1)}, s32[128,16]{0,1:T(8,128)}, u32[]{:S(2)}) copy-start(s32[128,16]{0,1:T(8,128)} %param.11) | copy-start | bytes 24580
  4.5 9.9 %collective-permute-start.1 = (bf16[4,256,128]{2,1,0:T(8,128)(2,1)S(1)}, bf16[4,256,128]{2,1,0:T(8,128)(2,1)S(1)}, u32[]{:S(2)}, u32[]{:S(2)}) collective-permute-start(bf16[4,256,128]{2,1,0:T(8,128)(2,1)S(1)} %shard_map.65.rest_0_), channel_id=1, source_target_pairs={{0,16},{8,24},{16,0},{24,8},{1,17},{9,25},{17,1},{25,9},{2,18},{10... | collective-permute-start | bytes 786440 | tf_op jit(solution)/shard_map/ppermute | solution.py:32
  10.3 9.5 %collective-permute-start.4 = (bf16[4,256,128]{2,1,0:T(8,128)(2,1)S(1)}, bf16[4,256,128]{2,1,0:T(8,128)(2,1)S(1)}, u32[]{:S(2)}, u32[]{:S(2)}) collective-permute-start(bf16[4,256,128]{2,1,0:T(8,128)(2,1)S(1)} %shard_map.67.after_ref), channel_id=1, source_target_pairs={{0,16},{8,24},{16,0},{24,8},{1,17},{9,25},{17,1},{25,9},{2,18},{10... | collective-permute-start | bytes 786440 | tf_op jit(solution)/shard_map/ppermute | solution.py:32
  14.5 8.2 %collective-permute-start.2 = (bf16[1040,128]{1,0:T(8,128)(2,1)S(1)}, bf16[1040,128]{1,0:T(8,128)(2,1)S(1)}, u32[]{:S(2)}, u32[]{:S(2)}) collective-permute-start(bf16[1040,128]{1,0:T(8,128)(2,1)S(1)} %pad_maximum_fusion.2.rest_0_.mixed_ref.refs_0_), channel_id=1, source_target_pairs={{0,2},{1,3},{2,0},{3,1},{4,6},{5,7},{6,4},{7,5},{8,10},{9,11},{10,... | collective-permute-start | bytes 798728 | tf_op jit(solution)/shard_map/ppermute | solution.py:32
  16.7 13.7 %collective-permute-start.3 = (bf16[1040,128]{1,0:T(8,128)(2,1)S(1)}, bf16[1040,128]{1,0:T(8,128)(2,1)S(1)}, u32[]{:S(2)}, u32[]{:S(2)}) collective-permute-start(bf16[1040,128]{1,0:T(8,128)(2,1)S(1)} %pad_maximum_fusion.2.rest_0_.mixed_ref.refs_0_), channel_id=1, source_target_pairs={{0,1},{1,0},{2,3},{3,2},{4,5},{5,4},{6,7},{7,6},{8,9},{9,8},{10,11... | collective-permute-start | bytes 798728 | tf_op jit(solution)/shard_map/ppermute | solution.py:32
  19.9 18.0 %collective-permute-start.6 = (bf16[1040,128]{1,0:T(8,128)(2,1)S(1)}, bf16[1040,128]{1,0:T(8,128)(2,1)S(1)}, u32[]{:S(2)}, u32[]{:S(2)}) collective-permute-start(bf16[1040,128]{1,0:T(8,128)(2,1)S(1)} %pad_maximum_fusion.1.after_ref.rest_0_.mixed_ref.value_ref.refs_0_), channel_id=1, source_target_pairs={{0,4},{1,5},{2,6},{3,7},{4,0},{5,1},{6,2},{7,3},{8,12},{9,13},{10,... | collective-permute-start | bytes 798728 | tf_op jit(solution)/shard_map/ppermute | solution.py:32
  22.7 9.0 %collective-permute-start.5 = (bf16[1040,128]{1,0:T(8,128)(2,1)S(1)}, bf16[1040,128]{1,0:T(8,128)(2,1)S(1)}, u32[]{:S(2)}, u32[]{:S(2)}) collective-permute-start(bf16[1040,128]{1,0:T(8,128)(2,1)S(1)} %shard_map.70), channel_id=1, source_target_pairs={{0,1},{1,0},{2,3},{3,2},{4,5},{5,4},{6,7},{7,6},{8,9},{9,8},{10,11... | collective-permute-start | bytes 798728 | tf_op jit(solution)/shard_map/ppermute | solution.py:32
  27.1 14.0 %collective-permute-start.8 = (bf16[1040,128]{1,0:T(8,128)(2,1)S(1)}, bf16[1040,128]{1,0:T(8,128)(2,1)S(1)}, u32[]{:S(2)}, u32[]{:S(2)}) collective-permute-start(bf16[1040,128]{1,0:T(8,128)(2,1)S(1)} %shard_map.77), channel_id=1, source_target_pairs={{0,1},{1,0},{2,3},{3,2},{4,5},{5,4},{6,7},{7,6},{8,9},{9,8},{10,11... | collective-permute-start | bytes 798728 | tf_op jit(solution)/shard_map/ppermute | solution.py:32
  32.9 15.8 %collective-permute-start.7 = (bf16[4,256,128]{2,1,0:T(8,128)(2,1)S(1)}, bf16[4,256,128]{2,1,0:T(8,128)(2,1)S(1)}, u32[]{:S(2)}, u32[]{:S(2)}) collective-permute-start(bf16[4,256,128]{2,1,0:T(8,128)(2,1)S(1)} %shard_map.74.after_ref), channel_id=1, source_target_pairs={{0,4},{1,5},{2,6},{3,7},{4,0},{5,1},{6,2},{7,3},{8,12},{9,13},{10,... | collective-permute-start | bytes 786440 | tf_op jit(solution)/shard_map/ppermute | solution.py:32
  38.0 4.4 %collective-permute-start.9 = (bf16[272,128]{1,0:T(8,128)(2,1)S(1)}, bf16[272,128]{1,0:T(8,128)(2,1)S(1)}, u32[]{:S(2)}, u32[]{:S(2)}) collective-permute-start(bf16[272,128]{1,0:T(8,128)(2,1)S(1)} %get-tuple-element.16), channel_id=1, source_target_pairs={{0,1},{1,0},{2,3},{3,2},{4,5},{5,4},{6,7},{7,6},{8,9},{9,8},{10,11... | collective-permute-start | bytes 208904 | tf_op jit(solution)/shard_map/ppermute | solution.py:32
  39.4 5.7 %collective-permute-start.10 = (bf16[768,128]{1,0:T(8,128)(2,1)S(1)}, bf16[768,128]{1,0:T(8,128)(2,1)S(1)}, u32[]{:S(2)}, u32[]{:S(2)}) collective-permute-start(bf16[768,128]{1,0:T(8,128)(2,1)S(1)} %get-tuple-element.15.refs_7_), channel_id=1, source_target_pairs={{0,1},{1,0},{2,3},{3,2},{4,5},{5,4},{6,7},{7,6},{8,9},{9,8},{10,11... | collective-permute-start | bytes 589832 | tf_op jit(solution)/shard_map/ppermute | solution.py:32
  43.0 5.5 %collective-permute-start.11 = (bf16[1,256,128]{2,1,0:T(8,128)(2,1)S(1)}, bf16[1,256,128]{2,1,0:T(8,128)(2,1)S(1)}, u32[]{:S(2)}, u32[]{:S(2)}) collective-permute-start(bf16[1,256,128]{2,1,0:T(8,128)(2,1)S(1)} %shard_map.79.refs_6_), channel_id=1, source_target_pairs={{0,2},{1,3},{2,0},{3,1},{4,6},{5,7},{6,4},{7,5},{8,10},{9,11},{10,... | collective-permute-start | bytes 196616 | tf_op jit(solution)/shard_map/ppermute | solution.py:32
  45.8 5.9 %collective-permute-start.12 = (bf16[3,256,128]{2,1,0:T(8,128)(2,1)S(1)}, bf16[3,256,128]{2,1,0:T(8,128)(2,1)S(1)}, u32[]{:S(2)}, u32[]{:S(2)}) collective-permute-start(bf16[3,256,128]{2,1,0:T(8,128)(2,1)S(1)} %shard_map.80.refs_7_), channel_id=1, source_target_pairs={{0,2},{1,3},{2,0},{3,1},{4,6},{5,7},{6,4},{7,5},{8,10},{9,11},{10,... | collective-permute-start | bytes 589832 | tf_op jit(solution)/shard_map/ppermute | solution.py:32

commit v14 on v10

--- a/solution.py
+++ b/solution.py
@@ -398,7 +398,6 @@
     [turned] = ordered(across, [(0, sizes[0] * square)], outer)
     near = [inner, across, beside] + send([turned], [1])
     local_inner = local_sum(0, [outer])
-    local_outer = local_sum(1, [local_inner])
     far_beside = send(ordered(outer, [(0, sizes[1] * square)], local_inner), [1])
     straight = [0] * len(near)
     counts = [sizes[1] - sizes[1] // 2, sizes[1] // 2]
@@ -410,13 +409,14 @@
         steps = [[value[index] for value in passed] for index in range(len(pieces))]
         return passed[0][-1], [send(values, [1] * len(values)) for values in steps]
 
-    behind = local_outer
+    behind = local_inner
     near_hots = one_hots(near, high, behind)
     near_away = away_sums(sizes[0], near, straight, near_hots, high, behind)
     near_back = send(near_away, high)
     behind, far_next = pass_far(near_away[0])
     stay_inner = stay_sum(sizes[0], 0, near, straight, near_hots, local_inner, [behind])
-    after = stay_inner
+    local_outer = local_sum(1, [stay_inner])
+    after = local_outer
     far_hots = None
     far_away, far_lists = [], []
     for index, (first, _) in enumerate(pieces):

time: 52.6 us -> 58 us (1.10)
  waiting for transfers between devices: 9.22 us -> 13.5 us
  starting transfers between devices: 19.2 us -> 20.3 us
    ppermute x13, waiting for transfers between devices: 9.22 us -> 13.5 us  [swap(): return lax.ppermute(value, axis, [(i, i ^ mask) for i in range(count)])]
    ppermute x13, starting transfers between devices: 19.2 us -> 20.3 us  [swap(): return lax.ppermute(value, axis, [(i, i ^ mask) for i in range(count)])]
  transfers between devices with their start and end apart: 13 -> 13, of which waited for: 6 -> 5; matrix products, arithmetic and copies ran while one was open for 2% -> 2% of each run, Pallas kernels for 35% -> 32%
where the time goes in v14:
time: 58 us; the launch traced here: 57.8 us
  starting transfers between devices  20.3 us (35%)
  Pallas kernels  19.9 us (34%)
  waiting for transfers between devices  13.5 us (23%)
  other arithmetic  2.11 us (4%)
  local copies, waits for them, and re-layouts  1.78 us (3%)
    ppermute x13, starting transfers between devices, swap(): return lax.ppermute(value, axis, [(i, i ^ mask) for i in range(count)])  20.3 us
    ppermute x13, waiting for transfers between devices, swap(): return lax.ppermute(value, axis, [(i, i ^ mask) for i in range(count)])  13.5 us
    pallas_call x4, Pallas kernels, mix(): pl.pallas_call(functools.partial(mix_kernel, group, firsts[chunk]), out_s...  6.01 us
    pallas_call x2, Pallas kernels, local_sum(): pl.pallas_call(local_kernel, out_shape=jax.ShapeDtypeStruct((sizes[chunk]...  5.58 us
    pallas_call x1, Pallas kernels, prepare(): pl.pallas_call(prepare_kernel, out_shape=(jax.ShapeDtypeStruct((square, l...  3.36 us
    pallas_call x3, Pallas kernels, stay_sum(): pl.pallas_call(functools.partial(stay_kernel, offsets, skip), out_shape=j...  2.3 us
    pallas_call x3, Pallas kernels, away_sums(): pl.pallas_call(functools.partial(away_kernel, offsets), out_shape=(block,...  2.3 us
  transfers between devices with their start and end apart: 13, of which 5 were waited for; matrix products, arithmetic and copies ran while one was open for 2% of the time, Pallas kernels for 32%

profile of v14, /device:TPU:0, one launch (start us, length us, event | category | flops | bytes accessed | tf_op | source)
XLA Modules:
  0.0 57.8 jit_solution(16090730977958939105)
XLA Ops:
  0.5 1.0 %copy-done = bf16[8,16,16,128]{3,2,1,0:T(8,128)(2,1)S(1)} copy-done((bf16[8,16,16,128]{3,2,1,0:T(8,128)(2,1)S(1)}, bf16[8,16,16,128]{3,2,1,0:T(8,128)(2,1)}, u32[]{:S(2)}) %copy-start) | copy-done | bytes 524312
  1.5 0.8 %fusion = (bf16[8,128]{1,0:T(8,128)(2,1)S(1)}, bf16[8,128]{1,0:T(8,128)(2,1)S(1)}) fusion(f32[8,128]{1,0:T(8,128)} %param.8, f32[8]{0:T(128)} %param.9), kind=kLoop, calls=%fused_computation.10 | loop fusion | flops 4096 | bytes 8224 | tf_op jit(solution)/shard_map/convert
  3.0 1.4 %shard_map.65.rest_0_ = bf16[4,256,128]{2,1,0:T(8,128)(2,1)S(1)} custom-call(s32[8,128]{1,0:T(8,128)S(1)} %broadcast_in_dim.2.shift_rows_ref, bf16[16,128]{1,0:T(8,128)(2,1)S(1)} %pad_maximum_fusion.3.coupling_ref, bf16[8,256,128]{2,1,0:T(8,128)(2,1)S(1)} %shard_map.64.own_ref, bf16[8,256,128]{2,1,0:T(8,128)(2,1)S(1)} %collective-permute-done.mate_ref), custom_call_target="tpu_custom_call" | custom-call | flops 500000000 | bytes 1000000 | tf_op jit(solution)/shard_map/pallas_call | solution.py:285
  4.5 2.8 %collective-permute-start.1 = (bf16[4,256,128]{2,1,0:T(8,128)(2,1)S(1)}, bf16[4,256,128]{2,1,0:T(8,128)(2,1)S(1)}, u32[]{:S(2)}, u32[]{:S(2)}) collective-permute-start(bf16[4,256,128]{2,1,0:T(8,128)(2,1)S(1)} %shard_map.65.rest_0_), channel_id=1, source_target_pairs={{0,16},{8,24},{16,0},{24,8},{1,17},{9,25},{17,1},{25,9},{2,18},{10... | collective-permute-start | bytes 786440 | tf_op jit(solution)/shard_map/ppermute | solution.py:32
  7.3 1.6 %shard_map.66.rest_0_ = f32[4,256,128]{2,1,0:T(8,128)S(1)} custom-call(s32[8,128]{1,0:T(8,128)S(1)} %broadcast_in_dim.2.shift_rows_ref, bf16[16,128]{1,0:T(8,128)(2,1)S(1)} %pad_maximum_fusion.3.coupling_ref, bf16[8,256,128]{2,1,0:T(8,128)(2,1)S(1)} %shard_map.64.own_ref, bf16[8,256,128]{2,1,0:T(8,128)(2,1)S(1)} %collective-permute-done.mate_ref, ...), custom_call_target="tpu_custom_call" | custom-call | flops 500000000 | bytes 1000000 | tf_op jit(solution)/shard_map/pallas_call | solution.py:285
  8.9 1.4 %shard_map.67.after_ref = bf16[4,256,128]{2,1,0:T(8,128)(2,1)S(1)} custom-call(s32[8,128]{1,0:T(8,128)S(1)} %broadcast_in_dim.2.shift_rows_ref, bf16[16,128]{1,0:T(8,128)(2,1)S(1)} %pad_maximum_fusion.3.coupling_ref, bf16[8,256,128]{2,1,0:T(8,128)(2,1)S(1)} %shard_map.64.own_ref, bf16[8,256,128]{2,1,0:T(8,128)(2,1)S(1)} %collective-permute-done.mate_ref, ...), custom_call_target="tpu_custom_call" | custom-call | flops 500000000 | bytes 1000000 | tf_op jit(solution)/shard_map/pallas_call | solution.py:285
  10.4 3.4 %shard_map.68 = (bf16[256,3584]{1,0:T(8,128)(2,1)S(1)}, bf16[256,512]{1,0:T(8,128)(2,1)S(1)}, bf16[1792,128]{1,0:T(8,128)(2,1)S(1)}, bf16[16,128]{1,0:T(8,128)(2,1)S(1)}) custom-call(bf16[16,16,16]{2,1,0:T(8,128)(2,1)S(1)} %copy-done.1, s32[16,128]{1,0:T(8,128)S(1)} %bitcast.7, bf16[4,256,128]{2,1,0:T(8,128)(2,1)S(1)} %shard_map.67.after_ref), custom_call_target="tpu_custom_call" | custom-call | flops 2000000000 | bytes 3000000 | tf_op jit(solution)/shard_map/pallas_call | solution.py:300
  14.5 2.2 %collective-permute-start.2 = (bf16[1040,128]{1,0:T(8,128)(2,1)S(1)}, bf16[1040,128]{1,0:T(8,128)(2,1)S(1)}, u32[]{:S(2)}, u32[]{:S(2)}) collective-permute-start(bf16[1040,128]{1,0:T(8,128)(2,1)S(1)} %pad_maximum_fusion.2.rest_0_.mixed_ref.refs_0_), channel_id=1, source_target_pairs={{0,2},{1,3},{2,0},{3,1},{4,6},{5,7},{6,4},{7,5},{8,10},{9,11},{10,... | collective-permute-start | bytes 798728 | tf_op jit(solution)/shard_map/ppermute | solution.py:32
  16.7 1.5 %collective-permute-start.3 = (bf16[1040,128]{1,0:T(8,128)(2,1)S(1)}, bf16[1040,128]{1,0:T(8,128)(2,1)S(1)}, u32[]{:S(2)}, u32[]{:S(2)}) collective-permute-start(bf16[1040,128]{1,0:T(8,128)(2,1)S(1)} %pad_maximum_fusion.2.rest_0_.mixed_ref.refs_0_), channel_id=1, source_target_pairs={{0,1},{1,0},{2,3},{3,2},{4,5},{5,4},{6,7},{7,6},{8,9},{9,8},{10,11... | collective-permute-start | bytes 798728 | tf_op jit(solution)/shard_map/ppermute | solution.py:32
  18.2 1.6 %shard_map.69 = f32[4,256,128]{2,1,0:T(8,128)S(1)} custom-call(s32[8,128]{1,0:T(8,128)S(1)} %broadcast_in_dim.2.shift_rows_ref, bf16[16,128]{1,0:T(8,128)(2,1)S(1)} %pad_maximum_fusion.3.coupling_ref, bf16[8,256,128]{2,1,0:T(8,128)(2,1)S(1)} %shard_map.64.own_ref, bf16[8,256,128]{2,1,0:T(8,128)(2,1)S(1)} %collective-permute-done.mate_ref, ...), custom_call_target="tpu_custom_call" | custom-call | flops 500000000 | bytes 1000000 | tf_op jit(solution)/shard_map/pallas_call | solution.py:285
  19.9 2.4 %collective-permute-done.2.value_ref.refs_1_ = bf16[1040,128]{1,0:T(8,128)(2,1)S(1)} collective-permute-done((bf16[1040,128]{1,0:T(8,128)(2,1)S(1)}, bf16[1040,128]{1,0:T(8,128)(2,1)S(1)}, u32[]{:S(2)}, u32[]{:S(2)}) %collective-permute-start.2) | collective-permute-done | bytes 266272 | tf_op jit(solution)/shard_map/ppermute | solution.py:32
  22.3 1.8 %collective-permute-start.5 = (bf16[1040,128]{1,0:T(8,128)(2,1)S(1)}, bf16[1040,128]{1,0:T(8,128)(2,1)S(1)}, u32[]{:S(2)}, u32[]{:S(2)}) collective-permute-start(bf16[1040,128]{1,0:T(8,128)(2,1)S(1)} %shard_map.70), channel_id=1, source_target_pairs={{0,1},{1,0},{2,3},{3,2},{4,5},{5,4},{6,7},{7,6},{8,9},{9,8},{10,11... | collective-permute-start | bytes 798728 | tf_op jit(solution)/shard_map/ppermute | solution.py:32
  24.1 2.6 %collective-permute-start.6 = (bf16[1040,128]{1,0:T(8,128)(2,1)S(1)}, bf16[1040,128]{1,0:T(8,128)(2,1)S(1)}, u32[]{:S(2)}, u32[]{:S(2)}) collective-permute-start(bf16[1040,128]{1,0:T(8,128)(2,1)S(1)} %pad_maximum_fusion.1.after_ref.rest_0_.value_ref.mixed_ref.refs_0_), channel_id=1, source_target_pairs={{0,4},{1,5},{2,6},{3,7},{4,0},{5,1},{6,2},{7,3},{8,12},{9,13},{10,... | collective-permute-start | bytes 798728 | tf_op jit(solution)/shard_map/ppermute | solution.py:32
  26.7 2.8 %shard_map.71.refs_4_.refs_6_.after_ref = f32[4,256,128]{2,1,0:T(8,128)S(1)} custom-call(bf16[1040,128]{1,0:T(8,128)(2,1)S(1)} %pad_maximum_fusion.2.rest_0_.mixed_ref.refs_0_, bf16[1792,128]{1,0:T(8,128)(2,1)S(1)} %get-tuple-element.12.rest_1_.hot_ref, bf16[256,3584]{1,0:T(8,128)(2,1)S(1)} %get-tuple-element.13.k_ref, ...), custom_call_target="tpu_custom_call" | custom-call | flops 2000000000 | bytes 3000000 | tf_op jit(solution)/shard_map/pallas_call | solution.py:315
  30.2 1.0 %shard_map.73.after_ref = bf16[4,256,128]{2,1,0:T(8,128)(2,1)S(1)} custom-call(bf16[1040,128]{1,0:T(8,128)(2,1)S(1)} %pad_maximum_fusion.2.rest_0_.mixed_ref.refs_0_, bf16[1040,128]{1,0:T(8,128)(2,1)S(1)} %collective-permute-done.2.value_ref.refs_1_, bf16[1040,128]{1,0:T(8,128)(2,1)S(1)} %collective-permute-done.3.refs_2_, ...), custom_call_target="tpu_custom_call" | custom-call | flops 1000000000 | bytes 3000000 | tf_op jit(solution)/shard_map/pallas_call | solution.py:373
  31.2 4.0 %collective-permute-start.7 = (bf16[4,256,128]{2,1,0:T(8,128)(2,1)S(1)}, bf16[4,256,128]{2,1,0:T(8,128)(2,1)S(1)}, u32[]{:S(2)}, u32[]{:S(2)}) collective-permute-start(bf16[4,256,128]{2,1,0:T(8,128)(2,1)S(1)} %shard_map.73.after_ref), channel_id=1, source_target_pairs={{0,4},{1,5},{2,6},{3,7},{4,0},{5,1},{6,2},{7,3},{8,12},{9,13},{10,... | collective-permute-start | bytes 786440 | tf_op jit(solution)/shard_map/ppermute | solution.py:32
  35.2 8.3 %collective-permute-done.6.value_ref.refs_1_ = bf16[1040,128]{1,0:T(8,128)(2,1)S(1)} collective-permute-done((bf16[1040,128]{1,0:T(8,128)(2,1)S(1)}, bf16[1040,128]{1,0:T(8,128)(2,1)S(1)}, u32[]{:S(2)}, u32[]{:S(2)}) %collective-permute-start.6) | collective-permute-done | bytes 266272 | tf_op jit(solution)/shard_map/ppermute | solution.py:32
  44.2 1.5 %collective-permute-start.10 = (bf16[512,128]{1,0:T(8,128)(2,1)S(1)}, bf16[512,128]{1,0:T(8,128)(2,1)S(1)}, u32[]{:S(2)}, u32[]{:S(2)}) collective-permute-start(bf16[512,128]{1,0:T(8,128)(2,1)S(1)} %get-tuple-element.15.refs_7_), channel_id=1, source_target_pairs={{0,1},{1,0},{2,3},{3,2},{4,5},{5,4},{6,7},{7,6},{8,9},{9,8},{10,11... | collective-permute-start | bytes 393224 | tf_op jit(solution)/shard_map/ppermute | solution.py:32
  45.7 1.0 %shard_map.75.rest_0_ = f32[4,256,128]{2,1,0:T(8,128)S(1)} custom-call(bf16[1040,128]{1,0:T(8,128)(2,1)S(1)} %pad_maximum_fusion.2.rest_0_.mixed_ref.refs_0_, bf16[1040,128]{1,0:T(8,128)(2,1)S(1)} %collective-permute-done.2.value_ref.refs_1_, bf16[1040,128]{1,0:T(8,128)(2,1)S(1)} %collective-permute-done.3.refs_2_, ...), custom_call_target="tpu_custom_call" | custom-call | flops 4000000000 | bytes 3000000 | tf_op jit(solution)/shard_map/pallas_call | solution.py:383
  46.7 2.8 %shard_map.77.refs_4_.refs_6_ = f32[4,256,128]{2,1,0:T(8,128)S(1)} custom-call(bf16[1040,128]{1,0:T(8,128)(2,1)S(1)} %pad_maximum_fusion.1.after_ref.rest_0_.value_ref.mixed_ref.refs_0_, bf16[1792,128]{1,0:T(8,128)(2,1)S(1)} %get-tuple-element.12.rest_1_.hot_ref, bf16[256,3584]{1,0:T(8,128)(2,1)S(1)} %get-tuple-element.13.k_ref, ...), custom_call_target="tpu_custom_call" | custom-call | flops 2000000000 | bytes 3000000 | tf_op jit(solution)/shard_map/pallas_call | solution.py:315
  51.4 1.7 %collective-permute-start.12 = (bf16[2,256,128]{2,1,0:T(8,128)(2,1)S(1)}, bf16[2,256,128]{2,1,0:T(8,128)(2,1)S(1)}, u32[]{:S(2)}, u32[]{:S(2)}) collective-permute-start(bf16[2,256,128]{2,1,0:T(8,128)(2,1)S(1)} %shard_map.80.refs_7_), channel_id=1, source_target_pairs={{0,2},{1,3},{2,0},{3,1},{4,6},{5,7},{6,4},{7,5},{8,10},{9,11},{10,... | collective-permute-start | bytes 393224 | tf_op jit(solution)/shard_map/ppermute | solution.py:32
  54.5 0.8 %collective-permute-done.11 = bf16[2,256,128]{2,1,0:T(8,128)(2,1)S(1)} collective-permute-done((bf16[2,256,128]{2,1,0:T(8,128)(2,1)S(1)}, bf16[2,256,128]{2,1,0:T(8,128)(2,1)S(1)}, u32[]{:S(2)}, u32[]{:S(2)}) %collective-permute-start.11) | collective-permute-done | bytes 131104 | tf_op jit(solution)/shard_map/ppermute | solution.py:32
  55.4 1.4 %collective-permute-done.12 = bf16[2,256,128]{2,1,0:T(8,128)(2,1)S(1)} collective-permute-done((bf16[2,256,128]{2,1,0:T(8,128)(2,1)S(1)}, bf16[2,256,128]{2,1,0:T(8,128)(2,1)S(1)}, u32[]{:S(2)}, u32[]{:S(2)}) %collective-permute-start.12) | collective-permute-done | bytes 131104 | tf_op jit(solution)/shard_map/ppermute | solution.py:32
  56.8 1.0 %pad_maximum_fusion = f32[8,256,128]{2,1,0:T(8,128)} fusion(f32[2,256,128]{2,1,0:T(8,128)S(1)} %convert_add_fusion.1, f32[2,256,128]{2,1,0:T(8,128)S(1)} %convert_add_fusion.2, f32[4,256,128]{2,1,0:T(8,128)S(1)} %convert_add_fusion), kind=kLoop, calls=%fused_computation | loop fusion | flops 524288 | bytes 2097152 | tf_op jit(solution)/shard_map/concatenate | solution.py:444
  (38 shorter events, 6.7 us)
Async XLA Ops:
  0.0 2.3 %collective-permute-start = (bf16[8,256,128]{2,1,0:T(8,128)(2,1)}, bf16[8,256,128]{2,1,0:T(8,128)(2,1)S(1)}, u32[]{:S(2)}, u32[]{:S(2)}) collective-permute-start(bf16[8,256,128]{2,1,0:T(8,128)(2,1)} %bitcast.5), channel_id=1, source_target_pairs={{0,8},{8,0},{16,24},{24,16},{1,9},{9,1},{17,25},{25,17},{2,10},{10... | collective-permute-start | bytes 1572872 | tf_op jit(solution)/shard_map/ppermute | solution.py:32
  0.5 1.0 %copy-start = (bf16[8,16,16,128]{3,2,1,0:T(8,128)(2,1)S(1)}, bf16[8,16,16,128]{3,2,1,0:T(8,128)(2,1)}, u32[]{:S(2)}) copy-start(bf16[8,16,16,128]{3,2,1,0:T(8,128)(2,1)} %param.6) | copy-start | bytes 1572868
  4.5 5.9 %copy-start.1 = (bf16[16,16,16]{2,1,0:T(8,128)(2,1)S(1)}, bf16[16,16,16]{2,1,0:T(8,128)(2,1)}, u32[]{:S(2)}) copy-start(bf16[16,16,16]{2,1,0:T(8,128)(2,1)} %derivative_ref.1) | copy-start | bytes 24580
  4.5 5.9 %copy-start.2 = (s32[128,16]{0,1:T(8,128)S(1)}, s32[128,16]{0,1:T(8,128)}, u32[]{:S(2)}) copy-start(s32[128,16]{0,1:T(8,128)} %param.11) | copy-start | bytes 24580
  4.5 9.9 %collective-permute-start.1 = (bf16[4,256,128]{2,1,0:T(8,128)(2,1)S(1)}, bf16[4,256,128]{2,1,0:T(8,128)(2,1)S(1)}, u32[]{:S(2)}, u32[]{:S(2)}) collective-permute-start(bf16[4,256,128]{2,1,0:T(8,128)(2,1)S(1)} %shard_map.65.rest_0_), channel_id=1, source_target_pairs={{0,16},{8,24},{16,0},{24,8},{1,17},{9,25},{17,1},{25,9},{2,18},{10... | collective-permute-start | bytes 786440 | tf_op jit(solution)/shard_map/ppermute | solution.py:32
  10.3 9.5 %collective-permute-start.4 = (bf16[4,256,128]{2,1,0:T(8,128)(2,1)S(1)}, bf16[4,256,128]{2,1,0:T(8,128)(2,1)S(1)}, u32[]{:S(2)}, u32[]{:S(2)}) collective-permute-start(bf16[4,256,128]{2,1,0:T(8,128)(2,1)S(1)} %shard_map.67.after_ref), channel_id=1, source_target_pairs={{0,16},{8,24},{16,0},{24,8},{1,17},{9,25},{17,1},{25,9},{2,18},{10... | collective-permute-start | bytes 786440 | tf_op jit(solution)/shard_map/ppermute | solution.py:32
  14.5 7.8 %collective-permute-start.2 = (bf16[1040,128]{1,0:T(8,128)(2,1)S(1)}, bf16[1040,128]{1,0:T(8,128)(2,1)S(1)}, u32[]{:S(2)}, u32[]{:S(2)}) collective-permute-start(bf16[1040,128]{1,0:T(8,128)(2,1)S(1)} %pad_maximum_fusion.2.rest_0_.mixed_ref.refs_0_), channel_id=1, source_target_pairs={{0,2},{1,3},{2,0},{3,1},{4,6},{5,7},{6,4},{7,5},{8,10},{9,11},{10,... | collective-permute-start | bytes 798728 | tf_op jit(solution)/shard_map/ppermute | solution.py:32
  16.7 13.3 %collective-permute-start.3 = (bf16[1040,128]{1,0:T(8,128)(2,1)S(1)}, bf16[1040,128]{1,0:T(8,128)(2,1)S(1)}, u32[]{:S(2)}, u32[]{:S(2)}) collective-permute-start(bf16[1040,128]{1,0:T(8,128)(2,1)S(1)} %pad_maximum_fusion.2.rest_0_.mixed_ref.refs_0_), channel_id=1, source_target_pairs={{0,1},{1,0},{2,3},{3,2},{4,5},{5,4},{6,7},{7,6},{8,9},{9,8},{10,11... | collective-permute-start | bytes 798728 | tf_op jit(solution)/shard_map/ppermute | solution.py:32
  22.3 7.7 %collective-permute-start.5 = (bf16[1040,128]{1,0:T(8,128)(2,1)S(1)}, bf16[1040,128]{1,0:T(8,128)(2,1)S(1)}, u32[]{:S(2)}, u32[]{:S(2)}) collective-permute-start(bf16[1040,128]{1,0:T(8,128)(2,1)S(1)} %shard_map.70), channel_id=1, source_target_pairs={{0,1},{1,0},{2,3},{3,2},{4,5},{5,4},{6,7},{7,6},{8,9},{9,8},{10,11... | collective-permute-start | bytes 798728 | tf_op jit(solution)/shard_map/ppermute | solution.py:32
  24.1 19.5 %collective-permute-start.6 = (bf16[1040,128]{1,0:T(8,128)(2,1)S(1)}, bf16[1040,128]{1,0:T(8,128)(2,1)S(1)}, u32[]{:S(2)}, u32[]{:S(2)}) collective-permute-start(bf16[1040,128]{1,0:T(8,128)(2,1)S(1)} %pad_maximum_fusion.1.after_ref.rest_0_.value_ref.mixed_ref.refs_0_), channel_id=1, source_target_pairs={{0,4},{1,5},{2,6},{3,7},{4,0},{5,1},{6,2},{7,3},{8,12},{9,13},{10,... | collective-permute-start | bytes 798728 | tf_op jit(solution)/shard_map/ppermute | solution.py:32
  29.5 20.0 %collective-permute-start.8 = (bf16[1040,128]{1,0:T(8,128)(2,1)S(1)}, bf16[1040,128]{1,0:T(8,128)(2,1)S(1)}, u32[]{:S(2)}, u32[]{:S(2)}) collective-permute-start(bf16[1040,128]{1,0:T(8,128)(2,1)S(1)} %shard_map.76), channel_id=1, source_target_pairs={{0,1},{1,0},{2,3},{3,2},{4,5},{5,4},{6,7},{7,6},{8,9},{9,8},{10,11... | collective-permute-start | bytes 798728 | tf_op jit(solution)/shard_map/ppermute | solution.py:32
  31.2 23.3 %collective-permute-start.7 = (bf16[4,256,128]{2,1,0:T(8,128)(2,1)S(1)}, bf16[4,256,128]{2,1,0:T(8,128)(2,1)S(1)}, u32[]{:S(2)}, u32[]{:S(2)}) collective-permute-start(bf16[4,256,128]{2,1,0:T(8,128)(2,1)S(1)} %shard_map.73.after_ref), channel_id=1, source_target_pairs={{0,4},{1,5},{2,6},{3,7},{4,0},{5,1},{6,2},{7,3},{8,12},{9,13},{10,... | collective-permute-start | bytes 786440 | tf_op jit(solution)/shard_map/ppermute | solution.py:32
  43.6 5.9 %collective-permute-start.9 = (bf16[528,128]{1,0:T(8,128)(2,1)S(1)}, bf16[528,128]{1,0:T(8,128)(2,1)S(1)}, u32[]{:S(2)}, u32[]{:S(2)}) collective-permute-start(bf16[528,128]{1,0:T(8,128)(2,1)S(1)} %get-tuple-element.16), channel_id=1, source_target_pairs={{0,1},{1,0},{2,3},{3,2},{4,5},{5,4},{6,7},{7,6},{8,9},{9,8},{10,11... | collective-permute-start | bytes 405512 | tf_op jit(solution)/shard_map/ppermute | solution.py:32
  44.2 6.6 %collective-permute-start.10 = (bf16[512,128]{1,0:T(8,128)(2,1)S(1)}, bf16[512,128]{1,0:T(8,128)(2,1)S(1)}, u32[]{:S(2)}, u32[]{:S(2)}) collective-permute-start(bf16[512,128]{1,0:T(8,128)(2,1)S(1)} %get-tuple-element.15.refs_7_), channel_id=1, source_target_pairs={{0,1},{1,0},{2,3},{3,2},{4,5},{5,4},{6,7},{7,6},{8,9},{9,8},{10,11... | collective-permute-start | bytes 393224 | tf_op jit(solution)/shard_map/ppermute | solution.py:32
  50.3 5.0 %collective-permute-start.11 = (bf16[2,256,128]{2,1,0:T(8,128)(2,1)S(1)}, bf16[2,256,128]{2,1,0:T(8,128)(2,1)S(1)}, u32[]{:S(2)}, u32[]{:S(2)}) collective-permute-start(bf16[2,256,128]{2,1,0:T(8,128)(2,1)S(1)} %shard_map.79.refs_6_), channel_id=1, source_target_pairs={{0,2},{1,3},{2,0},{3,1},{4,6},{5,7},{6,4},{7,5},{8,10},{9,11},{10,... | collective-permute-start | bytes 393224 | tf_op jit(solution)/shard_map/ppermute | solution.py:32
  51.4 5.4 %collective-permute-start.12 = (bf16[2,256,128]{2,1,0:T(8,128)(2,1)S(1)}, bf16[2,256,128]{2,1,0:T(8,128)(2,1)S(1)}, u32[]{:S(2)}, u32[]{:S(2)}) collective-permute-start(bf16[2,256,128]{2,1,0:T(8,128)(2,1)S(1)} %shard_map.80.refs_7_), channel_id=1, source_target_pairs={{0,2},{1,3},{2,0},{3,1},{4,6},{5,7},{6,4},{7,5},{8,10},{9,11},{10,... | collective-permute-start | bytes 393224 | tf_op jit(solution)/shard_map/ppermute | solution.py:32
